TPU v7x, 32 devices: a whole 2x2x4 slice. The times are simulated.
32 devices in a mesh: dp: 2 (over core), expert: 16 (over z, y, x).
Axes of the slice: x: 2, y: 2, z: 4, core: 2. Of those that a mesh axis runs over, the one named last changes fastest.
Arguments:
- hidden: bfloat16 [4096, 2048], P(('dp', 'expert')), may hold values from -6 to 6
- lengths: int32 [2, 3], P('dp'), may hold values from 1 to 1024, 2048 in all within a row
- slots: int32 [4096], P('dp'), may hold values from 0 to 2047, as said below
- routes: int32 [4096, 8], P(('dp', 'expert')), may hold values from 0 to 15, all different within a row
- order: int32 [4096, 8], P(('dp', 'expert')), may hold values from 0 to 1023, as said below
- gain_in: bfloat16 [2048], P(('dp', 'expert')), may hold values from 0.099609375 to 1.8984375
- w_query: bfloat16 [2048, 4096], P(('dp', 'expert')), may hold values from -0.125 to 0.125
- key_projection_weight: bfloat16 [2048, 512], P(('dp', 'expert')), may hold values from -0.125 to 0.125
- value_projection_weight: bfloat16 [2048, 512], P(('dp', 'expert')), may hold values from -0.125 to 0.125
- gain_q: bfloat16 [128], P(('dp', 'expert')), may hold values from 0.099609375 to 1.8984375
- gain_k: bfloat16 [128], P(('dp', 'expert')), may hold values from 0.099609375 to 1.8984375
- w_out: bfloat16 [4096, 2048], P(('dp', 'expert')), may hold values from -0.75 to 0.75
- gain_mid: bfloat16 [2048], P(('dp', 'expert')), may hold values from 0.099609375 to 1.8984375
- w_router: bfloat16 [2048, 16], P(('dp', 'expert')), may hold values from -0.0625 to 0.0625
- w_gate: bfloat16 [16, 2048, 768], P('expert', 'dp'), may hold values from -0.125 to 0.125
- w_up: bfloat16 [16, 2048, 768], P('expert', 'dp'), may hold values from -0.125 to 0.125
- w_down: bfloat16 [16, 768, 2048], P('expert', None, 'dp'), may hold values from -0.625 to 0.625
- cotangent: bfloat16 [4096, 2048], P(('dp', 'expert')), may hold values from -6 to 6
Outputs:
- result: bfloat16 [4096, 2048], P(('dp', 'expert'))
- grad_hidden: bfloat16 [4096, 2048], P(('dp', 'expert'))
- grad_gain_in: float32 [2048], P(('dp', 'expert'))
- grad_w_query: float32 [2048, 4096], P(('dp', 'expert'))
- grad_w_key: float32 [2048, 512], P(('dp', 'expert'))
- grad_w_value: float32 [2048, 512], P(('dp', 'expert'))
- grad_gain_q: float32 [128], P(('dp', 'expert'))
- grad_gain_k: float32 [128], P(('dp', 'expert'))
- grad_w_out: float32 [4096, 2048], P(('dp', 'expert'))
- grad_gain_mid: float32 [2048], P(('dp', 'expert'))
- grad_w_router: float32 [2048, 16], P(('dp', 'expert'))
- grad_w_gate: float32 [16, 2048, 768], P('expert', 'dp')
- grad_w_up: float32 [16, 2048, 768], P('expert', 'dp')
- grad_w_down: float32 [16, 768, 2048], P('expert', None, 'dp')
Inputs may be any that keep to these rules, and one draw needn't show every extreme that they name: `slots`: within the 2048 rows of each index of dp, every place 0 to 2047 occurs once. `lengths`: each row sums to 2048; its largest entry is 1024. `routes`: A token's 8 experts are different. `order`: within the 128 rows of each device, every number 0 to 1023 occurs once.
All inputs are finite; a program needn't handle non-finite values.
Results may differ from a plain program's by a relative error of at most 0.017.
Values may be sent and summed in bfloat16 or wider, within the bound.
No kernel may reach another device: no remote copies, remote signals or barrier semaphores. Data moves between devices by JAX's collectives and lax.ppermute only.
A program may use at most 384 MiB of HBM per device.

v0:
```python
import math

import jax
import jax.numpy as jnp
from jax import lax
from jax.sharding import PartitionSpec as P

MODEL_WIDTH = 2048
QUERY_HEADS = 32
KEY_VALUE_HEADS = 4
HEAD_SIZE = 128
TOP = 8


EPS = 1e-06
THETA = 1000000.0
MASKED = -1e30


def rms_scale(values, scaling):
    return values * lax.rsqrt(jnp.mean(values * values, axis=-1, keepdims=True) + EPS) * scaling


def rotate(values, cosine, sine_table):
    half = values.shape[-1] // 2
    turned = jnp.concatenate([-values[..., half:], values[..., :half]], axis=-1)
    return values * cosine + turned * sine_table


def rotary_tables(position, width):
    index_float = jnp.arange(width // 2, dtype=jnp.float32)
    freq = jnp.power(jnp.float32(THETA), -2.0 * index_float / width)
    angle = position.astype(jnp.float32)[:, None] * freq[None, :]
    cosine = jnp.concatenate([jnp.cos(angle), jnp.cos(angle)], axis=-1)[:, None, :]
    sine_table = jnp.concatenate([jnp.sin(angle), jnp.sin(angle)], axis=-1)[:, None, :]
    return (cosine, sine_table)


def places(slot_rows, lengths_row):
    seq_ends = jnp.cumsum(lengths_row)
    starts = seq_ends - lengths_row
    segment = jnp.sum((slot_rows[:, None] >= seq_ends[None, :]).astype(jnp.int32), axis=1)
    chosen = segment[:, None] == jnp.arange(lengths_row.shape[0], dtype=jnp.int32)[None, :]
    start_of = jnp.sum(jnp.where(chosen, starts[None, :], 0), axis=1)
    return (segment, slot_rows - start_of)


def fill_slots(route_rows, order_rows, experts, capacity):
    pair_count = route_rows.shape[0] * route_rows.shape[1]
    expert_of = route_rows.reshape(pair_count)
    order_key = order_rows.reshape(pair_count)
    numbered = jnp.arange(pair_count, dtype=jnp.int32)
    inverse = jnp.zeros((pair_count,), jnp.int32).at[order_key].set(numbered)
    ordered = expert_of[inverse]
    onehot = (ordered[:, None] == jnp.arange(experts, dtype=jnp.int32)[None, :]).astype(jnp.int32)
    running = jnp.cumsum(onehot, axis=0)
    rank_of = (jnp.sum(running * onehot, axis=1) - 1)[order_key]
    kept_pairs = rank_of < capacity
    slot_id = jnp.where(kept_pairs, expert_of * capacity + rank_of, experts * capacity)
    return (kept_pairs, slot_id)


def body(
    hidden,
    lengths,
    slots,
    routes,
    order,
    gain_in,
    w_query,
    key_projection_weight,
    value_projection_weight,
    gain_q,
    gain_k,
    w_out,
    gain_mid,
    w_router,
    w_gate,
    w_up,
    w_down,
    cotangent,
):
    local_token_count = hidden.shape[0]
    experts = w_router.shape[1]
    capacity = max(2, (local_token_count * TOP * 9 + 8 * experts - 1) // (8 * experts))
    query_heads_per_group = QUERY_HEADS // KEY_VALUE_HEADS
    block_heads = math.gcd(query_heads_per_group, max(1, 512 // local_token_count))
    blocks = QUERY_HEADS // block_heads
    score_scale = HEAD_SIZE ** (-0.5)
    pair_count = local_token_count * TOP
    key_value_width = KEY_VALUE_HEADS * HEAD_SIZE
    slot_count = experts * capacity
    my_index = lax.axis_index("expert")
    own_slots = lax.dynamic_slice_in_dim(slots, my_index * local_token_count, local_token_count)
    seg_query, position = places(own_slots, lengths[0])
    seg_key, key_position = places(slots, lengths[0])
    cosine, sine_table = rotary_tables(position, HEAD_SIZE)
    visible = (seg_query[:, None] == seg_key[None, :]) & (slots[None, :] <= own_slots[:, None])
    dense_full = (
        lax.all_gather(gain_in, ("dp", "expert"), axis=0, tiled=True),
        lax.all_gather(w_query, ("dp", "expert"), axis=0, tiled=True),
        lax.all_gather(key_projection_weight, ("dp", "expert"), axis=0, tiled=True),
        lax.all_gather(value_projection_weight, ("dp", "expert"), axis=0, tiled=True),
        lax.all_gather(gain_q, ("dp", "expert"), axis=0, tiled=True),
        lax.all_gather(gain_k, ("dp", "expert"), axis=0, tiled=True),
        lax.all_gather(w_out, ("dp", "expert"), axis=0, tiled=True),
        lax.all_gather(gain_mid, ("dp", "expert"), axis=0, tiled=True),
        lax.all_gather(w_router, ("dp", "expert"), axis=0, tiled=True),
    )
    (
        full_in,
        full_query,
        full_key,
        full_value,
        full_qgain,
        full_kgain,
        full_out,
        full_mid,
        full_router,
    ) = dense_full
    x_float = hidden.astype(jnp.float32)
    norm_one, norm_one_back = jax.vjp(rms_scale, x_float, full_in.astype(jnp.float32))
    normalized_input_first = norm_one.astype(jnp.bfloat16)
    query_proj = jnp.dot(
        normalized_input_first, full_query, preferred_element_type=jnp.float32
    ).reshape(local_token_count, QUERY_HEADS, HEAD_SIZE)
    key_projected = jnp.dot(
        normalized_input_first, full_key, preferred_element_type=jnp.float32
    ).reshape(local_token_count, KEY_VALUE_HEADS, HEAD_SIZE)
    value_reduced = jnp.dot(
        normalized_input_first, full_value, preferred_element_type=jnp.float32
    ).astype(jnp.bfloat16)

    def head_norm(projected, scaling):
        return rotate(rms_scale(projected, scaling), cosine, sine_table)

    query_turned, query_back = jax.vjp(head_norm, query_proj, full_qgain.astype(jnp.float32))
    key_turned, key_returned_gradient = jax.vjp(
        head_norm, key_projected, full_kgain.astype(jnp.float32)
    )
    query_reduced = query_turned.astype(jnp.bfloat16)
    key_low = key_turned.astype(jnp.bfloat16)
    own_keys = jnp.concatenate(
        [key_low.reshape(local_token_count, key_value_width), value_reduced], axis=1
    )
    gathered = lax.all_gather(own_keys, "expert", axis=0, tiled=True)
    query_blocks = query_reduced.reshape(
        local_token_count, blocks, block_heads, HEAD_SIZE
    ).transpose(1, 0, 2, 3)
    block_numbers = jnp.arange(blocks, dtype=jnp.int32)

    def forward_block(block_items):
        query_rows, block_index = block_items
        kv_head = block_index * block_heads // query_heads_per_group
        key_rows = lax.dynamic_slice_in_dim(gathered, kv_head * HEAD_SIZE, HEAD_SIZE, 1)
        value_rows = lax.dynamic_slice_in_dim(
            gathered, key_value_width + kv_head * HEAD_SIZE, HEAD_SIZE, 1
        )
        scores = (
            jnp.einsum("qrd,kd->rqk", query_rows, key_rows, preferred_element_type=jnp.float32)
            * score_scale
        )
        scores = jnp.where(visible[None], scores, MASKED)
        top_score = jnp.max(scores, axis=-1, keepdims=True)
        exponent = jnp.exp(scores - top_score)
        row_total = jnp.sum(exponent, axis=-1, keepdims=True)
        weights = (exponent / row_total).astype(jnp.bfloat16)
        mixed_rows = jnp.einsum(
            "rqk,kd->qrd", weights, value_rows, preferred_element_type=jnp.float32
        )
        return (mixed_rows, top_score + jnp.log(row_total))

    attention_blocks, log_sums = lax.map(forward_block, (query_blocks, block_numbers))
    attended = (
        attention_blocks.transpose(1, 0, 2, 3)
        .reshape(local_token_count, QUERY_HEADS * HEAD_SIZE)
        .astype(jnp.bfloat16)
    )
    x_one = x_float + jnp.dot(attended, full_out, preferred_element_type=jnp.float32)
    norm_two, norm_two_back = jax.vjp(rms_scale, x_one, full_mid.astype(jnp.float32))
    xn_two = norm_two.astype(jnp.bfloat16)
    logits = jnp.dot(xn_two, full_router, preferred_element_type=jnp.float32)
    chooser = routes[:, :, None] == jnp.arange(experts, dtype=jnp.int32)[None, None, :]
    chosen = jnp.sum(jnp.where(chooser, logits[:, None, :], 0.0), axis=-1)
    gate_probs = jax.nn.softmax(chosen, axis=-1)
    kept_pairs, slot_id = fill_slots(routes, order, experts, capacity)
    kept_rows = kept_pairs.reshape(local_token_count, TOP)
    pair_number = jnp.arange(pair_count, dtype=jnp.int32)
    source = (
        jnp.zeros((slot_count + 1,), jnp.int32).at[slot_id].set(pair_number // TOP)[:slot_count]
    )
    filled = jnp.zeros((slot_count + 1,), jnp.int32).at[slot_id].set(1)[:slot_count] > 0
    owner_pair = jnp.zeros((slot_count + 1,), jnp.int32).at[slot_id].set(pair_number)[:slot_count]
    safe_slot = jnp.where(kept_pairs, slot_id, 0)
    sending = jnp.where(filled[:, None], xn_two[source], jnp.zeros((), jnp.bfloat16)).reshape(
        experts, capacity, MODEL_WIDTH
    )
    arrived = lax.all_to_all(sending, "expert", split_axis=0, concat_axis=1, tiled=True)
    expert_full = (
        lax.all_gather(w_gate, "dp", axis=1, tiled=True),
        lax.all_gather(w_up, "dp", axis=1, tiled=True),
        lax.all_gather(w_down, "dp", axis=2, tiled=True),
    )
    gate_full, up_full, down_full = expert_full
    gate_pre = jnp.einsum("erd,edf->erf", arrived, gate_full, preferred_element_type=jnp.float32)
    up_pre = jnp.einsum("erd,edf->erf", arrived, up_full, preferred_element_type=jnp.float32)
    activation = (jax.nn.silu(gate_pre) * up_pre).astype(jnp.bfloat16)
    returned = jnp.einsum(
        "erf,efd->erd", activation, down_full, preferred_element_type=jnp.float32
    ).astype(jnp.bfloat16)
    combined = lax.all_to_all(returned, "expert", split_axis=1, concat_axis=0, tiled=True).reshape(
        slot_count, MODEL_WIDTH
    )
    picked = (
        jnp.where(kept_pairs[:, None], combined[safe_slot], jnp.zeros((), jnp.bfloat16))
        .reshape(local_token_count, TOP, MODEL_WIDTH)
        .astype(jnp.float32)
    )
    weighted = jnp.where(kept_rows, gate_probs, 0.0)
    mixture = jnp.sum(weighted[:, :, None] * picked, axis=1)
    result = (x_one + mixture).astype(jnp.bfloat16)
    upstream = cotangent.astype(jnp.float32)
    again_dense = (
        lax.all_gather(gain_in, ("dp", "expert"), axis=0, tiled=True),
        lax.all_gather(w_query, ("dp", "expert"), axis=0, tiled=True),
        lax.all_gather(key_projection_weight, ("dp", "expert"), axis=0, tiled=True),
        lax.all_gather(value_projection_weight, ("dp", "expert"), axis=0, tiled=True),
        lax.all_gather(gain_q, ("dp", "expert"), axis=0, tiled=True),
        lax.all_gather(gain_k, ("dp", "expert"), axis=0, tiled=True),
        lax.all_gather(w_out, ("dp", "expert"), axis=0, tiled=True),
        lax.all_gather(gain_mid, ("dp", "expert"), axis=0, tiled=True),
        lax.all_gather(w_router, ("dp", "expert"), axis=0, tiled=True),
    )
    again_keys = lax.all_gather(own_keys, "expert", axis=0, tiled=True)
    again_experts = (
        lax.all_gather(w_gate, "dp", axis=1, tiled=True),
        lax.all_gather(w_up, "dp", axis=1, tiled=True),
        lax.all_gather(w_down, "dp", axis=2, tiled=True),
    )
    query_again = again_dense[1]
    key_again = again_dense[2]
    value_again = again_dense[3]
    out_again = again_dense[6]
    router_again = again_dense[8]
    gate_again, up_again, down_again = again_experts
    gate_grad = jnp.where(kept_rows, jnp.sum(upstream[:, None, :] * picked, axis=-1), 0.0)
    slot_gate = weighted.reshape(pair_count)[owner_pair]
    back_send = (
        jnp.where(filled[:, None], slot_gate[:, None] * upstream[source], 0.0)
        .astype(jnp.bfloat16)
        .reshape(experts, capacity, MODEL_WIDTH)
    )
    arrived_grad = lax.all_to_all(back_send, "expert", split_axis=0, concat_axis=1, tiled=True)
    act_grad = jnp.einsum(
        "erd,efd->erf", arrived_grad, down_again, preferred_element_type=jnp.float32
    )
    grad_down = jnp.einsum(
        "erf,erd->efd", activation, arrived_grad, preferred_element_type=jnp.float32
    )
    logistic = jax.nn.sigmoid(gate_pre)
    gate_low = (act_grad * up_pre * logistic * (1.0 + gate_pre * (1.0 - logistic))).astype(
        jnp.bfloat16
    )
    up_low = (act_grad * gate_pre * logistic).astype(jnp.bfloat16)
    grad_gate = jnp.einsum("erd,erf->edf", arrived, gate_low, preferred_element_type=jnp.float32)
    grad_up = jnp.einsum("erd,erf->edf", arrived, up_low, preferred_element_type=jnp.float32)
    slot_grad = (
        jnp.einsum("erf,edf->erd", gate_low, gate_again, preferred_element_type=jnp.float32)
        + jnp.einsum("erf,edf->erd", up_low, up_again, preferred_element_type=jnp.float32)
    ).astype(jnp.bfloat16)
    expert_grads = (
        lax.psum_scatter(
            grad_gate.astype(jnp.bfloat16), "dp", scatter_dimension=1, tiled=True
        ).astype(jnp.float32),
        lax.psum_scatter(
            grad_up.astype(jnp.bfloat16), "dp", scatter_dimension=1, tiled=True
        ).astype(jnp.float32),
        lax.psum_scatter(
            grad_down.astype(jnp.bfloat16), "dp", scatter_dimension=2, tiled=True
        ).astype(jnp.float32),
    )
    came_back = lax.all_to_all(
        slot_grad, "expert", split_axis=1, concat_axis=0, tiled=True
    ).reshape(slot_count, MODEL_WIDTH)
    pair_grad = jnp.where(
        kept_pairs[:, None], came_back[safe_slot].astype(jnp.float32), 0.0
    ).reshape(local_token_count, TOP, MODEL_WIDTH)
    chosen_grad = gate_probs * (gate_grad - jnp.sum(gate_probs * gate_grad, axis=-1, keepdims=True))
    logit_grad = jnp.sum(jnp.where(chooser, chosen_grad[:, :, None], 0.0), axis=1).astype(
        jnp.bfloat16
    )
    grad_router = jnp.dot(xn_two.T, logit_grad, preferred_element_type=jnp.float32)
    xn_two_grad = jnp.sum(pair_grad, axis=1) + jnp.dot(
        logit_grad, router_again.T, preferred_element_type=jnp.float32
    )
    x_one_norm_grad, grad_mid = norm_two_back(xn_two_grad)
    x_one_grad = upstream + x_one_norm_grad
    branch_grad = x_one_grad.astype(jnp.bfloat16)
    grad_out = jnp.dot(attended.T, branch_grad, preferred_element_type=jnp.float32)
    attended_grad = jnp.dot(branch_grad, out_again.T, preferred_element_type=jnp.float32).astype(
        jnp.bfloat16
    )
    grad_blocks = attended_grad.reshape(
        local_token_count, blocks, block_heads, HEAD_SIZE
    ).transpose(1, 0, 2, 3)

    def backward_block(key_terms, block_items):
        query_rows, grad_rows, log_sum, block_index = block_items
        kv_head = block_index * block_heads // query_heads_per_group
        key_rows = lax.dynamic_slice_in_dim(again_keys, kv_head * HEAD_SIZE, HEAD_SIZE, 1)
        value_rows = lax.dynamic_slice_in_dim(
            again_keys, key_value_width + kv_head * HEAD_SIZE, HEAD_SIZE, 1
        )
        scores = (
            jnp.einsum("qrd,kd->rqk", query_rows, key_rows, preferred_element_type=jnp.float32)
            * score_scale
        )
        scores = jnp.where(visible[None], scores, MASKED)
        probs = jnp.exp(scores - log_sum)
        weights = probs.astype(jnp.bfloat16)
        prob_grad = jnp.einsum(
            "qrd,kd->rqk", grad_rows, value_rows, preferred_element_type=jnp.float32
        )
        row_inner = jnp.sum(probs * prob_grad, axis=-1, keepdims=True)
        score_grad = (probs * (prob_grad - row_inner)).astype(jnp.bfloat16)
        query_grad = (
            jnp.einsum("rqk,kd->qrd", score_grad, key_rows, preferred_element_type=jnp.float32)
            * score_scale
        )
        key_grad = (
            jnp.einsum("rqk,qrd->kd", score_grad, query_rows, preferred_element_type=jnp.float32)
            * score_scale
        )
        value_grad = jnp.einsum(
            "rqk,qrd->kd", weights, grad_rows, preferred_element_type=jnp.float32
        )
        old_key = lax.dynamic_slice_in_dim(key_terms, kv_head * HEAD_SIZE, HEAD_SIZE, 1)
        key_terms = lax.dynamic_update_slice_in_dim(
            key_terms, old_key + key_grad, kv_head * HEAD_SIZE, 1
        )
        old_value = lax.dynamic_slice_in_dim(
            key_terms, key_value_width + kv_head * HEAD_SIZE, HEAD_SIZE, 1
        )
        key_terms = lax.dynamic_update_slice_in_dim(
            key_terms, old_value + value_grad, key_value_width + kv_head * HEAD_SIZE, 1
        )
        return (key_terms, query_grad)

    start_terms = jnp.zeros((again_keys.shape[0], 2 * key_value_width), jnp.float32)
    key_terms, query_grads = lax.scan(
        backward_block, start_terms, (query_blocks, grad_blocks, log_sums, block_numbers)
    )
    local_key_gradients = lax.psum_scatter(key_terms, "expert", scatter_dimension=0, tiled=True)
    query_grad_all = query_grads.transpose(1, 0, 2, 3).reshape(
        local_token_count, QUERY_HEADS, HEAD_SIZE
    )
    query_proj_grad, grad_qgain = query_back(query_grad_all)
    key_projected_gradient, key_gain_gradient = key_returned_gradient(
        local_key_gradients[:, :key_value_width].reshape(
            local_token_count, KEY_VALUE_HEADS, HEAD_SIZE
        )
    )
    query_low_grad = query_proj_grad.reshape(local_token_count, QUERY_HEADS * HEAD_SIZE).astype(
        jnp.bfloat16
    )
    key_low_grad = key_projected_gradient.reshape(local_token_count, key_value_width).astype(
        jnp.bfloat16
    )
    value_low_grad = local_key_gradients[:, key_value_width:].astype(jnp.bfloat16)
    grad_query = jnp.dot(
        normalized_input_first.T, query_low_grad, preferred_element_type=jnp.float32
    )
    grad_key = jnp.dot(normalized_input_first.T, key_low_grad, preferred_element_type=jnp.float32)
    grad_value = jnp.dot(
        normalized_input_first.T, value_low_grad, preferred_element_type=jnp.float32
    )
    xn_one_grad = jnp.dot(query_low_grad, query_again.T, preferred_element_type=jnp.float32)
    xn_one_grad = xn_one_grad + jnp.dot(
        key_low_grad, key_again.T, preferred_element_type=jnp.float32
    )
    xn_one_grad = xn_one_grad + jnp.dot(
        value_low_grad, value_again.T, preferred_element_type=jnp.float32
    )
    x_norm_grad, grad_in = norm_one_back(xn_one_grad)
    input_grad = (x_one_grad + x_norm_grad).astype(jnp.bfloat16)
    dense_grads = (
        lax.psum_scatter(grad_in, ("dp", "expert"), scatter_dimension=0, tiled=True),
        lax.psum_scatter(grad_query, ("dp", "expert"), scatter_dimension=0, tiled=True),
        lax.psum_scatter(grad_key, ("dp", "expert"), scatter_dimension=0, tiled=True),
        lax.psum_scatter(grad_value, ("dp", "expert"), scatter_dimension=0, tiled=True),
        lax.psum_scatter(grad_qgain, ("dp", "expert"), scatter_dimension=0, tiled=True),
        lax.psum_scatter(key_gain_gradient, ("dp", "expert"), scatter_dimension=0, tiled=True),
        lax.psum_scatter(grad_out, ("dp", "expert"), scatter_dimension=0, tiled=True),
        lax.psum_scatter(grad_mid, ("dp", "expert"), scatter_dimension=0, tiled=True),
        lax.psum_scatter(grad_router, ("dp", "expert"), scatter_dimension=0, tiled=True),
    )
    return (
        result,
        input_grad,
        dense_grads[0],
        dense_grads[1],
        dense_grads[2],
        dense_grads[3],
        dense_grads[4],
        dense_grads[5],
        dense_grads[6],
        dense_grads[7],
        dense_grads[8],
        expert_grads[0],
        expert_grads[1],
        expert_grads[2],
    )


def solution(mesh):
    in_specs = (
        P(("dp", "expert"), None),
        P("dp", None),
        P("dp"),
        P(("dp", "expert"), None),
        P(("dp", "expert"), None),
        P(("dp", "expert")),
        P(("dp", "expert"), None),
        P(("dp", "expert"), None),
        P(("dp", "expert"), None),
        P(("dp", "expert")),
        P(("dp", "expert")),
        P(("dp", "expert"), None),
        P(("dp", "expert")),
        P(("dp", "expert"), None),
        P("expert", "dp", None),
        P("expert", "dp", None),
        P("expert", None, "dp"),
        P(("dp", "expert"), None),
    )
    out_specs = (
        P(("dp", "expert"), None),
        P(("dp", "expert"), None),
        P(("dp", "expert")),
        P(("dp", "expert"), None),
        P(("dp", "expert"), None),
        P(("dp", "expert"), None),
        P(("dp", "expert")),
        P(("dp", "expert")),
        P(("dp", "expert"), None),
        P(("dp", "expert")),
        P(("dp", "expert"), None),
        P("expert", "dp", None),
        P("expert", "dp", None),
        P("expert", None, "dp"),
    )
    return jax.shard_map(body, mesh=mesh, in_specs=in_specs, out_specs=out_specs, check_vma=False)
```

profile of v0, /device:TPU:0, one launch (start us, length us, event | category | flops | bytes accessed | tf_op | source)
XLA Modules:
  0.0 3520.1 jit_solution(17603504830715052464)
XLA Ops:
  13.7 42.3 %all-reduce.13 = (bf16[2048]{0:T(1024)(128)(2,1)S(1)}, bf16[128]{0:T(256)(128)(2,1)S(1)}, bf16[128]{0:T(256)(128)(2,1)S(1)}, bf16[2048]{0:T(1024)(128)(2,1)S(1)}) all-reduce(bf16[2048]{0:T(1024)(128)(2,1)S(1)} %dynamic-update-slice, bf16[128]{0:T(256)(128)(2,1)S(1)} %dynamic-update-slice.1, ...), channel_id=1, replica_groups=mesh['dp'=2,'expert'=16] {'dp','expert'}, use_global_device_ids=true, to_apply=%add.4 | all-reduce | flops 4352 | bytes 17408
  61.0 9.9 all-gather.10.cloned.1.call-done
  74.7 54.3 %all-gather.12.cloned.1.call-done = bf16[2048,512]{1,0:T(8,128)(2,1)} async-done(((bf16[64,512]{1,0:T(8,128)(2,1)}), bf16[2048,512]{1,0:T(8,128)(2,1)}) %all-gather.12.cloned.1.call-update) | async-done | bytes 2097168 | tf_op jit(solution)/shard_map/all_gather | solution.py:103
  162.3 83.4 %all-gather.16.cloned.1.call-done = bf16[2048,4096]{1,0:T(8,128)(2,1)} async-done(((bf16[64,4096]{1,0:T(8,128)(2,1)}), bf16[2048,4096]{1,0:T(8,128)(2,1)}) %all-gather.16.cloned.1.call-update) | async-done | bytes 16777232 | tf_op jit(solution)/shard_map/all_gather | solution.py:101
  245.8 9.5 fusion.125
  273.6 49.6 %all-gather.14.cloned.1.call-done = bf16[2048,1024]{1,0:T(8,128)(2,1)} async-done(((bf16[128,1024]{1,0:T(8,128)(2,1)}), bf16[2048,1024]{1,0:T(8,128)(2,1)}) %all-gather.14.cloned.1.call-update) | async-done | bytes 4194320 | tf_op jit(solution)/shard_map/all_gather | solution.py:146
  323.3 138.3 %while.32 = (s32[]{:T(128)}, bf16[8,128,4,128]{1,3,2,0:T(8,128)(2,1)S(1)}, f32[8,4,128,1]{2,1,3,0:T(4,128)}, s32[8]{0:T(128)S(1)}, bf16[2048,1024]{1,0:T(8,128)(...) while((s32[]{:T(128)}, ...), condition=%wide.region_10.11_spmd.clone.clone, body=%wide.region_7.10_spmd.clone.sunk.clone | while | flops 546045440 | bytes 39750552 | solution.py:173
  330.2 6.6 copy.236
  347.5 6.5 copy.236
  364.8 6.5 copy.236
  382.1 6.7 copy.236
  399.5 6.5 copy.236
  416.8 6.5 copy.236
  434.0 6.5 copy.236
  451.3 6.5 copy.236
  462.9 8.5 multiply_reduce_fusion.6
  471.7 5.9 gather_fusion.2
  477.7 4.9 broadcast_select_fusion
  482.5 5.4 all-to-all-start
  489.7 13.6 all-gather.20.cloned.1.call-done
  503.2 74.2 %all-to-all-done = bf16[16,72,2048]{2,1,0:T(8,128)(2,1)} async-done(((bf16[16,72,2048]{2,1,0:T(8,128)(2,1)}), bf16[16,72,2048]{2,1,0:T(8,128)(2,1)}, u32[]{:S(2)}, u32[]{:S(2)}) %all-to-all-start) | async-done | bytes 4718624 | tf_op jit(solution)/shard_map/all_to_all | solution.py:198
  577.5 8.9 fusion.62
  586.4 10.2 multiply_convert_fusion.2
  596.6 6.6 fusion.53
  603.2 27.6 copy.233
  631.3 29.7 reduce.3
  661.0 13.2 reshape.708
  674.3 22.5 all-to-all-start.1
  696.9 155.8 %all-gather = bf16[32,64,16]{1,2,0:T(8,128)(2,1)S(1)} all-gather(bf16[1,64,16]{1,2,0:T(8,128)(2,1)S(1)} %bitcast.355), channel_id=1, replica_groups=mesh['dp'=2,'expert'=16] {'dp','expert'}, dimensions={0}, use_global_device_ids=true | all-gather | bytes 67584 | tf_op jit(solution)/shard_map/all_gather | solution.py:108
  857.5 7.1 gather_fusion.5
  865.0 12.8 reshape.709
  877.8 8.8 copy.230
  886.6 11.8 gather_fusion.3
  902.0 4.6 gather_fusion.4
  906.7 4.7 select_convert_fusion
  911.4 108.6 %all_to_all.16 = bf16[16,72,2048]{2,1,0:T(8,128)(2,1)S(1)} all-to-all(bf16[16,72,2048]{2,1,0:T(8,128)(2,1)S(1)} %select_convert_fusion), channel_id=1, replica_groups=mesh['dp'=2,'expert'=16] {'expert'}, dimensions={0} | all-to-all | bytes 9437184 | tf_op jit(solution)/shard_map/all_to_all | solution.py:253
  1020.0 6.0 multiply_convert_fusion
  1030.0 5.7 fusion.52
  1035.7 27.6 copy.232
  1063.3 29.7 reduce.4
  1093.0 13.3 reshape.706
  1111.1 86.5 %all-to-all-done.3 = bf16[16,2,73728]{2,1,0:T(2,128)(2,1)} async-done(((bf16[16,2,73728]{2,1,0:T(2,128)(2,1)}), bf16[16,2,73728]{2,1,0:T(2,128)(2,1)}, u32[]{:S(2)}, u32[]{:S(2)}) %all-to-all-start.3) | async-done | bytes 4718624 | tf_op jit(solution)/shard_map/all_to_all | solution.py:282
  1197.6 13.0 reshape.707
  1210.6 8.8 copy.229
  1219.3 11.7 gather_fusion.6
  1231.1 9.9 fusion.50
  1243.3 11.4 convolution_convert_fusion.1
  1262.2 157.0 %while.33 = (s32[]{:T(128)}, f32[2048,1024]{1,0:T(8,128)}, f32[8,128,4,128]{1,3,2,0:T(8,128)}, s32[8]{0:T(128)S(1)}, bf16[2048,1024]{1,0:T(8,128)(2,1)}, /*index...) while((s32[]{:T(128)}, f32[2048,1024]{1,0:T(8,128)}, ...), condition=%wide.region_30.31_spmd.clone.clone, body=%wide.region_28.30_spmd.clone.sunk.clone | while | flops 1353252352 | bytes 55343036 | solution.py:350
  1422.1 8.9 fusion.66
  1431.1 8.1 fusion.64
  1439.2 9.2 fusion.65
  1448.6 163.4 %reduce-scatter.12.cloned.1.call-done = f32[128,1024]{1,0:T(8,128)} async-done(((f32[2048,1024]{1,0:T(8,128)}), f32[128,1024]{1,0:T(8,128)}) %reduce-scatter.12.cloned.1.call-update) | async-done | bytes 524304 | tf_op jit(solution)/shard_map/reduce_scatter | solution.py:353
  1627.2 13.2 fusion.123
  1641.7 13.1 fusion.87
  1654.8 99.9 %reduce-scatter.28.cloned.1.call-done = f32[64,16]{1,0:T(8,128)} async-done(((f32[2048,16]{1,0:T(8,128)}), f32[64,16]{1,0:T(8,128)}) %reduce-scatter.28.cloned.1.call-update) | async-done | bytes 4112
  1756.1 9.3 reduce-scatter.26.cloned.1.call-done
  1768.9 11.4 reduce-scatter.22.cloned.1.call-done
  1783.6 11.0 reduce-scatter.24.cloned.1.call-done
  1797.9 12.5 fusion.136
  1814.3 41.7 %all-reduce.12 = (f32[2048]{0:T(1024)S(1)}, f32[128]{0:T(128)S(1)}, f32[128]{0:T(128)S(1)}, f32[2048]{0:T(1024)S(1)}) all-reduce(f32[2048]{0:T(1024)S(1)} %get-tuple-element.286, f32[128]{0:T(128)S(1)} %get-tuple-element.284, f32[128]{0:T(128)S(1)} %get-tuple-element.288, ...), channel_id=3, replica_groups=mesh['dp'=2,'expert'=16] {'dp','expert'}, use_global_device_ids=true, to_apply=%region_36.37.clone | all-reduce | flops 4352 | bytes 34816
  1859.5 83.8 %reduce-scatter.16.cloned.1.call-done = f32[64,512]{1,0:T(8,128)} async-done(((f32[2048,512]{1,0:T(8,128)}), f32[64,512]{1,0:T(8,128)}) %reduce-scatter.16.cloned.1.call-update) | async-done | bytes 131088 | tf_op jit(solution)/shard_map/reduce_scatter | solution.py:389
  1943.3 147.2 %reduce-scatter.18.cloned.1.call-done = f32[64,512]{1,0:T(8,128)} async-done(((f32[2048,512]{1,0:T(8,128)}), f32[64,512]{1,0:T(8,128)}) %reduce-scatter.18.cloned.1.call-update) | async-done | bytes 131088 | tf_op jit(solution)/shard_map/reduce_scatter | solution.py:390
  2090.5 707.7 %reduce-scatter.14.cloned.1.call-done = f32[64,4096]{1,0:T(8,128)} async-done(((f32[2048,4096]{1,0:T(8,128)}), f32[64,4096]{1,0:T(8,128)}) %reduce-scatter.14.cloned.1.call-update) | async-done | bytes 1048592 | tf_op jit(solution)/shard_map/reduce_scatter | solution.py:388
  2798.3 714.3 %reduce-scatter.20.cloned.1.call-done = f32[128,2048]{1,0:T(8,128)} async-done(((f32[4096,2048]{1,0:T(8,128)}), f32[128,2048]{1,0:T(8,128)}) %reduce-scatter.20.cloned.1.call-update) | async-done | bytes 1048592 | tf_op jit(solution)/shard_map/reduce_scatter | solution.py:393
  (494 shorter events, 365.9 us)
Async XLA Ops:
  8.0 62.8 %all-gather.10.cloned.1.call-start = ((), (), s32[]{:S(2)}) async-start(), calls=%async_computation.13 | async-start | bytes 2162688 | tf_op jit(solution)/shard_map/all_gather | solution.py:102
  8.7 120.3 %all-gather.12.cloned.1.call-start = ((), (), s32[]{:S(2)}) async-start(), calls=%async_computation.14 | async-start | bytes 2162688 | tf_op jit(solution)/shard_map/all_gather | solution.py:103
  9.5 236.3 %all-gather.16.cloned.1.call-start = ((), (), s32[]{:S(2)}) async-start(), calls=%async_computation.16 | async-start | bytes 17301504 | tf_op jit(solution)/shard_map/all_gather | solution.py:101
  10.2 313.0 %all-gather.14.cloned.1.call-start = ((), (), s32[]{:S(2)}) async-start(), calls=%async_computation.15 | async-start | bytes 4456448 | tf_op jit(solution)/shard_map/all_gather | solution.py:146
  56.0 189.8 %copy-start.24 = (f32[2048]{0:T(1024)}, f32[2048]{0:T(1024)S(1)}, u32[]{:S(2)}) copy-start(f32[2048]{0:T(1024)S(1)} %convert_element_type.175) | copy-start | bytes 24580
  59.4 11.5 copy-start.35
  59.5 210.2 %copy-start.27 = (f32[128,128]{1,0:T(8,128)}, f32[128,128]{1,0:T(8,128)S(1)}, u32[]{:S(2)}) copy-start(f32[128,128]{1,0:T(8,128)S(1)} %copy.166) | copy-start | bytes 196612
  59.5 11.3 copy-start.37
  59.6 210.1 %copy-start.29 = (f32[128,128]{1,0:T(8,128)}, f32[128,128]{1,0:T(8,128)S(1)}, u32[]{:S(2)}) copy-start(f32[128,128]{1,0:T(8,128)S(1)} %copy.167) | copy-start | bytes 196612
  59.7 14.7 copy-start.57
  60.9 12.3 copy-start.65
  60.9 184.8 %copy-start.51 = (f32[128]{0:T(128)}, f32[128]{0:T(128)S(1)}, u32[]{:S(2)}) copy-start(f32[128]{0:T(128)S(1)} %fusion.119) | copy-start | bytes 1540
  61.0 68.1 %copy-start.6 = (bf16[128,2048]{1,0:T(8,128)(2,1)S(1)}, bf16[128,2048]{1,0:T(8,128)(2,1)}, u32[]{:S(2)}) copy-start(bf16[128,2048]{1,0:T(8,128)(2,1)} %param.22) | copy-start | bytes 1572868
  73.2 57.9 %copy-start.16 = (f32[128,4,128]{2,1,0:T(4,128)}, f32[128,4,128]{2,1,0:T(4,128)S(1)}, u32[]{:S(2)}) copy-start(f32[128,4,128]{2,1,0:T(4,128)S(1)} %reshape.568) | copy-start | bytes 786436
  73.5 57.6 %copy-start.54 = (f32[128,4]{0,1:T(4,128)}, f32[128,4]{0,1:T(4,128)S(1)}, u32[]{:S(2)}) copy-start(f32[128,4]{0,1:T(4,128)S(1)} %copy.164) | copy-start | bytes 6148
  73.7 57.5 %copy-start.22 = (f32[128,4]{1,0:T(8,128)}, f32[128,4]{1,0:T(8,128)S(1)}, u32[]{:S(2)}) copy-start(f32[128,4]{1,0:T(8,128)S(1)} %copy.165) | copy-start | bytes 6148
  74.1 58.5 %copy-start.63 = (s32[128,8]{0,1:T(8,128)S(1)}, s32[128,8]{0,1:T(8,128)}, u32[]{:S(2)}) copy-start(s32[128,8]{0,1:T(8,128)} %param.26) | copy-start | bytes 12292
  74.1 58.7 %copy-start.45 = (s32[128,8]{0,1:T(8,128)S(1)}, s32[128,8]{0,1:T(8,128)}, u32[]{:S(2)}) copy-start(s32[128,8]{0,1:T(8,128)} %param.25) | copy-start | bytes 12292
  131.9 329.7 %all-gather.18.cloned.1.call-start = ((), (), s32[]{:S(2)}) async-start(), calls=%async_computation.17 | async-start | bytes 17301504 | tf_op jit(solution)/shard_map/all_gather | solution.py:106
  132.5 137.2 %copy-start.59 = (f32[128]{0:T(128)}, f32[128]{0:T(128)S(1)}, u32[]{:S(2)}) copy-start(f32[128]{0:T(128)S(1)} %convert_element_type.183) | copy-start | bytes 1540
  132.5 339.0 %copy-start.43 = (f32[2048]{0:T(1024)}, f32[2048]{0:T(1024)S(1)}, u32[]{:S(2)}) copy-start(f32[2048]{0:T(1024)S(1)} %convert_element_type.189) | copy-start | bytes 24580
  141.9 19.2 copy-start.31
  269.8 53.5 %copy-start.10 = (bf16[8,128,4,128]{1,3,2,0:T(8,128)(2,1)S(1)}, bf16[8,128,4,128]{1,3,2,0:T(8,128)(2,1)}, u32[]{:S(2)}) copy-start(bf16[8,128,4,128]{1,3,2,0:T(8,128)(2,1)} %broadcast_convert_fusion) | copy-start | bytes 3145732
  461.6 9.9 copy-start.33
  461.6 9.9 copy-start.47
  461.6 9.9 copy-start.49
  471.7 392.9 %copy-start = (bf16[128,2048]{1,0:T(8,128)(2,1)}, bf16[128,2048]{1,0:T(8,128)(2,1)S(1)}, u32[]{:S(2)}) copy-start(bf16[128,2048]{1,0:T(8,128)(2,1)S(1)} %multiply_convert_fusion.3) | copy-start | bytes 1572868
  482.5 95.0 %all-to-all-start = ((bf16[16,72,2048]{2,1,0:T(8,128)(2,1)}), bf16[16,72,2048]{2,1,0:T(8,128)(2,1)}, u32[]{:S(2)}, u32[]{:S(2)}) async-start(bf16[16,72,2048]{2,1,0:T(8,128)(2,1)} %broadcast_select_fusion), calls=%async_computation | async-start | bytes 9437184 | tf_op jit(solution)/shard_map/all_to_all | solution.py:198
  487.9 15.3 all-gather.20.cloned.1.call-start
  488.5 97.9 %all-gather.22.cloned.1.call-start = ((), (), s32[]{:S(2)}) async-start(), calls=%async_computation.19 | async-start | bytes 4718592 | tf_op jit(solution)/shard_map/all_gather | solution.py:201
  489.1 107.5 %all-gather.24.cloned.1.call-start = ((), (), s32[]{:S(2)}) async-start(), calls=%async_computation.20 | async-start | bytes 4718592 | tf_op jit(solution)/shard_map/all_gather | solution.py:202
  674.3 22.5 copy-start.20
  674.3 22.7 copy-start.64
  674.3 190.7 %all-to-all-start.1 = ((bf16[16,2,73728]{2,1,0:T(2,128)(2,1)}), bf16[16,2,73728]{2,1,0:T(2,128)(2,1)}, u32[]{:S(2)}, u32[]{:S(2)}) async-start(bf16[16,2,73728]{2,1,0:T(2,128)(2,1)} %reshape.708), calls=%async_computation.1 | async-start | bytes 9437184 | tf_op jit(solution)/shard_map/all_to_all | solution.py:211
  857.5 7.4 copy-start.46
  906.6 113.3 %copy-start.76 = (f32[1152,768]{1,0:T(8,128)S(1)}, f32[1152,768]{1,0:T(8,128)}, u32[]{:S(2)}) copy-start(f32[1152,768]{1,0:T(8,128)} %get-tuple-element.373) | copy-start | bytes 10616836
  911.4 108.6 %copy-start.71 = (bf16[1,768,2048]{2,1,0:T(8,128)(2,1)S(1)}, bf16[1,768,2048]{2,1,0:T(8,128)(2,1)}, u32[]{:S(2)}) copy-start(bf16[1,768,2048]{2,1,0:T(8,128)(2,1)} %all-gather.24.cloned.1.call-done) | copy-start | bytes 9437188
  911.4 108.6 %copy-start.73 = (f32[1152,768]{1,0:T(8,128)S(1)}, f32[1152,768]{1,0:T(8,128)}, u32[]{:S(2)}) copy-start(f32[1152,768]{1,0:T(8,128)} %fusion.62) | copy-start | bytes 10616836
  1106.3 91.3 %all-to-all-start.3 = ((bf16[16,2,73728]{2,1,0:T(2,128)(2,1)}), bf16[16,2,73728]{2,1,0:T(2,128)(2,1)}, u32[]{:S(2)}, u32[]{:S(2)}) async-start(bf16[16,2,73728]{2,1,0:T(2,128)(2,1)} %reshape.706), calls=%async_computation.3 | async-start | bytes 9437184 | tf_op jit(solution)/shard_map/all_to_all | solution.py:282
  1110.9 501.1 %reduce-scatter.12.cloned.1.call-start = ((), (), s32[]{:S(2)}) async-start(), calls=%async_computation.21 | async-start | bytes 8912896 | tf_op jit(solution)/shard_map/reduce_scatter | solution.py:353
  1231.1 9.9 copy-start.9
  1231.1 9.9 copy-start.44
  1231.1 9.9 copy-start.62
  1231.1 11.0 copy-start.68
  1419.2 335.5 %reduce-scatter.28.cloned.1.call-start = ((), (), s32[]{:S(2)}) async-start(), calls=%async_computation.29 | async-start | bytes 1081344
  1421.6 9.5 copy-start.75
  1421.6 343.8 %reduce-scatter.26.cloned.1.call-start = ((), (), s32[]{:S(2)}) async-start(), calls=%async_computation.28 | async-start | bytes 4718592 | tf_op jit(solution)/shard_map/reduce_scatter | solution.py:278
  1431.0 349.3 %reduce-scatter.22.cloned.1.call-start = ((), (), s32[]{:S(2)}) async-start(), calls=%async_computation.26 | async-start | bytes 4718592 | tf_op jit(solution)/shard_map/reduce_scatter | solution.py:272
  1439.2 355.4 %reduce-scatter.24.cloned.1.call-start = ((), (), s32[]{:S(2)}) async-start(), calls=%async_computation.27 | async-start | bytes 4718592 | tf_op jit(solution)/shard_map/reduce_scatter | solution.py:275
  1448.5 164.6 %copy-start.30 = (f32[128,128]{1,0:T(8,128)S(1)}, f32[128,128]{1,0:T(8,128)}, u32[]{:S(2)}) copy-start(f32[128,128]{1,0:T(8,128)} %copy-done.29) | copy-start | bytes 196612
  1448.5 164.9 %copy-start.17 = (f32[128,4,128]{2,1,0:T(4,128)S(1)}, f32[128,4,128]{2,1,0:T(4,128)}, u32[]{:S(2)}) copy-start(f32[128,4,128]{2,1,0:T(4,128)} %copy-done.16) | copy-start | bytes 786436
  1448.5 164.9 %copy-start.23 = (f32[128,4]{1,0:T(8,128)S(1)}, f32[128,4]{1,0:T(8,128)}, u32[]{:S(2)}) copy-start(f32[128,4]{1,0:T(8,128)} %copy-done.22) | copy-start | bytes 6148
  1448.5 164.9 %copy-start.28 = (f32[128,128]{1,0:T(8,128)S(1)}, f32[128,128]{1,0:T(8,128)}, u32[]{:S(2)}) copy-start(f32[128,128]{1,0:T(8,128)} %copy-done.27) | copy-start | bytes 196612
  1448.5 164.9 %copy-start.58 = (f32[128]{0:T(128)S(1)}, f32[128]{0:T(128)}, u32[]{:S(2)}) copy-start(f32[128]{0:T(128)} %copy-done.57) | copy-start | bytes 1540
  1448.5 165.5 %copy-start.55 = (f32[128,4]{0,1:T(4,128)S(1)}, f32[128,4]{0,1:T(4,128)}, u32[]{:S(2)}) copy-start(f32[128,4]{0,1:T(4,128)} %copy-done.54) | copy-start | bytes 6148
  1448.5 166.0 %copy-start.7 = (bf16[128,2048]{1,0:T(8,128)(2,1)S(1)}, bf16[128,2048]{1,0:T(8,128)(2,1)}, u32[]{:S(2)}) copy-start(bf16[128,2048]{1,0:T(8,128)(2,1)} %param.22) | copy-start | bytes 1572868
  1448.5 166.0 %copy-start.25 = (f32[2048]{0:T(1024)S(1)}, f32[2048]{0:T(1024)}, u32[]{:S(2)}) copy-start(f32[2048]{0:T(1024)} %copy-done.24) | copy-start | bytes 24580
  1448.5 166.0 %copy-start.52 = (f32[128]{0:T(128)S(1)}, f32[128]{0:T(128)}, u32[]{:S(2)}) copy-start(f32[128]{0:T(128)} %copy-done.51) | copy-start | bytes 1540
  1448.6 494.7 %reduce-scatter.16.cloned.1.call-start = ((), (), s32[]{:S(2)}) async-start(), calls=%async_computation.23 | async-start | bytes 4325376 | tf_op jit(solution)/shard_map/reduce_scatter | solution.py:389
  1617.3 473.2 %reduce-scatter.18.cloned.1.call-start = ((), (), s32[]{:S(2)}) async-start(), calls=%async_computation.24 | async-start | bytes 4325376 | tf_op jit(solution)/shard_map/reduce_scatter | solution.py:390
  1620.4 1177.9 %reduce-scatter.14.cloned.1.call-start = ((), (), s32[]{:S(2)}) async-start(), calls=%async_computation.22 | async-start | bytes 34603008 | tf_op jit(solution)/shard_map/reduce_scatter | solution.py:388
  1640.5 1872.1 %reduce-scatter.20.cloned.1.call-start = ((), (), s32[]{:S(2)}) async-start(), calls=%async_computation.25 | async-start | bytes 34603008 | tf_op jit(solution)/shard_map/reduce_scatter | solution.py:393
  1768.9 29.0 copy-start.14
  1813.3 45.1 %copy-start.66 = (f32[128]{0:T(128)S(1)}, f32[128]{0:T(128)}, u32[]{:S(2)}) copy-start(f32[128]{0:T(128)} %copy-done.65) | copy-start | bytes 1540
  (47 other events, 159.7 us)
Sparse Core Ops, SparseCore 0:
  11.7 59.0 all-gather.9
  73.7 55.2 all-gather.11
  132.0 113.7 all-gather.15
  249.0 74.2 all-gather.13
  326.1 113.4 all-gather.17
  1419.3 192.6 reduce-scatter.11
  1614.3 140.4 reduce-scatter.27
  1757.6 7.7 reduce-scatter.25
  1768.2 12.0 reduce-scatter.21
  1782.5 12.0 reduce-scatter.23
  1797.5 145.8 reduce-scatter.15
  1946.0 144.4 reduce-scatter.17
  2093.4 704.8 reduce-scatter.13
  2801.0 711.5 reduce-scatter.19
Sparse Core Ops, SparseCore 1:
  490.0 13.2 all-gather.19
  504.7 13.2 all-gather.21
  519.3 13.2 all-gather.23
where the time goes:
time: 3540 us; the launch traced here: 3520 us
  waiting for transfers between devices  2320 us (66%)
  blocking collectives  348 us (10%)
  matrix products  319 us (9%)
  local copies, waits for them, and re-layouts  312 us (9%)
  other arithmetic  154 us (4%)
    reduce_scatter x1, waiting for transfers between devices, body(): lax.psum_scatter(grad_out, ('dp', 'expert'), scatter_dimension=0, tiled=T...  714 us
    reduce_scatter x1, waiting for transfers between devices, body(): lax.psum_scatter(grad_query, ('dp', 'expert'), scatter_dimension=0, tiled...  708 us
    reduce_scatter x1, waiting for transfers between devices, body(): lax.psum_scatter(key_terms, 'expert', scatter_dimension=0, tiled=True)  163 us
    all_gather x1, blocking collectives, body(): lax.all_gather(w_router, ('dp', 'expert'), axis=0, tiled=True)  156 us
    reduce_scatter x1, waiting for transfers between devices, body(): lax.psum_scatter(grad_value, ('dp', 'expert'), scatter_dimension=0, tiled...  147 us
    all_to_all x1, blocking collectives, body(): lax.all_to_all(back_send, 'expert', split_axis=0, concat_axis=1, tiled=True)  109 us
    unnamed x18, waiting for transfers between devices  104 us
    all_to_all x1, waiting for transfers between devices, body(): lax.all_to_all(slot_grad, 'expert', split_axis=1, concat_axis=0, tiled=True)  86.5 us
  transfers between devices with their start and end apart: 20, of which 16 were waited for; matrix products, arithmetic and copies ran while one was open for 9% of the time, Pallas kernels for 0%

commit v1 on v0

v1 whole, which is shorter than its diff:
```python
import jax
import jax.numpy as jnp
from jax import lax
from jax.sharding import PartitionSpec as P

MODEL_WIDTH = 2048
QUERY_HEADS = 32
KEY_VALUE_HEADS = 4
HEAD_SIZE = 128
TOP = 8
PER_KV = QUERY_HEADS // KEY_VALUE_HEADS
QW = PER_KV * HEAD_SIZE

EPS = 1e-06
THETA = 1000000.0
MASKED = -1e30
BF = jnp.bfloat16
F32 = jnp.float32


def rms_scale(values, scaling):
    return values * lax.rsqrt(jnp.mean(values * values, axis=-1, keepdims=True) + EPS) * scaling


def rotate(values, cosine, sine_table):
    half = values.shape[-1] // 2
    turned = jnp.concatenate([-values[..., half:], values[..., :half]], axis=-1)
    return values * cosine + turned * sine_table


def rotary_tables(position, width):
    index_float = jnp.arange(width // 2, dtype=jnp.float32)
    freq = jnp.power(jnp.float32(THETA), -2.0 * index_float / width)
    angle = position.astype(jnp.float32)[:, None] * freq[None, :]
    cosine = jnp.concatenate([jnp.cos(angle), jnp.cos(angle)], axis=-1)[:, None, :]
    sine_table = jnp.concatenate([jnp.sin(angle), jnp.sin(angle)], axis=-1)[:, None, :]
    return (cosine, sine_table)


def places(slot_rows, lengths_row):
    seq_ends = jnp.cumsum(lengths_row)
    starts = seq_ends - lengths_row
    segment = jnp.sum((slot_rows[:, None] >= seq_ends[None, :]).astype(jnp.int32), axis=1)
    chosen = segment[:, None] == jnp.arange(lengths_row.shape[0], dtype=jnp.int32)[None, :]
    start_of = jnp.sum(jnp.where(chosen, starts[None, :], 0), axis=1)
    return (segment, slot_rows - start_of)


def pick(blocks, index):
    return lax.dynamic_index_in_dim(blocks, index, 0, keepdims=False)


def put(buffer, block, index):
    return lax.dynamic_update_index_in_dim(buffer, block, index, 0)


class Links:
    def __init__(self, n):
        self.n = n
        self.planes = n // KEY_VALUE_HEADS
        index = lax.axis_index("expert")
        self.g = lax.axis_index("dp")
        self.index = index
        self.a = index // KEY_VALUE_HEADS
        self.b = index % KEY_VALUE_HEADS

    def flip(self, value, k):
        return lax.ppermute(value, "expert", [(i, i ^ k) for i in range(self.n)])

    def onward(self, value):
        step = KEY_VALUE_HEADS
        return lax.ppermute(value, "expert", [(i, (i + step) % self.n) for i in range(self.n)])

    def twin(self, value):
        return lax.ppermute(value, "dp", [(0, 1), (1, 0)])

    def plane_gather(self, own):
        half = own.shape[0] // 2
        near_x = self.flip(own, 1)
        near_y = self.flip(own, 2)
        far_low = self.flip(near_x[:half], 2)
        far_high = self.flip(near_y[half:], 1)
        out = jnp.zeros((4,) + own.shape, own.dtype)
        out = put(out, own, self.b)
        out = put(out, near_x, self.b ^ 1)
        out = put(out, near_y, self.b ^ 2)
        return put(out, jnp.concatenate([far_low, far_high], axis=0), self.b ^ 3)

    def plane_exchange(self, blocks):
        out = jnp.zeros_like(blocks)
        out = put(out, pick(blocks, self.b), self.b)
        for k in (3, 1, 2):
            out = put(out, self.flip(pick(blocks, self.b ^ k), k), self.b ^ k)
        return out

    def plane_scatter(self, blocks):
        half = blocks.shape[1] // 2
        far = pick(blocks, self.b ^ 3)
        to_x = pick(blocks, self.b ^ 1)
        to_y = pick(blocks, self.b ^ 2)
        low = self.flip(far[:half], 2)
        high = self.flip(far[half:], 1)
        to_x = jnp.concatenate(
            [(to_x[:half].astype(F32) + low.astype(F32)).astype(BF), to_x[half:]], axis=0
        )
        to_y = jnp.concatenate(
            [to_y[:half], (to_y[half:].astype(F32) + high.astype(F32)).astype(BF)], axis=0
        )
        got_x = self.flip(to_x, 1)
        got_y = self.flip(to_y, 2)
        return pick(blocks, self.b).astype(F32) + got_x.astype(F32) + got_y.astype(F32)

    def line_gather(self, own):
        out = jnp.zeros((self.planes,) + own.shape, own.dtype)
        out = put(out, own, self.a)
        piece = own
        for step in range(1, self.planes):
            piece = self.onward(piece)
            out = put(out, piece, (self.a - step) % self.planes)
        return out

    def line_scatter(self, block_of):
        total = block_of((self.a - 1) % self.planes)
        for step in range(1, self.planes):
            came = self.onward(total.astype(BF))
            total = block_of((self.a - 1 - step) % self.planes) + came.astype(F32)
        return total

    def group_gather(self, own):
        out = jnp.zeros((self.planes, 4) + own.shape, own.dtype)
        piece = own
        for step in range(self.planes):
            if step:
                piece = self.onward(piece)
            out = put(out, self.plane_gather(piece), (self.a - step) % self.planes)
        return out

    def group_scatter(self, blocks):
        return self.line_scatter(lambda j: self.plane_scatter(pick(blocks, j)))

    def twin_gather(self, own):
        other = self.twin(own)
        first = self.g == 0
        return jnp.stack([jnp.where(first, own, other), jnp.where(first, other, own)])

    def twin_scatter(self, halves):
        return pick(halves, self.g) + self.twin(pick(halves, 1 - self.g).astype(BF)).astype(F32)


def body(
    hidden,
    lengths,
    slots,
    routes,
    order,
    gain_in,
    w_query,
    key_projection_weight,
    value_projection_weight,
    gain_q,
    gain_k,
    w_out,
    gain_mid,
    w_router,
    w_gate,
    w_up,
    w_down,
    cotangent,
):
    tokens = hidden.shape[0]
    experts = w_router.shape[1]
    links = Links(experts)
    planes = links.planes
    capacity = max(2, (tokens * TOP * 9 + 8 * experts - 1) // (8 * experts))
    score_scale = HEAD_SIZE ** (-0.5)
    block_tokens = 4 * tokens
    rows = gain_in.shape[0]
    head_part = gain_q.shape[0]
    devices = 2 * experts

    small = jnp.concatenate(
        [gain_in, gain_mid, gain_q, gain_k, w_router.reshape(rows * experts)], axis=0
    )
    small = lax.all_gather(small, ("dp", "expert"), axis=0, tiled=False)
    full_in = small[:, :rows].reshape(MODEL_WIDTH).astype(F32)
    full_mid = small[:, rows : 2 * rows].reshape(MODEL_WIDTH).astype(F32)
    at = 2 * rows
    full_qgain = small[:, at : at + head_part].reshape(HEAD_SIZE).astype(F32)
    at = at + head_part
    full_kgain = small[:, at : at + head_part].reshape(HEAD_SIZE).astype(F32)
    at = at + head_part
    full_router = small[:, at:].reshape(MODEL_WIDTH, experts)

    pairs = lax.all_gather(order * experts + routes, "expert", axis=0, tiled=True)

    block_hidden = links.plane_gather(hidden).reshape(block_tokens, MODEL_WIDTH)

    own_columns = jnp.concatenate(
        [
            w_query.reshape(rows, 4, QW),
            key_projection_weight.reshape(rows, 4, HEAD_SIZE),
            value_projection_weight.reshape(rows, 4, HEAD_SIZE),
        ],
        axis=2,
    ).transpose(1, 0, 2)
    qkv_width = QW + 2 * HEAD_SIZE
    w_qkv = links.plane_exchange(own_columns)
    w_qkv = links.line_gather(w_qkv)
    w_qkv = links.twin_gather(w_qkv).reshape(MODEL_WIDTH, qkv_width)

    head_rows = w_out.shape[0]
    to_block = []
    for g in range(2):
        for a in range(planes):
            for b in range(4):
                to_block.append(((b * 2 + g) * planes + a, g * experts + a * 4 + b))
    block_out = lax.ppermute(w_out, ("dp", "expert"), to_block)
    block_out = links.line_gather(block_out)
    block_out = links.twin_gather(block_out).reshape(QW, MODEL_WIDTH)

    gate_full = lax.all_gather(w_gate, "dp", axis=1, tiled=True)[0]
    up_full = lax.all_gather(w_up, "dp", axis=1, tiled=True)[0]
    down_full = lax.all_gather(w_down, "dp", axis=2, tiled=True)[0]

    upstream_all = links.group_gather(cotangent).reshape(experts, tokens, MODEL_WIDTH)

    block_slots = lax.dynamic_slice_in_dim(slots, links.a * block_tokens, block_tokens)
    seg_query, position = places(block_slots, lengths[0])
    seg_key, _ = places(slots, lengths[0])
    cosine, sine_table = rotary_tables(position, HEAD_SIZE)
    visible = (seg_query[:, None] == seg_key[None, :]) & (slots[None, :] <= block_slots[:, None])

    block_float = block_hidden.astype(F32)
    normalized = rms_scale(block_float, full_in).astype(BF)
    projected = jnp.dot(normalized, w_qkv, preferred_element_type=F32)
    query_proj = projected[:, :QW].reshape(block_tokens, PER_KV, HEAD_SIZE)
    key_proj = projected[:, QW : QW + HEAD_SIZE].reshape(block_tokens, 1, HEAD_SIZE)
    value_low = projected[:, QW + HEAD_SIZE :].astype(BF)

    def head_norm(values, scaling):
        return rotate(rms_scale(values, scaling), cosine, sine_table)

    query_turned, query_back = jax.vjp(head_norm, query_proj, full_qgain)
    key_turned, key_back = jax.vjp(head_norm, key_proj, full_kgain)
    key_low = key_turned.astype(BF).reshape(block_tokens, HEAD_SIZE)
    keys_values = links.line_gather(jnp.concatenate([key_low, value_low], axis=1)).reshape(
        planes * block_tokens, 2 * HEAD_SIZE
    )
    keys, values = keys_values[:, :HEAD_SIZE], keys_values[:, HEAD_SIZE:]
    query_heads = query_turned.astype(BF).transpose(1, 0, 2)

    def forward_head(query_rows):
        scores = (
            jnp.einsum("qd,kd->qk", query_rows, keys, preferred_element_type=F32) * score_scale
        )
        scores = jnp.where(visible, scores, MASKED)
        top_score = jnp.max(scores, axis=-1, keepdims=True)
        exponent = jnp.exp(scores - top_score)
        row_total = jnp.sum(exponent, axis=-1, keepdims=True)
        weights = (exponent / row_total).astype(BF)
        mixed_rows = jnp.einsum("qk,kd->qd", weights, values, preferred_element_type=F32)
        return (mixed_rows.astype(BF), top_score + jnp.log(row_total))

    attended_heads, log_sums = lax.map(forward_head, query_heads)
    attended = attended_heads.transpose(1, 0, 2).reshape(block_tokens, QW)

    branch = jnp.dot(attended, block_out, preferred_element_type=F32).astype(BF)
    branch = links.plane_scatter(branch.reshape(4, tokens, MODEL_WIDTH))
    x_float = hidden.astype(F32)
    x_one = x_float + branch
    norm_two, norm_two_back = jax.vjp(rms_scale, x_one, full_mid)
    xn_two = norm_two.astype(BF)

    rows_all = links.group_gather(xn_two).reshape(experts, tokens, MODEL_WIDTH)
    pair_routes = pairs % experts
    pair_order = pairs // experts
    hit = pair_routes == links.index
    routed = jnp.any(hit, axis=1).reshape(experts, tokens)
    place = jnp.sum(jnp.where(hit, pair_order, 0), axis=1).reshape(experts, tokens)
    before = routed[:, None, :] & (place[:, None, :] < place[:, :, None])
    rank = jnp.sum(before.astype(jnp.int32), axis=2)
    slot_numbers = jnp.arange(capacity, dtype=jnp.int32)
    select = (rank[:, None, :] == slot_numbers[None, :, None]) & routed[:, None, :]
    select_low = select.astype(BF)

    logits = jnp.dot(
        rows_all.reshape(experts * tokens, MODEL_WIDTH), full_router, preferred_element_type=F32
    )
    expert_numbers = jnp.arange(experts, dtype=jnp.int32)
    chooser = jnp.any(pair_routes[:, :, None] == expert_numbers[None, None, :], axis=1)
    chosen_top = jnp.max(jnp.where(chooser, logits, MASKED), axis=-1, keepdims=True)
    chosen_exp = jnp.where(chooser, jnp.exp(jnp.where(chooser, logits - chosen_top, 0.0)), 0.0)
    probs_all = chosen_exp / jnp.sum(chosen_exp, axis=-1, keepdims=True)
    own_probs = lax.dynamic_slice_in_dim(probs_all, links.index * tokens, tokens)
    expert_probs = jnp.sum(
        jnp.where(expert_numbers[None, :] == links.index, probs_all, 0.0), axis=1
    ).reshape(experts, tokens)
    slot_probs = jnp.sum(jnp.where(select, expert_probs[:, None, :], 0.0), axis=2)
    slot_count = experts * capacity

    def to_slots(all_rows):
        return (
            jnp.einsum("sct,std->scd", select_low, all_rows, preferred_element_type=F32)
            .astype(BF)
            .reshape(slot_count, MODEL_WIDTH)
        )

    def to_tokens(slot_rows):
        return (
            jnp.einsum(
                "sct,scd->std",
                select_low,
                slot_rows.reshape(experts, capacity, MODEL_WIDTH),
                preferred_element_type=F32,
            )
            .astype(BF)
            .reshape(planes, 4, tokens, MODEL_WIDTH)
        )

    slot_upstream = to_slots(upstream_all)
    arrived = to_slots(rows_all)
    gate_pre = jnp.dot(arrived, gate_full, preferred_element_type=F32)
    up_pre = jnp.dot(arrived, up_full, preferred_element_type=F32)
    activation = (jax.nn.silu(gate_pre) * up_pre).astype(BF)
    returned = jnp.dot(activation, down_full, preferred_element_type=F32).astype(BF)
    slot_probs_column = slot_probs.reshape(slot_count, 1)
    upstream_float = slot_upstream.astype(F32)
    out_grad = (slot_probs_column * upstream_float).astype(BF)
    act_grad = jnp.einsum("rd,fd->rf", out_grad, down_full, preferred_element_type=F32)
    logistic = jax.nn.sigmoid(gate_pre)
    gate_low = (act_grad * up_pre * logistic * (1.0 + gate_pre * (1.0 - logistic))).astype(BF)
    up_low = (act_grad * gate_pre * logistic).astype(BF)
    pair_grad = (
        jnp.einsum("rf,df->rd", gate_low, gate_full, preferred_element_type=F32)
        + jnp.einsum("rf,df->rd", up_low, up_full, preferred_element_type=F32)
    ).astype(BF)
    moe_grad = links.group_scatter(to_tokens(pair_grad))

    slot_gate_grad = jnp.sum(upstream_float * returned.astype(F32), axis=1).reshape(
        experts, capacity
    )
    gate_grads = jnp.sum(jnp.where(select, slot_gate_grad[:, :, None], 0.0), axis=1)
    gate_grads = lax.all_to_all(gate_grads, "expert", split_axis=0, concat_axis=0, tiled=True).T

    mixture = links.group_scatter(
        to_tokens((slot_probs_column * returned.astype(F32)).astype(BF))
    )
    result = (x_one + mixture).astype(BF)

    grad_down = jnp.einsum("rf,rd->fd", activation, out_grad, preferred_element_type=F32)
    grad_gate = jnp.einsum("rd,rf->df", arrived, gate_low, preferred_element_type=F32)
    grad_up = jnp.einsum("rd,rf->df", arrived, up_low, preferred_element_type=F32)
    ff = w_gate.shape[2]
    half_width = MODEL_WIDTH // 2
    grad_down = links.twin_scatter(grad_down.reshape(ff, 2, half_width).transpose(1, 0, 2))
    grad_gate = links.twin_scatter(grad_gate.reshape(2, half_width, ff))
    grad_up = links.twin_scatter(grad_up.reshape(2, half_width, ff))

    upstream = cotangent.astype(F32)
    chosen_grad = own_probs * (
        gate_grads - jnp.sum(own_probs * gate_grads, axis=-1, keepdims=True)
    )
    logit_grad = chosen_grad.astype(BF)
    grad_router = jnp.dot(xn_two.T, logit_grad, preferred_element_type=F32)
    xn_two_grad = moe_grad + jnp.dot(logit_grad, full_router.T, preferred_element_type=F32)
    x_one_norm_grad, grad_mid = norm_two_back(xn_two_grad)
    x_one_grad = upstream + x_one_norm_grad
    branch_grad = x_one_grad.astype(BF)

    block_grad = links.plane_gather(branch_grad).reshape(block_tokens, MODEL_WIDTH)
    attended_grad = jnp.einsum(
        "td,hd->th", block_grad, block_out, preferred_element_type=F32
    ).astype(BF)
    grad_heads = attended_grad.reshape(block_tokens, PER_KV, HEAD_SIZE).transpose(1, 0, 2)

    def backward_head(key_terms, head_items):
        query_rows, grad_rows, log_sum = head_items
        scores = (
            jnp.einsum("qd,kd->qk", query_rows, keys, preferred_element_type=F32) * score_scale
        )
        scores = jnp.where(visible, scores, MASKED)
        probs = jnp.exp(scores - log_sum)
        weights = probs.astype(BF)
        prob_grad = jnp.einsum("qd,kd->qk", grad_rows, values, preferred_element_type=F32)
        row_inner = jnp.sum(probs * prob_grad, axis=-1, keepdims=True)
        score_grad = (probs * (prob_grad - row_inner)).astype(BF)
        query_grad = (
            jnp.einsum("qk,kd->qd", score_grad, keys, preferred_element_type=F32) * score_scale
        )
        key_grad = (
            jnp.einsum("qk,qd->kd", score_grad, query_rows, preferred_element_type=F32)
            * score_scale
        )
        value_grad = jnp.einsum("qk,qd->kd", weights, grad_rows, preferred_element_type=F32)
        return ((key_terms[0] + key_grad, key_terms[1] + value_grad), query_grad)

    no_terms = jnp.zeros((planes * block_tokens, HEAD_SIZE), F32)
    key_terms, query_grads = lax.scan(
        backward_head, (no_terms, no_terms), (query_heads, grad_heads, log_sums)
    )
    key_terms = jnp.concatenate(key_terms, axis=1).reshape(planes, block_tokens, 2 * HEAD_SIZE)
    key_terms = links.line_scatter(lambda j: pick(key_terms, j))

    grad_out = jnp.einsum("th,td->hd", attended, block_grad, preferred_element_type=F32)
    grad_out = links.twin_scatter(grad_out.reshape(2, QW // 2, MODEL_WIDTH))
    grad_out = grad_out.astype(BF).reshape(planes, head_rows, MODEL_WIDTH)
    grad_out = links.line_scatter(lambda j: pick(grad_out, j).astype(F32)).astype(BF)
    grad_out = lax.ppermute(
        grad_out, ("dp", "expert"), [(there, here) for here, there in to_block]
    ).astype(F32)

    query_proj_grad, grad_qgain = query_back(query_grads.transpose(1, 0, 2))
    key_proj_grad, grad_kgain = key_back(key_terms[:, :HEAD_SIZE].reshape(key_proj.shape))
    proj_grad = jnp.concatenate(
        [
            query_proj_grad.reshape(block_tokens, QW).astype(BF),
            key_proj_grad.reshape(block_tokens, HEAD_SIZE).astype(BF),
            key_terms[:, HEAD_SIZE:].astype(BF),
        ],
        axis=1,
    )
    xn_one_grad = jnp.einsum("tc,dc->td", proj_grad, w_qkv, preferred_element_type=F32)
    xn_one_grad = links.plane_scatter(xn_one_grad.astype(BF).reshape(4, tokens, MODEL_WIDTH))
    _, norm_one_back = jax.vjp(rms_scale, x_float, full_in)
    x_norm_grad, grad_in = norm_one_back(xn_one_grad)
    input_grad = (x_one_grad + x_norm_grad).astype(BF)

    grad_qkv = jnp.einsum("td,tc->dc", normalized, proj_grad, preferred_element_type=F32)
    grad_qkv = links.twin_scatter(grad_qkv.reshape(2, MODEL_WIDTH // 2, qkv_width))
    grad_qkv = grad_qkv.astype(BF).reshape(planes, 4, rows, qkv_width)
    grad_qkv = links.line_scatter(lambda j: pick(grad_qkv, j).astype(F32)).astype(BF)
    grad_qkv = links.plane_exchange(grad_qkv).transpose(1, 0, 2).astype(F32)
    grad_query = grad_qkv[:, :, :QW].reshape(rows, 4 * QW)
    grad_key = grad_qkv[:, :, QW : QW + HEAD_SIZE].reshape(rows, 4 * HEAD_SIZE)
    grad_value = grad_qkv[:, :, QW + HEAD_SIZE :].reshape(rows, 4 * HEAD_SIZE)

    def sum_of(parts):
        packed = jnp.concatenate([part.reshape(devices, -1) for part in parts], axis=1)
        came = lax.all_to_all(packed, ("dp", "expert"), split_axis=0, concat_axis=0, tiled=True)
        return jnp.sum(came, axis=0)

    first = sum_of([grad_mid, grad_router])
    grad_mid = first[:rows]
    grad_router = first[rows:].reshape(rows, experts)
    last = sum_of([grad_in, grad_qgain, grad_kgain])
    grad_in = last[:rows]
    grad_qgain = last[rows : rows + head_part]
    grad_kgain = last[rows + head_part :]

    return (
        result,
        input_grad,
        grad_in,
        grad_query,
        grad_key,
        grad_value,
        grad_qgain,
        grad_kgain,
        grad_out,
        grad_mid,
        grad_router,
        grad_gate[None],
        grad_up[None],
        grad_down[None],
    )


def solution(mesh):
    every = ("dp", "expert")
    in_specs = (
        P(every, None),
        P("dp", None),
        P("dp"),
        P(every, None),
        P(every, None),
        P(every),
        P(every, None),
        P(every, None),
        P(every, None),
        P(every),
        P(every),
        P(every, None),
        P(every),
        P(every, None),
        P("expert", "dp", None),
        P("expert", "dp", None),
        P("expert", None, "dp"),
        P(every, None),
    )
    out_specs = (
        P(every, None),
        P(every, None),
        P(every),
        P(every, None),
        P(every, None),
        P(every, None),
        P(every),
        P(every),
        P(every, None),
        P(every),
        P(every, None),
        P("expert", "dp", None),
        P("expert", "dp", None),
        P("expert", None, "dp"),
    )
    return jax.shard_map(body, mesh=mesh, in_specs=in_specs, out_specs=out_specs, check_vma=False)
```

time: 3540 us -> 1170 us (0.33)
  waiting for transfers between devices: 2320 us -> 387 us
  blocking collectives: 348 us -> 43.5 us
  local copies, waits for them, and re-layouts: 312 us -> 153 us
  starting transfers between devices: 34.2 us -> 185 us
  matrix products: 319 us -> 250 us
  other arithmetic: 154 us -> 114 us
    reduce_scatter x8 -> x0, waiting for transfers between devices: 1850 us -> none  [the longest x1 714 us: body(): lax.psum_scatter(grad_out, ('dp', 'expert'), scatter_dimension=0, tiled=T...]
    ppermute x0 -> x125, waiting for transfers between devices: none -> 311 us  [the longest x86 160 us: flip(): return lax.ppermute(value, 'expert', [(i, i ^ k) for i in range(self.n)])]
    all_gather x8 -> x3, waiting for transfers between devices: 211 us -> 0.01 us  [the longest x1 0.01 us: body(): gate_full = lax.all_gather(w_gate, 'dp', axis=1, tiled=True)[0]]
    ppermute x0 -> x125, starting transfers between devices: none -> 175 us  [the longest x86 155 us: flip(): return lax.ppermute(value, 'expert', [(i, i ^ k) for i in range(self.n)])]
    all_to_all x3, waiting for transfers between devices: 161 us -> 20.5 us  [the longest x2 20.5 us: sum_of(): lax.all_to_all(packed, ('dp', 'expert'), split_axis=0, concat_axis=0, til...]
    all_gather x1, blocking collectives: 156 us -> 43.5 us  [body(): lax.all_gather(order * experts + routes, 'expert', axis=0, tiled=True)]
    all_to_all x1 -> x0, blocking collectives: 109 us -> none  [body(): lax.all_to_all(back_send, 'expert', split_axis=0, concat_axis=1, tiled=True)]
    unnamed x2 -> x0, blocking collectives: 84 us -> none
  transfers between devices with their start and end apart: 20 -> 132, of which waited for: 16 -> 62; matrix products, arithmetic and copies ran while one was open for 9% -> 39% of each run, Pallas kernels for 0% -> 0%
where the time goes in v1:
time: 1170 us; the launch traced here: 1150 us
  waiting for transfers between devices  387 us (33%)
  matrix products  250 us (21%)
  starting transfers between devices  185 us (16%)
  local copies, waits for them, and re-layouts  153 us (13%)
  other arithmetic  114 us (10%)
  blocking collectives  43.5 us (4%)
  between operations  19 us (2%)
    ppermute x86, waiting for transfers between devices, flip(): return lax.ppermute(value, 'expert', [(i, i ^ k) for i in range(self.n)])  160 us
    ppermute x86, starting transfers between devices, flip(): return lax.ppermute(value, 'expert', [(i, i ^ k) for i in range(self.n)])  155 us
    ppermute x30, waiting for transfers between devices, onward(): lax.ppermute(value, 'expert', [(i, (i + step) % self.n) for i in range(se...  151 us
    unnamed x5, waiting for transfers between devices  55.6 us
    all_gather x1, blocking collectives, body(): lax.all_gather(order * experts + routes, 'expert', axis=0, tiled=True)  43.5 us
    unnamed x303, local copies, waits for them, and re-layouts  37.3 us
    dot_general x8, matrix products, backward_head(): jnp.einsum('qk,qd->kd', weights, grad_rows, preferred_element_type=F32)  24.2 us
  transfers between devices with their start and end apart: 132, of which 62 were waited for; matrix products, arithmetic and copies ran while one was open for 39% of the time, Pallas kernels for 0%

profile of v1, /device:TPU:0, one launch (start us, length us, event | category | flops | bytes accessed | tf_op | source)
XLA Modules:
  0.0 1153.6 jit_solution(3816651025290325817)
XLA Ops:
  34.3 43.5 %all_gather.20 = s32[2048,8]{0,1:T(8,128)S(1)} all-gather(s32[128,8]{0,1:T(8,128)S(1)} %multiply_add_fusion.1), channel_id=1, replica_groups=mesh['dp'=2,'expert'=16] {'expert'}, dimensions={0}, use_global_device_ids=true | all-gather | bytes 69632 | tf_op jit(solution)/shard_map/all_gather | solution.py:194
  82.6 54.5 %all-reduce.7.cloned.1.call-done = bf16[37120]{0:T(1024)(128)(2,1)} async-done(((bf16[37120]{0:T(1024)(128)(2,1)}), bf16[37120]{0:T(1024)(128)(2,1)}) %all-reduce.7.cloned.1.call-update) | async-done | bytes 74256
  146.9 4.1 collective-permute-done.5
  153.2 4.2 collective-permute-done.6
  179.6 30.8 %collective-permute-start.64 = (bf16[64,2048]{1,0:T(8,128)(2,1)}, bf16[64,2048]{1,0:T(8,128)(2,1)}, u32[]{:S(2)}, u32[]{:S(2)}) collective-permute-start(bf16[64,2048]{1,0:T(8,128)(2,1)} %slice.631), channel_id=1, source_target_pairs={{0,1},{1,0},{2,3},{3,2},{4,5},{5,4},{6,7},{7,6},{8,9},{9,8},{10,11... | collective-permute-start | bytes 786440 | tf_op jit(solution)/shard_map/ppermute | solution.py:68
  215.8 7.7 collective-permute-start.15
  229.1 4.0 multiply_convert_fusion.1
  242.4 6.3 collective-permute-done.67
  253.2 4.7 collective-permute-done.69
  259.0 7.6 collective-permute-done.8
  266.6 11.2 collective-permute-done.16
  279.2 33.5 %collective-permute-done.17 = bf16[128,2048]{1,0:T(8,128)(2,1)S(1)} collective-permute-done((bf16[128,2048]{1,0:T(8,128)(2,1)S(1)}, bf16[128,2048]{1,0:T(8,128)(2,1)S(1)}, u32[]{:S(2)}, u32[]{:S(2)}) %collective-permute-start.17) | collective-permute-done | bytes 524320 | tf_op jit(solution)/shard_map/ppermute | solution.py:72
  316.8 11.9 %collective-permute-done.77 = bf16[128,2048]{1,0:T(8,128)(2,1)S(1)} collective-permute-done((bf16[128,2048]{1,0:T(8,128)(2,1)S(1)}, bf16[128,2048]{1,0:T(8,128)(2,1)S(1)}, u32[]{:S(2)}, u32[]{:S(2)}) %collective-permute-start.77) | collective-permute-done | bytes 524320 | tf_op jit(solution)/shard_map/ppermute | solution.py:68
  345.8 7.0 collective-permute-done.11
  354.9 6.1 collective-permute-done.12
  361.3 8.1 collective-permute-done.13
  370.4 46.1 %while.28 = (s32[]{:T(128)}, bf16[8,512,128]{1,2,0:T(8,128)(2,1)S(1)}, f32[8,512,1]{1,2,0:T(1,128)}, bf16[8,512,128]{2,1,0:T(8,128)(2,1)}, bf16[2048,128]{1,0:T(...) while((s32[]{:T(128)}, ...), condition=%wide.region_10.11_spmd.clone, body=%wide.region_7.10_spmd.clone.sunk | while | flops 548470272 | bytes 14459009 | solution.py:264
  416.5 5.0 convolution_convert_fusion.5
  423.8 7.1 collective-permute-done.19
  436.0 6.2 collective-permute-done.22
  442.2 4.4 collective-permute-done.20
  450.0 6.9 convolution_convert_fusion.3
  457.4 5.5 collective-permute-done.24
  475.6 8.8 collective-permute-done.29
  489.5 4.2 collective-permute-done.31
  494.9 9.9 collective-permute-done.34
  512.6 5.3 collective-permute-done.39
  520.2 4.2 collective-permute-done.41
  533.4 8.9 fusion.45
  542.3 10.3 multiply_convert_fusion.5
  552.6 10.5 fusion.29
  563.2 5.8 select_reduce_fusion.3
  573.1 4.0 all-to-all-start
  577.1 6.8 copy.168
  584.0 10.2 multiply_convert_fusion.3
  594.2 6.1 fusion.59
  600.3 6.1 fusion.57
  606.4 6.3 fusion.43
  612.7 7.0 add_convert_fusion
  632.5 9.2 fusion.31
  641.7 4.7 convolution_convert_fusion.2
  656.1 6.8 copy.175
  662.9 6.9 fusion.55
  685.6 4.1 collective-permute-done.86
  691.2 4.1 collective-permute-done.82
  711.9 4.1 collective-permute-done.48
  716.1 5.6 collective-permute-done.44
  736.3 5.4 collective-permute-done.55
  763.3 6.7 collective-permute-done.49
  778.6 5.6 collective-permute-done.59
  790.5 4.5 fusion.36
  798.6 5.9 collective-permute-done.98
  804.5 7.1 collective-permute-done.60
  832.0 6.3 collective-permute-done.102
  844.7 120.8 %while.29 = (s32[]{:T(128)}, f32[2048,128]{1,0:T(8,128)S(1)}, f32[2048,128]{1,0:T(8,128)}, f32[8,512,128]{2,1,0:T(8,128)}, bf16[8,512,128]{2,1,0:T(8,128)(2,1)},...) while((s32[]{:T(128)}, f32[2048,128]{1,0:T(8,128)S(1)}, ...), condition=%wide.region_26.27_spmd.clone, body=%wide.region_24.26_spmd.clone.sunk | while | flops 1356135936 | bytes 71596272 | solution.py:398
  981.1 4.9 collective-permute-done.104
  987.5 6.8 collective-permute-done.105
  1000.9 4.0 copy-done.26
  1046.7 12.6 %collective-permute-done.111 = bf16[4,64,1280]{2,1,0:T(8,128)(2,1)} collective-permute-done((bf16[4,64,1280]{2,1,0:T(8,128)(2,1)}, bf16[4,64,1280]{2,1,0:T(8,128)(2,1)}, u32[]{:S(2)}, u32[]{:S(2)}) %collective-permute-start.111) | collective-permute-done | bytes 655392 | tf_op jit(solution)/shard_map/ppermute | solution.py:72
  1060.8 9.9 collective-permute-done.119
  1072.7 12.1 %collective-permute-done.112 = bf16[4,64,1280]{2,1,0:T(8,128)(2,1)S(1)} collective-permute-done((bf16[4,64,1280]{2,1,0:T(8,128)(2,1)S(1)}, bf16[4,64,1280]{2,1,0:T(8,128)(2,1)S(1)}, u32[]{:S(2)}, u32[]{:S(2)}) %collective-permute-start.112) | collective-permute-done | bytes 655392 | tf_op jit(solution)/shard_map/ppermute | solution.py:72
  1088.5 20.5 %all-to-all-done.1 = f32[32,1,72]{2,1,0:T(1,128)S(1)} async-done(((f32[32,1,72]{2,1,0:T(1,128)}), f32[32,1,72]{2,1,0:T(1,128)S(1)}, u32[]{:S(2)}, u32[]{:S(2)}) %all-to-all-start.1) | async-done | bytes 9248 | tf_op jit(solution)/shard_map/all_to_all | solution.py:439
  1116.7 12.1 %collective-permute-start.115 = (bf16[64,1280]{1,0:T(8,128)(2,1)S(1)}, bf16[64,1280]{1,0:T(8,128)(2,1)S(1)}, u32[]{:S(2)}, u32[]{:S(2)}) collective-permute-start(bf16[64,1280]{1,0:T(8,128)(2,1)S(1)} %get-tuple-element.435), channel_id=1, source_target_pairs={{0,1},{1,0},{2,3},{3,2},{4,5},{5,4},{6,7},{7,6},{8,9},{9,8},{10,11... | collective-permute-start | bytes 491528 | tf_op jit(solution)/shard_map/ppermute | solution.py:68
  1128.8 11.3 collective-permute-start.116
  (950 shorter events, 558.1 us)
Async XLA Ops:
  8.0 129.1 %all-reduce.7.cloned.1.call-start = ((), (), s32[]{:S(2)}) async-start(), calls=%async_computation.6 | async-start | bytes 151552
  12.8 520.6 %all-gather.5.cloned.1.call-start = ((), (), s32[]{:S(2)}) async-start(), calls=%async_computation.3 | async-start | bytes 4718592 | tf_op jit(solution)/shard_map/all_gather | solution.py:221
  13.4 528.9 %all-gather.7.cloned.1.call-start = ((), (), s32[]{:S(2)}) async-start(), calls=%async_computation.4 | async-start | bytes 4718592 | tf_op jit(solution)/shard_map/all_gather | solution.py:222
  14.0 538.6 %all-gather.9.cloned.1.call-start = ((), (), s32[]{:S(2)}) async-start(), calls=%async_computation.5 | async-start | bytes 4718592 | tf_op jit(solution)/shard_map/all_gather | solution.py:223
  14.0 147.4 %collective-permute-start = (bf16[128,2048]{1,0:T(8,128)(2,1)S(1)}, bf16[128,2048]{1,0:T(8,128)(2,1)}, u32[]{:S(2)}, u32[]{:S(2)}) collective-permute-start(bf16[128,2048]{1,0:T(8,128)(2,1)S(1)} %copy-done.21), channel_id=1, source_target_pairs={{0,1},{1,0},{2,3},{3,2},{4,5},{5,4},{6,7},{7,6},{8,9},{9,8},{10,11... | collective-permute-start | bytes 1572872 | tf_op jit(solution)/shard_map/ppermute | solution.py:68
  17.1 147.1 %collective-permute-start.1 = (bf16[128,2048]{1,0:T(8,128)(2,1)S(1)}, bf16[128,2048]{1,0:T(8,128)(2,1)}, u32[]{:S(2)}, u32[]{:S(2)}) collective-permute-start(bf16[128,2048]{1,0:T(8,128)(2,1)S(1)} %copy-done.21), channel_id=1, source_target_pairs={{0,2},{1,3},{2,0},{3,1},{4,6},{5,7},{6,4},{7,5},{8,10},{9,11},{10,... | collective-permute-start | bytes 1572872 | tf_op jit(solution)/shard_map/ppermute | solution.py:68
  18.6 148.0 %collective-permute-start.61 = (bf16[128,2048]{1,0:T(8,128)(2,1)S(1)}, bf16[128,2048]{1,0:T(8,128)(2,1)}, u32[]{:S(2)}, u32[]{:S(2)}) collective-permute-start(bf16[128,2048]{1,0:T(8,128)(2,1)S(1)} %copy-done.32), channel_id=1, source_target_pairs={{0,1},{1,0},{2,3},{3,2},{4,5},{5,4},{6,7},{7,6},{8,9},{9,8},{10,11... | collective-permute-start | bytes 1572872 | tf_op jit(solution)/shard_map/ppermute | solution.py:68
  19.1 151.9 %collective-permute-start.62 = (bf16[128,2048]{1,0:T(8,128)(2,1)S(1)}, bf16[128,2048]{1,0:T(8,128)(2,1)}, u32[]{:S(2)}, u32[]{:S(2)}) collective-permute-start(bf16[128,2048]{1,0:T(8,128)(2,1)S(1)} %copy-done.32), channel_id=1, source_target_pairs={{0,2},{1,3},{2,0},{3,1},{4,6},{5,7},{6,4},{7,5},{8,10},{9,11},{10,... | collective-permute-start | bytes 1572872 | tf_op jit(solution)/shard_map/ppermute | solution.py:68
  22.8 121.0 %collective-permute-start.4 = (bf16[64,1280]{1,0:T(8,128)(2,1)}, bf16[64,1280]{1,0:T(8,128)(2,1)}, u32[]{:S(2)}, u32[]{:S(2)}) collective-permute-start(bf16[64,1280]{1,0:T(8,128)(2,1)} %bitcast.687), channel_id=1, source_target_pairs={{0,3},{1,2},{2,1},{3,0},{4,7},{5,6},{6,5},{7,4},{8,11},{9,10},{10,... | collective-permute-start | bytes 491528 | tf_op jit(solution)/shard_map/ppermute | solution.py:68
  157.3 54.4 %collective-permute-start.65 = (bf16[128,2048]{1,0:T(8,128)(2,1)S(1)}, bf16[128,2048]{1,0:T(8,128)(2,1)}, u32[]{:S(2)}, u32[]{:S(2)}) collective-permute-start(bf16[128,2048]{1,0:T(8,128)(2,1)S(1)} %copy-done.32), channel_id=1, source_target_pairs={{0,4},{1,5},{2,6},{3,7},{4,8},{5,9},{6,10},{7,11},{8,12},{9,13},{1... | collective-permute-start | bytes 1572872 | tf_op jit(solution)/shard_map/ppermute | solution.py:72
  164.2 76.6 %collective-permute-start.7 = (bf16[4,64,1280]{2,1,0:T(8,128)(2,1)}, bf16[4,64,1280]{2,1,0:T(8,128)(2,1)}, u32[]{:S(2)}, u32[]{:S(2)}) collective-permute-start(bf16[4,64,1280]{2,1,0:T(8,128)(2,1)} %bitcast_dynamic-update-slice_fusion.46), channel_id=1, source_target_pairs={{0,4},{1,5},{2,6},{3,7},{4,8},{5,9},{6,10},{7,11},{8,12},{9,13},{1... | collective-permute-start | bytes 1966088 | tf_op jit(solution)/shard_map/ppermute | solution.py:72
  166.6 49.2 %collective-permute-start.3 = (bf16[64,2048]{1,0:T(8,128)(2,1)S(1)}, bf16[64,2048]{1,0:T(8,128)(2,1)S(1)}, u32[]{:S(2)}, u32[]{:S(2)}) collective-permute-start(bf16[64,2048]{1,0:T(8,128)(2,1)S(1)} %slice.607), channel_id=1, source_target_pairs={{0,1},{1,0},{2,3},{3,2},{4,5},{5,4},{6,7},{7,6},{8,9},{9,8},{10,11... | collective-permute-start | bytes 786440 | tf_op jit(solution)/shard_map/ppermute | solution.py:68
  171.0 52.5 %collective-permute-start.2 = (bf16[64,2048]{1,0:T(8,128)(2,1)S(1)}, bf16[64,2048]{1,0:T(8,128)(2,1)S(1)}, u32[]{:S(2)}, u32[]{:S(2)}) collective-permute-start(bf16[64,2048]{1,0:T(8,128)(2,1)S(1)} %slice.606), channel_id=1, source_target_pairs={{0,2},{1,3},{2,0},{3,1},{4,6},{5,7},{6,4},{7,5},{8,10},{9,11},{10,... | collective-permute-start | bytes 786440 | tf_op jit(solution)/shard_map/ppermute | solution.py:68
  179.6 54.1 %collective-permute-start.64 = (bf16[64,2048]{1,0:T(8,128)(2,1)}, bf16[64,2048]{1,0:T(8,128)(2,1)}, u32[]{:S(2)}, u32[]{:S(2)}) collective-permute-start(bf16[64,2048]{1,0:T(8,128)(2,1)} %slice.631), channel_id=1, source_target_pairs={{0,1},{1,0},{2,3},{3,2},{4,5},{5,4},{6,7},{7,6},{8,9},{9,8},{10,11... | collective-permute-start | bytes 786440 | tf_op jit(solution)/shard_map/ppermute | solution.py:68
  213.0 22.7 %collective-permute-start.63 = (bf16[64,2048]{1,0:T(8,128)(2,1)}, bf16[64,2048]{1,0:T(8,128)(2,1)}, u32[]{:S(2)}, u32[]{:S(2)}) collective-permute-start(bf16[64,2048]{1,0:T(8,128)(2,1)} %slice.630), channel_id=1, source_target_pairs={{0,2},{1,3},{2,0},{3,1},{4,6},{5,7},{6,4},{7,5},{8,10},{9,11},{10,... | collective-permute-start | bytes 786440 | tf_op jit(solution)/shard_map/ppermute | solution.py:68
  215.8 35.1 %collective-permute-start.15 = (bf16[128,2048]{1,0:T(8,128)(2,1)}, bf16[128,2048]{1,0:T(8,128)(2,1)}, u32[]{:S(2)}, u32[]{:S(2)}) collective-permute-start(bf16[128,2048]{1,0:T(8,128)(2,1)} %collective-permute-done.14), channel_id=1, source_target_pairs={{0,4},{1,5},{2,6},{3,7},{4,8},{5,9},{6,10},{7,11},{8,12},{9,13},{1... | collective-permute-start | bytes 1572872 | tf_op jit(solution)/shard_map/ppermute | solution.py:72
  223.5 25.3 %collective-permute-start.66 = (bf16[128,2048]{1,0:T(8,128)(2,1)}, bf16[128,2048]{1,0:T(8,128)(2,1)S(1)}, u32[]{:S(2)}, u32[]{:S(2)}) collective-permute-start(bf16[128,2048]{1,0:T(8,128)(2,1)} %collective-permute-done.65), channel_id=1, source_target_pairs={{0,1},{1,0},{2,3},{3,2},{4,5},{5,4},{6,7},{7,6},{8,9},{9,8},{10,11... | collective-permute-start | bytes 1572872 | tf_op jit(solution)/shard_map/ppermute | solution.py:68
  240.8 25.8 %collective-permute-start.8 = (bf16[4,64,1280]{2,1,0:T(8,128)(2,1)}, bf16[4,64,1280]{2,1,0:T(8,128)(2,1)S(1)}, u32[]{:S(2)}, u32[]{:S(2)}) collective-permute-start(bf16[4,64,1280]{2,1,0:T(8,128)(2,1)} %collective-permute-done.7), channel_id=1, source_target_pairs={{0,4},{1,5},{2,6},{3,7},{4,8},{5,9},{6,10},{7,11},{8,12},{9,13},{1... | collective-permute-start | bytes 1966088 | tf_op jit(solution)/shard_map/ppermute | solution.py:72
  250.9 27.0 %collective-permute-start.16 = (bf16[128,2048]{1,0:T(8,128)(2,1)}, bf16[128,2048]{1,0:T(8,128)(2,1)S(1)}, u32[]{:S(2)}, u32[]{:S(2)}) collective-permute-start(bf16[128,2048]{1,0:T(8,128)(2,1)} %collective-permute-done.15), channel_id=1, source_target_pairs={{0,4},{1,5},{2,6},{3,7},{4,8},{5,9},{6,10},{7,11},{8,12},{9,13},{1... | collective-permute-start | bytes 1572872 | tf_op jit(solution)/shard_map/ppermute | solution.py:72
  252.6 25.5 %collective-permute-start.71 = (bf16[128,2048]{1,0:T(8,128)(2,1)S(1)}, bf16[128,2048]{1,0:T(8,128)(2,1)S(1)}, u32[]{:S(2)}, u32[]{:S(2)}) collective-permute-start(bf16[128,2048]{1,0:T(8,128)(2,1)S(1)} %collective-permute-done.70), channel_id=1, source_target_pairs={{0,1},{1,0},{2,3},{3,2},{4,5},{5,4},{6,7},{7,6},{8,9},{9,8},{10,11... | collective-permute-start | bytes 1572872 | tf_op jit(solution)/shard_map/ppermute | solution.py:68
  257.9 20.0 %collective-permute-start.72 = (bf16[128,2048]{1,0:T(8,128)(2,1)S(1)}, bf16[128,2048]{1,0:T(8,128)(2,1)S(1)}, u32[]{:S(2)}, u32[]{:S(2)}) collective-permute-start(bf16[128,2048]{1,0:T(8,128)(2,1)S(1)} %collective-permute-done.70), channel_id=1, source_target_pairs={{0,2},{1,3},{2,0},{3,1},{4,6},{5,7},{6,4},{7,5},{8,10},{9,11},{10,... | collective-permute-start | bytes 1572872 | tf_op jit(solution)/shard_map/ppermute | solution.py:68
  258.7 54.8 %collective-permute-start.75 = (bf16[128,2048]{1,0:T(8,128)(2,1)S(1)}, bf16[128,2048]{1,0:T(8,128)(2,1)S(1)}, u32[]{:S(2)}, u32[]{:S(2)}) collective-permute-start(bf16[128,2048]{1,0:T(8,128)(2,1)S(1)} %collective-permute-done.70), channel_id=1, source_target_pairs={{0,4},{1,5},{2,6},{3,7},{4,8},{5,9},{6,10},{7,11},{8,12},{9,13},{1... | collective-permute-start | bytes 1572872 | tf_op jit(solution)/shard_map/ppermute | solution.py:72
  266.6 46.2 %collective-permute-start.9 = (bf16[4,64,1280]{2,1,0:T(8,128)(2,1)S(1)}, bf16[4,64,1280]{2,1,0:T(8,128)(2,1)S(1)}, u32[]{:S(2)}, u32[]{:S(2)}) collective-permute-start(bf16[4,64,1280]{2,1,0:T(8,128)(2,1)S(1)} %collective-permute-done.8), channel_id=1, source_target_pairs={{0,4},{1,5},{2,6},{3,7},{4,8},{5,9},{6,10},{7,11},{8,12},{9,13},{1... | collective-permute-start | bytes 1966088 | tf_op jit(solution)/shard_map/ppermute | solution.py:72
  277.9 34.8 %collective-permute-start.17 = (bf16[128,2048]{1,0:T(8,128)(2,1)S(1)}, bf16[128,2048]{1,0:T(8,128)(2,1)S(1)}, u32[]{:S(2)}, u32[]{:S(2)}) collective-permute-start(bf16[128,2048]{1,0:T(8,128)(2,1)S(1)} %collective-permute-done.16), channel_id=1, source_target_pairs={{0,4},{1,5},{2,6},{3,7},{4,8},{5,9},{6,10},{7,11},{8,12},{9,13},{1... | collective-permute-start | bytes 1572872 | tf_op jit(solution)/shard_map/ppermute | solution.py:72
  278.0 37.1 %collective-permute-start.74 = (bf16[64,2048]{1,0:T(8,128)(2,1)S(1)}, bf16[64,2048]{1,0:T(8,128)(2,1)S(1)}, u32[]{:S(2)}, u32[]{:S(2)}) collective-permute-start(bf16[64,2048]{1,0:T(8,128)(2,1)S(1)} %slice.635), channel_id=1, source_target_pairs={{0,1},{1,0},{2,3},{3,2},{4,5},{5,4},{6,7},{7,6},{8,9},{9,8},{10,11... | collective-permute-start | bytes 786440 | tf_op jit(solution)/shard_map/ppermute | solution.py:68
  278.1 37.4 %collective-permute-start.73 = (bf16[64,2048]{1,0:T(8,128)(2,1)S(1)}, bf16[64,2048]{1,0:T(8,128)(2,1)S(1)}, u32[]{:S(2)}, u32[]{:S(2)}) collective-permute-start(bf16[64,2048]{1,0:T(8,128)(2,1)S(1)} %slice.634), channel_id=1, source_target_pairs={{0,2},{1,3},{2,0},{3,1},{4,6},{5,7},{6,4},{7,5},{8,10},{9,11},{10,... | collective-permute-start | bytes 786440 | tf_op jit(solution)/shard_map/ppermute | solution.py:68
  312.8 19.5 %collective-permute-start.18 = (bf16[4,128,2048]{2,1,0:T(8,128)(2,1)S(1)}, bf16[4,128,2048]{2,1,0:T(8,128)(2,1)S(1)}, u32[]{:S(2)}, u32[]{:S(2)}) collective-permute-start(bf16[4,128,2048]{2,1,0:T(8,128)(2,1)S(1)} %bitcast_dynamic-update-slice_fusion.31), channel_id=1, source_target_pairs={{0,16},{16,0},{1,17},{17,1},{2,18},{18,2},{3,19},{19,3},{4,20},{20... | collective-permute-start | bytes 6291464 | tf_op jit(solution)/shard_map/ppermute | solution.py:75
  312.9 22.1 %collective-permute-start.10 = (bf16[4,4,64,1280]{3,2,1,0:T(8,128)(2,1)S(1)}, bf16[4,4,64,1280]{3,2,1,0:T(8,128)(2,1)S(1)}, u32[]{:S(2)}, u32[]{:S(2)}) collective-permute-start(bf16[4,4,64,1280]{3,2,1,0:T(8,128)(2,1)S(1)} %bitcast_dynamic-update-slice_fusion), channel_id=1, source_target_pairs={{0,16},{16,0},{1,17},{17,1},{2,18},{18,2},{3,19},{19,3},{4,20},{20... | collective-permute-start | bytes 7864328 | tf_op jit(solution)/shard_map/ppermute | solution.py:75
  329.5 104.0 %collective-permute-start.79 = (bf16[64,2048]{1,0:T(8,128)(2,1)}, bf16[64,2048]{1,0:T(8,128)(2,1)}, u32[]{:S(2)}, u32[]{:S(2)}) collective-permute-start(bf16[64,2048]{1,0:T(8,128)(2,1)} %slice.637), channel_id=1, source_target_pairs={{0,1},{1,0},{2,3},{3,2},{4,5},{5,4},{6,7},{7,6},{8,9},{9,8},{10,11... | collective-permute-start | bytes 786440 | tf_op jit(solution)/shard_map/ppermute | solution.py:68
  330.9 102.6 %collective-permute-start.78 = (bf16[64,2048]{1,0:T(8,128)(2,1)}, bf16[64,2048]{1,0:T(8,128)(2,1)}, u32[]{:S(2)}, u32[]{:S(2)}) collective-permute-start(bf16[64,2048]{1,0:T(8,128)(2,1)} %slice.636), channel_id=1, source_target_pairs={{0,2},{1,3},{2,0},{3,1},{4,6},{5,7},{6,4},{7,5},{8,10},{9,11},{10,... | collective-permute-start | bytes 786440 | tf_op jit(solution)/shard_map/ppermute | solution.py:68
  465.1 20.1 %collective-permute-start.28 = (bf16[128,2048]{1,0:T(8,128)(2,1)S(1)}, bf16[128,2048]{1,0:T(8,128)(2,1)S(1)}, u32[]{:S(2)}, u32[]{:S(2)}) collective-permute-start(bf16[128,2048]{1,0:T(8,128)(2,1)S(1)} %collective-permute-done.27), channel_id=1, source_target_pairs={{0,1},{1,0},{2,3},{3,2},{4,5},{5,4},{6,7},{7,6},{8,9},{9,8},{10,11... | collective-permute-start | bytes 1572872 | tf_op jit(solution)/shard_map/ppermute | solution.py:68
  467.2 19.3 %collective-permute-start.32 = (bf16[128,2048]{1,0:T(8,128)(2,1)S(1)}, bf16[128,2048]{1,0:T(8,128)(2,1)S(1)}, u32[]{:S(2)}, u32[]{:S(2)}) collective-permute-start(bf16[128,2048]{1,0:T(8,128)(2,1)S(1)} %collective-permute-done.27), channel_id=1, source_target_pairs={{0,4},{1,5},{2,6},{3,7},{4,8},{5,9},{6,10},{7,11},{8,12},{9,13},{1... | collective-permute-start | bytes 1572872 | tf_op jit(solution)/shard_map/ppermute | solution.py:72
  573.1 100.7 %all-to-all-start = ((f32[16,1,128]{2,1,0:T(1,128)}), f32[16,1,128]{2,1,0:T(1,128)}, u32[]{:S(2)}, u32[]{:S(2)}) async-start(f32[16,1,128]{2,1,0:T(1,128)} %bitcast.149), calls=%async_computation | async-start | bytes 16384 | tf_op jit(solution)/shard_map/all_to_all | solution.py:343
  626.7 47.9 %collective-permute-start.80 = (bf16[64,2048]{1,0:T(8,128)(2,1)}, bf16[64,2048]{1,0:T(8,128)(2,1)S(1)}, u32[]{:S(2)}, u32[]{:S(2)}) collective-permute-start(bf16[64,2048]{1,0:T(8,128)(2,1)} %get-tuple-element.365), channel_id=1, source_target_pairs={{0,2},{1,3},{2,0},{3,1},{4,6},{5,7},{6,4},{7,5},{8,10},{9,11},{10,... | collective-permute-start | bytes 786440 | tf_op jit(solution)/shard_map/ppermute | solution.py:68
  628.4 46.5 %collective-permute-start.92 = (bf16[64,2048]{1,0:T(8,128)(2,1)}, bf16[64,2048]{1,0:T(8,128)(2,1)S(1)}, u32[]{:S(2)}, u32[]{:S(2)}) collective-permute-start(bf16[64,2048]{1,0:T(8,128)(2,1)} %get-tuple-element.367), channel_id=1, source_target_pairs={{0,2},{1,3},{2,0},{3,1},{4,6},{5,7},{6,4},{7,5},{8,10},{9,11},{10,... | collective-permute-start | bytes 786440 | tf_op jit(solution)/shard_map/ppermute | solution.py:68
  628.7 48.0 %collective-permute-start.88 = (bf16[64,2048]{1,0:T(8,128)(2,1)S(1)}, bf16[64,2048]{1,0:T(8,128)(2,1)S(1)}, u32[]{:S(2)}, u32[]{:S(2)}) collective-permute-start(bf16[64,2048]{1,0:T(8,128)(2,1)S(1)} %get-tuple-element.369), channel_id=1, source_target_pairs={{0,2},{1,3},{2,0},{3,1},{4,6},{5,7},{6,4},{7,5},{8,10},{9,11},{10,... | collective-permute-start | bytes 786440 | tf_op jit(solution)/shard_map/ppermute | solution.py:68
  630.4 48.2 %collective-permute-start.84 = (bf16[64,2048]{1,0:T(8,128)(2,1)}, bf16[64,2048]{1,0:T(8,128)(2,1)}, u32[]{:S(2)}, u32[]{:S(2)}) collective-permute-start(bf16[64,2048]{1,0:T(8,128)(2,1)} %get-tuple-element.371), channel_id=1, source_target_pairs={{0,2},{1,3},{2,0},{3,1},{4,6},{5,7},{6,4},{7,5},{8,10},{9,11},{10,... | collective-permute-start | bytes 786440 | tf_op jit(solution)/shard_map/ppermute | solution.py:68
  630.7 49.8 %collective-permute-start.94 = (bf16[64,2048]{1,0:T(8,128)(2,1)}, bf16[64,2048]{1,0:T(8,128)(2,1)}, u32[]{:S(2)}, u32[]{:S(2)}) collective-permute-start(bf16[64,2048]{1,0:T(8,128)(2,1)} %get-tuple-element.373), channel_id=1, source_target_pairs={{0,1},{1,0},{2,3},{3,2},{4,5},{5,4},{6,7},{7,6},{8,9},{9,8},{10,11... | collective-permute-start | bytes 786440 | tf_op jit(solution)/shard_map/ppermute | solution.py:68
  678.7 19.8 %collective-permute-start.42 = (bf16[64,2048]{1,0:T(8,128)(2,1)}, bf16[64,2048]{1,0:T(8,128)(2,1)S(1)}, u32[]{:S(2)}, u32[]{:S(2)}) collective-permute-start(bf16[64,2048]{1,0:T(8,128)(2,1)} %get-tuple-element.389), channel_id=1, source_target_pairs={{0,2},{1,3},{2,0},{3,1},{4,6},{5,7},{6,4},{7,5},{8,10},{9,11},{10,... | collective-permute-start | bytes 786440 | tf_op jit(solution)/shard_map/ppermute | solution.py:68
  680.5 19.8 %collective-permute-start.54 = (bf16[64,2048]{1,0:T(8,128)(2,1)}, bf16[64,2048]{1,0:T(8,128)(2,1)S(1)}, u32[]{:S(2)}, u32[]{:S(2)}) collective-permute-start(bf16[64,2048]{1,0:T(8,128)(2,1)} %get-tuple-element.391), channel_id=1, source_target_pairs={{0,2},{1,3},{2,0},{3,1},{4,6},{5,7},{6,4},{7,5},{8,10},{9,11},{10,... | collective-permute-start | bytes 786440 | tf_op jit(solution)/shard_map/ppermute | solution.py:68
  700.6 21.1 %collective-permute-start.44 = (bf16[64,2048]{1,0:T(8,128)(2,1)S(1)}, bf16[64,2048]{1,0:T(8,128)(2,1)S(1)}, u32[]{:S(2)}, u32[]{:S(2)}) collective-permute-start(bf16[64,2048]{1,0:T(8,128)(2,1)S(1)} %copy-done.84), channel_id=1, source_target_pairs={{0,1},{1,0},{2,3},{3,2},{4,5},{5,4},{6,7},{7,6},{8,9},{9,8},{10,11... | collective-permute-start | bytes 786440 | tf_op jit(solution)/shard_map/ppermute | solution.py:68
  705.1 23.3 %collective-permute-start.95 = (bf16[128,2048]{1,0:T(8,128)(2,1)S(1)}, bf16[128,2048]{1,0:T(8,128)(2,1)S(1)}, u32[]{:S(2)}, u32[]{:S(2)}) collective-permute-start(bf16[128,2048]{1,0:T(8,128)(2,1)S(1)} %pad_maximum_fusion.23), channel_id=1, source_target_pairs={{0,2},{1,3},{2,0},{3,1},{4,6},{5,7},{6,4},{7,5},{8,10},{9,11},{10,... | collective-permute-start | bytes 1572872 | tf_op jit(solution)/shard_map/ppermute | solution.py:68
  706.8 26.1 %collective-permute-start.93 = (bf16[128,2048]{1,0:T(8,128)(2,1)S(1)}, bf16[128,2048]{1,0:T(8,128)(2,1)S(1)}, u32[]{:S(2)}, u32[]{:S(2)}) collective-permute-start(bf16[128,2048]{1,0:T(8,128)(2,1)S(1)} %pad_maximum_fusion.22), channel_id=1, source_target_pairs={{0,1},{1,0},{2,3},{3,2},{4,5},{5,4},{6,7},{7,6},{8,9},{9,8},{10,11... | collective-permute-start | bytes 1572872 | tf_op jit(solution)/shard_map/ppermute | solution.py:68
  710.5 34.1 %collective-permute-start.91 = (bf16[128,2048]{1,0:T(8,128)(2,1)S(1)}, bf16[128,2048]{1,0:T(8,128)(2,1)S(1)}, u32[]{:S(2)}, u32[]{:S(2)}) collective-permute-start(bf16[128,2048]{1,0:T(8,128)(2,1)S(1)} %pad_maximum_fusion.21), channel_id=1, source_target_pairs={{0,2},{1,3},{2,0},{3,1},{4,6},{5,7},{6,4},{7,5},{8,10},{9,11},{10,... | collective-permute-start | bytes 1572872 | tf_op jit(solution)/shard_map/ppermute | solution.py:68
  728.3 19.0 %collective-permute-start.89 = (bf16[128,2048]{1,0:T(8,128)(2,1)S(1)}, bf16[128,2048]{1,0:T(8,128)(2,1)S(1)}, u32[]{:S(2)}, u32[]{:S(2)}) collective-permute-start(bf16[128,2048]{1,0:T(8,128)(2,1)S(1)} %pad_maximum_fusion.20), channel_id=1, source_target_pairs={{0,1},{1,0},{2,3},{3,2},{4,5},{5,4},{6,7},{7,6},{8,9},{9,8},{10,11... | collective-permute-start | bytes 1572872 | tf_op jit(solution)/shard_map/ppermute | solution.py:68
  732.9 22.6 %collective-permute-start.53 = (bf16[128,2048]{1,0:T(8,128)(2,1)S(1)}, bf16[128,2048]{1,0:T(8,128)(2,1)S(1)}, u32[]{:S(2)}, u32[]{:S(2)}) collective-permute-start(bf16[128,2048]{1,0:T(8,128)(2,1)S(1)} %pad_maximum_fusion.13), channel_id=1, source_target_pairs={{0,2},{1,3},{2,0},{3,1},{4,6},{5,7},{6,4},{7,5},{8,10},{9,11},{10,... | collective-permute-start | bytes 1572872 | tf_op jit(solution)/shard_map/ppermute | solution.py:68
  735.7 19.9 %collective-permute-start.51 = (bf16[128,2048]{1,0:T(8,128)(2,1)S(1)}, bf16[128,2048]{1,0:T(8,128)(2,1)S(1)}, u32[]{:S(2)}, u32[]{:S(2)}) collective-permute-start(bf16[128,2048]{1,0:T(8,128)(2,1)S(1)} %pad_maximum_fusion.12), channel_id=1, source_target_pairs={{0,1},{1,0},{2,3},{3,2},{4,5},{5,4},{6,7},{7,6},{8,9},{9,8},{10,11... | collective-permute-start | bytes 1572872 | tf_op jit(solution)/shard_map/ppermute | solution.py:68
  755.6 31.9 %collective-permute-start.122 = (bf16[1024,768]{1,0:T(8,128)(2,1)S(1)}, bf16[1024,768]{1,0:T(8,128)(2,1)S(1)}, u32[]{:S(2)}, u32[]{:S(2)}) collective-permute-start(bf16[1024,768]{1,0:T(8,128)(2,1)S(1)} %fusion.61), channel_id=1, source_target_pairs={{0,16},{16,0},{1,17},{17,1},{2,18},{18,2},{3,19},{19,3},{4,20},{20... | collective-permute-start | bytes 4718600 | tf_op jit(solution)/shard_map/ppermute | solution.py:75
  759.7 18.9 %collective-permute-start.47 = (bf16[128,2048]{1,0:T(8,128)(2,1)S(1)}, bf16[128,2048]{1,0:T(8,128)(2,1)S(1)}, u32[]{:S(2)}, u32[]{:S(2)}) collective-permute-start(bf16[128,2048]{1,0:T(8,128)(2,1)S(1)} %pad_maximum_fusion.10), channel_id=1, source_target_pairs={{0,1},{1,0},{2,3},{3,2},{4,5},{5,4},{6,7},{7,6},{8,9},{9,8},{10,11... | collective-permute-start | bytes 1572872 | tf_op jit(solution)/shard_map/ppermute | solution.py:68
  762.3 21.9 %collective-permute-start.59 = (bf16[128,2048]{1,0:T(8,128)(2,1)S(1)}, bf16[128,2048]{1,0:T(8,128)(2,1)S(1)}, u32[]{:S(2)}, u32[]{:S(2)}) collective-permute-start(bf16[128,2048]{1,0:T(8,128)(2,1)S(1)} %fusion.98), channel_id=1, source_target_pairs={{0,4},{1,5},{2,6},{3,7},{4,8},{5,9},{6,10},{7,11},{8,12},{9,13},{1... | collective-permute-start | bytes 1572872 | tf_op jit(solution)/shard_map/ppermute | solution.py:72
  778.6 42.4 %collective-permute-start.123 = (bf16[1024,768]{1,0:T(8,128)(2,1)}, bf16[1024,768]{1,0:T(8,128)(2,1)}, u32[]{:S(2)}, u32[]{:S(2)}) collective-permute-start(bf16[1024,768]{1,0:T(8,128)(2,1)} %fusion.62), channel_id=1, source_target_pairs={{0,16},{16,0},{1,17},{17,1},{2,18},{18,2},{3,19},{19,3},{4,20},{20... | collective-permute-start | bytes 4718600 | tf_op jit(solution)/shard_map/ppermute | solution.py:75
  788.7 22.9 %collective-permute-start.60 = (bf16[128,2048]{1,0:T(8,128)(2,1)}, bf16[128,2048]{1,0:T(8,128)(2,1)S(1)}, u32[]{:S(2)}, u32[]{:S(2)}) collective-permute-start(bf16[128,2048]{1,0:T(8,128)(2,1)} %fusion.101), channel_id=1, source_target_pairs={{0,4},{1,5},{2,6},{3,7},{4,8},{5,9},{6,10},{7,11},{8,12},{9,13},{1... | collective-permute-start | bytes 1572872 | tf_op jit(solution)/shard_map/ppermute | solution.py:72
  796.5 216.0 %collective-permute-start.124 = (bf16[768,1024]{1,0:T(8,128)(2,1)}, bf16[768,1024]{1,0:T(8,128)(2,1)}, u32[]{:S(2)}, u32[]{:S(2)}) collective-permute-start(bf16[768,1024]{1,0:T(8,128)(2,1)} %fusion.63), channel_id=1, source_target_pairs={{0,16},{16,0},{1,17},{17,1},{2,18},{18,2},{3,19},{19,3},{4,20},{20... | collective-permute-start | bytes 4718600 | tf_op jit(solution)/shard_map/ppermute | solution.py:75
  825.4 190.7 %all-to-all-start.2 = ((f32[32,1,1088]{2,1,0:T(1,128)}), f32[32,1,1088]{2,1,0:T(1,128)S(1)}, u32[]{:S(2)}, u32[]{:S(2)}) async-start(f32[32,1,1088]{2,1,0:T(1,128)} %copy.167), calls=%async_computation.2 | async-start | bytes 294912 | tf_op jit(solution)/shard_map/all_to_all | solution.py:439
  974.7 49.1 %collective-permute-start.117 = (bf16[512,2048]{1,0:T(8,128)(2,1)}, bf16[512,2048]{1,0:T(8,128)(2,1)}, u32[]{:S(2)}, u32[]{:S(2)}) collective-permute-start(bf16[512,2048]{1,0:T(8,128)(2,1)} %fusion.49), channel_id=1, source_target_pairs={{0,16},{16,0},{1,17},{17,1},{2,18},{18,2},{3,19},{19,3},{4,20},{20... | collective-permute-start | bytes 6291464 | tf_op jit(solution)/shard_map/ppermute | solution.py:75
  1006.6 22.2 %collective-permute-start.110 = (bf16[1024,1280]{1,0:T(8,128)(2,1)}, bf16[1024,1280]{1,0:T(8,128)(2,1)}, u32[]{:S(2)}, u32[]{:S(2)}) collective-permute-start(bf16[1024,1280]{1,0:T(8,128)(2,1)} %fusion.47), channel_id=1, source_target_pairs={{0,16},{16,0},{1,17},{17,1},{2,18},{18,2},{3,19},{19,3},{4,20},{20... | collective-permute-start | bytes 7864328 | tf_op jit(solution)/shard_map/ppermute | solution.py:75
  1033.5 25.9 %collective-permute-start.111 = (bf16[4,64,1280]{2,1,0:T(8,128)(2,1)}, bf16[4,64,1280]{2,1,0:T(8,128)(2,1)}, u32[]{:S(2)}, u32[]{:S(2)}) collective-permute-start(bf16[4,64,1280]{2,1,0:T(8,128)(2,1)} %dynamic-slice_bitcast_fusion), channel_id=1, source_target_pairs={{0,4},{1,5},{2,6},{3,7},{4,8},{5,9},{6,10},{7,11},{8,12},{9,13},{1... | collective-permute-start | bytes 1966088 | tf_op jit(solution)/shard_map/ppermute | solution.py:72
  1038.5 70.4 %all-to-all-start.1 = ((f32[32,1,72]{2,1,0:T(1,128)}), f32[32,1,72]{2,1,0:T(1,128)S(1)}, u32[]{:S(2)}, u32[]{:S(2)}) async-start(f32[32,1,72]{2,1,0:T(1,128)} %bitcast.180), calls=%async_computation.1 | async-start | bytes 32768 | tf_op jit(solution)/shard_map/all_to_all | solution.py:439
  1046.6 24.1 %collective-permute-start.119 = (bf16[128,2048]{1,0:T(8,128)(2,1)S(1)}, bf16[128,2048]{1,0:T(8,128)(2,1)S(1)}, u32[]{:S(2)}, u32[]{:S(2)}) collective-permute-start(bf16[128,2048]{1,0:T(8,128)(2,1)S(1)} %fusion.79), channel_id=1, source_target_pairs={{0,4},{1,5},{2,6},{3,7},{4,8},{5,9},{6,10},{7,11},{8,12},{9,13},{1... | collective-permute-start | bytes 1572872 | tf_op jit(solution)/shard_map/ppermute | solution.py:72
  1060.7 24.0 %collective-permute-start.112 = (bf16[4,64,1280]{2,1,0:T(8,128)(2,1)S(1)}, bf16[4,64,1280]{2,1,0:T(8,128)(2,1)S(1)}, u32[]{:S(2)}, u32[]{:S(2)}) collective-permute-start(bf16[4,64,1280]{2,1,0:T(8,128)(2,1)S(1)} %fusion.65), channel_id=1, source_target_pairs={{0,4},{1,5},{2,6},{3,7},{4,8},{5,9},{6,10},{7,11},{8,12},{9,13},{1... | collective-permute-start | bytes 1966088 | tf_op jit(solution)/shard_map/ppermute | solution.py:72
  1072.7 36.3 %collective-permute-start.120 = (bf16[128,2048]{1,0:T(8,128)(2,1)}, bf16[128,2048]{1,0:T(8,128)(2,1)}, u32[]{:S(2)}, u32[]{:S(2)}) collective-permute-start(bf16[128,2048]{1,0:T(8,128)(2,1)} %fusion.80), channel_id=1, source_target_pairs={{0,4},{1,5},{2,6},{3,7},{4,8},{5,9},{6,10},{7,11},{8,12},{9,13},{1... | collective-permute-start | bytes 1572872 | tf_op jit(solution)/shard_map/ppermute | solution.py:72
  1085.8 25.3 %collective-permute-start.113 = (bf16[4,64,1280]{2,1,0:T(8,128)(2,1)}, bf16[4,64,1280]{2,1,0:T(8,128)(2,1)}, u32[]{:S(2)}, u32[]{:S(2)}) collective-permute-start(bf16[4,64,1280]{2,1,0:T(8,128)(2,1)} %fusion.66), channel_id=1, source_target_pairs={{0,4},{1,5},{2,6},{3,7},{4,8},{5,9},{6,10},{7,11},{8,12},{9,13},{1... | collective-permute-start | bytes 1966088 | tf_op jit(solution)/shard_map/ppermute | solution.py:72
  1112.5 27.7 %collective-permute-start.114 = (bf16[64,1280]{1,0:T(8,128)(2,1)S(1)}, bf16[64,1280]{1,0:T(8,128)(2,1)S(1)}, u32[]{:S(2)}, u32[]{:S(2)}) collective-permute-start(bf16[64,1280]{1,0:T(8,128)(2,1)S(1)} %get-tuple-element.436), channel_id=1, source_target_pairs={{0,3},{1,2},{2,1},{3,0},{4,7},{5,6},{6,5},{7,4},{8,11},{9,10},{10,... | collective-permute-start | bytes 491528 | tf_op jit(solution)/shard_map/ppermute | solution.py:68
  1116.7 23.4 %collective-permute-start.115 = (bf16[64,1280]{1,0:T(8,128)(2,1)S(1)}, bf16[64,1280]{1,0:T(8,128)(2,1)S(1)}, u32[]{:S(2)}, u32[]{:S(2)}) collective-permute-start(bf16[64,1280]{1,0:T(8,128)(2,1)S(1)} %get-tuple-element.435), channel_id=1, source_target_pairs={{0,1},{1,0},{2,3},{3,2},{4,5},{5,4},{6,7},{7,6},{8,9},{9,8},{10,11... | collective-permute-start | bytes 491528 | tf_op jit(solution)/shard_map/ppermute | solution.py:68
  (229 other events, 2577.3 us)
Sparse Core Ops, SparseCore 0:
  15.0 122.0 all-reduce.6
Sparse Core Ops, SparseCore 1:
  14.8 14.7 all-gather.4
  31.0 13.2 all-gather.6
  45.6 13.2 all-gather.8

commit v2 on v1

v2 whole, which is shorter than its diff:
```python
import jax
import jax.numpy as jnp
from jax import lax
from jax.experimental import pallas as pl
from jax.experimental.pallas import tpu as pltpu
from jax.sharding import PartitionSpec as P

MODEL_WIDTH = 2048
QUERY_HEADS = 32
KEY_VALUE_HEADS = 4
HEAD_SIZE = 128
TOP = 8
PER_KV = QUERY_HEADS // KEY_VALUE_HEADS
QW = PER_KV * HEAD_SIZE

EPS = 1e-06
THETA = 1000000.0
MASKED = -1e30
BF = jnp.bfloat16
F32 = jnp.float32


def rms_scale(values, scaling):
    return values * lax.rsqrt(jnp.mean(values * values, axis=-1, keepdims=True) + EPS) * scaling


def rotary_tables(position):
    half = HEAD_SIZE // 2
    index_float = jnp.arange(half, dtype=jnp.float32)
    freq = jnp.power(jnp.float32(THETA), -2.0 * index_float / HEAD_SIZE)
    angle = position.astype(jnp.float32)[:, None] * freq[None, :]
    cosine, sine = jnp.cos(angle), jnp.sin(angle)
    return (
        jnp.concatenate([cosine, cosine], axis=-1),
        jnp.concatenate([-sine, sine], axis=-1),
    )


def project_kernel(planes, ids_ref, x_ref, cos_ref, sin_ref, gains_ref, *refs):
    pieces, (w_ref, proj_ref, turned_ref) = refs[: 2 * planes], refs[2 * planes :]
    mine_a, mine_b, mine_g = ids_ref[0], ids_ref[1], ids_ref[2]
    last = pl.program_id(0) == pl.num_programs(0) - 1
    rows = pieces[0].shape[0] // 4
    for number, piece in enumerate(pieces):
        g = mine_g ^ (number // planes)
        a = lax.rem(mine_a + planes - number % planes, planes)
        for k in range(4):
            at = pl.multiple_of(((g * planes + a) * 4 + (mine_b ^ k)) * rows, rows)
            w_ref[pl.ds(at, rows), :] = piece[k * rows : (k + 1) * rows, :]
    projected = jnp.dot(x_ref[...], w_ref[...], preferred_element_type=F32)
    proj_ref[...] = projected

    def turn(values, gain):
        scaled = (
            values * lax.rsqrt(jnp.mean(values * values, axis=-1, keepdims=True) + EPS) * gain
        )
        swapped = pltpu.roll(scaled, HEAD_SIZE // 2, 1)
        return scaled * cos_ref[...] + swapped * sin_ref[...]

    gain_q, gain_k = gains_ref[0:1], gains_ref[1:2]
    first, second = projected[:, :HEAD_SIZE], projected[:, HEAD_SIZE:]
    turned_ref[:, :HEAD_SIZE] = turn(first, jnp.where(last, gain_k, gain_q)).astype(BF)
    turned_ref[:, HEAD_SIZE:] = jnp.where(last, second, turn(second, gain_q)).astype(BF)


def project(ids, rows_in, cosine, sine, gains, *pieces):
    count, width = rows_in.shape
    height, columns = pieces[0].shape
    step = 2 * HEAD_SIZE
    whole = lambda array: pl.BlockSpec(array.shape, lambda i: (0, 0))
    strip = lambda height: pl.BlockSpec((height, step), lambda i: (0, i))
    return pl.pallas_call(
        lambda *refs: project_kernel(len(pieces) // 2, *refs),
        grid=(columns // step,),
        in_specs=[pl.BlockSpec(memory_space=pltpu.SMEM)]
        + [whole(rows_in), whole(cosine), whole(sine), whole(gains)]
        + [strip(height)] * len(pieces),
        out_specs=[strip(width), strip(count), strip(count)],
        out_shape=[
            jax.ShapeDtypeStruct((width, columns), BF),
            jax.ShapeDtypeStruct((count, columns), F32),
            jax.ShapeDtypeStruct((count, columns), BF),
        ],
        compiler_params=pltpu.CompilerParams(vmem_limit_bytes=32 * 2**20),
    )(ids, rows_in, cosine, sine, gains, *pieces)


def unturn_kernel(grad_ref, proj_ref, cos_ref, sin_ref, gain_ref, out_ref, gain_grad_ref):
    @pl.when(pl.program_id(0) == 0)
    def _():
        gain_grad_ref[...] = jnp.zeros_like(gain_grad_ref)

    grad, values = grad_ref[...], proj_ref[...]
    grad = grad * cos_ref[...] + pltpu.roll(grad * sin_ref[...], HEAD_SIZE // 2, 1)
    scale = lax.rsqrt(jnp.mean(values * values, axis=-1, keepdims=True) + EPS)
    gain_grad_ref[...] += jnp.sum(grad * values * scale, axis=0, keepdims=True)
    grad = grad * gain_ref[...]
    inner = jnp.mean(grad * values, axis=-1, keepdims=True)
    out_ref[...] = (scale * grad - values * (scale * scale * scale * inner)).astype(BF)


def unturn(grad, projected, first_head, cosine, sine, gain):
    count, columns = grad.shape
    block = (count, HEAD_SIZE)
    whole = lambda array: pl.BlockSpec(array.shape, lambda i: (0, 0))
    return pl.pallas_call(
        unturn_kernel,
        grid=(columns // HEAD_SIZE,),
        in_specs=[
            pl.BlockSpec(block, lambda i: (0, i)),
            pl.BlockSpec(block, lambda i: (0, i + first_head)),
            whole(cosine),
            whole(sine),
            whole(gain),
        ],
        out_specs=[pl.BlockSpec(block, lambda i: (0, i)), whole(gain)],
        out_shape=[
            jax.ShapeDtypeStruct((count, columns), BF),
            jax.ShapeDtypeStruct(gain.shape, F32),
        ],
    )(grad, projected, cosine, sine, gain)


def table_kernel(capacity, ids_ref, pairs_ref, send_ref, keep_ref, chosen_ref):
    mine_a, mine_b = ids_ref[0], ids_ref[1]
    slots, tokens = send_ref.shape[1:]
    experts = chosen_ref.shape[2]
    numbers = lax.broadcasted_iota(jnp.int32, (slots, tokens), 0).astype(F32)
    nowhere = 1e6

    def table(source, expert, k):
        hit = pairs_ref[0, source, 0] == expert.astype(F32)
        order = pairs_ref[0, source, 1] * 32.0 + pairs_ref[0, source, 2]
        place = jnp.min(jnp.where(hit, order, nowhere), axis=0, keepdims=True)
        across = jnp.broadcast_to(place, (tokens, tokens))
        before = jnp.where(across.T < across, 1.0, 0.0)
        rank = jnp.sum(before, axis=0, keepdims=True)
        inside = (place < nowhere) & (rank < capacity)
        rank = jnp.where(inside, rank + k * capacity, -1.0)
        return jnp.where(numbers == rank, 1.0, 0.0)

    send = keep = chosen = 0.0
    for k in range(4):
        send = send + table(0, mine_a * 4 + (mine_b ^ k), k)
        kept = table(k, mine_a * 4 + mine_b, k)
        keep = keep + kept
        routes = pairs_ref[0, k, 0]
        expert_rows = lax.broadcasted_iota(jnp.int32, (experts, tokens), 0).astype(F32)
        chooser = sum(
            jnp.where(routes[j : j + 1] == expert_rows, 1.0, 0.0) for j in range(TOP)
        )
        chosen = chosen + lax.dot_general(
            kept.astype(BF),
            chooser.astype(BF),
            (((1,), (1,)), ((), ())),
            preferred_element_type=F32,
        )
    send_ref[0] = send.astype(BF)
    keep_ref[0] = keep.astype(BF)
    chosen_ref[0] = chosen


def slot_tables(ids, pairs, capacity, experts):
    planes, _, _, _, tokens = pairs.shape
    slots = 4 * capacity
    block = lambda *shape: pl.BlockSpec((1,) + shape, lambda i: (i,) + (0,) * len(shape))
    return pl.pallas_call(
        lambda *refs: table_kernel(capacity, *refs),
        grid=(planes,),
        in_specs=[pl.BlockSpec(memory_space=pltpu.SMEM), block(4, 3, TOP, tokens)],
        out_specs=[block(slots, tokens), block(slots, tokens), block(slots, experts)],
        out_shape=[
            jax.ShapeDtypeStruct((planes, slots, tokens), BF),
            jax.ShapeDtypeStruct((planes, slots, tokens), BF),
            jax.ShapeDtypeStruct((planes, slots, experts), F32),
        ],
    )(ids, pairs)


def places(slot_rows, lengths_row):
    seq_ends = jnp.cumsum(lengths_row)
    starts = seq_ends - lengths_row
    segment = jnp.sum((slot_rows[:, None] >= seq_ends[None, :]).astype(jnp.int32), axis=1)
    chosen = segment[:, None] == jnp.arange(lengths_row.shape[0], dtype=jnp.int32)[None, :]
    start_of = jnp.sum(jnp.where(chosen, starts[None, :], 0), axis=1)
    return (segment, slot_rows - start_of)


def pick(blocks, index):
    return lax.dynamic_index_in_dim(blocks, index, 0, keepdims=False)


class Rounds:
    def __init__(self):
        self.active = {}
        self.asked = {}
        self.values = {}
        self.flags = set()
        self.count = 0

    def start(self, task):
        self.count += 1
        self.active[self.count] = (task, None)
        return self.count

    def wait(self, flag):
        while flag not in self.flags:
            yield None

    def until(self, *wanted):
        while True:
            for number, (task, came) in list(self.active.items()):
                if self.asked.get(number) is not None:
                    continue
                try:
                    self.asked[number] = task.send(came)
                except StopIteration as end:
                    self.values[number] = end.value
                    del self.active[number]
                    self.asked.pop(number, None)
            if all(number in self.values for number in wanted):
                break
            asked = {number: calls for number, calls in self.asked.items() if calls is not None}
            given = {number: [args for _, args in calls] for number, calls in asked.items()}
            given = lax.optimization_barrier(given)
            for number, calls in asked.items():
                came = [call(*args) for (call, _), args in zip(calls, given[number])]
                self.active[number] = (self.active[number][0], came)
            self.asked = {}
        values = [self.values[number] for number in wanted]
        return values[0] if len(values) == 1 else values

    def run(self, task):
        return self.until(self.start(task))


def later(count, task):
    for _ in range(count):
        yield []
    return (yield from task)


def work(function, *args):
    (result,) = yield [(function, args)]
    return result


class Links:
    def __init__(self, n):
        self.n = n
        self.planes = n // KEY_VALUE_HEADS
        index = lax.axis_index("expert")
        self.g = lax.axis_index("dp")
        self.index = index
        self.a = index // KEY_VALUE_HEADS
        self.b = index % KEY_VALUE_HEADS
        self.flips = [None] + [lambda v, k=k: self.flip(v, k) for k in (1, 2, 3)]
        self.shifts = [None] + [lambda v, s=s: self.shift(v, s) for s in range(1, self.planes)]
        self.backs = [None] + [lambda v, s=s: self.shift(v, -s) for s in range(1, self.planes)]

    def flip(self, value, k):
        return lax.ppermute(value, "expert", [(i, i ^ k) for i in range(self.n)])

    def shift(self, value, step):
        step = step * KEY_VALUE_HEADS
        return lax.ppermute(value, "expert", [(i, (i + step) % self.n) for i in range(self.n)])

    def onward(self, value):
        return self.shift(value, 1)

    def twin(self, value):
        return lax.ppermute(value, "dp", [(0, 1), (1, 0)])

    def behind(self, step):
        return (self.a - step) % self.planes

    def natural(self, blocks):
        odd, high = self.b % 2 == 1, self.b >= 2
        pair = [jnp.where(odd, blocks[q ^ 1], blocks[q]) for q in range(4)]
        return [jnp.where(high, pair[q ^ 2], pair[q]) for q in range(4)]

    def natural_line(self, blocks):
        twice = jnp.concatenate([blocks[::-1], blocks[::-1]], axis=0)
        return lax.dynamic_slice_in_dim(twice, self.planes - 1 - self.a, self.planes, 0)

    def plane_gather(self, own):
        half = own.shape[0] // 2
        near_x, near_y = yield [(self.flips[1], (own,)), (self.flips[2], (own,))]
        low, high = yield [(self.flips[2], (near_x[:half],)), (self.flips[1], (near_y[half:],))]
        return jnp.concatenate([own, near_x, near_y, low, high], axis=0)

    def plane_exchange(self, blocks):
        came = yield [(self.flips[k], (blocks[k],)) for k in (3, 1, 2)]
        return [blocks[0], came[1], came[2], came[0]]

    def plane_scatter(self, total):
        count = total.shape[0] // 4
        half = count // 2
        cut = lambda k, low, high: total[k * count + low : k * count + high]
        low, high = yield [
            (self.flips[2], (cut(3, 0, half).astype(BF),)),
            (self.flips[1], (cut(3, half, count).astype(BF),)),
        ]
        to_x = jnp.concatenate([cut(1, 0, half) + low.astype(F32), cut(1, half, count)], axis=0)
        to_y = jnp.concatenate([cut(2, 0, half), cut(2, half, count) + high.astype(F32)], axis=0)
        got_x, got_y = yield [
            (self.flips[1], (to_x.astype(BF),)),
            (self.flips[2], (to_y.astype(BF),)),
        ]
        return cut(0, 0, count) + got_x.astype(F32) + got_y.astype(F32)

    def line_scatter(self, blocks):
        total = blocks[1]
        for step in range(1, self.planes):
            (came,) = yield [(self.onward, (total.astype(BF),))]
            total = blocks[(1 + step) % self.planes] + came.astype(F32)
        return total

    def line_scatter_direct(self, blocks):
        steps = range(1, self.planes)
        came = yield [(self.backs[s], (blocks[s].astype(BF),)) for s in steps]
        return sum((block.astype(F32) for block in came), blocks[0])

    def small_scatter(self, blocks):
        blocks = blocks.reshape(2, self.planes, 4, -1)
        (came,) = yield [(self.twin, (pick(blocks, 1 - self.g),))]
        blocks = pick(blocks, self.g) + came
        came = yield [
            (self.shifts[step], (pick(blocks, (self.a + step) % self.planes),))
            for step in range(1, self.planes)
        ]
        total = sum(came, pick(blocks, self.a))
        came = yield [(self.flips[k], (pick(total, self.b ^ k),)) for k in (3, 1, 2)]
        return sum(came, pick(total, self.b))

    def twin_scatter(self, own, other):
        (came,) = yield [(self.twin, (other.astype(BF),))]
        return own + came.astype(F32)


def body(
    hidden,
    lengths,
    slots,
    routes,
    order,
    gain_in,
    w_query,
    key_projection_weight,
    value_projection_weight,
    gain_q,
    gain_k,
    w_out,
    gain_mid,
    w_router,
    w_gate,
    w_up,
    w_down,
    cotangent,
):
    tokens = hidden.shape[0]
    experts = w_router.shape[1]
    links = Links(experts)
    planes = links.planes
    capacity = max(2, (tokens * TOP * 9 + 8 * experts - 1) // (8 * experts))
    score_scale = HEAD_SIZE ** (-0.5)
    block_tokens = 4 * tokens
    rows = gain_in.shape[0]
    head_part = gain_q.shape[0]
    devices = 2 * experts

    rounds = Rounds()
    spread = rounds.start
    slot_count = 4 * capacity

    gate_full = lax.all_gather(w_gate, "dp", axis=1, tiled=True)[0]
    up_full = lax.all_gather(w_up, "dp", axis=1, tiled=True)[0]
    down_full = lax.all_gather(w_down, "dp", axis=2, tiled=True)[0]

    lanes = 128
    gains = jnp.concatenate([gain_in, gain_mid, gain_q, gain_k], axis=0)
    gain_count = gains.shape[0]
    gains = jnp.pad(gains, (0, -gain_count % lanes)).reshape(-1, lanes)
    router_rows = rows * experts // lanes
    small = jnp.concatenate([w_router.reshape(-1, lanes), gains], axis=0)
    small = jnp.pad(small, ((0, -small.shape[0] % 8), (0, 0)))
    small_rows = small.shape[0]
    pairs = jnp.concatenate([part.T.astype(BF) for part in (routes, order // 32, order % 32)])
    expert_numbers = jnp.arange(experts, dtype=jnp.int32)
    ids = jnp.stack([links.a, links.b, links.g]).astype(jnp.int32)
    tables = {}

    def gather_small():
        (other,) = yield [(links.twin, (small,))]
        piece = jnp.concatenate([small, other, pairs], axis=0)
        blocks = yield from links.plane_exchange([piece] * 4)
        line = jnp.concatenate(blocks, axis=0)
        came = yield [(links.shifts[s], (line,)) for s in range(1, planes)]
        line = jnp.stack([line] + came).reshape(planes, 4, piece.shape[0], lanes)
        all_pairs = line[:, :, 2 * small_rows :].astype(F32)
        all_pairs = all_pairs.reshape(planes, 4, 3, TOP, tokens)
        tables["send"], tables["keep"], tables["keep_chooser"] = slot_tables(
            ids, all_pairs, capacity, experts
        )
        line = links.natural_line(line[:, :, : 2 * small_rows])
        line = jnp.stack(links.natural([line[:, k] for k in range(4)]), axis=1)
        line = line.reshape(experts, 2, small_rows, lanes)
        first, second = line[:, 0], line[:, 1]
        swap = links.g == 1
        return jnp.concatenate(
            [jnp.where(swap, second, first), jnp.where(swap, first, second)], axis=0
        )

    small_task = spread(gather_small())

    qkv_width = QW + 2 * HEAD_SIZE

    def own_columns(b):
        cut = lambda array, width: lax.dynamic_slice_in_dim(array, b * width, width, 1)
        return jnp.concatenate(
            [
                cut(w_query, QW),
                cut(key_projection_weight, HEAD_SIZE),
                cut(value_projection_weight, HEAD_SIZE),
            ],
            axis=1,
        )

    def gather_qkv():
        blocks = yield from links.plane_exchange([own_columns(links.b ^ k) for k in range(4)])
        pieces, others = [jnp.concatenate(blocks, axis=0)], []
        for _ in range(1, planes):
            came = yield [(links.onward, (pieces[-1],)), (links.twin, (pieces[-1],))]
            pieces.append(came[0])
            others.append(came[1])
        others += yield [(links.twin, (pieces[-1],))]
        return pieces + others

    qkv_task = spread(gather_qkv())
    hidden_task = spread(later(1, links.plane_gather(hidden)))

    def choose(piece, step):
        rows_out = jnp.dot(tables["send"][step], piece, preferred_element_type=F32).astype(BF)
        return by_place(rows_out)

    def by_place(slot_rows):
        return [slot_rows[k * capacity : (k + 1) * capacity] for k in range(4)]

    def gather_upstream():
        pieces, out = [cotangent], []
        plan = [(0, True, None), (3, True, 0), (0, False, 1), (0, False, 2)]
        plan += [(2, True, None), (0, False, 3)]
        if planes != 4:
            plan = [(4, True, None)] + [(0, s < planes - 2, s) for s in range(planes)]
        for idle, hop, step in plan:
            for _ in range(idle):
                yield []
            asks = [(links.onward, (pieces[-1],))] if hop else []
            if step is not None:
                blocks = choose(pieces[step], step)
                asks += [(links.flips[k], (blocks[k],)) for k in (1, 2, 3)]
            came = yield asks
            if hop:
                pieces.append(came[0])
            if step is not None:
                out.append(jnp.concatenate([blocks[0]] + came[-3:], axis=0))
        return out

    upstream_task = spread(gather_upstream())

    head_rows = w_out.shape[0]
    to_block = [
        ((b * 2 + g) * planes + a, g * experts + a * 4 + b)
        for g in range(2)
        for a in range(planes)
        for b in range(4)
    ]
    from_block = [(there, here) for here, there in to_block]
    to_blocks = lambda value: lax.ppermute(value, ("dp", "expert"), to_block)
    from_blocks = lambda value: lax.ppermute(value, ("dp", "expert"), from_block)

    def gather_out():
        yield from rounds.wait("project")
        pieces, others = [], []
        pieces += yield [(to_blocks, (w_out,))]
        yield from rounds.wait("attend")
        for step in range(1, planes):
            if step == planes - 1:
                yield []
            came = yield [(links.onward, (pieces[-1],)), (links.twin, (pieces[-1],))]
            pieces.append(came[0])
            others.append(came[1])
        others += yield [(links.twin, (pieces[-1],))]
        return jnp.concatenate(pieces + others, axis=0)

    out_task = spread(gather_out())

    device_of = jnp.stack(
        [links.behind(s) * 4 + (links.b ^ k) for s in range(planes) for k in range(4)]
    )
    all_slots = slots.reshape(experts, tokens)[device_of].reshape(experts * tokens)
    block_slots = all_slots[:block_tokens]
    seg_key, key_position = places(all_slots, lengths[0])
    seg_query, position = seg_key[:block_tokens], key_position[:block_tokens]
    cosine, sine = rotary_tables(position)
    visible = (seg_query[:, None] == seg_key[None, :]) & (
        all_slots[None, :] <= block_slots[:, None]
    )

    small_all, block_hidden = rounds.until(small_task, hidden_task)
    full_router = small_all[:, :router_rows].reshape(MODEL_WIDTH, experts)
    gains = small_all[:, router_rows:].reshape(devices, -1)
    full_in = gains[:, :rows].reshape(MODEL_WIDTH).astype(F32)
    full_mid = gains[:, rows : 2 * rows].reshape(MODEL_WIDTH).astype(F32)
    head_gains = gains[:, 2 * rows : gain_count].reshape(devices, 2, head_part).swapaxes(0, 1)
    head_gains = head_gains.reshape(2, HEAD_SIZE).astype(F32)

    block_float = block_hidden.astype(F32)
    normalized = rms_scale(block_float, full_in).astype(BF)
    qkv_pieces = rounds.until(qkv_task)

    rounds.flags.add("project")
    w_qkv, projected, turned = rounds.run(
        work(project, ids, normalized, cosine, sine, head_gains, *qkv_pieces)
    )

    def gather_keys(own):
        came = yield [(links.shifts[s], (own,)) for s in range(1, planes)]
        return jnp.concatenate([own] + came, axis=0)

    keys_values = rounds.run(gather_keys(turned[:, QW:]))
    keys, values = keys_values[:, :HEAD_SIZE], keys_values[:, HEAD_SIZE:]

    def forward_head(query_rows, keys, values):
        scores = (
            jnp.einsum("qd,kd->qk", query_rows, keys, preferred_element_type=F32) * score_scale
        )
        scores = jnp.where(visible, scores, MASKED)
        top_score = jnp.max(scores, axis=-1, keepdims=True)
        exponent = jnp.exp(scores - top_score)
        row_total = jnp.sum(exponent, axis=-1, keepdims=True)
        weights = (exponent / row_total).astype(BF)
        mixed_rows = jnp.einsum("qk,kd->qd", weights, values, preferred_element_type=F32)
        return (mixed_rows.astype(BF), top_score + jnp.log(row_total))

    part_heads = 2
    parts = PER_KV // part_heads
    part_width = part_heads * HEAD_SIZE

    def head_of(array, head):
        return array[:, head * HEAD_SIZE : (head + 1) * HEAD_SIZE]

    def part_of(array, part):
        return array[:, part * part_width : (part + 1) * part_width]

    def forward_part(query_rows, keys, values):
        came = [forward_head(head_of(query_rows, h), keys, values) for h in range(part_heads)]
        return (jnp.concatenate([c[0] for c in came], axis=1), [c[1] for c in came])

    rounds.flags.add("attend")
    attended, log_sums = [], []
    for part in range(parts):
        got = rounds.run(work(forward_part, part_of(turned, part), keys, values))
        attended.append(got[0])
        log_sums.append(got[1])
    attended = jnp.concatenate(attended, axis=1)
    order_of = [(t, s) for t in range(2) for s in range(planes)]
    attended = jnp.concatenate(
        [
            lax.dynamic_slice_in_dim(
                attended, ((links.g ^ t) * planes + links.behind(s)) * head_rows, head_rows, 1
            )
            for t, s in order_of
        ],
        axis=1,
    )
    block_out = rounds.until(out_task)

    branch = jnp.dot(attended, block_out, preferred_element_type=F32)
    branch = rounds.run(links.plane_scatter(branch))
    x_float = hidden.astype(F32)
    x_one = x_float + branch
    norm_two, norm_two_back = jax.vjp(rms_scale, x_one, full_mid)
    xn_two = norm_two.astype(BF)

    own_chooser = jnp.any(routes[:, :, None] == expert_numbers, axis=1)

    def masked_softmax(logits, chooser):
        top = jnp.max(jnp.where(chooser, logits, MASKED), axis=-1, keepdims=True)
        exponent = jnp.where(chooser, jnp.exp(jnp.where(chooser, logits - top, 0.0)), 0.0)
        total = jnp.sum(exponent, axis=-1, keepdims=True)
        return exponent / jnp.where(total > 0.0, total, 1.0)

    upstream_slots = rounds.until(upstream_task)

    def expert_step(arrived, slot_upstream, keep_chooser):
        logits = jnp.dot(arrived, full_router, preferred_element_type=F32)
        probs = masked_softmax(logits, keep_chooser > 0.0)
        slot_probs = jnp.sum(
            jnp.where(expert_numbers == links.index, probs, 0.0), axis=1, keepdims=True
        )
        gate_pre = jnp.dot(arrived, gate_full, preferred_element_type=F32)
        up_pre = jnp.dot(arrived, up_full, preferred_element_type=F32)
        logistic = jax.nn.sigmoid(gate_pre)
        activation = (gate_pre * logistic * up_pre).astype(BF)
        returned = jnp.dot(activation, down_full, preferred_element_type=F32).astype(BF)
        upstream_float = slot_upstream.astype(F32)
        out_grad = (slot_probs * upstream_float).astype(BF)
        act_grad = jnp.einsum("rd,fd->rf", out_grad, down_full, preferred_element_type=F32)
        gate_low = (act_grad * up_pre * logistic * (1.0 + gate_pre * (1.0 - logistic))).astype(BF)
        up_low = (act_grad * gate_pre * logistic).astype(BF)
        pair_grad = (
            jnp.einsum("rf,df->rd", gate_low, gate_full, preferred_element_type=F32)
            + jnp.einsum("rf,df->rd", up_low, up_full, preferred_element_type=F32)
        ).astype(BF)
        returned_float = returned.astype(F32)
        gate_grad = jnp.sum(upstream_float * returned_float, axis=1)
        mixed = (slot_probs * returned_float).astype(BF)
        return (pair_grad, gate_grad, mixed, arrived, activation, out_grad, gate_low, up_low)

    def sum_slots(blocks, step):
        return jnp.einsum(
            "ct,cd->td",
            tables["send"][step],
            jnp.concatenate(blocks, axis=0),
            preferred_element_type=F32,
        )

    made = []

    def return_gates():
        slot_grads = jnp.stack([piece[1] for piece in made]).reshape(planes, 4, capacity, 1)
        keep = tables["keep"].reshape(planes, 4, capacity, tokens) > 0.0
        grads = jnp.sum(jnp.where(keep, slot_grads, 0.0), axis=2)
        came = yield [(links.backs[s], (grads[s],)) for s in range(1, planes)]
        line = jnp.stack([grads[0]] + came)
        blocks = yield from links.plane_exchange([line[:, k] for k in range(4)])
        line = jnp.stack(links.natural(blocks), axis=1)
        twice = jnp.concatenate([line, line], axis=0)
        line = lax.dynamic_slice_in_dim(twice, (planes - links.a) % planes, planes, 0)
        return line.reshape(experts, tokens)

    def return_mixture():
        sums, total = {}, None
        for step in range(planes):
            place = (step + 1) % planes
            blocks = by_place(made[place][2])
            asks = [(links.flips[k], (blocks[k],)) for k in (1, 2, 3)]
            if step > 1:
                asks += [(links.onward, (total.astype(BF),))]
            came = yield asks
            sums[step] = sum_slots([blocks[0]] + came[:3], place)
            if step == 0:
                total = sums[0]
            elif step > 1:
                total = came[3].astype(F32) + sums[step - 1]
        (came,) = yield [(links.onward, (total.astype(BF),))]
        return came.astype(F32) + sums[planes - 1]

    def experts_there_and_back():
        piece, ready, sums, total = xn_two, None, {}, None
        for step in range(planes + 3):
            asks = []
            if step < planes:
                blocks = choose(piece, step)
                asks += [(links.flips[k], (blocks[k],)) for k in (1, 2, 3)]
            if 2 <= step < planes + 2:
                back = by_place(made[step - 2][0])
                asks += [(links.flips[k], (back[k],)) for k in (1, 2, 3)]
            if step < planes - 1:
                asks += [(links.onward, (piece,))]
            if step >= 4:
                asks += [(links.onward, (total.astype(BF),))]
            if 1 <= step <= planes:
                args = (ready, upstream_slots[step - 1], tables["keep_chooser"][step - 1])
                asks += [(expert_step, args)]
            if step == planes + 1:
                tables["gates"] = spread(return_gates())
                tables["mixture"] = spread(return_mixture())
            came = yield asks
            if step < planes:
                ready = jnp.concatenate([blocks[0]] + came[:3], axis=0)
                came = came[3:]
            if 2 <= step < planes + 2:
                sums[step - 2] = sum_slots([back[0]] + came[:3], step - 2)
                came = came[3:]
            if step < planes - 1:
                piece, came = came[0], came[1:]
            if step >= 4:
                total, came = came[0].astype(F32) + sums[(step - 2) % planes], came[1:]
            elif step == 3:
                total = sums[1]
            if 1 <= step <= planes:
                made.append(came[0])
        return total

    moe_grad = rounds.run(experts_there_and_back())
    stacked = lambda place: jnp.concatenate([piece[place] for piece in made], axis=0)

    def by_rows(rows_in, grads_in):
        return jnp.einsum("rd,rf->df", rows_in, grads_in, preferred_element_type=F32)

    half_width = MODEL_WIDTH // 2

    def half_of(array, which):
        return lax.dynamic_slice_in_dim(array, which * half_width, half_width, 1)

    def gate_up_gradient(place):
        rows_in, grads_in = stacked(3), stacked(place)
        other, own = yield [
            (by_rows, (half_of(rows_in, 1 - links.g), grads_in)),
            (by_rows, (half_of(rows_in, links.g), grads_in)),
        ]
        return (yield from links.twin_scatter(own, other))

    def down_gradient():
        rows_in, grads_in = stacked(4), stacked(5)
        other, own = yield [
            (by_rows, (rows_in, half_of(grads_in, 1 - links.g))),
            (by_rows, (rows_in, half_of(grads_in, links.g))),
        ]
        return (yield from links.twin_scatter(own, other))

    gate_task = spread(gate_up_gradient(6))
    up_task = spread(later(1, gate_up_gradient(7)))
    down_task = spread(later(2, down_gradient()))
    own_logits = jnp.dot(xn_two, full_router, preferred_element_type=F32)
    own_probs = masked_softmax(own_logits, own_chooser)
    gate_grads = rounds.until(tables["gates"]).T

    upstream = cotangent.astype(F32)
    chosen_grad = own_probs * (
        gate_grads - jnp.sum(own_probs * gate_grads, axis=-1, keepdims=True)
    )
    logit_grad = chosen_grad.astype(BF)
    xn_two_grad = moe_grad + jnp.dot(logit_grad, full_router.T, preferred_element_type=F32)
    x_one_norm_grad, grad_mid = norm_two_back(xn_two_grad)
    x_one_grad = upstream + x_one_norm_grad
    branch_grad = x_one_grad.astype(BF)

    block_grad = rounds.run(links.plane_gather(branch_grad))
    attended_grad = jnp.einsum(
        "td,hd->th", block_grad, block_out, preferred_element_type=F32
    ).astype(BF)
    attended_grad = jnp.concatenate(
        [
            lax.dynamic_slice_in_dim(
                attended_grad,
                ((links.g ^ (h // planes)) * planes + links.behind(h % planes)) * head_rows,
                head_rows,
                1,
            )
            for h in range(2 * planes)
        ],
        axis=1,
    )

    def scatter_out():
        grad = yield from work(
            lambda rows_in, grads_in: jnp.einsum(
                "th,td->hd", rows_in, grads_in, preferred_element_type=F32
            ),
            attended,
            block_grad,
        )
        grad = yield from links.twin_scatter(grad[: QW // 2], grad[QW // 2 :])
        blocks = [grad[s * head_rows : (s + 1) * head_rows] for s in range(planes)]
        grad = yield from links.line_scatter(blocks)
        grad = yield from work(from_blocks, grad.astype(BF))
        return grad.astype(F32)

    grad_out_task = spread(scatter_out())

    def sum_of(parts):
        return links.small_scatter(
            jnp.concatenate([part.reshape(devices, -1) for part in parts], axis=1)
        )

    grad_router = jnp.dot(xn_two.T, logit_grad, preferred_element_type=F32)
    first_task = spread(sum_of([grad_mid, grad_router]))

    def backward_head(query_rows, grad_rows, log_sum, keys, values):
        scores = (
            jnp.einsum("qd,kd->qk", query_rows, keys, preferred_element_type=F32) * score_scale
        )
        scores = jnp.where(visible, scores, MASKED)
        probs = jnp.exp(scores - log_sum)
        weights = probs.astype(BF)
        prob_grad = jnp.einsum("qd,kd->qk", grad_rows, values, preferred_element_type=F32)
        row_inner = jnp.sum(probs * prob_grad, axis=-1, keepdims=True)
        score_grad = (probs * (prob_grad - row_inner)).astype(BF)
        query_grad = (
            jnp.einsum("qk,kd->qd", score_grad, keys, preferred_element_type=F32) * score_scale
        )
        key_grad = (
            jnp.einsum("qk,qd->kd", score_grad, query_rows, preferred_element_type=F32)
            * score_scale
        )
        value_grad = jnp.einsum("qk,qd->kd", weights, grad_rows, preferred_element_type=F32)
        return (query_grad, key_grad, value_grad)

    def backward_part(query_rows, grad_rows, log_sum, keys, values):
        came = [
            backward_head(head_of(query_rows, h), head_of(grad_rows, h), log_sum[h], keys, values)
            for h in range(part_heads)
        ]
        query_grad = jnp.concatenate([c[0] for c in came], axis=1)
        key_terms = jnp.concatenate([sum(c[1] for c in came), sum(c[2] for c in came)], axis=1)
        return (query_grad, key_terms)

    def to_owners(grads_in, scatter):
        other, own = yield [
            (by_rows, (half_of(normalized, 1 - links.g), grads_in)),
            (by_rows, (half_of(normalized, links.g), grads_in)),
        ]
        grad = yield from links.twin_scatter(own, other)
        grad = grad.reshape(planes, 4 * rows, grads_in.shape[1])
        grad = yield from scatter([pick(grad, links.behind(s)) for s in range(planes)])
        grad = grad.astype(BF).reshape(4, rows, grads_in.shape[1])
        blocks = yield from links.plane_exchange([pick(grad, links.b ^ k) for k in range(4)])
        return links.natural(blocks)

    query_low_grads, query_tasks, key_terms, grad_qgain = [], [], None, None
    for part in range(parts):
        got = rounds.run(
            work(
                backward_part,
                part_of(turned, part),
                part_of(attended_grad, part),
                log_sums[part],
                keys,
                values,
            )
        )
        key_terms = got[1] if part == 0 else key_terms + got[1]
        proj_grad, gain_grad = unturn(
            got[0], projected, part * part_heads, cosine, sine, head_gains[0:1]
        )
        grad_qgain = gain_grad if part == 0 else grad_qgain + gain_grad
        query_low_grads.append(proj_grad)
        if part % 2:
            low_grads = jnp.concatenate(query_low_grads[-2:], axis=1)
            task = to_owners(low_grads, links.line_scatter)
            if part == parts - 1:
                task = later(1, task)
            query_tasks.append(spread(task))
    key_terms = rounds.run(
        links.line_scatter_direct(
            [key_terms[s * block_tokens : (s + 1) * block_tokens] for s in range(planes)]
        )
    )

    key_proj_grad, grad_kgain = unturn(
        key_terms[:, :HEAD_SIZE], projected, PER_KV, cosine, sine, head_gains[1:2]
    )
    key_value_grad = jnp.concatenate([key_proj_grad, key_terms[:, HEAD_SIZE:].astype(BF)], axis=1)
    key_value_task = spread(to_owners(key_value_grad, links.line_scatter_direct))
    proj_grad = jnp.concatenate(query_low_grads + [key_value_grad], axis=1)
    xn_one_grad = jnp.einsum("tc,dc->td", proj_grad, w_qkv, preferred_element_type=F32)
    _, block_back = jax.vjp(lambda gain: rms_scale(block_float, gain), full_in)
    (grad_in,) = block_back(xn_one_grad)
    last_task = spread(sum_of([grad_in, grad_qgain, grad_kgain]))
    xn_one_grad = rounds.run(links.plane_scatter(xn_one_grad))
    _, norm_one_back = jax.vjp(lambda values: rms_scale(values, full_in), x_float)
    (x_norm_grad,) = norm_one_back(xn_one_grad)
    input_grad = (x_one_grad + x_norm_grad).astype(BF)

    grad_gate, grad_up, grad_down, mixture, grad_out = rounds.until(
        gate_task, up_task, down_task, tables["mixture"], grad_out_task
    )
    first, last, grad_kv, *grad_query = rounds.until(
        first_task, last_task, key_value_task, *query_tasks
    )
    result = (x_one + mixture).astype(BF)
    whole = lambda blocks: jnp.concatenate(blocks, axis=1).astype(F32)
    grad_query = whole([half[b] for b in range(4) for half in grad_query])
    grad_key = whole([block[:, :HEAD_SIZE] for block in grad_kv])
    grad_value = whole([block[:, HEAD_SIZE:] for block in grad_kv])
    grad_mid = first[:rows]
    grad_router = first[rows:].reshape(rows, experts)
    grad_in = last[:rows]
    grad_qgain = last[rows : rows + head_part]
    grad_kgain = last[rows + head_part :]

    return (
        result,
        input_grad,
        grad_in,
        grad_query,
        grad_key,
        grad_value,
        grad_qgain,
        grad_kgain,
        grad_out,
        grad_mid,
        grad_router,
        grad_gate[None],
        grad_up[None],
        grad_down[None],
    )


def solution(mesh):
    every = ("dp", "expert")
    in_specs = (
        P(every, None),
        P("dp", None),
        P("dp"),
        P(every, None),
        P(every, None),
        P(every),
        P(every, None),
        P(every, None),
        P(every, None),
        P(every),
        P(every),
        P(every, None),
        P(every),
        P(every, None),
        P("expert", "dp", None),
        P("expert", "dp", None),
        P("expert", None, "dp"),
        P(every, None),
    )
    out_specs = (
        P(every, None),
        P(every, None),
        P(every),
        P(every, None),
        P(every, None),
        P(every, None),
        P(every),
        P(every),
        P(every, None),
        P(every),
        P(every, None),
        P("expert", "dp", None),
        P("expert", "dp", None),
        P("expert", None, "dp"),
    )
    return jax.shard_map(body, mesh=mesh, in_specs=in_specs, out_specs=out_specs, check_vma=False)
```

time: 1170 us -> 873 us (0.75)
  waiting for transfers between devices: 387 us -> 289 us
  local copies, waits for them, and re-layouts: 153 us -> 83.3 us
  matrix products: 250 us -> 189 us
  blocking collectives: 43.5 us -> 0 us
  Pallas kernels: 0 us -> 25.8 us
  other arithmetic: 114 us -> 92.7 us
  starting transfers between devices: 185 us -> 164 us
    unnamed x5 -> x3, waiting for transfers between devices: 55.6 us -> 1.39 us
    ppermute x86 -> x88, starting transfers between devices: 155 us -> 105 us  [flip(): return lax.ppermute(value, 'expert', [(i, i ^ k) for i in range(self.n)])]
    all_gather x1 -> x0, blocking collectives: 43.5 us -> none  [body(): lax.all_gather(order * experts + routes, 'expert', axis=0, tiled=True)]
    ppermute x32 -> x50, starting transfers between devices: 19.8 us -> 57.5 us  [the longest x48 55 us: shift(): lax.ppermute(value, 'expert', [(i, (i + step) % self.n) for i in range(se...]
    convert_element_type x29 -> x22, other arithmetic: 48.4 us -> 19.1 us  [the longest x6 7.63 us: line_scatter(): came, = (yield [(self.onward, (total.astype(BF),))])]
    dynamic_update_slice x78 -> x0, local copies, waits for them, and re-layouts: 28.3 us -> none  [the longest x54 22.6 us: put(): return lax.dynamic_update_index_in_dim(buffer, block, index, 0)]
    pallas_call x0 -> x7, Pallas kernels: none -> 25.8 us  [the longest x5 12.3 us: unturn(): pl.pallas_call(unturn_kernel, grid=(columns // HEAD_SIZE,), in_specs=[pl....]
    ppermute x86 -> x88, waiting for transfers between devices: 160 us -> 138 us  [flip(): return lax.ppermute(value, 'expert', [(i, i ^ k) for i in range(self.n)])]
  transfers between devices with their start and end apart: 132 -> 159, of which waited for: 62 -> 60; matrix products, arithmetic and copies ran while one was open for 39% -> 38% of each run, Pallas kernels for 0% -> 3%
where the time goes in v2:
time: 873 us; the launch traced here: 863 us
  waiting for transfers between devices  289 us (33%)
  matrix products  189 us (22%)
  starting transfers between devices  164 us (19%)
  other arithmetic  92.7 us (11%)
  local copies, waits for them, and re-layouts  83.3 us (10%)
  Pallas kernels  25.8 us (3%)
  between operations  18.3 us (2%)
    ppermute x48, waiting for transfers between devices, shift(): lax.ppermute(value, 'expert', [(i, (i + step) % self.n) for i in range(se...  148 us
    ppermute x88, waiting for transfers between devices, flip(): return lax.ppermute(value, 'expert', [(i, i ^ k) for i in range(self.n)])  138 us
    ppermute x88, starting transfers between devices, flip(): return lax.ppermute(value, 'expert', [(i, i ^ k) for i in range(self.n)])  105 us
    ppermute x48, starting transfers between devices, shift(): lax.ppermute(value, 'expert', [(i, (i + step) % self.n) for i in range(se...  55 us
    unnamed x444, local copies, waits for them, and re-layouts  40.2 us
    dot_general x12, matrix products, by_rows(): jnp.einsum('rd,rf->df', rows_in, grads_in, preferred_element_type=F32)  32.1 us
  transfers between devices with their start and end apart: 159, of which 60 were waited for; matrix products, arithmetic and copies ran while one was open for 38% of the time, Pallas kernels for 3%

profile of v2, /device:TPU:0, one launch (start us, length us, event | category | flops | bytes accessed | tf_op | source)
XLA Modules:
  0.0 862.6 jit_solution(12632195569797169292)
XLA Ops:
  28.2 9.4 %collective-permute-done.5 = bf16[56,128]{1,0:T(8,128)(2,1)S(1)} collective-permute-done((bf16[56,128]{1,0:T(8,128)(2,1)S(1)}, bf16[56,128]{1,0:T(8,128)(2,1)S(1)}, u32[]{:S(2)}, u32[]{:S(2)}) %collective-permute-start.5) | collective-permute-done | bytes 14368 | tf_op jit(solution)/shard_map/ppermute | solution.py:262
  39.0 3.2 collective-permute-done.6
  56.4 3.7 shard_map.281
  84.1 14.0 %collective-permute-done.17.refs_8_ = bf16[256,1280]{1,0:T(8,128)(2,1)S(1)} collective-permute-done((bf16[256,1280]{1,0:T(8,128)(2,1)S(1)}, bf16[256,1280]{1,0:T(8,128)(2,1)S(1)}, u32[]{:S(2)}, u32[]{:S(2)}) %collective-permute-start.17) | collective-permute-done | bytes 655392 | tf_op jit(solution)/shard_map/ppermute | solution.py:266
  100.2 13.4 %collective-permute-done.23 = bf16[128,2048]{1,0:T(8,128)(2,1)S(1)} collective-permute-done((bf16[128,2048]{1,0:T(8,128)(2,1)}, bf16[128,2048]{1,0:T(8,128)(2,1)S(1)}, u32[]{:S(2)}, u32[]{:S(2)}) %collective-permute-start.23) | collective-permute-done | bytes 524320 | tf_op jit(solution)/shard_map/ppermute | solution.py:266
  117.2 9.8 %shard_map.282 = (bf16[2048,1280]{1,0:T(8,128)(2,1)S(1)}, f32[512,1280]{1,0:T(8,128)S(1)}, bf16[512,1280]{1,0:T(8,128)(2,1)S(1)}) custom-call(s32[3]{0:T(128)S(1)} %copy-done.5, bf16[512,2048]{1,0:T(8,128)(2,1)S(1)} %fusion.2.refs_1_, f32[512,128]{1,0:T(8,128)S(1)} %get-tuple-element.297.refs_2_.cos_ref, f32[512,128]{1,0:T(8,128)S(1)} %get-tuple-element.298.refs_3_.sin_ref, ...), custom_call_target="tpu_custom_call" | custom-call | tf_op jit(solution)/shard_map/pallas_call | solution.py:72
  129.7 3.6 collective-permute-start.26
  142.1 8.8 %collective-permute-done.25 = bf16[512,256]{1,0:T(8,128)(2,1)S(1)} collective-permute-done((bf16[512,256]{1,0:T(8,128)(2,1)S(1)}, bf16[512,256]{1,0:T(8,128)(2,1)S(1)}, u32[]{:S(2)}, u32[]{:S(2)}) %collective-permute-start.25) | collective-permute-done | bytes 262176 | tf_op jit(solution)/shard_map/ppermute | solution.py:266
  151.8 3.1 collective-permute-start.57
  159.6 4.3 collective-permute-start.58
  166.0 7.8 collective-permute-done.57
  173.8 3.4 collective-permute-done.58
  177.3 13.3 %collective-permute-done.59 = bf16[72,2048]{1,0:T(8,128)(2,1)S(1)} collective-permute-done((bf16[72,2048]{1,0:T(8,128)(2,1)S(1)}, bf16[72,2048]{1,0:T(8,128)(2,1)S(1)}, u32[]{:S(2)}, u32[]{:S(2)}) %collective-permute-start.59) | collective-permute-done | bytes 294944 | tf_op jit(solution)/shard_map/ppermute | solution.py:262
  194.2 6.9 collective-permute-start.27
  206.9 6.1 collective-permute-done.27
  215.6 3.0 collective-permute-start.29
  224.6 6.9 collective-permute-done.29
  239.0 9.9 %collective-permute-done.30 = bf16[128,2048]{1,0:T(8,128)(2,1)S(1)} collective-permute-done((bf16[128,2048]{1,0:T(8,128)(2,1)S(1)}, bf16[128,2048]{1,0:T(8,128)(2,1)S(1)}, u32[]{:S(2)}, u32[]{:S(2)}) %collective-permute-start.30) | collective-permute-done | bytes 524320 | tf_op jit(solution)/shard_map/ppermute | solution.py:266
  258.7 3.9 collective-permute-done.35
  269.7 7.1 collective-permute-done.68
  277.9 7.9 collective-permute-done.37
  291.0 6.1 collective-permute-done.40
  297.1 5.4 collective-permute-done.42
  312.2 4.0 fusion.43
  317.5 4.4 fusion.25
  321.9 3.9 multiply_convert_fusion.19
  383.2 5.4 collective-permute-done.65
  406.9 3.3 fusion.29
  410.2 3.1 fusion.73
  413.4 2.9 constant_dynamic-slice_fusion.34
  423.0 4.3 collective-permute-start.73
  436.7 3.3 collective-permute-done.76
  450.3 3.5 convolution_convert_fusion.12
  453.8 4.0 fusion.485
  462.0 10.7 %collective-permute-done.78 = bf16[72,2048]{1,0:T(8,128)(2,1)S(1)} collective-permute-done((bf16[72,2048]{1,0:T(8,128)(2,1)S(1)}, bf16[72,2048]{1,0:T(8,128)(2,1)S(1)}, u32[]{:S(2)}, u32[]{:S(2)}) %collective-permute-start.78) | collective-permute-done | bytes 294944 | tf_op jit(solution)/shard_map/ppermute | solution.py:262
  487.9 5.1 convolution_convert_fusion.11
  495.4 4.0 fusion.486
  501.2 9.9 %collective-permute-done.95 = bf16[128,2048]{1,0:T(8,128)(2,1)S(1)} collective-permute-done((bf16[128,2048]{1,0:T(8,128)(2,1)}, bf16[128,2048]{1,0:T(8,128)(2,1)S(1)}, u32[]{:S(2)}, u32[]{:S(2)}) %collective-permute-start.95) | collective-permute-done | bytes 524320 | tf_op jit(solution)/shard_map/ppermute | solution.py:262
  518.3 3.5 convolution_convert_fusion.10
  532.1 9.3 %collective-permute-done.96 = bf16[128,2048]{1,0:T(8,128)(2,1)S(1)} collective-permute-done((bf16[128,2048]{1,0:T(8,128)(2,1)S(1)}, bf16[128,2048]{1,0:T(8,128)(2,1)S(1)}, u32[]{:S(2)}, u32[]{:S(2)}) %collective-permute-start.96) | collective-permute-done | bytes 524320 | tf_op jit(solution)/shard_map/ppermute | solution.py:266
  558.2 3.2 copy-done.34
  592.3 3.6 collective-permute-start.110
  600.9 3.4 add_bitcast_fusion.2
  604.4 5.0 collective-permute-done.105
  609.4 3.2 collective-permute-done.102
  615.1 3.6 add_bitcast_fusion.1
  618.7 4.0 add_bitcast_fusion
  649.9 4.3 convolution_add_fusion.2
  673.1 5.3 fusion.436
  685.3 3.5 collective-permute-start.114
  692.2 3.5 collective-permute-done.114
  697.0 16.3 %collective-permute-done.115 = bf16[512,256]{1,0:T(8,128)(2,1)} collective-permute-done((bf16[512,256]{1,0:T(8,128)(2,1)}, bf16[512,256]{1,0:T(8,128)(2,1)}, u32[]{:S(2)}, u32[]{:S(2)}) %collective-permute-start.115) | collective-permute-done | bytes 262176 | tf_op jit(solution)/shard_map/ppermute | solution.py:266
  720.2 9.1 %fusion.439 = (bf16[512,2048]{1,0:T(8,128)(2,1)}, f32[2048]{0:T(1024)S(1)}, f32[512,2048]{1,0:T(8,128)}) fusion(f32[512]{0:T(512)S(1)} %copy-done.151, bf16[512,2048]{1,0:T(8,128)(2,1)} %constant_dynamic-update-slice_fusion.13, bf16[512,1280]{1,0:T(8,128)(2,1)} %get-tuple-element.578, bf16[2048,1280]{1,0:T(8,128)(2,1)} %copy-done.6), kind=kOutput, calls=%fused_computation.833 | convolution fusion | flops 2689595392 | bytes 14952448 | tf_op jit(solution)/shard_map/tc,dc->td/dot_general | solution.py:859
  742.6 3.2 collective-permute-done.121
  746.9 3.0 collective-permute-done.122
  759.2 3.0 collective-permute-start.126
  765.9 4.0 collective-permute-done.125
  769.9 13.9 %collective-permute-done.126 = f32[4,72]{1,0:T(4,128)S(1)} collective-permute-done((f32[4,72]{1,0:T(4,128)S(1)}, f32[4,72]{1,0:T(4,128)S(1)}, u32[]{:S(2)}, u32[]{:S(2)}) %collective-permute-start.126) | collective-permute-done | bytes 1184 | tf_op jit(solution)/shard_map/ppermute | solution.py:266
  788.7 8.7 %collective-permute-done.124 = bf16[128,2048]{1,0:T(8,128)(2,1)S(1)} collective-permute-done((bf16[128,2048]{1,0:T(8,128)(2,1)}, bf16[128,2048]{1,0:T(8,128)(2,1)S(1)}, u32[]{:S(2)}, u32[]{:S(2)}) %collective-permute-start.124) | collective-permute-done | bytes 524320 | tf_op jit(solution)/shard_map/ppermute | solution.py:262
  801.3 3.2 collective-permute-start.132
  809.3 3.8 collective-permute-done.138
  817.7 8.9 %collective-permute-done.137 = bf16[256,512]{1,0:T(8,128)(2,1)S(1)} collective-permute-done((bf16[256,512]{1,0:T(8,128)(2,1)S(1)}, bf16[256,512]{1,0:T(8,128)(2,1)S(1)}, u32[]{:S(2)}, u32[]{:S(2)}) %collective-permute-start.137) | collective-permute-done | bytes 262176 | tf_op jit(solution)/shard_map/ppermute | solution.py:266
  833.8 4.7 collective-permute-done.141
  839.3 7.5 collective-permute-done.142
  (1086 shorter events, 466.8 us)
Async XLA Ops:
  7.3 304.9 %all-gather.6.cloned.1.call-start = ((), (), s32[]{:S(2)}) async-start(), calls=%async_computation.1 | async-start | bytes 4718592 | tf_op jit(solution)/shard_map/all_gather | solution.py:377
  8.0 309.5 %all-gather.8.cloned.1.call-start = ((), (), s32[]{:S(2)}) async-start(), calls=%async_computation.2 | async-start | bytes 4718592 | tf_op jit(solution)/shard_map/all_gather | solution.py:378
  8.8 313.1 %all-gather.4.cloned.1.call-start = ((), (), s32[]{:S(2)}) async-start(), calls=%async_computation | async-start | bytes 4718592 | tf_op jit(solution)/shard_map/all_gather | solution.py:376
  14.1 53.8 %collective-permute-start.13 = (bf16[128,2048]{1,0:T(8,128)(2,1)}, bf16[128,2048]{1,0:T(8,128)(2,1)}, u32[]{:S(2)}, u32[]{:S(2)}) collective-permute-start(bf16[128,2048]{1,0:T(8,128)(2,1)} %param.35), channel_id=1, source_target_pairs={{0,4},{1,5},{2,6},{3,7},{4,8},{5,9},{6,10},{7,11},{8,12},{9,13},{1... | collective-permute-start | bytes 1572872 | tf_op jit(solution)/shard_map/ppermute | solution.py:266
  42.2 72.0 %collective-permute-start.18 = (bf16[256,1280]{1,0:T(8,128)(2,1)S(1)}, bf16[256,1280]{1,0:T(8,128)(2,1)S(1)}, u32[]{:S(2)}, u32[]{:S(2)}) collective-permute-start(bf16[256,1280]{1,0:T(8,128)(2,1)S(1)} %pad_maximum_fusion.13.refs_5_), channel_id=1, source_target_pairs={{0,16},{16,0},{1,17},{17,1},{2,18},{18,2},{3,19},{19,3},{4,20},{20... | collective-permute-start | bytes 1966088 | tf_op jit(solution)/shard_map/ppermute | solution.py:272
  50.8 26.7 %collective-permute-start.14 = (bf16[64,2048]{1,0:T(8,128)(2,1)}, bf16[64,2048]{1,0:T(8,128)(2,1)}, u32[]{:S(2)}, u32[]{:S(2)}) collective-permute-start(bf16[64,2048]{1,0:T(8,128)(2,1)} %slice.753), channel_id=1, source_target_pairs={{0,2},{1,3},{2,0},{3,1},{4,6},{5,7},{6,4},{7,5},{8,10},{9,11},{10,... | collective-permute-start | bytes 786440 | tf_op jit(solution)/shard_map/ppermute | solution.py:262
  53.2 27.0 %collective-permute-start.15 = (bf16[64,2048]{1,0:T(8,128)(2,1)}, bf16[64,2048]{1,0:T(8,128)(2,1)}, u32[]{:S(2)}, u32[]{:S(2)}) collective-permute-start(bf16[64,2048]{1,0:T(8,128)(2,1)} %slice.754), channel_id=1, source_target_pairs={{0,1},{1,0},{2,3},{3,2},{4,5},{5,4},{6,7},{7,6},{8,9},{9,8},{10,11... | collective-permute-start | bytes 786440 | tf_op jit(solution)/shard_map/ppermute | solution.py:262
  54.6 24.5 %collective-permute-start.16 = (bf16[256,1280]{1,0:T(8,128)(2,1)S(1)}, bf16[256,1280]{1,0:T(8,128)(2,1)S(1)}, u32[]{:S(2)}, u32[]{:S(2)}) collective-permute-start(bf16[256,1280]{1,0:T(8,128)(2,1)S(1)} %collective-permute-done.7.refs_6_), channel_id=1, source_target_pairs={{0,4},{1,5},{2,6},{3,7},{4,8},{5,9},{6,10},{7,11},{8,12},{9,13},{1... | collective-permute-start | bytes 1966088 | tf_op jit(solution)/shard_map/ppermute | solution.py:266
  67.9 47.8 %collective-permute-start.19 = (bf16[256,1280]{1,0:T(8,128)(2,1)S(1)}, bf16[256,1280]{1,0:T(8,128)(2,1)}, u32[]{:S(2)}, u32[]{:S(2)}) collective-permute-start(bf16[256,1280]{1,0:T(8,128)(2,1)S(1)} %collective-permute-done.7.refs_6_), channel_id=1, source_target_pairs={{0,16},{16,0},{1,17},{17,1},{2,18},{18,2},{3,19},{19,3},{4,20},{20... | collective-permute-start | bytes 1966088 | tf_op jit(solution)/shard_map/ppermute | solution.py:272
  98.7 31.0 %collective-permute-start.43 = (bf16[72,2048]{1,0:T(8,128)(2,1)S(1)}, bf16[72,2048]{1,0:T(8,128)(2,1)S(1)}, u32[]{:S(2)}, u32[]{:S(2)}) collective-permute-start(bf16[72,2048]{1,0:T(8,128)(2,1)S(1)} %copy-done.127), channel_id=1, source_target_pairs={{0,1},{1,0},{2,3},{3,2},{4,5},{5,4},{6,7},{7,6},{8,9},{9,8},{10,11... | collective-permute-start | bytes 884744 | tf_op jit(solution)/shard_map/ppermute | solution.py:262
  114.2 20.7 %collective-permute-start.44 = (bf16[72,2048]{1,0:T(8,128)(2,1)S(1)}, bf16[72,2048]{1,0:T(8,128)(2,1)S(1)}, u32[]{:S(2)}, u32[]{:S(2)}) collective-permute-start(bf16[72,2048]{1,0:T(8,128)(2,1)S(1)} %copy-done.126), channel_id=1, source_target_pairs={{0,2},{1,3},{2,0},{3,1},{4,6},{5,7},{6,4},{7,5},{8,10},{9,11},{10,... | collective-permute-start | bytes 884744 | tf_op jit(solution)/shard_map/ppermute | solution.py:262
  115.7 19.2 %collective-permute-start.45 = (bf16[72,2048]{1,0:T(8,128)(2,1)S(1)}, bf16[72,2048]{1,0:T(8,128)(2,1)S(1)}, u32[]{:S(2)}, u32[]{:S(2)}) collective-permute-start(bf16[72,2048]{1,0:T(8,128)(2,1)S(1)} %copy-done.125), channel_id=1, source_target_pairs={{0,3},{1,2},{2,1},{3,0},{4,7},{5,6},{6,5},{7,4},{8,11},{9,10},{10,... | collective-permute-start | bytes 884744 | tf_op jit(solution)/shard_map/ppermute | solution.py:262
  129.5 21.3 %collective-permute-start.25 = (bf16[512,256]{1,0:T(8,128)(2,1)S(1)}, bf16[512,256]{1,0:T(8,128)(2,1)S(1)}, u32[]{:S(2)}, u32[]{:S(2)}) collective-permute-start(bf16[512,256]{1,0:T(8,128)(2,1)S(1)} %get-tuple-element.310), channel_id=1, source_target_pairs={{0,8},{1,9},{2,10},{3,11},{4,12},{5,13},{6,14},{7,15},{8,0},{9,1},... | collective-permute-start | bytes 786440 | tf_op jit(solution)/shard_map/ppermute | solution.py:266
  129.7 22.0 %collective-permute-start.26 = (bf16[512,256]{1,0:T(8,128)(2,1)S(1)}, bf16[512,256]{1,0:T(8,128)(2,1)S(1)}, u32[]{:S(2)}, u32[]{:S(2)}) collective-permute-start(bf16[512,256]{1,0:T(8,128)(2,1)S(1)} %get-tuple-element.310), channel_id=1, source_target_pairs={{0,12},{1,13},{2,14},{3,15},{4,0},{5,1},{6,2},{7,3},{8,4},{9,5},{1... | collective-permute-start | bytes 786440 | tf_op jit(solution)/shard_map/ppermute | solution.py:266
  136.0 23.6 %collective-permute-start.50 = (bf16[72,2048]{1,0:T(8,128)(2,1)S(1)}, bf16[72,2048]{1,0:T(8,128)(2,1)S(1)}, u32[]{:S(2)}, u32[]{:S(2)}) collective-permute-start(bf16[72,2048]{1,0:T(8,128)(2,1)S(1)} %copy-done.123), channel_id=1, source_target_pairs={{0,1},{1,0},{2,3},{3,2},{4,5},{5,4},{6,7},{7,6},{8,9},{9,8},{10,11... | collective-permute-start | bytes 884744 | tf_op jit(solution)/shard_map/ppermute | solution.py:262
  136.7 27.2 %collective-permute-start.51 = (bf16[72,2048]{1,0:T(8,128)(2,1)S(1)}, bf16[72,2048]{1,0:T(8,128)(2,1)S(1)}, u32[]{:S(2)}, u32[]{:S(2)}) collective-permute-start(bf16[72,2048]{1,0:T(8,128)(2,1)S(1)} %copy-done.122), channel_id=1, source_target_pairs={{0,2},{1,3},{2,0},{3,1},{4,6},{5,7},{6,4},{7,5},{8,10},{9,11},{10,... | collective-permute-start | bytes 884744 | tf_op jit(solution)/shard_map/ppermute | solution.py:262
  140.6 23.9 %collective-permute-start.52 = (bf16[72,2048]{1,0:T(8,128)(2,1)S(1)}, bf16[72,2048]{1,0:T(8,128)(2,1)S(1)}, u32[]{:S(2)}, u32[]{:S(2)}) collective-permute-start(bf16[72,2048]{1,0:T(8,128)(2,1)S(1)} %copy-done.121), channel_id=1, source_target_pairs={{0,3},{1,2},{2,1},{3,0},{4,7},{5,6},{6,5},{7,4},{8,11},{9,10},{10,... | collective-permute-start | bytes 884744 | tf_op jit(solution)/shard_map/ppermute | solution.py:262
  150.8 40.8 %collective-permute-start.22 = (bf16[128,2048]{1,0:T(8,128)(2,1)S(1)}, bf16[128,2048]{1,0:T(8,128)(2,1)S(1)}, u32[]{:S(2)}, u32[]{:S(2)}) collective-permute-start(bf16[128,2048]{1,0:T(8,128)(2,1)S(1)} %copy-done.193), channel_id=1, source_target_pairs={{0,0},{8,1},{16,2},{24,3},{1,4},{9,5},{17,6},{25,7},{2,8},{10,9},{... | collective-permute-start | bytes 1572872 | tf_op jit(solution)/shard_map/ppermute | solution.py:479
  151.8 22.1 %collective-permute-start.57 = (bf16[72,2048]{1,0:T(8,128)(2,1)S(1)}, bf16[72,2048]{1,0:T(8,128)(2,1)S(1)}, u32[]{:S(2)}, u32[]{:S(2)}) collective-permute-start(bf16[72,2048]{1,0:T(8,128)(2,1)S(1)} %get-tuple-element.361), channel_id=1, source_target_pairs={{0,1},{1,0},{2,3},{3,2},{4,5},{5,4},{6,7},{7,6},{8,9},{9,8},{10,11... | collective-permute-start | bytes 884744 | tf_op jit(solution)/shard_map/ppermute | solution.py:262
  163.9 26.6 %collective-permute-start.59 = (bf16[72,2048]{1,0:T(8,128)(2,1)S(1)}, bf16[72,2048]{1,0:T(8,128)(2,1)S(1)}, u32[]{:S(2)}, u32[]{:S(2)}) collective-permute-start(bf16[72,2048]{1,0:T(8,128)(2,1)S(1)} %get-tuple-element.363), channel_id=1, source_target_pairs={{0,3},{1,2},{2,1},{3,0},{4,7},{5,6},{6,5},{7,4},{8,11},{9,10},{10,... | collective-permute-start | bytes 884744 | tf_op jit(solution)/shard_map/ppermute | solution.py:262
  164.5 41.9 %collective-permute-start.28 = (bf16[128,2048]{1,0:T(8,128)(2,1)S(1)}, bf16[128,2048]{1,0:T(8,128)(2,1)S(1)}, u32[]{:S(2)}, u32[]{:S(2)}) collective-permute-start(bf16[128,2048]{1,0:T(8,128)(2,1)S(1)} %collective-permute-done.23), channel_id=1, source_target_pairs={{0,4},{1,5},{2,6},{3,7},{4,8},{5,9},{6,10},{7,11},{8,12},{9,13},{1... | collective-permute-start | bytes 1572872 | tf_op jit(solution)/shard_map/ppermute | solution.py:266
  201.1 47.9 %collective-permute-start.31 = (bf16[128,2048]{1,0:T(8,128)(2,1)S(1)}, bf16[128,2048]{1,0:T(8,128)(2,1)S(1)}, u32[]{:S(2)}, u32[]{:S(2)}) collective-permute-start(bf16[128,2048]{1,0:T(8,128)(2,1)S(1)} %collective-permute-done.22), channel_id=1, source_target_pairs={{0,16},{16,0},{1,17},{17,1},{2,18},{18,2},{3,19},{19,3},{4,20},{20... | collective-permute-start | bytes 1572872 | tf_op jit(solution)/shard_map/ppermute | solution.py:272
  218.6 30.4 %collective-permute-start.32 = (bf16[128,2048]{1,0:T(8,128)(2,1)S(1)}, bf16[128,2048]{1,0:T(8,128)(2,1)S(1)}, u32[]{:S(2)}, u32[]{:S(2)}) collective-permute-start(bf16[128,2048]{1,0:T(8,128)(2,1)S(1)} %collective-permute-done.27), channel_id=1, source_target_pairs={{0,16},{16,0},{1,17},{17,1},{2,18},{18,2},{3,19},{19,3},{4,20},{20... | collective-permute-start | bytes 1572872 | tf_op jit(solution)/shard_map/ppermute | solution.py:272
  262.9 22.9 %collective-permute-start.37 = (bf16[128,2048]{1,0:T(8,128)(2,1)S(1)}, bf16[128,2048]{1,0:T(8,128)(2,1)S(1)}, u32[]{:S(2)}, u32[]{:S(2)}) collective-permute-start(bf16[128,2048]{1,0:T(8,128)(2,1)S(1)} %pad_maximum_fusion.14), channel_id=1, source_target_pairs={{0,1},{1,0},{2,3},{3,2},{4,5},{5,4},{6,7},{7,6},{8,9},{9,8},{10,11... | collective-permute-start | bytes 1572872 | tf_op jit(solution)/shard_map/ppermute | solution.py:262
  263.4 22.4 %collective-permute-start.38 = (bf16[128,2048]{1,0:T(8,128)(2,1)S(1)}, bf16[128,2048]{1,0:T(8,128)(2,1)S(1)}, u32[]{:S(2)}, u32[]{:S(2)}) collective-permute-start(bf16[128,2048]{1,0:T(8,128)(2,1)S(1)} %pad_maximum_fusion.15), channel_id=1, source_target_pairs={{0,2},{1,3},{2,0},{3,1},{4,6},{5,7},{6,4},{7,5},{8,10},{9,11},{10,... | collective-permute-start | bytes 1572872 | tf_op jit(solution)/shard_map/ppermute | solution.py:262
  307.4 26.3 %collective-permute-start.47 = (bf16[72,2048]{1,0:T(8,128)(2,1)}, bf16[72,2048]{1,0:T(8,128)(2,1)}, u32[]{:S(2)}, u32[]{:S(2)}) collective-permute-start(bf16[72,2048]{1,0:T(8,128)(2,1)} %get-tuple-element.348), channel_id=1, source_target_pairs={{0,1},{1,0},{2,3},{3,2},{4,5},{5,4},{6,7},{7,6},{8,9},{9,8},{10,11... | collective-permute-start | bytes 884744 | tf_op jit(solution)/shard_map/ppermute | solution.py:262
  307.7 25.9 %collective-permute-start.48 = (bf16[72,2048]{1,0:T(8,128)(2,1)}, bf16[72,2048]{1,0:T(8,128)(2,1)}, u32[]{:S(2)}, u32[]{:S(2)}) collective-permute-start(bf16[72,2048]{1,0:T(8,128)(2,1)} %get-tuple-element.349), channel_id=1, source_target_pairs={{0,2},{1,3},{2,0},{3,1},{4,6},{5,7},{6,4},{7,5},{8,10},{9,11},{10,... | collective-permute-start | bytes 884744 | tf_op jit(solution)/shard_map/ppermute | solution.py:262
  309.3 24.3 %collective-permute-start.49 = (bf16[72,2048]{1,0:T(8,128)(2,1)}, bf16[72,2048]{1,0:T(8,128)(2,1)}, u32[]{:S(2)}, u32[]{:S(2)}) collective-permute-start(bf16[72,2048]{1,0:T(8,128)(2,1)} %get-tuple-element.350), channel_id=1, source_target_pairs={{0,3},{1,2},{2,1},{3,0},{4,7},{5,6},{6,5},{7,4},{8,11},{9,10},{10,... | collective-permute-start | bytes 884744 | tf_op jit(solution)/shard_map/ppermute | solution.py:262
  310.9 24.0 %collective-permute-start.46 = (bf16[128,2048]{1,0:T(8,128)(2,1)}, bf16[128,2048]{1,0:T(8,128)(2,1)}, u32[]{:S(2)}, u32[]{:S(2)}) collective-permute-start(bf16[128,2048]{1,0:T(8,128)(2,1)} %collective-permute-done.39), channel_id=1, source_target_pairs={{0,4},{1,5},{2,6},{3,7},{4,8},{5,9},{6,10},{7,11},{8,12},{9,13},{1... | collective-permute-start | bytes 1572872 | tf_op jit(solution)/shard_map/ppermute | solution.py:266
  360.8 19.6 %collective-permute-start.61 = (bf16[72,2048]{1,0:T(8,128)(2,1)S(1)}, bf16[72,2048]{1,0:T(8,128)(2,1)}, u32[]{:S(2)}, u32[]{:S(2)}) collective-permute-start(bf16[72,2048]{1,0:T(8,128)(2,1)S(1)} %copy-done.130), channel_id=1, source_target_pairs={{0,2},{1,3},{2,0},{3,1},{4,6},{5,7},{6,4},{7,5},{8,10},{9,11},{10,... | collective-permute-start | bytes 884744 | tf_op jit(solution)/shard_map/ppermute | solution.py:262
  363.9 19.3 %collective-permute-start.63 = (bf16[72,2048]{1,0:T(8,128)(2,1)}, bf16[72,2048]{1,0:T(8,128)(2,1)}, u32[]{:S(2)}, u32[]{:S(2)}) collective-permute-start(bf16[72,2048]{1,0:T(8,128)(2,1)} %get-tuple-element.370), channel_id=1, source_target_pairs={{0,1},{1,0},{2,3},{3,2},{4,5},{5,4},{6,7},{7,6},{8,9},{9,8},{10,11... | collective-permute-start | bytes 884744 | tf_op jit(solution)/shard_map/ppermute | solution.py:262
  380.4 96.3 %collective-permute-start.84 = (bf16[72,2048]{1,0:T(8,128)(2,1)}, bf16[72,2048]{1,0:T(8,128)(2,1)}, u32[]{:S(2)}, u32[]{:S(2)}) collective-permute-start(bf16[72,2048]{1,0:T(8,128)(2,1)} %get-tuple-element.397), channel_id=1, source_target_pairs={{0,1},{1,0},{2,3},{3,2},{4,5},{5,4},{6,7},{7,6},{8,9},{9,8},{10,11... | collective-permute-start | bytes 884744 | tf_op jit(solution)/shard_map/ppermute | solution.py:262
  391.1 28.5 %collective-permute-start.70 = (bf16[72,2048]{1,0:T(8,128)(2,1)}, bf16[72,2048]{1,0:T(8,128)(2,1)}, u32[]{:S(2)}, u32[]{:S(2)}) collective-permute-start(bf16[72,2048]{1,0:T(8,128)(2,1)} %get-tuple-element.380), channel_id=1, source_target_pairs={{0,1},{1,0},{2,3},{3,2},{4,5},{5,4},{6,7},{7,6},{8,9},{9,8},{10,11... | collective-permute-start | bytes 884744 | tf_op jit(solution)/shard_map/ppermute | solution.py:262
  392.3 27.4 %collective-permute-start.71 = (bf16[72,2048]{1,0:T(8,128)(2,1)}, bf16[72,2048]{1,0:T(8,128)(2,1)}, u32[]{:S(2)}, u32[]{:S(2)}) collective-permute-start(bf16[72,2048]{1,0:T(8,128)(2,1)} %get-tuple-element.381), channel_id=1, source_target_pairs={{0,2},{1,3},{2,0},{3,1},{4,6},{5,7},{6,4},{7,5},{8,10},{9,11},{10,... | collective-permute-start | bytes 884744 | tf_op jit(solution)/shard_map/ppermute | solution.py:262
  392.3 27.4 %collective-permute-start.72 = (bf16[72,2048]{1,0:T(8,128)(2,1)}, bf16[72,2048]{1,0:T(8,128)(2,1)}, u32[]{:S(2)}, u32[]{:S(2)}) collective-permute-start(bf16[72,2048]{1,0:T(8,128)(2,1)} %get-tuple-element.382), channel_id=1, source_target_pairs={{0,3},{1,2},{2,1},{3,0},{4,7},{5,6},{6,5},{7,4},{8,11},{9,10},{10,... | collective-permute-start | bytes 884744 | tf_op jit(solution)/shard_map/ppermute | solution.py:262
  394.7 25.0 %collective-permute-start.69 = (bf16[128,2048]{1,0:T(8,128)(2,1)}, bf16[128,2048]{1,0:T(8,128)(2,1)}, u32[]{:S(2)}, u32[]{:S(2)}) collective-permute-start(bf16[128,2048]{1,0:T(8,128)(2,1)} %convolution_convert_fusion.9), channel_id=1, source_target_pairs={{0,4},{1,5},{2,6},{3,7},{4,8},{5,9},{6,10},{7,11},{8,12},{9,13},{1... | collective-permute-start | bytes 1572872 | tf_op jit(solution)/shard_map/ppermute | solution.py:266
  459.7 20.8 %collective-permute-start.83 = (bf16[128,2048]{1,0:T(8,128)(2,1)S(1)}, bf16[128,2048]{1,0:T(8,128)(2,1)S(1)}, u32[]{:S(2)}, u32[]{:S(2)}) collective-permute-start(bf16[128,2048]{1,0:T(8,128)(2,1)S(1)} %add_convert_fusion.3), channel_id=1, source_target_pairs={{0,4},{1,5},{2,6},{3,7},{4,8},{5,9},{6,10},{7,11},{8,12},{9,13},{1... | collective-permute-start | bytes 1572872 | tf_op jit(solution)/shard_map/ppermute | solution.py:266
  475.0 37.0 %collective-permute-start.91 = (bf16[72,2048]{1,0:T(8,128)(2,1)}, bf16[72,2048]{1,0:T(8,128)(2,1)}, u32[]{:S(2)}, u32[]{:S(2)}) collective-permute-start(bf16[72,2048]{1,0:T(8,128)(2,1)} %get-tuple-element.404), channel_id=1, source_target_pairs={{0,1},{1,0},{2,3},{3,2},{4,5},{5,4},{6,7},{7,6},{8,9},{9,8},{10,11... | collective-permute-start | bytes 884744 | tf_op jit(solution)/shard_map/ppermute | solution.py:262
  476.7 36.2 %collective-permute-start.92 = (bf16[72,2048]{1,0:T(8,128)(2,1)}, bf16[72,2048]{1,0:T(8,128)(2,1)}, u32[]{:S(2)}, u32[]{:S(2)}) collective-permute-start(bf16[72,2048]{1,0:T(8,128)(2,1)} %get-tuple-element.405), channel_id=1, source_target_pairs={{0,2},{1,3},{2,0},{3,1},{4,6},{5,7},{6,4},{7,5},{8,10},{9,11},{10,... | collective-permute-start | bytes 884744 | tf_op jit(solution)/shard_map/ppermute | solution.py:262
  477.9 36.8 %collective-permute-start.93 = (bf16[72,2048]{1,0:T(8,128)(2,1)}, bf16[72,2048]{1,0:T(8,128)(2,1)}, u32[]{:S(2)}, u32[]{:S(2)}) collective-permute-start(bf16[72,2048]{1,0:T(8,128)(2,1)} %get-tuple-element.406), channel_id=1, source_target_pairs={{0,3},{1,2},{2,1},{3,0},{4,7},{5,6},{6,5},{7,4},{8,11},{9,10},{10,... | collective-permute-start | bytes 884744 | tf_op jit(solution)/shard_map/ppermute | solution.py:262
  487.2 27.5 %collective-permute-start.90 = (bf16[128,2048]{1,0:T(8,128)(2,1)}, bf16[128,2048]{1,0:T(8,128)(2,1)}, u32[]{:S(2)}, u32[]{:S(2)}) collective-permute-start(bf16[128,2048]{1,0:T(8,128)(2,1)} %convolution_convert_fusion.8), channel_id=1, source_target_pairs={{0,4},{1,5},{2,6},{3,7},{4,8},{5,9},{6,10},{7,11},{8,12},{9,13},{1... | collective-permute-start | bytes 1572872 | tf_op jit(solution)/shard_map/ppermute | solution.py:266
  512.0 19.0 %collective-permute-start.98 = (bf16[72,2048]{1,0:T(8,128)(2,1)}, bf16[72,2048]{1,0:T(8,128)(2,1)S(1)}, u32[]{:S(2)}, u32[]{:S(2)}) collective-permute-start(bf16[72,2048]{1,0:T(8,128)(2,1)} %get-tuple-element.413), channel_id=1, source_target_pairs={{0,2},{1,3},{2,0},{3,1},{4,6},{5,7},{6,4},{7,5},{8,10},{9,11},{10,... | collective-permute-start | bytes 884744 | tf_op jit(solution)/shard_map/ppermute | solution.py:262
  512.8 19.2 %collective-permute-start.99 = (bf16[72,2048]{1,0:T(8,128)(2,1)}, bf16[72,2048]{1,0:T(8,128)(2,1)S(1)}, u32[]{:S(2)}, u32[]{:S(2)}) collective-permute-start(bf16[72,2048]{1,0:T(8,128)(2,1)} %get-tuple-element.414), channel_id=1, source_target_pairs={{0,3},{1,2},{2,1},{3,0},{4,7},{5,6},{6,5},{7,4},{8,11},{9,10},{10,... | collective-permute-start | bytes 884744 | tf_op jit(solution)/shard_map/ppermute | solution.py:262
  525.0 74.0 %collective-permute-start.153 = (bf16[1024,768]{1,0:T(8,128)(2,1)}, bf16[1024,768]{1,0:T(8,128)(2,1)}, u32[]{:S(2)}, u32[]{:S(2)}) collective-permute-start(bf16[1024,768]{1,0:T(8,128)(2,1)} %convolution_convert_fusion.12), channel_id=1, source_target_pairs={{0,16},{16,0},{1,17},{17,1},{2,18},{18,2},{3,19},{19,3},{4,20},{20... | collective-permute-start | bytes 4718600 | tf_op jit(solution)/shard_map/ppermute | solution.py:272
  529.6 62.5 %collective-permute-start.103 = (bf16[72,2048]{1,0:T(8,128)(2,1)}, bf16[72,2048]{1,0:T(8,128)(2,1)}, u32[]{:S(2)}, u32[]{:S(2)}) collective-permute-start(bf16[72,2048]{1,0:T(8,128)(2,1)} %get-tuple-element.420), channel_id=1, source_target_pairs={{0,1},{1,0},{2,3},{3,2},{4,5},{5,4},{6,7},{7,6},{8,9},{9,8},{10,11... | collective-permute-start | bytes 884744 | tf_op jit(solution)/shard_map/ppermute | solution.py:262
  531.1 61.2 %collective-permute-start.104 = (bf16[72,2048]{1,0:T(8,128)(2,1)}, bf16[72,2048]{1,0:T(8,128)(2,1)}, u32[]{:S(2)}, u32[]{:S(2)}) collective-permute-start(bf16[72,2048]{1,0:T(8,128)(2,1)} %get-tuple-element.421), channel_id=1, source_target_pairs={{0,2},{1,3},{2,0},{3,1},{4,6},{5,7},{6,4},{7,5},{8,10},{9,11},{10,... | collective-permute-start | bytes 884744 | tf_op jit(solution)/shard_map/ppermute | solution.py:262
  532.1 83.0 %collective-permute-start.154 = (bf16[1024,768]{1,0:T(8,128)(2,1)}, bf16[1024,768]{1,0:T(8,128)(2,1)}, u32[]{:S(2)}, u32[]{:S(2)}) collective-permute-start(bf16[1024,768]{1,0:T(8,128)(2,1)} %convolution_convert_fusion.11), channel_id=1, source_target_pairs={{0,16},{16,0},{1,17},{17,1},{2,18},{18,2},{3,19},{19,3},{4,20},{20... | collective-permute-start | bytes 4718600 | tf_op jit(solution)/shard_map/ppermute | solution.py:272
  549.0 19.2 %collective-permute-start.106 = (f32[4,4,1088]{2,1,0:T(4,128)}, f32[4,4,1088]{2,1,0:T(4,128)}, u32[]{:S(2)}, u32[]{:S(2)}) collective-permute-start(f32[4,4,1088]{2,1,0:T(4,128)} %fusion.307), channel_id=1, source_target_pairs={{0,16},{16,0},{1,17},{17,1},{2,18},{18,2},{3,19},{19,3},{4,20},{20... | collective-permute-start | bytes 208904 | tf_op jit(solution)/shard_map/ppermute | solution.py:272
  570.7 25.9 %collective-permute-start.108 = (f32[4,1088]{1,0:T(4,128)S(1)}, f32[4,1088]{1,0:T(4,128)S(1)}, u32[]{:S(2)}, u32[]{:S(2)}) collective-permute-start(f32[4,1088]{1,0:T(4,128)S(1)} %get-tuple-element.442), channel_id=1, source_target_pairs={{0,4},{1,5},{2,6},{3,7},{4,8},{5,9},{6,10},{7,11},{8,12},{9,13},{1... | collective-permute-start | bytes 52232 | tf_op jit(solution)/shard_map/ppermute | solution.py:266
  597.5 21.2 %collective-permute-start.155 = (bf16[768,1024]{1,0:T(8,128)(2,1)S(1)}, bf16[768,1024]{1,0:T(8,128)(2,1)S(1)}, u32[]{:S(2)}, u32[]{:S(2)}) collective-permute-start(bf16[768,1024]{1,0:T(8,128)(2,1)S(1)} %copy-done.192), channel_id=1, source_target_pairs={{0,16},{16,0},{1,17},{17,1},{2,18},{18,2},{3,19},{19,3},{4,20},{20... | collective-permute-start | bytes 4718600 | tf_op jit(solution)/shard_map/ppermute | solution.py:272
  598.1 24.6 %collective-permute-start.107 = (bf16[512,2048]{1,0:T(8,128)(2,1)S(1)}, bf16[512,2048]{1,0:T(8,128)(2,1)S(1)}, u32[]{:S(2)}, u32[]{:S(2)}) collective-permute-start(bf16[512,2048]{1,0:T(8,128)(2,1)S(1)} %copy-done.56), channel_id=1, source_target_pairs={{0,16},{16,0},{1,17},{17,1},{2,18},{18,2},{3,19},{19,3},{4,20},{20... | collective-permute-start | bytes 6291464 | tf_op jit(solution)/shard_map/ppermute | solution.py:272
  632.2 127.0 %collective-permute-start.150 = (f32[1088]{0:T(1024)S(1)}, f32[1088]{0:T(1024)S(1)}, u32[]{:S(2)}, u32[]{:S(2)}) collective-permute-start(f32[1088]{0:T(1024)S(1)} %get-tuple-element.516), channel_id=1, source_target_pairs={{0,3},{1,2},{2,1},{3,0},{4,7},{5,6},{6,5},{7,4},{8,11},{9,10},{10,... | collective-permute-start | bytes 13064 | tf_op jit(solution)/shard_map/ppermute | solution.py:262
  634.1 128.1 %collective-permute-start.151 = (f32[1088]{0:T(1024)S(1)}, f32[1088]{0:T(1024)S(1)}, u32[]{:S(2)}, u32[]{:S(2)}) collective-permute-start(f32[1088]{0:T(1024)S(1)} %get-tuple-element.517), channel_id=1, source_target_pairs={{0,1},{1,0},{2,3},{3,2},{4,5},{5,4},{6,7},{7,6},{8,9},{9,8},{10,11... | collective-permute-start | bytes 13064 | tf_op jit(solution)/shard_map/ppermute | solution.py:262
  634.5 19.7 %collective-permute-start.111 = (bf16[128,2048]{1,0:T(8,128)(2,1)}, bf16[128,2048]{1,0:T(8,128)(2,1)}, u32[]{:S(2)}, u32[]{:S(2)}) collective-permute-start(bf16[128,2048]{1,0:T(8,128)(2,1)} %slice.1152), channel_id=1, source_target_pairs={{0,4},{1,5},{2,6},{3,7},{4,8},{5,9},{6,10},{7,11},{8,12},{9,13},{1... | collective-permute-start | bytes 1572872 | tf_op jit(solution)/shard_map/ppermute | solution.py:266
  688.7 24.6 %collective-permute-start.115 = (bf16[512,256]{1,0:T(8,128)(2,1)}, bf16[512,256]{1,0:T(8,128)(2,1)}, u32[]{:S(2)}, u32[]{:S(2)}) collective-permute-start(bf16[512,256]{1,0:T(8,128)(2,1)} %get-tuple-element.467), channel_id=1, source_target_pairs={{0,8},{1,9},{2,10},{3,11},{4,12},{5,13},{6,14},{7,15},{8,0},{9,1},... | collective-permute-start | bytes 786440 | tf_op jit(solution)/shard_map/ppermute | solution.py:266
  689.2 24.2 %collective-permute-start.116 = (bf16[512,256]{1,0:T(8,128)(2,1)}, bf16[512,256]{1,0:T(8,128)(2,1)}, u32[]{:S(2)}, u32[]{:S(2)}) collective-permute-start(bf16[512,256]{1,0:T(8,128)(2,1)} %get-tuple-element.468), channel_id=1, source_target_pairs={{0,4},{1,5},{2,6},{3,7},{4,8},{5,9},{6,10},{7,11},{8,12},{9,13},{1... | collective-permute-start | bytes 786440 | tf_op jit(solution)/shard_map/ppermute | solution.py:266
  695.8 66.9 %collective-permute-start.152 = (f32[1088]{0:T(1024)S(1)}, f32[1088]{0:T(1024)S(1)}, u32[]{:S(2)}, u32[]{:S(2)}) collective-permute-start(f32[1088]{0:T(1024)S(1)} %get-tuple-element.518), channel_id=1, source_target_pairs={{0,2},{1,3},{2,0},{3,1},{4,6},{5,7},{6,4},{7,5},{8,10},{9,11},{10,... | collective-permute-start | bytes 13064 | tf_op jit(solution)/shard_map/ppermute | solution.py:262
  713.4 21.5 %collective-permute-start.117 = (bf16[128,2048]{1,0:T(8,128)(2,1)}, bf16[128,2048]{1,0:T(8,128)(2,1)}, u32[]{:S(2)}, u32[]{:S(2)}) collective-permute-start(bf16[128,2048]{1,0:T(8,128)(2,1)} %fusion.221), channel_id=1, source_target_pairs={{0,4},{1,5},{2,6},{3,7},{4,8},{5,9},{6,10},{7,11},{8,12},{9,13},{1... | collective-permute-start | bytes 1572872 | tf_op jit(solution)/shard_map/ppermute | solution.py:266
  749.8 35.3 %collective-permute-start.149 = (bf16[128,2048]{1,0:T(8,128)(2,1)}, bf16[128,2048]{1,0:T(8,128)(2,1)S(1)}, u32[]{:S(2)}, u32[]{:S(2)}) collective-permute-start(bf16[128,2048]{1,0:T(8,128)(2,1)} %fusion.218), channel_id=1, source_target_pairs={{0,0},{1,8},{2,16},{3,24},{4,1},{5,9},{6,17},{7,25},{8,2},{9,10},{... | collective-permute-start | bytes 1572872 | tf_op jit(solution)/shard_map/ppermute | solution.py:480
  759.2 24.6 %collective-permute-start.126 = (f32[4,72]{1,0:T(4,128)S(1)}, f32[4,72]{1,0:T(4,128)S(1)}, u32[]{:S(2)}, u32[]{:S(2)}) collective-permute-start(f32[4,72]{1,0:T(4,128)S(1)} %get-tuple-element.489), channel_id=1, source_target_pairs={{0,8},{1,9},{2,10},{3,11},{4,12},{5,13},{6,14},{7,15},{8,0},{9,1},... | collective-permute-start | bytes 3464 | tf_op jit(solution)/shard_map/ppermute | solution.py:266
  762.3 22.8 %collective-permute-start.127 = (f32[4,72]{1,0:T(4,128)S(1)}, f32[4,72]{1,0:T(4,128)S(1)}, u32[]{:S(2)}, u32[]{:S(2)}) collective-permute-start(f32[4,72]{1,0:T(4,128)S(1)} %get-tuple-element.490), channel_id=1, source_target_pairs={{0,12},{1,13},{2,14},{3,15},{4,0},{5,1},{6,2},{7,3},{8,4},{9,5},{1... | collective-permute-start | bytes 3464 | tf_op jit(solution)/shard_map/ppermute | solution.py:266
  764.0 22.8 %collective-permute-start.128 = (bf16[256,512]{1,0:T(8,128)(2,1)}, bf16[256,512]{1,0:T(8,128)(2,1)S(1)}, u32[]{:S(2)}, u32[]{:S(2)}) collective-permute-start(bf16[256,512]{1,0:T(8,128)(2,1)} %fusion.235), channel_id=1, source_target_pairs={{0,4},{1,5},{2,6},{3,7},{4,8},{5,9},{6,10},{7,11},{8,12},{9,13},{1... | collective-permute-start | bytes 786440 | tf_op jit(solution)/shard_map/ppermute | solution.py:266
  804.8 25.0 %collective-permute-start.134 = (bf16[64,512]{1,0:T(8,128)(2,1)S(1)}, bf16[64,512]{1,0:T(8,128)(2,1)S(1)}, u32[]{:S(2)}, u32[]{:S(2)}) collective-permute-start(bf16[64,512]{1,0:T(8,128)(2,1)S(1)} %get-tuple-element.501), channel_id=1, source_target_pairs={{0,3},{1,2},{2,1},{3,0},{4,7},{5,6},{6,5},{7,4},{8,11},{9,10},{10,... | collective-permute-start | bytes 196616 | tf_op jit(solution)/shard_map/ppermute | solution.py:262
  806.0 24.3 %collective-permute-start.135 = (bf16[64,512]{1,0:T(8,128)(2,1)S(1)}, bf16[64,512]{1,0:T(8,128)(2,1)S(1)}, u32[]{:S(2)}, u32[]{:S(2)}) collective-permute-start(bf16[64,512]{1,0:T(8,128)(2,1)S(1)} %get-tuple-element.502), channel_id=1, source_target_pairs={{0,2},{1,3},{2,0},{3,1},{4,6},{5,7},{6,4},{7,5},{8,10},{9,11},{10,... | collective-permute-start | bytes 196616 | tf_op jit(solution)/shard_map/ppermute | solution.py:262
  (299 other events, 3670.5 us)
Sparse Core Ops, SparseCore 0:
  9.7 14.8 all-gather.5
  26.1 13.2 all-gather.7
  40.9 13.2 all-gather.3

commit v3 on v2

v3 whole, which is shorter than its diff:
```python
import jax
import jax.numpy as jnp
from jax import lax
from jax.experimental import pallas as pl
from jax.experimental.pallas import tpu as pltpu
from jax.sharding import PartitionSpec as P

MODEL_WIDTH = 2048
QUERY_HEADS = 32
KEY_VALUE_HEADS = 4
HEAD_SIZE = 128
TOP = 8
PER_KV = QUERY_HEADS // KEY_VALUE_HEADS
QW = PER_KV * HEAD_SIZE

EPS = 1e-06
THETA = 1000000.0
MASKED = -1e30
BF = jnp.bfloat16
F32 = jnp.float32


def rms_scale(values, scaling):
    return values * lax.rsqrt(jnp.mean(values * values, axis=-1, keepdims=True) + EPS) * scaling


def rotary_tables(position):
    half = HEAD_SIZE // 2
    index_float = jnp.arange(half, dtype=jnp.float32)
    freq = jnp.power(jnp.float32(THETA), -2.0 * index_float / HEAD_SIZE)
    angle = position.astype(jnp.float32)[:, None] * freq[None, :]
    cosine, sine = jnp.cos(angle), jnp.sin(angle)
    return (
        jnp.concatenate([cosine, cosine], axis=-1),
        jnp.concatenate([-sine, sine], axis=-1),
    )


def project_kernel(starts_ref, x_ref, cos_ref, sin_ref, gains_ref, *refs):
    pieces, (w_ref, proj_ref, turned_ref) = refs[:-3], refs[-3:]
    last = pl.program_id(0) == pl.num_programs(0) - 1
    rows = pieces[0].shape[0] // 4
    for number, piece in enumerate(pieces):
        for k in range(4):
            at = pl.multiple_of(starts_ref[number * 4 + k], rows)
            w_ref[pl.ds(at, rows), :] = piece[k * rows : (k + 1) * rows, :]
    projected = jnp.dot(x_ref[...], w_ref[...], preferred_element_type=F32)
    proj_ref[...] = projected

    def turn(values, gain):
        scaled = (
            values * lax.rsqrt(jnp.mean(values * values, axis=-1, keepdims=True) + EPS) * gain
        )
        swapped = pltpu.roll(scaled, HEAD_SIZE // 2, 1)
        return scaled * cos_ref[...] + swapped * sin_ref[...]

    gain_q, gain_k = gains_ref[0:1], gains_ref[1:2]
    first, second = projected[:, :HEAD_SIZE], projected[:, HEAD_SIZE:]
    turned_ref[:, :HEAD_SIZE] = turn(first, jnp.where(last, gain_k, gain_q)).astype(BF)
    turned_ref[:, HEAD_SIZE:] = jnp.where(last, second, turn(second, gain_q)).astype(BF)


def project(starts, rows_in, cosine, sine, gains, *pieces):
    count, width = rows_in.shape
    height, columns = pieces[0].shape
    step = 2 * HEAD_SIZE
    whole = lambda array: pl.BlockSpec(array.shape, lambda i: (0, 0))
    strip = lambda height: pl.BlockSpec((height, step), lambda i: (0, i))
    return pl.pallas_call(
        project_kernel,
        grid=(columns // step,),
        in_specs=[pl.BlockSpec(memory_space=pltpu.SMEM)]
        + [whole(rows_in), whole(cosine), whole(sine), whole(gains)]
        + [strip(height)] * len(pieces),
        out_specs=[strip(width), strip(count), strip(count)],
        out_shape=[
            jax.ShapeDtypeStruct((width, columns), BF),
            jax.ShapeDtypeStruct((count, columns), F32),
            jax.ShapeDtypeStruct((count, columns), BF),
        ],
        cost_estimate=pl.CostEstimate(
            flops=2 * count * width * columns,
            bytes_accessed=2 * (count + columns) * width,
            transcendentals=0,
        ),
        compiler_params=pltpu.CompilerParams(vmem_limit_bytes=60 * 2**20),
    )(starts, rows_in, cosine, sine, gains, *pieces)


def unturned(grad, values, cosine, sine, gain):
    grad = grad * cosine + pltpu.roll(grad * sine, HEAD_SIZE // 2, 1)
    scale = lax.rsqrt(jnp.mean(values * values, axis=-1, keepdims=True) + EPS)
    gain_grad = jnp.sum(grad * values * scale, axis=0, keepdims=True)
    grad = grad * gain
    inner = jnp.mean(grad * values, axis=-1, keepdims=True)
    return (scale * grad - values * (scale * scale * scale * inner)).astype(BF), gain_grad


def unturn_kernel(grad_ref, proj_ref, cos_ref, sin_ref, gain_ref, out_ref, gain_grad_ref):
    out_ref[...], gain_grad_ref[...] = unturned(
        grad_ref[...], proj_ref[...], cos_ref[...], sin_ref[...], gain_ref[...]
    )


def unturn(grad, projected, cosine, sine, gain):
    return pl.pallas_call(
        unturn_kernel,
        out_shape=[
            jax.ShapeDtypeStruct(grad.shape, BF),
            jax.ShapeDtypeStruct(gain.shape, F32),
        ],
    )(grad, projected, cosine, sine, gain)


def input_kernel(grad_ref, w_ref, hidden_ref, scale_ref, out_ref, gain_grad_ref):
    dims = (((1,), (1,)), ((), ()))
    out = lax.dot_general(grad_ref[...], w_ref[...], dims, preferred_element_type=F32)
    out_ref[...] = out
    gain_grad_ref[...] = jnp.sum(
        out * hidden_ref[...].astype(F32) * scale_ref[...], axis=0, keepdims=True
    )


def input_gradient(proj_grad, weights, hidden, scale):
    count, columns = proj_grad.shape
    width = weights.shape[0]
    step = 256
    whole = lambda array: pl.BlockSpec(array.shape, lambda i: (0, 0))
    strip = lambda height: pl.BlockSpec((height, step), lambda i: (0, i))
    return pl.pallas_call(
        input_kernel,
        grid=(width // step,),
        in_specs=[
            whole(proj_grad),
            pl.BlockSpec((step, columns), lambda i: (i, 0)),
            strip(count),
            whole(scale),
        ],
        out_specs=[strip(count), strip(1)],
        out_shape=[
            jax.ShapeDtypeStruct((count, width), F32),
            jax.ShapeDtypeStruct((1, width), F32),
        ],
        cost_estimate=pl.CostEstimate(
            flops=2 * count * width * columns,
            bytes_accessed=6 * (count + columns) * width,
            transcendentals=0,
        ),
        compiler_params=pltpu.CompilerParams(vmem_limit_bytes=24 * 2**20),
    )(proj_grad, weights, hidden, scale)


def forward_kernel(q_ref, kv_ref, vt_ref, place_ref, low_ref, high_ref, out_ref, p_ref):
    count, queries = p_ref.shape
    step = min(512, count)
    chunks = [slice(at, at + step) for at in range(0, count, step)]
    q, low, high = q_ref[...], low_ref[...], high_ref[...]
    top = jnp.full((1, queries), MASKED, F32)
    for chunk in chunks:
        place = place_ref[chunk, :]
        seen = (place >= low) & (place <= high)
        scores = lax.dot_general(
            kv_ref[chunk, :HEAD_SIZE], q, (((1,), (1,)), ((), ())), preferred_element_type=F32
        )
        scores = jnp.where(seen, scores * HEAD_SIZE**-0.5, MASKED)
        p_ref[chunk, :] = scores
        top = jnp.maximum(top, jnp.max(scores, axis=0, keepdims=True))
    total = jnp.zeros((1, queries), F32)
    for chunk in chunks:
        exponent = jnp.exp(p_ref[chunk, :] - top)
        p_ref[chunk, :] = exponent
        total = total + jnp.sum(exponent, axis=0, keepdims=True)
    share = 1.0 / total
    out = jnp.zeros((HEAD_SIZE, queries), F32)
    for chunk in chunks:
        probs = (p_ref[chunk, :] * share).astype(BF)
        out = out + jnp.dot(vt_ref[:, chunk], probs, preferred_element_type=F32)
    out_ref[...] = out.T.astype(BF)


def attention_blocks(rows, count):
    step = min(rows, 512 * 2048 // count)
    whole = lambda array: pl.BlockSpec(array.shape, lambda i, j: (0, 0))
    head = pl.BlockSpec((step, HEAD_SIZE), lambda i, j: (j, i))
    along = pl.BlockSpec((1, step), lambda i, j: (0, j))
    down = pl.BlockSpec((step, HEAD_SIZE), lambda i, j: (j, 0))
    limit = (32 if count <= 2048 else 60) * 2**20
    return step, whole, head, along, down, limit


def attention_forward(q, keys_values, values_turned, place, low, high):
    rows, columns = q.shape
    count = keys_values.shape[0]
    step, whole, head, along, _, limit = attention_blocks(rows, count)
    return pl.pallas_call(
        forward_kernel,
        grid=(columns // HEAD_SIZE, rows // step),
        in_specs=[head, whole(keys_values), whole(values_turned), whole(place), along, along],
        out_specs=head,
        out_shape=jax.ShapeDtypeStruct(q.shape, BF),
        scratch_shapes=[pltpu.VMEM((count, step), F32)],
        cost_estimate=pl.CostEstimate(
            flops=8 * rows * columns * count, bytes_accessed=4 * rows * columns, transcendentals=0
        ),
        compiler_params=pltpu.CompilerParams(vmem_limit_bytes=limit),
    )(q, keys_values, values_turned, place, low, high)


def backward_kernel(
    q_ref, grad_ref, proj_ref, kv_ref, kt_ref, place_ref, low_ref, high_ref, cos_ref, sin_ref,
    gain_ref, out_ref, dkv_ref, gain_grad_ref, p_ref, dp_ref,
):
    @pl.when((pl.program_id(0) == 0) & (pl.program_id(1) == 0))
    def _():
        dkv_ref[...] = jnp.zeros_like(dkv_ref)
        gain_grad_ref[...] = jnp.zeros_like(gain_grad_ref)

    count, queries = p_ref.shape
    step = min(512, count)
    chunks = [slice(at, at + step) for at in range(0, count, step)]
    scale = HEAD_SIZE**-0.5
    q, grad = q_ref[...], grad_ref[...]
    low, high = low_ref[...], high_ref[...]

    def across(left, right):
        dims = (((1,), (1,)), ((), ()))
        return lax.dot_general(left, right, dims, preferred_element_type=F32)

    top = jnp.full((1, queries), MASKED, F32)
    for chunk in chunks:
        place = place_ref[chunk, :]
        seen = (place >= low) & (place <= high)
        scores = jnp.where(seen, across(kv_ref[chunk, :HEAD_SIZE], q) * scale, MASKED)
        p_ref[chunk, :] = scores
        top = jnp.maximum(top, jnp.max(scores, axis=0, keepdims=True))
    total = inner = jnp.zeros((1, queries), F32)
    for chunk in chunks:
        exponent = jnp.exp(p_ref[chunk, :] - top)
        p_ref[chunk, :] = exponent
        total = total + jnp.sum(exponent, axis=0, keepdims=True)
        prob_grad = across(kv_ref[chunk, HEAD_SIZE:], grad)
        dp_ref[chunk, :] = prob_grad
        inner = inner + jnp.sum(exponent * prob_grad, axis=0, keepdims=True)
    share = 1.0 / total
    inner = inner * share
    dq = jnp.zeros((HEAD_SIZE, queries), F32)
    for chunk in chunks:
        probs = p_ref[chunk, :] * share
        score_grad = (probs * (dp_ref[chunk, :] - inner)).astype(BF)
        dkv_ref[chunk, HEAD_SIZE:] += jnp.dot(probs.astype(BF), grad, preferred_element_type=F32)
        dkv_ref[chunk, :HEAD_SIZE] += (
            jnp.dot(score_grad, q, preferred_element_type=F32) * scale
        )
        dq = dq + jnp.dot(kt_ref[:, chunk], score_grad, preferred_element_type=F32)
    out_ref[...], gain_grad = unturned(
        dq.T * scale, proj_ref[...], cos_ref[...], sin_ref[...], gain_ref[...]
    )
    gain_grad_ref[...] += gain_grad


def attention_backward(
    q, grad, projected, keys_values, keys_turned, place, low, high, cosine, sine, gain
):
    rows, columns = q.shape
    count = keys_values.shape[0]
    step, whole, head, along, down, limit = attention_blocks(rows, count)
    return pl.pallas_call(
        backward_kernel,
        grid=(columns // HEAD_SIZE, rows // step),
        in_specs=[head, head, head, whole(keys_values), whole(keys_turned), whole(place)]
        + [along, along, down, down, whole(gain)],
        out_specs=[head, whole(keys_values), whole(gain)],
        out_shape=[
            jax.ShapeDtypeStruct(q.shape, BF),
            jax.ShapeDtypeStruct(keys_values.shape, F32),
            jax.ShapeDtypeStruct(gain.shape, F32),
        ],
        scratch_shapes=[pltpu.VMEM((count, step), F32)] * 2,
        cost_estimate=pl.CostEstimate(
            flops=10 * rows * columns * count, bytes_accessed=8 * rows * columns, transcendentals=0
        ),
        compiler_params=pltpu.CompilerParams(vmem_limit_bytes=limit),
    )(q, grad, projected, keys_values, keys_turned, place, low, high, cosine, sine, gain)


def choose_kernel(blocks, table_ref, piece_ref, *refs):
    chosen = jnp.dot(table_ref[...], piece_ref[...], preferred_element_type=F32)
    back_refs, out_refs = refs[:-blocks], refs[-blocks:]
    count = out_refs[0].shape[0]
    width = piece_ref.shape[1]
    for k, out_ref in enumerate(out_refs):
        part = chosen[k * count : (k + 1) * count].astype(BF)
        if back_refs:
            out_ref[:, :width] = part
            out_ref[:, width:] = back_refs[k][...]
        else:
            out_ref[...] = part


def choose_rows(table, piece, blocks, backs=()):
    width = piece.shape[1] + (backs[0].shape[1] if backs else 0)
    shape = (table.shape[0] // blocks, width)
    return pl.pallas_call(
        lambda *refs: choose_kernel(blocks, *refs),
        out_shape=[jax.ShapeDtypeStruct(shape, BF)] * blocks,
        compiler_params=pltpu.CompilerParams(vmem_limit_bytes=16 * 2**20),
    )(table, piece, *backs)


def collect_kernel(blocks, table_ref, *refs):
    width = refs[-1].shape[1]
    rows_in = [ref[:, ref.shape[1] - width :].astype(F32) for ref in refs[:blocks]]
    stack = jnp.concatenate(rows_in, axis=0).astype(BF)
    total = jnp.dot(table_ref[...], stack, preferred_element_type=F32)
    if len(refs) > blocks + 1:
        total = total + refs[blocks][...].astype(F32)
    refs[-1][...] = total.astype(refs[-1].dtype)


def collect_rows(table, blocks, width, more=None, kind=BF):
    extra = [] if more is None else [more]
    return pl.pallas_call(
        lambda *refs: collect_kernel(len(blocks), *refs),
        out_shape=jax.ShapeDtypeStruct((table.shape[0], width), kind),
        compiler_params=pltpu.CompilerParams(vmem_limit_bytes=24 * 2**20),
    )(table, *blocks, *extra)


def expert_kernel(blocks, me_ref, *refs):
    rows_refs, upstream_refs = refs[:blocks], refs[blocks : 2 * blocks]
    refs = refs[2 * blocks :]
    chooser_ref, router_ref, gate_ref, up_ref, down_ref = refs[:5]
    back_refs, mixed_refs = refs[5 : 5 + blocks], refs[5 + blocks : 5 + 2 * blocks]
    refs = refs[5 + 2 * blocks :]
    rows_ref, act_ref, out_grad_ref, gate_low_ref, up_low_ref = refs[:5]
    upstream_ref, share_ref, returned_ref, pair_ref = refs[5:]
    step = pl.program_id(0)
    across = (((1,), (1,)), ((), ()))

    @pl.when(step == 0)
    def _():
        whole = lambda parts: jnp.concatenate([ref[...].astype(F32) for ref in parts], axis=0)
        rows_in = whole(rows_refs).astype(BF)
        upstream = whole(upstream_refs)
        logits = jnp.dot(rows_in, router_ref[...], preferred_element_type=F32)
        chosen = chooser_ref[...] > 0.0
        top = jnp.max(jnp.where(chosen, logits, MASKED), axis=1, keepdims=True)
        exponent = jnp.where(chosen, jnp.exp(jnp.where(chosen, logits - top, 0.0)), 0.0)
        total = jnp.sum(exponent, axis=1, keepdims=True)
        number = lax.broadcasted_iota(jnp.int32, exponent.shape, 1)
        mine = jnp.sum(jnp.where(number == me_ref[0], exponent, 0.0), axis=1, keepdims=True)
        share = mine / jnp.where(total > 0.0, total, 1.0)
        rows_ref[...] = rows_in
        upstream_ref[...] = upstream
        out_grad_ref[...] = (share * upstream).astype(BF)
        share_ref[...] = jnp.broadcast_to(share, share_ref.shape)
        returned_ref[...] = jnp.zeros_like(returned_ref)
        pair_ref[...] = jnp.zeros_like(pair_ref)

    rows_in, out_grad = rows_ref[...], out_grad_ref[...]
    gate, up, down = gate_ref[...], up_ref[...], down_ref[...]
    gate_pre = jnp.dot(rows_in, gate, preferred_element_type=F32)
    up_pre = jnp.dot(rows_in, up, preferred_element_type=F32)
    act_grad = lax.dot_general(out_grad, down, across, preferred_element_type=F32)
    logistic = jax.nn.sigmoid(gate_pre)
    silu = gate_pre * logistic
    act = (silu * up_pre).astype(BF)
    gate_low = (act_grad * up_pre * logistic * (1.0 + gate_pre * (1.0 - logistic))).astype(BF)
    up_low = (act_grad * silu).astype(BF)
    act_ref[...], gate_low_ref[...], up_low_ref[...] = act, gate_low, up_low
    returned_ref[...] += jnp.dot(act, down, preferred_element_type=F32)
    pair_ref[...] += lax.dot_general(
        gate_low, gate, across, preferred_element_type=F32
    ) + lax.dot_general(up_low, up, across, preferred_element_type=F32)

    @pl.when(step == pl.num_programs(0) - 1)
    def _():
        returned = returned_ref[...].astype(BF).astype(F32)
        gate_grad = jnp.sum(upstream_ref[...] * returned, axis=1, keepdims=True)
        mixed = share_ref[:, :1] * returned
        pair = pair_ref[...]
        count = rows_refs[0].shape[0]
        width = pair.shape[1]
        number = lax.broadcasted_iota(jnp.int32, share_ref.shape, 1)
        gates = jnp.where(number == me_ref[0], gate_grad, 0.0)
        for k in range(blocks):
            part = slice(k * count, (k + 1) * count)
            back_refs[k][:, :width] = pair[part].astype(BF)
            back_refs[k][:, width:] = gates[part].astype(BF)
            mixed_refs[k][...] = mixed[part].astype(BF)


def expert_rows(me, rows_in, upstream, chooser, router, gate, up, down):
    blocks = len(rows_in)
    block = upstream[0].shape
    slots, width = blocks * block[0], block[1]
    ff = gate.shape[1]
    step = 256
    lanes = 128
    whole = lambda shape: pl.BlockSpec(shape, lambda i: (0, 0))
    columns = lambda height: pl.BlockSpec((height, step), lambda i: (0, i))
    shape = jax.ShapeDtypeStruct
    out = [((block[0], width + lanes), BF)] * blocks + [(block, BF)] * blocks
    out_specs = [whole(dims) for dims, _ in out]
    out_specs += [whole((slots, width)), columns(slots), whole((slots, width))]
    out_specs += [columns(slots)] * 2
    out += [((slots, width), BF), ((slots, ff), BF), ((slots, width), BF)]
    out += [((slots, ff), BF)] * 2
    return pl.pallas_call(
        lambda *refs: expert_kernel(blocks, *refs),
        grid=(ff // step,),
        in_specs=[pl.BlockSpec(memory_space=pltpu.SMEM)]
        + [whole(block)] * (2 * blocks)
        + [whole(chooser.shape), whole(router.shape)]
        + [columns(width), columns(width), pl.BlockSpec((step, width), lambda i: (i, 0))],
        out_specs=out_specs,
        out_shape=[shape(dims, kind) for dims, kind in out],
        scratch_shapes=[
            pltpu.VMEM((slots, width), F32),
            pltpu.VMEM((slots, lanes), F32),
            pltpu.VMEM((slots, width), F32),
            pltpu.VMEM((slots, width), F32),
        ],
        cost_estimate=pl.CostEstimate(
            flops=12 * slots * width * ff, bytes_accessed=6 * width * ff, transcendentals=0
        ),
        compiler_params=pltpu.CompilerParams(vmem_limit_bytes=44 * 2**20),
    )(me, *rows_in, *upstream, chooser, router, gate, up, down)


def table_kernel(capacity, ids_ref, pairs_ref, send_ref, back_ref, chosen_ref):
    mine_a, mine_b = ids_ref[0], ids_ref[1]
    slots, tokens = send_ref.shape[1:]
    experts = chosen_ref.shape[2]
    numbers = lax.broadcasted_iota(jnp.int32, (slots, tokens), 0).astype(F32)
    nowhere = 1e6

    def table(source, expert, k):
        hit = pairs_ref[0, source, 0] == expert.astype(F32)
        order = pairs_ref[0, source, 1] * 32.0 + pairs_ref[0, source, 2]
        place = jnp.min(jnp.where(hit, order, nowhere), axis=0, keepdims=True)
        across = jnp.broadcast_to(place, (tokens, tokens))
        before = jnp.where(across.T < across, 1.0, 0.0)
        rank = jnp.sum(before, axis=0, keepdims=True)
        inside = (place < nowhere) & (rank < capacity)
        rank = jnp.where(inside, rank + k * capacity, -1.0)
        return jnp.where(numbers == rank, 1.0, 0.0)

    send = chosen = 0.0
    for k in range(4):
        send = send + table(0, mine_a * 4 + (mine_b ^ k), k)
        kept = table(k, mine_a * 4 + mine_b, k)
        routes = pairs_ref[0, k, 0]
        expert_rows = lax.broadcasted_iota(jnp.int32, (experts, tokens), 0).astype(F32)
        chooser = sum(
            jnp.where(routes[j : j + 1] == expert_rows, 1.0, 0.0) for j in range(TOP)
        )
        chosen = chosen + lax.dot_general(
            kept.astype(BF),
            chooser.astype(BF),
            (((1,), (1,)), ((), ())),
            preferred_element_type=F32,
        )
    send_ref[0] = send.astype(BF)
    back_ref[0] = send.T.astype(BF)
    chosen_ref[0] = chosen


def slot_tables(ids, pairs, capacity, experts):
    planes, _, _, _, tokens = pairs.shape
    slots = 4 * capacity
    block = lambda *shape: pl.BlockSpec((1,) + shape, lambda i: (i,) + (0,) * len(shape))
    return pl.pallas_call(
        lambda *refs: table_kernel(capacity, *refs),
        grid=(planes,),
        in_specs=[pl.BlockSpec(memory_space=pltpu.SMEM), block(4, 3, TOP, tokens)],
        out_specs=[block(slots, tokens), block(tokens, slots), block(slots, experts)],
        out_shape=[
            jax.ShapeDtypeStruct((planes, slots, tokens), BF),
            jax.ShapeDtypeStruct((planes, tokens, slots), BF),
            jax.ShapeDtypeStruct((planes, slots, experts), F32),
        ],
    )(ids, pairs)


def places(slot_rows, lengths_row):
    seq_ends = jnp.cumsum(lengths_row)
    starts = seq_ends - lengths_row
    segment = jnp.sum((slot_rows[:, None] >= seq_ends[None, :]).astype(jnp.int32), axis=1)
    chosen = segment[:, None] == jnp.arange(lengths_row.shape[0], dtype=jnp.int32)[None, :]
    start_of = jnp.sum(jnp.where(chosen, starts[None, :], 0), axis=1)
    return (segment, slot_rows - start_of)


def pick(blocks, index):
    return lax.dynamic_index_in_dim(blocks, index, 0, keepdims=False)


class Rounds:
    def __init__(self):
        self.active = {}
        self.asked = {}
        self.values = {}
        self.count = 0

    def start(self, task):
        self.count += 1
        self.active[self.count] = (task, None)
        return self.count

    def until(self, *wanted):
        while True:
            while waiting := [number for number in self.active if number not in self.asked]:
                for number in waiting:
                    task, came = self.active[number]
                    try:
                        self.asked[number] = task.send(came)
                    except StopIteration as end:
                        self.values[number] = end.value
                        del self.active[number]
            if all(number in self.values for number in wanted):
                break
            asked = self.asked
            given = {number: [args for _, args in calls] for number, calls in asked.items()}
            given = lax.optimization_barrier(given)
            came = {
                number: [call(*args) for (call, _), args in zip(calls, given[number])]
                for number, calls in asked.items()
            }
            came = lax.optimization_barrier(came)
            for number, results in came.items():
                self.active[number] = (self.active[number][0], results)
            self.asked = {}
        values = [self.values[number] for number in wanted]
        return values[0] if len(values) == 1 else values

    def run(self, task):
        return self.until(self.start(task))


def hold(count, *values):
    for _ in range(count):
        (values,) = yield [(lambda *v: v, values)]
    return values


def later(count, task):
    yield from hold(count)
    return (yield from task)


def work(function, *args):
    (result,) = yield [(function, args)]
    return result


class Links:
    def __init__(self, n):
        self.n = n
        self.planes = n // 4
        index = lax.axis_index("expert")
        self.g = lax.axis_index("dp")
        self.index = index
        self.p = index % 4
        self.l = index // 4
        self.square = n == 16
        if self.square:
            self.a = index % 2 + index // 8 * 2
            self.b = index // 2 % 4
        else:
            self.a, self.b = self.l, self.p
        masks = (0, 2, 4, 6) if self.square else (0, 1, 2, 3)
        self.places = [lambda v, k=k: self.flip(v, k) for k in range(4)]
        self.heads = [lambda v, m=m: self.flip(v, m) for m in masks]
        self.shifts = [lambda v, s=s: self.shift(v, s) for s in range(self.planes)]
        self.backs = [lambda v, s=s: self.shift(v, -s) for s in range(self.planes)]

    def device(self, a, b):
        return a % 2 + b * 2 + a // 2 * 8 if self.square else a * 4 + b

    def block(self, r):
        return self.a ^ r if self.square else (self.a - r) % self.planes

    def flip(self, value, mask):
        return lax.ppermute(value, "expert", [(i, i ^ mask) for i in range(self.n)])

    def shift(self, value, step):
        return lax.ppermute(
            value, "expert", [(i, (i + step * 4) % self.n) for i in range(self.n)]
        )

    def onward(self, value):
        return self.shift(value, 1)

    def twin(self, value):
        return lax.ppermute(value, "dp", [(0, 1), (1, 0)])

    def natural(self, blocks, mine):
        odd, high = mine % 2 == 1, mine >= 2
        pair = [jnp.where(odd, blocks[q ^ 1], blocks[q]) for q in range(4)]
        return [jnp.where(high, pair[q ^ 2], pair[q]) for q in range(4)]

    def turned_line(self, blocks):
        twice = jnp.concatenate([blocks[::-1], blocks[::-1]], axis=0)
        return lax.dynamic_slice_in_dim(twice, self.planes - 1 - self.l, self.planes, 0)

    def head_gather(self, own):
        half = own.shape[0] // 2
        near_x, near_y = yield [(self.heads[1], (own,)), (self.heads[2], (own,))]
        low, high = yield [(self.heads[2], (near_x[:half],)), (self.heads[1], (near_y[half:],))]
        return jnp.concatenate([own, near_x, near_y, low, high], axis=0)

    def exchange(self, flips, blocks):
        came = yield [(flips[k], (blocks[k],)) for k in (3, 1, 2)]
        return [blocks[0], came[1], came[2], came[0]]

    def head_scatter(self, total):
        count = total.shape[0] // 4
        half = count // 2
        cut = lambda k, low, high: total[k * count + low : k * count + high]
        low, high = yield [
            (self.heads[2], (cut(3, 0, half).astype(BF),)),
            (self.heads[1], (cut(3, half, count).astype(BF),)),
        ]
        to_x = jnp.concatenate([cut(1, 0, half) + low.astype(F32), cut(1, half, count)], axis=0)
        to_y = jnp.concatenate([cut(2, 0, half), cut(2, half, count) + high.astype(F32)], axis=0)
        got_x, got_y = yield [
            (self.heads[1], (to_x.astype(BF),)),
            (self.heads[2], (to_y.astype(BF),)),
        ]
        return cut(0, 0, count) + got_x.astype(F32) + got_y.astype(F32)

    def block_gather(self, own, idle=(0, 0)):
        if not self.square:
            came = yield [(shift, (own,)) for shift in self.shifts[1:]]
            return [own] + came
        x, z = (lambda v: self.flip(v, 1)), (lambda v: self.flip(v, 8))
        half = own.shape[0] // 2
        near, low = yield [(x, (own,)), (z, (own[:half],))]
        near, low = yield from hold(idle[0], near, low)
        high, far_low = yield [(z, (own[half:],)), (x, (low,))]
        high, far_low = yield from hold(idle[1], high, far_low)
        (far_high,) = yield [(x, (high,))]
        return [
            own,
            near,
            jnp.concatenate([low, high], axis=0),
            jnp.concatenate([far_low, far_high], axis=0),
        ]

    def block_gather_short(self, own):
        if not self.square:
            came = yield [(shift, (own,)) for shift in self.shifts[1:]]
            return [own] + came
        x, z = (lambda v: self.flip(v, 1)), (lambda v: self.flip(v, 8))
        near, across = yield [(x, (own,)), (z, (own,))]
        (far,) = yield [(x, (across,))]
        return [own, near, across, far]

    def block_scatter(self, blocks, split=False, idle=0):
        if not self.square:
            came = yield [
                (back, (block.astype(BF),)) for back, block in zip(self.backs[1:], blocks[1:])
            ]
            return sum((block.astype(F32) for block in came), blocks[0].astype(F32))
        x, z = (lambda v: self.flip(v, 1)), (lambda v: self.flip(v, 8))
        (came,) = yield [(x, (blocks[3].astype(BF),))]
        (came,) = yield from hold(idle, came)
        across = (blocks[2].astype(F32) + came.astype(F32)).astype(BF)
        half = across.shape[0] // 2 if split else across.shape[0]
        near, got = yield [(x, (blocks[1].astype(BF),)), (z, (across[:half],))]
        if split:
            (more,) = yield [(z, (across[half:],))]
            got = jnp.concatenate([got, more], axis=0)
        return blocks[0].astype(F32) + near.astype(F32) + got.astype(F32)

    def twin_scatter(self, make, own, other, idle=None):
        low = lambda *args: make(*args).astype(BF)
        (block,) = yield [(low, other)]
        (came,) = yield [(self.twin, (block,))]
        if idle is None:
            return make(*own) + came.astype(F32)
        (came,) = yield from hold(idle, came)
        (total,) = yield [(lambda came, *args: make(*args) + came.astype(F32), (came, *own))]
        return total


def body(
    hidden,
    lengths,
    slots,
    routes,
    order,
    gain_in,
    w_query,
    key_projection_weight,
    value_projection_weight,
    gain_q,
    gain_k,
    w_out,
    gain_mid,
    w_router,
    w_gate,
    w_up,
    w_down,
    cotangent,
):
    tokens = hidden.shape[0]
    experts = w_router.shape[1]
    links = Links(experts)
    planes = links.planes
    capacity = max(2, (tokens * TOP * 9 + 8 * experts - 1) // (8 * experts))
    block_tokens = 4 * tokens
    rows = gain_in.shape[0]
    head_part = gain_q.shape[0]
    devices = 2 * experts

    rounds = Rounds()
    spread = rounds.start
    slot_count = 4 * capacity

    gate_full = lax.all_gather(w_gate, "dp", axis=1, tiled=True)[0]
    up_full = lax.all_gather(w_up, "dp", axis=1, tiled=True)[0]
    down_full = lax.all_gather(w_down, "dp", axis=2, tiled=True)[0]

    lanes = 128
    gains = jnp.concatenate([gain_in, gain_mid, gain_q, gain_k], axis=0)
    gain_count = gains.shape[0]
    gains = jnp.pad(gains, (0, -gain_count % lanes)).reshape(-1, lanes)
    router_rows = rows * experts // lanes
    small = jnp.concatenate([w_router.reshape(-1, lanes), gains], axis=0)
    small = jnp.pad(small, ((0, -small.shape[0] % 8), (0, 0)))
    small_rows = small.shape[0]
    pairs = jnp.concatenate([part.T.astype(BF) for part in (routes, order // 32, order % 32)])
    expert_numbers = jnp.arange(experts, dtype=jnp.int32)
    ids = jnp.stack([links.l, links.p]).astype(jnp.int32)
    tables = {}

    def gather_small():
        piece = jnp.concatenate([small, pairs], axis=0)
        blocks = yield from links.exchange(links.places, [piece] * 4)
        line = jnp.stack(blocks)
        if links.square:
            low, high = (lambda v: links.flip(v, 4)), (lambda v: links.flip(v, 8))
            (near,) = yield [(low, (line,))]
            line = jnp.stack([line, near])
            (across,) = yield [(high, (line,))]
            line = jnp.stack([line[0], line[1], across[0], across[1]])
        else:
            came = yield [(shift, (line,)) for shift in links.shifts[1:]]
            line = jnp.stack([line] + came)
            yield from hold(1)
        own_small = line[:, :, :small_rows]
        (other_small,) = yield [(links.twin, (own_small,))]
        return (yield from work(sort_small, line, other_small, rounds.values[hidden_task]))

    def sort_small(line, other_small, block_hidden):
        if links.square:
            line = jnp.stack(links.natural([line[r] for r in range(4)], links.l))
            other_small = jnp.stack(links.natural([other_small[r] for r in range(4)], links.l))
        else:
            line, other_small = links.turned_line(line), links.turned_line(other_small)
        all_pairs = links.turned_line(line[:, :, small_rows:]).astype(F32)
        all_pairs = all_pairs.reshape(planes, 4, 3, TOP, tokens)
        found = slot_tables(ids, all_pairs, capacity, experts)
        tables["send"], tables["back"], tables["chooser"] = found
        line = jnp.stack([line[:, :, :small_rows], other_small], axis=2)
        line = jnp.stack(links.natural([line[:, k] for k in range(4)], links.p), axis=1)
        line = line.reshape(experts, 2, small_rows, lanes)
        first, second = line[:, 0], line[:, 1]
        swap = links.g == 1
        small_all = jnp.concatenate(
            [jnp.where(swap, second, first), jnp.where(swap, first, second)], axis=0
        )
        gains = small_all[:, router_rows:].reshape(devices, -1)
        head_gains = gains[:, 2 * rows : gain_count].reshape(devices, 2, head_part)
        values = block_hidden.astype(F32)
        scale = lax.rsqrt(jnp.mean(values * values, axis=-1, keepdims=True) + EPS)
        full_in = gains[:, :rows].reshape(MODEL_WIDTH).astype(F32)
        return (
            (values * scale * full_in).astype(BF),
            scale,
            small_all[:, :router_rows].reshape(MODEL_WIDTH, experts),
            full_in,
            gains[:, rows : 2 * rows].reshape(MODEL_WIDTH).astype(F32),
            head_gains.swapaxes(0, 1).reshape(2, HEAD_SIZE).astype(F32),
        )

    small_task = spread(gather_small())

    qkv_width = QW + 2 * HEAD_SIZE

    def own_columns(b):
        cut = lambda array, width: lax.dynamic_slice_in_dim(array, b * width, width, 1)
        return jnp.concatenate(
            [
                cut(w_query, QW),
                cut(key_projection_weight, HEAD_SIZE),
                cut(value_projection_weight, HEAD_SIZE),
            ],
            axis=1,
        )

    def gather_qkv():
        blocks = [own_columns(links.b ^ k) for k in range(4)]
        blocks = yield from links.exchange(links.heads, blocks)
        pieces = yield from links.block_gather(jnp.concatenate(blocks, axis=0))
        others = yield [(links.twin, (piece,)) for piece in pieces]
        return pieces + others

    qkv_task = spread(gather_qkv())
    hidden_task = spread(later(1, links.head_gather(hidden)))

    aligned = capacity % 8 == 0

    def choose(piece, step, backs=()):
        found = choose_rows(tables["send"][step], piece, 4 if aligned else 1, as_blocks(backs))
        return found if aligned else by_place(found[0])

    def by_place(slot_rows):
        return [slot_rows[k * capacity : (k + 1) * capacity] for k in range(4)]

    def as_blocks(blocks):
        return blocks if aligned or not blocks else [jnp.concatenate(blocks, axis=0)]

    def collect(blocks, step, width, more=None, kind=BF):
        return collect_rows(tables["back"][step], as_blocks(blocks), width, more, kind)

    def in_places(own, came):
        return [own, came[0], came[1], came[2]]

    def to_places(blocks):
        return [(links.places[k], (blocks[k],)) for k in (1, 2, 3)]

    def gather_upstream():
        pieces, out = [cotangent], []
        plan = [(8, True, 0)] + [(0, s < planes - 1, s) for s in range(1, planes)]
        for idle, hop, step in plan:
            yield from hold(idle)
            asks = [(links.onward, (pieces[-1],))] if hop else []
            if step is not None:
                blocks = choose(pieces[step], step)
                asks += to_places(blocks)
            came = yield asks
            if hop:
                pieces.append(came[0])
            if step is not None:
                out.append(in_places(blocks[0], came[-3:]))
        return out

    upstream_task = spread(gather_upstream())

    head_rows = w_out.shape[0]
    to_block = [
        ((b * 2 + g) * planes + a, g * experts + links.device(a, b))
        for g in range(2)
        for a in range(planes)
        for b in range(4)
    ]
    from_block = [(there, here) for here, there in to_block]
    to_blocks = lambda value: lax.ppermute(value, ("dp", "expert"), to_block)
    from_blocks = lambda value: lax.ppermute(value, ("dp", "expert"), from_block)

    def gather_out():
        (own,) = yield [(to_blocks, (w_out,))]
        (own,) = yield from hold(1, own)
        pieces = yield from links.block_gather(own, (1, 0))
        pieces = jnp.concatenate(pieces, axis=0)
        (others,) = yield [(links.twin, (pieces,))]
        return jnp.concatenate([pieces, others], axis=0)

    out_task = spread(later(3, gather_out()))

    device_of = jnp.stack(
        [links.device(links.block(r), links.b ^ k) for r in range(planes) for k in range(4)]
    )
    starts = jnp.concatenate([(links.g ^ t) * experts + device_of for t in range(2)]) * rows
    all_slots = slots.reshape(experts, tokens)[device_of].reshape(experts * tokens)
    _, position = places(all_slots[:block_tokens], lengths[0])
    cosine, sine = rotary_tables(position)
    high = all_slots[:block_tokens]
    low = high - position

    found, block_hidden, qkv_pieces = rounds.until(small_task, hidden_task, qkv_task)
    normalized, block_scale, full_router, full_in, full_mid, head_gains = found
    w_qkv, projected, turned = rounds.run(
        work(project, starts, normalized, cosine, sine, head_gains, *qkv_pieces)
    )
    keys_values = jnp.concatenate(
        rounds.run(links.block_gather_short(turned[:, QW:])), axis=0
    )
    keys_turned = keys_values[:, :HEAD_SIZE].T
    values_turned = keys_values[:, HEAD_SIZE:].T
    place_column = all_slots[:, None]
    low, high = low[None, :], high[None, :]

    def part_of(array, part, parts):
        width = array.shape[1] // parts
        return array[:, part * width : (part + 1) * width]

    def forward_part(query_rows):
        return attention_forward(query_rows, keys_values, values_turned, place_column, low, high)

    attended = [
        rounds.run(work(forward_part, part_of(turned[:, :QW], part, 4)))
        for part in range(4)
    ]
    attended = jnp.concatenate(attended, axis=1)
    attended = jnp.concatenate(
        [
            lax.dynamic_slice_in_dim(
                attended, ((links.g ^ t) * planes + links.block(r)) * head_rows, head_rows, 1
            )
            for t in range(2)
            for r in range(planes)
        ],
        axis=1,
    )
    block_out = rounds.until(out_task)

    branch = jnp.dot(attended, block_out, preferred_element_type=F32)
    branch = rounds.run(links.head_scatter(branch))
    x_float = hidden.astype(F32)
    x_one = x_float + branch
    norm_two, norm_two_back = jax.vjp(rms_scale, x_one, full_mid)
    xn_two = norm_two.astype(BF)

    own_chooser = jnp.any(routes[:, :, None] == expert_numbers, axis=1)

    def masked_softmax(logits, chooser):
        top = jnp.max(jnp.where(chooser, logits, MASKED), axis=-1, keepdims=True)
        exponent = jnp.where(chooser, jnp.exp(jnp.where(chooser, logits - top, 0.0)), 0.0)
        total = jnp.sum(exponent, axis=-1, keepdims=True)
        return exponent / jnp.where(total > 0.0, total, 1.0)

    upstream_slots = rounds.until(upstream_task)
    me = links.index.astype(jnp.int32)[None]
    made = []

    def expert_step(step, *rows_in):
        found = expert_rows(
            me,
            as_blocks(list(rows_in)),
            as_blocks(upstream_slots[step]),
            tables["chooser"][step],
            full_router,
            gate_full,
            up_full,
            down_full,
        )
        if aligned:
            return (found[:4], found[4:8], found[8:])
        return (by_place(found[0]), by_place(found[1]), found[2:])

    def return_mixture():
        blocks = made[1][1]
        back = yield to_places(blocks)
        total = collect(in_places(blocks[0], back), 1, MODEL_WIDTH)
        yield from hold(2)
        (came,) = yield [(links.onward, (total,))]
        blocks = made[2][1]
        back = yield to_places(blocks)
        total = collect(in_places(blocks[0], back), 2, MODEL_WIDTH, came)
        for step in range(3, planes):
            blocks = made[step][1]
            came, *back = yield [(links.onward, (total,))] + to_places(blocks)
            total = collect(in_places(blocks[0], back), step, MODEL_WIDTH, came)
        (came,) = yield [(links.onward, (total,))]
        blocks = made[0][1]
        back = yield to_places(blocks)
        return collect(in_places(blocks[0], back), 0, MODEL_WIDTH, came, F32)

    def experts_there_and_back():
        piece, ready, own_plane, total = xn_two, None, None, None
        wide = MODEL_WIDTH + lanes
        for step in range(planes + 3):
            asks = []
            back = made[step - 2][0] if 2 <= step < planes + 2 else []
            blocks = back
            if step < planes:
                blocks = choose(piece, step, back)
            if blocks:
                asks += to_places(blocks)
            if step < planes - 1:
                asks += [(links.onward, (piece,))]
            if step >= 4:
                asks += [(links.onward, (total,))]
            if 1 <= step <= planes:
                asks += [(lambda *v, s=step - 1: expert_step(s, *v), tuple(ready))]
            if step == planes + 2:
                tables["mixture"] = spread(return_mixture())
            came = yield asks
            if blocks:
                ready, came = in_places(blocks[0], came[:3]), came[3:]
            if step < planes - 1:
                piece, came = came[0], came[1:]
            if step >= 4:
                hop, came = came[0], came[1:]
            if 1 <= step <= planes:
                made.append(came[0])
            if step == 2:
                own_plane = collect(ready, 0, wide, None, F32)
            elif step == 3:
                total = collect(ready, 1, wide)
            elif step >= 4 and step < planes + 2:
                total = collect(ready, step - 2, wide, hop)
        return own_plane + hop.astype(F32)

    moe_grad = rounds.run(experts_there_and_back())
    gate_grads = moe_grad[:, MODEL_WIDTH : MODEL_WIDTH + experts]
    moe_grad = moe_grad[:, :MODEL_WIDTH]
    stacked = lambda place: jnp.concatenate([piece[2][place] for piece in made], axis=0)

    def by_rows(rows_in, grads_in):
        return jnp.einsum("rd,rf->df", rows_in, grads_in, preferred_element_type=F32)

    half_width = MODEL_WIDTH // 2

    def half_of(array, which):
        return lax.dynamic_slice_in_dim(array, which * half_width, half_width, 1)

    def gate_up_gradient(place):
        rows_in, grads_in = stacked(0), stacked(place)
        return links.twin_scatter(
            by_rows,
            (half_of(rows_in, links.g), grads_in),
            (half_of(rows_in, 1 - links.g), grads_in),
            idle=8,
        )

    def down_gradient():
        rows_in, grads_in = stacked(1), stacked(2)
        return links.twin_scatter(
            by_rows,
            (rows_in, half_of(grads_in, links.g)),
            (rows_in, half_of(grads_in, 1 - links.g)),
            idle=3,
        )

    gate_task = spread(gate_up_gradient(3))
    up_task = spread(later(1, gate_up_gradient(4)))
    down_task = spread(later(7, down_gradient()))
    own_logits = jnp.dot(xn_two, full_router, preferred_element_type=F32)
    own_probs = masked_softmax(own_logits, own_chooser)

    upstream = cotangent.astype(F32)
    chosen_grad = own_probs * (
        gate_grads - jnp.sum(own_probs * gate_grads, axis=-1, keepdims=True)
    )
    logit_grad = chosen_grad.astype(BF)
    xn_two_grad = moe_grad + jnp.dot(logit_grad, full_router.T, preferred_element_type=F32)
    x_one_norm_grad, grad_mid = norm_two_back(xn_two_grad)
    x_one_grad = upstream + x_one_norm_grad
    branch_grad = x_one_grad.astype(BF)

    block_grad = rounds.run(links.head_gather(branch_grad))

    def head_gradients(block_grad, block_out):
        grad = jnp.einsum("td,hd->th", block_grad, block_out, preferred_element_type=F32)
        grad = grad.astype(BF)
        parts = []
        for head in range(2 * planes):
            twin, place = links.g ^ (head // planes), links.block(head % planes)
            if links.square:
                place = links.a ^ (head % planes)
            at = (twin * planes + place) * head_rows
            parts.append(lax.dynamic_slice_in_dim(grad, at, head_rows, 1))
        return jnp.concatenate(parts, axis=1)

    heads_task = spread(work(head_gradients, block_grad, block_out))

    def scatter_out():
        half = QW // 2
        grad = yield from links.twin_scatter(
            lambda rows_in, grads_in: jnp.einsum(
                "th,td->hd", rows_in, grads_in, preferred_element_type=F32
            ),
            (attended[:, :half], block_grad),
            (attended[:, half:], block_grad),
        )
        grad = grad.astype(BF)
        blocks = [grad[r * head_rows : (r + 1) * head_rows] for r in range(planes)]
        grad = yield from links.block_scatter(blocks, split=True)
        (grad,) = yield from hold(2, grad.astype(BF))
        grad = yield from work(from_blocks, grad)
        return grad.astype(F32)

    grad_out_task = spread(scatter_out())

    def owners_blocks(grad):
        blocks = []
        for r in range(planes):
            owners = [links.device(links.block(r), links.b ^ k) for k in range(4)]
            parts = [lax.dynamic_slice_in_dim(grad, owner * rows, rows, 0) for owner in owners]
            blocks.append(jnp.concatenate(parts, axis=0))
        return blocks

    def half_rows(array, which):
        return lax.dynamic_slice_in_dim(array, which * (MODEL_WIDTH // 2), MODEL_WIDTH // 2, 0)

    def query_gradient(grads_in, extra, idle):
        def make(which):
            grad = by_rows(half_of(normalized, which), grads_in)
            if extra is not None:
                grad = jnp.concatenate([grad, half_rows(extra, which)], axis=1)
            return grad

        grad = yield from links.twin_scatter(make, (links.g,), (1 - links.g,))
        blocks = yield from hold(idle[0], *owners_blocks(grad.astype(BF)))
        grad = yield from links.block_scatter(blocks, idle=idle[1])
        return grad.astype(BF)

    def exchange_owners(grad):
        grad = grad.reshape(4, rows, grad.shape[1])
        return links.exchange(links.heads, [grad[k] for k in range(4)])

    def key_value_gradient(key_value_grad, proj_grad):
        half = lambda which: by_rows(half_of(normalized, which), key_value_grad)
        found, other, own = yield [
            (input_gradient, (proj_grad, w_qkv, block_hidden, block_scale)),
            (half, (1 - links.g,)),
            (half, (links.g,)),
        ]
        xn_one_grad, grad_in = found
        tables["scatter"] = spread(links.head_scatter(xn_one_grad))
        sums = jnp.concatenate([grad_qgain, grad_kgain]).reshape(2, devices, head_part)
        sums = jnp.pad(sums, ((0, 0), (0, 0), (0, rows - head_part)))
        sums = jnp.concatenate([grad_in, sums.reshape(2, MODEL_WIDTH)], axis=0).T
        sums = jnp.pad(sums, ((0, 0), (0, lanes - sums.shape[1])))
        both = lambda grad, which: jnp.concatenate([grad, half_rows(sums, which)], axis=1)
        (came,) = yield [(links.twin, (both(other, 1 - links.g).astype(BF),))]
        grad = (both(own, links.g) + came.astype(F32)).astype(BF)
        grad = yield from links.block_scatter(owners_blocks(grad))
        return (yield from exchange_owners(grad.astype(BF)))

    attended_grad = rounds.until(heads_task)
    grad_router = jnp.dot(xn_two.T, logit_grad, preferred_element_type=F32)
    first = jnp.concatenate([grad_router, grad_mid[:, None]], axis=1)
    first = jnp.pad(first, ((0, 0), (0, lanes - first.shape[1])))
    query_low_grads, query_tasks, key_terms, grad_qgain = [], [], None, None
    parts = 4
    for part in range(parts):
        got = rounds.run(
            work(
                lambda *args: attention_backward(
                    *args,
                    keys_values,
                    keys_turned,
                    place_column,
                    low,
                    high,
                    cosine,
                    sine,
                    head_gains[0:1],
                ),
                part_of(turned[:, :QW], part, parts),
                part_of(attended_grad, part, parts),
                part_of(projected[:, :QW], part, parts),
            )
        )
        query_low_grads.append(got[0])
        key_terms = got[1] if part == 0 else key_terms + got[1]
        grad_qgain = got[2] if part == 0 else grad_qgain + got[2]
        if part % 2:
            low_grads = jnp.concatenate(query_low_grads[-2:], axis=1)
            more, idle = (None, (1, 0)) if query_tasks else (first, (0, 1))
            query_tasks.append(spread(query_gradient(low_grads, more, idle)))
    key_terms = rounds.run(
        links.block_scatter(
            [key_terms[r * block_tokens : (r + 1) * block_tokens] for r in range(planes)]
        )
    )

    key_proj_grad, grad_kgain = unturn(
        key_terms[:, :HEAD_SIZE],
        projected[:, QW : QW + HEAD_SIZE],
        cosine,
        sine,
        head_gains[1:2],
    )
    key_value_grad = jnp.concatenate([key_proj_grad, key_terms[:, HEAD_SIZE:].astype(BF)], axis=1)
    proj_grad = jnp.concatenate(query_low_grads + [key_value_grad], axis=1)
    key_value_task = spread(key_value_gradient(key_value_grad, proj_grad))
    one, two = rounds.until(*query_tasks)
    query_task = spread(exchange_owners(jnp.concatenate([one, two], axis=1)))
    xn_one_grad = rounds.until(tables["scatter"])
    _, norm_one_back = jax.vjp(lambda values: rms_scale(values, full_in), x_float)
    (x_norm_grad,) = norm_one_back(xn_one_grad)
    input_grad = (x_one_grad + x_norm_grad).astype(BF)

    grad_gate, grad_up, grad_down, mixture, grad_out, grad_query, grad_kv = rounds.until(
        gate_task,
        up_task,
        down_task,
        tables["mixture"],
        grad_out_task,
        query_task,
        key_value_task,
    )
    result = (x_one + mixture).astype(BF)
    half = QW // 2
    first = sum(block[:, half : half + lanes].astype(F32) for block in grad_query)
    last = sum(block[:, 2 * HEAD_SIZE :].astype(F32) for block in grad_kv)

    def whole(blocks):
        return jnp.concatenate(links.natural(blocks, links.b), axis=1).astype(F32)

    grad_query = whole(
        [
            jnp.concatenate([block[:, :half], block[:, half + lanes :]], axis=1)
            for block in grad_query
        ]
    )
    grad_key = whole([block[:, :HEAD_SIZE] for block in grad_kv])
    grad_value = whole([block[:, HEAD_SIZE : 2 * HEAD_SIZE] for block in grad_kv])
    grad_router, grad_mid = first[:, :experts], first[:, experts]
    grad_in = last[:, 0]
    grad_qgain, grad_kgain = last[:head_part, 1], last[:head_part, 2]

    return (
        result,
        input_grad,
        grad_in,
        grad_query,
        grad_key,
        grad_value,
        grad_qgain,
        grad_kgain,
        grad_out,
        grad_mid,
        grad_router,
        grad_gate[None],
        grad_up[None],
        grad_down[None],
    )


def solution(mesh):
    every = ("dp", "expert")
    in_specs = (
        P(every, None),
        P("dp", None),
        P("dp"),
        P(every, None),
        P(every, None),
        P(every),
        P(every, None),
        P(every, None),
        P(every, None),
        P(every),
        P(every),
        P(every, None),
        P(every),
        P(every, None),
        P("expert", "dp", None),
        P("expert", "dp", None),
        P("expert", None, "dp"),
        P(every, None),
    )
    out_specs = (
        P(every, None),
        P(every, None),
        P(every),
        P(every, None),
        P(every, None),
        P(every, None),
        P(every),
        P(every),
        P(every, None),
        P(every),
        P(every, None),
        P("expert", "dp", None),
        P("expert", "dp", None),
        P("expert", None, "dp"),
    )
    return jax.shard_map(body, mesh=mesh, in_specs=in_specs, out_specs=out_specs, check_vma=False)
```

time: 873 us -> 763 us (0.87)
  matrix products: 189 us -> 56.6 us
  Pallas kernels: 25.8 us -> 145 us
  waiting for transfers between devices: 289 us -> 191 us
  local copies, waits for them, and re-layouts: 83.3 us -> 131 us
  other arithmetic: 92.7 us -> 53.3 us
    dot_general x102 -> x1, matrix products: 151 us -> 4.55 us  [head_gradients(): jnp.einsum('td,hd->th', block_grad, block_out, preferred_element_type=F32)]
    pallas_call x6 -> x31, Pallas kernels: 22.1 us -> 141 us  [the longest x4 45.4 us: expert_rows(): pl.pallas_call(lambda *refs: expert_kernel(blocks, *refs), grid=(ff // st...]
    ppermute x136 -> x113, waiting for transfers between devices: 286 us -> 187 us  [the longest x101 177 us: flip(): return lax.ppermute(value, 'expert', [(i, i ^ mask) for i in range(self.n)])]
    unnamed x444 -> x527, local copies, waits for them, and re-layouts: 40.2 us -> 72.4 us
    ppermute x136 -> x113, starting transfers between devices: 160 us -> 141 us  [the longest x101 128 us: flip(): return lax.ppermute(value, 'expert', [(i, i ^ mask) for i in range(self.n)])]
    ppermute x18 -> x13, starting transfers between devices: 1.61 us -> 12.4 us  [twin(): return lax.ppermute(value, 'dp', [(0, 1), (1, 0)])]
    convert_element_type x29 -> x18, other arithmetic: 21.8 us -> 12.8 us  [the longest x5 4.06 us: block_scatter(): across = (blocks[2].astype(F32) + came.astype(F32)).astype(BF)]
    concatenate x35 -> x25, other arithmetic: 21.9 us -> 14.6 us  [the longest x8 5.5 us: owners_blocks(): blocks.append(jnp.concatenate(parts, axis=0))]
  transfers between devices with their start and end apart: 159 -> 131, of which waited for: 60 -> 54; matrix products, arithmetic and copies ran while one was open for 38% -> 21% of each run, Pallas kernels for 3% -> 18%
where the time goes in v3:
time: 763 us; the launch traced here: 753 us
  waiting for transfers between devices  191 us (25%)
  starting transfers between devices  159 us (21%)
  Pallas kernels  145 us (19%)
  local copies, waits for them, and re-layouts  131 us (17%)
  matrix products  56.6 us (7%)
  other arithmetic  53.3 us (7%)
  between operations  17.6 us (2%)
    ppermute x101, waiting for transfers between devices, flip(): return lax.ppermute(value, 'expert', [(i, i ^ mask) for i in range(self.n)])  177 us
    ppermute x101, starting transfers between devices, flip(): return lax.ppermute(value, 'expert', [(i, i ^ mask) for i in range(self.n)])  128 us
    unnamed x527, local copies, waits for them, and re-layouts  72.4 us
    pallas_call x4, Pallas kernels, expert_rows(): pl.pallas_call(lambda *refs: expert_kernel(blocks, *refs), grid=(ff // st...  45.4 us
    pallas_call x4, Pallas kernels, attention_backward(): pl.pallas_call(backward_kernel, grid=(columns // HEAD_SIZE, rows // step)...  40 us
    dot_general x12, matrix products, by_rows(): jnp.einsum('rd,rf->df', rows_in, grads_in, preferred_element_type=F32)  39.9 us
    pallas_call x4, Pallas kernels, attention_forward(): pl.pallas_call(forward_kernel, grid=(columns // HEAD_SIZE, rows // step),...  19.1 us
  transfers between devices with their start and end apart: 131, of which 54 were waited for; matrix products, arithmetic and copies ran while one was open for 21% of the time, Pallas kernels for 18%

profile of v3, /device:TPU:0, one launch (start us, length us, event | category | flops | bytes accessed | tf_op | source)
XLA Modules:
  0.0 752.7 jit_solution(3250245514180141481)
XLA Ops:
  13.8 4.0 collective-permute-start.3
  18.4 2.8 collective-permute-start
  25.3 3.4 collective-permute-done.2
  44.8 8.1 %collective-permute-done.6 = bf16[4,40,128]{2,1,0:T(8,128)(2,1)S(1)} collective-permute-done((bf16[4,40,128]{2,1,0:T(8,128)(2,1)S(1)}, bf16[4,40,128]{2,1,0:T(8,128)(2,1)S(1)}, u32[]{:S(2)}, u32[]{:S(2)}) %collective-permute-start.6) | collective-permute-done | bytes 40992 | tf_op jit(solution)/shard_map/ppermute | solution.py:585
  57.3 7.2 collective-permute-start.14
  65.8 5.8 collective-permute-done.11
  76.7 4.0 collective-permute-done.17
  84.2 9.0 %collective-permute-start.19 = (bf16[256,1280]{1,0:T(8,128)(2,1)}, bf16[256,1280]{1,0:T(8,128)(2,1)}, u32[]{:S(2)}, u32[]{:S(2)}) collective-permute-start(bf16[256,1280]{1,0:T(8,128)(2,1)} %pad_maximum_fusion.3.refs_0_), channel_id=1, source_target_pairs={{0,16},{16,0},{1,17},{17,1},{2,18},{18,2},{3,19},{19,3},{4,20},{20... | collective-permute-start | bytes 1966088 | tf_op jit(solution)/shard_map/ppermute | solution.py:596
  101.3 3.7 shard_map.281
  105.0 10.2 %collective-permute-start.24 = (bf16[64,2048]{1,0:T(8,128)(2,1)}, bf16[64,2048]{1,0:T(8,128)(2,1)}, u32[]{:S(2)}, u32[]{:S(2)}) collective-permute-start(bf16[64,2048]{1,0:T(8,128)(2,1)} %get-tuple-element.658), channel_id=1, source_target_pairs={{0,8},{1,9},{2,10},{3,11},{4,12},{5,13},{6,14},{7,15},{8,0},{9,1},... | collective-permute-start | bytes 786440 | tf_op jit(solution)/shard_map/ppermute | solution.py:585
  118.3 11.3 %shard_map.283 = (bf16[2048,1280]{1,0:T(8,128)(2,1)}, f32[512,1280]{1,0:T(8,128)}, bf16[512,1280]{1,0:T(8,128)(2,1)}) custom-call(s32[32]{0:T(128)} %add_multiply_fusion.1.starts_ref, bf16[512,2048]{1,0:T(8,128)(2,1)} %fusion.2.x_ref, f32[512,128]{1,0:T(8,128)} %get-tuple-element.661.cos_ref, f32[512,128]{1,0:T(8,128)} %get-tuple-element.662.sin_ref, ...), custom_call_target="tpu_custom_call" | custom-call | flops 2684354560 | bytes 7340032 | tf_op jit(solution)/shard_map/pallas_call | solution.py:69
  137.5 3.7 collective-permute-done.25
  141.2 7.4 collective-permute-done.26
  154.6 6.8 collective-permute-done.27
  178.1 4.8 shard_map.284
  187.4 2.9 collective-permute-start.35
  199.8 4.8 shard_map.286
  209.2 4.8 shard_map.288
  217.6 3.2 constant_dynamic-update-slice_fusion.27
  220.8 3.2 collective-permute-done.41.refs_6_
  224.0 5.3 collective-permute-done.42.refs_7_
  234.9 4.8 shard_map.290
  241.3 3.9 collective-permute-done.45.refs_7_
  250.9 6.5 fusion.98
  260.5 4.4 collective-permute-done.47
  274.3 5.0 collective-permute-done.49
  292.3 3.0 collective-permute-done.51.refs_2_
  295.2 3.8 collective-permute-done.52.refs_3_
  311.8 11.2 %shard_map.293 = (bf16[72,2176]{1,0:T(8,128)(2,1)S(1)}, bf16[72,2176]{1,0:T(8,128)(2,1)S(1)}, bf16[72,2176]{1,0:T(8,128)(2,1)S(1)}, bf16[72,2176]{1,0:T(8,128)(2...) custom-call(s32[1]{0:T(128)} %bitcast.69.refs_0_, ...), custom_call_target="tpu_custom_call" | custom-call | flops 5435817984 | bytes 9437184 | tf_op jit(solution)/shard_map/pallas_call | solution.py:409
  330.9 11.3 %shard_map.295 = (bf16[72,2176]{1,0:T(8,128)(2,1)S(1)}, bf16[72,2176]{1,0:T(8,128)(2,1)S(1)}, bf16[72,2176]{1,0:T(8,128)(2,1)S(1)}, bf16[72,2176]{1,0:T(8,128)(2...) custom-call(s32[1]{0:T(128)} %bitcast.69.refs_0_, ...), custom_call_target="tpu_custom_call" | custom-call | flops 5435817984 | bytes 9437184 | tf_op jit(solution)/shard_map/pallas_call | solution.py:409
  343.4 5.8 collective-permute-done.61.refs_4_
  358.6 11.6 %shard_map.297 = (bf16[72,2176]{1,0:T(8,128)(2,1)S(1)}, bf16[72,2176]{1,0:T(8,128)(2,1)}, bf16[72,2176]{1,0:T(8,128)(2,1)}, bf16[72,2176]{1,0:T(8,128)(2,1)}, bf...) custom-call(s32[1]{0:T(128)} %bitcast.69.refs_0_, ...), custom_call_target="tpu_custom_call" | custom-call | flops 5435817984 | bytes 9437184 | tf_op jit(solution)/shard_map/pallas_call | solution.py:409
  371.0 4.1 collective-permute-done.65.refs_4_
  383.7 11.2 %shard_map.299 = (bf16[72,2176]{1,0:T(8,128)(2,1)S(1)}, bf16[72,2176]{1,0:T(8,128)(2,1)S(1)}, bf16[72,2176]{1,0:T(8,128)(2,1)S(1)}, bf16[72,2176]{1,0:T(8,128)(2...) custom-call(s32[1]{0:T(128)} %bitcast.69.refs_0_, ...), custom_call_target="tpu_custom_call" | custom-call | flops 5435817984 | bytes 9437184 | tf_op jit(solution)/shard_map/pallas_call | solution.py:409
  404.4 4.4 collective-permute-done.70.refs_2_
  408.8 5.7 collective-permute-done.71.refs_3_
  421.1 4.3 constant_dynamic-slice_fusion.21
  425.5 5.8 collective-permute-done.76.refs_3_
  439.4 3.6 convolution_convert_fusion.3
  443.0 3.1 collective-permute-done.78
  448.3 2.8 fusion.83
  456.9 3.7 collective-permute-done.81
  462.7 4.5 convolution_convert_fusion.6
  469.1 8.8 %collective-permute-done.83.refs_5_ = bf16[128,2048]{1,0:T(8,128)(2,1)S(1)} collective-permute-done((bf16[128,2048]{1,0:T(8,128)(2,1)S(1)}, bf16[128,2048]{1,0:T(8,128)(2,1)S(1)}, u32[]{:S(2)}, u32[]{:S(2)}) %collective-permute-start.83) | collective-permute-done | bytes 524320 | tf_op jit(solution)/shard_map/ppermute | solution.py:588
  488.1 9.9 %shard_map.304 = (bf16[512,256]{1,0:T(8,128)(2,1)S(1)}, f32[2048,256]{1,0:T(8,128)S(1)}, f32[1,128]{1,0:T(1,128)S(1)}) custom-call(bf16[512,256]{1,0:T(8,128)(2,1)S(1)} %copy-done.77, bf16[512,256]{1,0:T(8,128)(2,1)S(1)} %get-tuple-element.973.grad_ref, f32[512,256]{1,0:T(8,128)S(1)} %get-tuple-element.974.proj_ref, bf16[2048,256]{1,0:T(8,128)(2,1)S(1)} %copy-done.21, ...), custom_call_target="tpu_custom_call" | custom-call | flops 2684354560 | bytes 1048576 | tf_op jit(solution)/shard_map/pallas_call | solution.py:267
  509.7 9.9 %shard_map.306 = (bf16[512,256]{1,0:T(8,128)(2,1)S(1)}, f32[2048,256]{1,0:T(8,128)S(1)}, f32[1,128]{1,0:T(1,128)S(1)}) custom-call(bf16[512,256]{1,0:T(8,128)(2,1)S(1)} %copy-done.75, bf16[512,256]{1,0:T(8,128)(2,1)S(1)} %get-tuple-element.996.grad_ref, f32[512,256]{1,0:T(8,128)S(1)} %get-tuple-element.997.proj_ref, bf16[2048,256]{1,0:T(8,128)(2,1)S(1)} %copy-done.21, ...), custom_call_target="tpu_custom_call" | custom-call | flops 2684354560 | bytes 1048576 | tf_op jit(solution)/shard_map/pallas_call | solution.py:267
  519.6 5.5 collective-permute-done.90.refs_2_
  525.1 4.6 collective-permute-done.92.refs_4_
  533.6 4.0 collective-permute-start.96
  542.4 10.1 %shard_map.308 = (bf16[512,256]{1,0:T(8,128)(2,1)S(1)}, f32[2048,256]{1,0:T(8,128)S(1)}, f32[1,128]{1,0:T(1,128)S(1)}) custom-call(bf16[512,256]{1,0:T(8,128)(2,1)S(1)} %copy-done.73, bf16[512,256]{1,0:T(8,128)(2,1)S(1)} %copy-done.79, f32[512,256]{1,0:T(8,128)S(1)} %copy-done.40, bf16[2048,256]{1,0:T(8,128)(2,1)S(1)} %copy-done.22, ...), custom_call_target="tpu_custom_call" | custom-call | flops 2684354560 | bytes 1048576 | tf_op jit(solution)/shard_map/pallas_call | solution.py:267
  552.6 5.3 collective-permute-done.96
  566.9 10.1 %shard_map.309 = (bf16[512,256]{1,0:T(8,128)(2,1)S(1)}, f32[2048,256]{1,0:T(8,128)S(1)}, f32[1,128]{1,0:T(1,128)S(1)}) custom-call(bf16[512,256]{1,0:T(8,128)(2,1)S(1)} %copy-done.71, bf16[512,256]{1,0:T(8,128)(2,1)S(1)} %copy-done.78, f32[512,256]{1,0:T(8,128)S(1)} %copy-done.39, bf16[2048,256]{1,0:T(8,128)(2,1)S(1)} %copy-done.22, ...), custom_call_target="tpu_custom_call" | custom-call | flops 2684354560 | bytes 1048576 | tf_op jit(solution)/shard_map/pallas_call | solution.py:267
  590.2 5.7 convolution_convert_fusion.1
  598.4 4.4 collective-permute-done.103
  615.2 5.7 collective-permute-done.107
  638.1 5.4 collective-permute-start.108
  646.9 2.8 fusion.11
  653.5 6.5 shard_map.312
  660.0 19.2 %collective-permute-done.110 = bf16[256,640]{0,1:T(8,128)(2,1)} collective-permute-done((bf16[256,640]{0,1:T(8,128)(2,1)}, bf16[256,640]{0,1:T(8,128)(2,1)}, u32[]{:S(2)}, u32[]{:S(2)}) %collective-permute-start.110) | collective-permute-done | bytes 327712 | tf_op jit(solution)/shard_map/ppermute | solution.py:585
  682.5 5.9 convert_add_fusion.2
  700.7 5.4 convert_add_fusion.1
  706.1 4.0 collective-permute-done.117
  710.1 4.8 collective-permute-done.116
  726.8 5.8 convert_add_fusion
  (962 shorter events, 350.4 us)
Async XLA Ops:
  7.2 301.8 %all-gather.4.cloned.1.call-start = ((), (), s32[]{:S(2)}) async-start(), calls=%async_computation | async-start | bytes 4718592 | tf_op jit(solution)/shard_map/all_gather | solution.py:722
  13.8 14.9 %collective-permute-start.3 = (bf16[64,1280]{1,0:T(8,128)(2,1)}, bf16[64,1280]{1,0:T(8,128)(2,1)S(1)}, u32[]{:S(2)}, u32[]{:S(2)}) collective-permute-start(bf16[64,1280]{1,0:T(8,128)(2,1)} %pad_maximum_fusion.29), channel_id=1, source_target_pairs={{0,6},{1,7},{2,4},{3,5},{4,2},{5,3},{6,0},{7,1},{8,14},{9,15},{10,... | collective-permute-start | bytes 491528 | tf_op jit(solution)/shard_map/ppermute | solution.py:585
  21.8 287.2 %all-gather.6.cloned.1.call-start = ((), (), s32[]{:S(2)}) async-start(), calls=%async_computation.1 | async-start | bytes 4718592 | tf_op jit(solution)/shard_map/all_gather | solution.py:723
  32.4 22.6 %collective-permute-start.7 = (bf16[256,1280]{1,0:T(8,128)(2,1)}, bf16[256,1280]{1,0:T(8,128)(2,1)}, u32[]{:S(2)}, u32[]{:S(2)}) collective-permute-start(bf16[256,1280]{1,0:T(8,128)(2,1)} %pad_maximum_fusion.3.refs_0_), channel_id=1, source_target_pairs={{0,1},{1,0},{2,3},{3,2},{4,5},{5,4},{6,7},{7,6},{8,9},{9,8},{10,11... | collective-permute-start | bytes 1966088 | tf_op jit(solution)/shard_map/ppermute | solution.py:585
  33.9 21.1 %collective-permute-start.10 = (bf16[128,2048]{1,0:T(8,128)(2,1)S(1)}, bf16[128,2048]{1,0:T(8,128)(2,1)S(1)}, u32[]{:S(2)}, u32[]{:S(2)}) collective-permute-start(bf16[128,2048]{1,0:T(8,128)(2,1)S(1)} %copy-done.151), channel_id=1, source_target_pairs={{0,4},{1,5},{2,6},{3,7},{4,0},{5,1},{6,2},{7,3},{8,12},{9,13},{10,... | collective-permute-start | bytes 1572872 | tf_op jit(solution)/shard_map/ppermute | solution.py:585
  35.6 19.4 %collective-permute-start.9 = (bf16[128,2048]{1,0:T(8,128)(2,1)S(1)}, bf16[128,2048]{1,0:T(8,128)(2,1)}, u32[]{:S(2)}, u32[]{:S(2)}) collective-permute-start(bf16[128,2048]{1,0:T(8,128)(2,1)S(1)} %copy-done.151), channel_id=1, source_target_pairs={{0,2},{1,3},{2,0},{3,1},{4,6},{5,7},{6,4},{7,5},{8,10},{9,11},{10,... | collective-permute-start | bytes 1572872 | tf_op jit(solution)/shard_map/ppermute | solution.py:585
  40.1 14.9 %collective-permute-start.8 = (bf16[128,1280]{1,0:T(8,128)(2,1)}, bf16[128,1280]{1,0:T(8,128)(2,1)S(1)}, u32[]{:S(2)}, u32[]{:S(2)}) collective-permute-start(bf16[128,1280]{1,0:T(8,128)(2,1)} %pad_maximum_fusion.9), channel_id=1, source_target_pairs={{0,8},{1,9},{2,10},{3,11},{4,12},{5,13},{6,14},{7,15},{8,0},{9,1},... | collective-permute-start | bytes 983048 | tf_op jit(solution)/shard_map/ppermute | solution.py:585
  56.0 15.5 %collective-permute-start.12 = (bf16[128,1280]{1,0:T(8,128)(2,1)S(1)}, bf16[128,1280]{1,0:T(8,128)(2,1)S(1)}, u32[]{:S(2)}, u32[]{:S(2)}) collective-permute-start(bf16[128,1280]{1,0:T(8,128)(2,1)S(1)} %pad_maximum_fusion.10), channel_id=1, source_target_pairs={{0,8},{1,9},{2,10},{3,11},{4,12},{5,13},{6,14},{7,15},{8,0},{9,1},... | collective-permute-start | bytes 983048 | tf_op jit(solution)/shard_map/ppermute | solution.py:585
  100.0 29.6 %collective-permute-start.23 = (bf16[128,2048]{1,0:T(8,128)(2,1)}, bf16[128,2048]{1,0:T(8,128)(2,1)}, u32[]{:S(2)}, u32[]{:S(2)}) collective-permute-start(bf16[128,2048]{1,0:T(8,128)(2,1)} %copy-done.162), channel_id=1, source_target_pairs={{0,1},{1,0},{2,3},{3,2},{4,5},{5,4},{6,7},{7,6},{8,9},{9,8},{10,11... | collective-permute-start | bytes 1572872 | tf_op jit(solution)/shard_map/ppermute | solution.py:585
  105.0 24.6 %collective-permute-start.24 = (bf16[64,2048]{1,0:T(8,128)(2,1)}, bf16[64,2048]{1,0:T(8,128)(2,1)}, u32[]{:S(2)}, u32[]{:S(2)}) collective-permute-start(bf16[64,2048]{1,0:T(8,128)(2,1)} %get-tuple-element.658), channel_id=1, source_target_pairs={{0,8},{1,9},{2,10},{3,11},{4,12},{5,13},{6,14},{7,15},{8,0},{9,1},... | collective-permute-start | bytes 786440 | tf_op jit(solution)/shard_map/ppermute | solution.py:585
  162.1 21.6 %collective-permute-start.30 = (bf16[128,2048]{1,0:T(8,128)(2,1)S(1)}, bf16[128,2048]{1,0:T(8,128)(2,1)}, u32[]{:S(2)}, u32[]{:S(2)}) collective-permute-start(bf16[128,2048]{1,0:T(8,128)(2,1)S(1)} %copy-done.4), channel_id=1, source_target_pairs={{0,4},{1,5},{2,6},{3,7},{4,8},{5,9},{6,10},{7,11},{8,12},{9,13},{1... | collective-permute-start | bytes 1572872 | tf_op jit(solution)/shard_map/ppermute | solution.py:588
  163.6 20.1 %collective-permute-start.31 = (bf16[72,2048]{1,0:T(8,128)(2,1)}, bf16[72,2048]{1,0:T(8,128)(2,1)}, u32[]{:S(2)}, u32[]{:S(2)}) collective-permute-start(bf16[72,2048]{1,0:T(8,128)(2,1)} %get-tuple-element.689), channel_id=1, source_target_pairs={{0,1},{1,0},{2,3},{3,2},{4,5},{5,4},{6,7},{7,6},{8,9},{9,8},{10,11... | collective-permute-start | bytes 884744 | tf_op jit(solution)/shard_map/ppermute | solution.py:585
  163.9 19.8 %collective-permute-start.32 = (bf16[72,2048]{1,0:T(8,128)(2,1)}, bf16[72,2048]{1,0:T(8,128)(2,1)}, u32[]{:S(2)}, u32[]{:S(2)}) collective-permute-start(bf16[72,2048]{1,0:T(8,128)(2,1)} %get-tuple-element.690), channel_id=1, source_target_pairs={{0,2},{1,3},{2,0},{3,1},{4,6},{5,7},{6,4},{7,5},{8,10},{9,11},{10,... | collective-permute-start | bytes 884744 | tf_op jit(solution)/shard_map/ppermute | solution.py:585
  165.0 18.7 %collective-permute-start.33 = (bf16[72,2048]{1,0:T(8,128)(2,1)}, bf16[72,2048]{1,0:T(8,128)(2,1)}, u32[]{:S(2)}, u32[]{:S(2)}) collective-permute-start(bf16[72,2048]{1,0:T(8,128)(2,1)} %get-tuple-element.691), channel_id=1, source_target_pairs={{0,3},{1,2},{2,1},{3,0},{4,7},{5,6},{6,5},{7,4},{8,11},{9,10},{10,... | collective-permute-start | bytes 884744 | tf_op jit(solution)/shard_map/ppermute | solution.py:585
  167.1 16.6 %collective-permute-start.34 = (bf16[64,2048]{1,0:T(8,128)(2,1)}, bf16[64,2048]{1,0:T(8,128)(2,1)}, u32[]{:S(2)}, u32[]{:S(2)}) collective-permute-start(bf16[64,2048]{1,0:T(8,128)(2,1)} %collective-permute-done.27), channel_id=1, source_target_pairs={{0,1},{1,0},{2,3},{3,2},{4,5},{5,4},{6,7},{7,6},{8,9},{9,8},{10,11... | collective-permute-start | bytes 786440 | tf_op jit(solution)/shard_map/ppermute | solution.py:585
  187.3 20.0 %collective-permute-start.39 = (bf16[512,2048]{1,0:T(8,128)(2,1)}, bf16[512,2048]{1,0:T(8,128)(2,1)}, u32[]{:S(2)}, u32[]{:S(2)}) collective-permute-start(bf16[512,2048]{1,0:T(8,128)(2,1)} %get-tuple-element.708), channel_id=1, source_target_pairs={{0,16},{16,0},{1,17},{17,1},{2,18},{18,2},{3,19},{19,3},{4,20},{20... | collective-permute-start | bytes 6291464 | tf_op jit(solution)/shard_map/ppermute | solution.py:596
  187.4 20.0 %collective-permute-start.35 = (bf16[128,2048]{1,0:T(8,128)(2,1)}, bf16[128,2048]{1,0:T(8,128)(2,1)S(1)}, u32[]{:S(2)}, u32[]{:S(2)}) collective-permute-start(bf16[128,2048]{1,0:T(8,128)(2,1)} %collective-permute-done.30.refs_1_), channel_id=1, source_target_pairs={{0,4},{1,5},{2,6},{3,7},{4,8},{5,9},{6,10},{7,11},{8,12},{9,13},{1... | collective-permute-start | bytes 1572872 | tf_op jit(solution)/shard_map/ppermute | solution.py:588
  190.3 118.6 %all-gather.8.cloned.1.call-start = ((), (), s32[]{:S(2)}) async-start(), calls=%async_computation.2 | async-start | bytes 4718592 | tf_op jit(solution)/shard_map/all_gather | solution.py:724
  191.2 15.4 %collective-permute-start.37 = (bf16[72,2048]{1,0:T(8,128)(2,1)}, bf16[72,2048]{1,0:T(8,128)(2,1)S(1)}, u32[]{:S(2)}, u32[]{:S(2)}) collective-permute-start(bf16[72,2048]{1,0:T(8,128)(2,1)} %copy-done.135), channel_id=1, source_target_pairs={{0,2},{1,3},{2,0},{3,1},{4,6},{5,7},{6,4},{7,5},{8,10},{9,11},{10,... | collective-permute-start | bytes 884744 | tf_op jit(solution)/shard_map/ppermute | solution.py:585
  191.4 15.2 %collective-permute-start.38 = (bf16[72,2048]{1,0:T(8,128)(2,1)}, bf16[72,2048]{1,0:T(8,128)(2,1)S(1)}, u32[]{:S(2)}, u32[]{:S(2)}) collective-permute-start(bf16[72,2048]{1,0:T(8,128)(2,1)} %copy-done.134), channel_id=1, source_target_pairs={{0,3},{1,2},{2,1},{3,0},{4,7},{5,6},{6,5},{7,4},{8,11},{9,10},{10,... | collective-permute-start | bytes 884744 | tf_op jit(solution)/shard_map/ppermute | solution.py:585
  208.5 21.6 %collective-permute-start.40 = (bf16[128,2048]{1,0:T(8,128)(2,1)S(1)}, bf16[128,2048]{1,0:T(8,128)(2,1)S(1)}, u32[]{:S(2)}, u32[]{:S(2)}) collective-permute-start(bf16[128,2048]{1,0:T(8,128)(2,1)S(1)} %collective-permute-done.35.refs_1_), channel_id=1, source_target_pairs={{0,4},{1,5},{2,6},{3,7},{4,8},{5,9},{6,10},{7,11},{8,12},{9,13},{1... | collective-permute-start | bytes 1572872 | tf_op jit(solution)/shard_map/ppermute | solution.py:588
  303.0 20.2 %collective-permute-start.58 = (bf16[128,2048]{1,0:T(8,128)(2,1)}, bf16[128,2048]{1,0:T(8,128)(2,1)}, u32[]{:S(2)}, u32[]{:S(2)}) collective-permute-start(bf16[128,2048]{1,0:T(8,128)(2,1)} %collective-permute-done.54.refs_1_), channel_id=1, source_target_pairs={{0,4},{1,5},{2,6},{3,7},{4,8},{5,9},{6,10},{7,11},{8,12},{9,13},{1... | collective-permute-start | bytes 1572872 | tf_op jit(solution)/shard_map/ppermute | solution.py:588
  305.5 17.6 %collective-permute-start.55 = (bf16[72,2048]{1,0:T(8,128)(2,1)}, bf16[72,2048]{1,0:T(8,128)(2,1)}, u32[]{:S(2)}, u32[]{:S(2)}) collective-permute-start(bf16[72,2048]{1,0:T(8,128)(2,1)} %get-tuple-element.756), channel_id=1, source_target_pairs={{0,1},{1,0},{2,3},{3,2},{4,5},{5,4},{6,7},{7,6},{8,9},{9,8},{10,11... | collective-permute-start | bytes 884744 | tf_op jit(solution)/shard_map/ppermute | solution.py:585
  306.6 16.4 %collective-permute-start.56 = (bf16[72,2048]{1,0:T(8,128)(2,1)}, bf16[72,2048]{1,0:T(8,128)(2,1)}, u32[]{:S(2)}, u32[]{:S(2)}) collective-permute-start(bf16[72,2048]{1,0:T(8,128)(2,1)} %get-tuple-element.757), channel_id=1, source_target_pairs={{0,2},{1,3},{2,0},{3,1},{4,6},{5,7},{6,4},{7,5},{8,10},{9,11},{10,... | collective-permute-start | bytes 884744 | tf_op jit(solution)/shard_map/ppermute | solution.py:585
  307.4 15.7 %collective-permute-start.57 = (bf16[72,2048]{1,0:T(8,128)(2,1)}, bf16[72,2048]{1,0:T(8,128)(2,1)}, u32[]{:S(2)}, u32[]{:S(2)}) collective-permute-start(bf16[72,2048]{1,0:T(8,128)(2,1)} %get-tuple-element.758), channel_id=1, source_target_pairs={{0,3},{1,2},{2,1},{3,0},{4,7},{5,6},{6,5},{7,4},{8,11},{9,10},{10,... | collective-permute-start | bytes 884744 | tf_op jit(solution)/shard_map/ppermute | solution.py:585
  325.2 17.2 %collective-permute-start.59 = (bf16[72,4224]{1,0:T(8,128)(2,1)S(1)}, bf16[72,4224]{1,0:T(8,128)(2,1)S(1)}, u32[]{:S(2)}, u32[]{:S(2)}) collective-permute-start(bf16[72,4224]{1,0:T(8,128)(2,1)S(1)} %get-tuple-element.799), channel_id=1, source_target_pairs={{0,1},{1,0},{2,3},{3,2},{4,5},{5,4},{6,7},{7,6},{8,9},{9,8},{10,11... | collective-permute-start | bytes 1824776 | tf_op jit(solution)/shard_map/ppermute | solution.py:585
  326.4 17.0 %collective-permute-start.60 = (bf16[72,4224]{1,0:T(8,128)(2,1)S(1)}, bf16[72,4224]{1,0:T(8,128)(2,1)S(1)}, u32[]{:S(2)}, u32[]{:S(2)}) collective-permute-start(bf16[72,4224]{1,0:T(8,128)(2,1)S(1)} %get-tuple-element.800), channel_id=1, source_target_pairs={{0,2},{1,3},{2,0},{3,1},{4,6},{5,7},{6,4},{7,5},{8,10},{9,11},{10,... | collective-permute-start | bytes 1824776 | tf_op jit(solution)/shard_map/ppermute | solution.py:585
  327.2 22.0 %collective-permute-start.61 = (bf16[72,4224]{1,0:T(8,128)(2,1)S(1)}, bf16[72,4224]{1,0:T(8,128)(2,1)S(1)}, u32[]{:S(2)}, u32[]{:S(2)}) collective-permute-start(bf16[72,4224]{1,0:T(8,128)(2,1)S(1)} %get-tuple-element.801), channel_id=1, source_target_pairs={{0,3},{1,2},{2,1},{3,0},{4,7},{5,6},{6,5},{7,4},{8,11},{9,10},{10,... | collective-permute-start | bytes 1824776 | tf_op jit(solution)/shard_map/ppermute | solution.py:585
  350.7 20.3 %collective-permute-start.63 = (bf16[72,4224]{1,0:T(8,128)(2,1)}, bf16[72,4224]{1,0:T(8,128)(2,1)S(1)}, u32[]{:S(2)}, u32[]{:S(2)}) collective-permute-start(bf16[72,4224]{1,0:T(8,128)(2,1)} %get-tuple-element.836), channel_id=1, source_target_pairs={{0,1},{1,0},{2,3},{3,2},{4,5},{5,4},{6,7},{7,6},{8,9},{9,8},{10,11... | collective-permute-start | bytes 1824776 | tf_op jit(solution)/shard_map/ppermute | solution.py:585
  352.8 18.2 %collective-permute-start.64 = (bf16[72,4224]{1,0:T(8,128)(2,1)}, bf16[72,4224]{1,0:T(8,128)(2,1)S(1)}, u32[]{:S(2)}, u32[]{:S(2)}) collective-permute-start(bf16[72,4224]{1,0:T(8,128)(2,1)} %get-tuple-element.837), channel_id=1, source_target_pairs={{0,2},{1,3},{2,0},{3,1},{4,6},{5,7},{6,4},{7,5},{8,10},{9,11},{10,... | collective-permute-start | bytes 1824776 | tf_op jit(solution)/shard_map/ppermute | solution.py:585
  354.8 20.3 %collective-permute-start.65 = (bf16[72,4224]{1,0:T(8,128)(2,1)S(1)}, bf16[72,4224]{1,0:T(8,128)(2,1)S(1)}, u32[]{:S(2)}, u32[]{:S(2)}) collective-permute-start(bf16[72,4224]{1,0:T(8,128)(2,1)S(1)} %get-tuple-element.838), channel_id=1, source_target_pairs={{0,3},{1,2},{2,1},{3,0},{4,7},{5,6},{6,5},{7,4},{8,11},{9,10},{10,... | collective-permute-start | bytes 1824776 | tf_op jit(solution)/shard_map/ppermute | solution.py:585
  375.6 21.0 %collective-permute-start.69 = (bf16[128,2176]{1,0:T(8,128)(2,1)S(1)}, bf16[128,2176]{1,0:T(8,128)(2,1)S(1)}, u32[]{:S(2)}, u32[]{:S(2)}) collective-permute-start(bf16[128,2176]{1,0:T(8,128)(2,1)S(1)} %shard_map.298), channel_id=1, source_target_pairs={{0,4},{1,5},{2,6},{3,7},{4,8},{5,9},{6,10},{7,11},{8,12},{9,13},{1... | collective-permute-start | bytes 1671176 | tf_op jit(solution)/shard_map/ppermute | solution.py:588
  377.2 18.6 %collective-permute-start.66 = (bf16[72,2176]{1,0:T(8,128)(2,1)}, bf16[72,2176]{1,0:T(8,128)(2,1)S(1)}, u32[]{:S(2)}, u32[]{:S(2)}) collective-permute-start(bf16[72,2176]{1,0:T(8,128)(2,1)} %get-tuple-element.867), channel_id=1, source_target_pairs={{0,1},{1,0},{2,3},{3,2},{4,5},{5,4},{6,7},{7,6},{8,9},{9,8},{10,11... | collective-permute-start | bytes 940040 | tf_op jit(solution)/shard_map/ppermute | solution.py:585
  379.3 16.5 %collective-permute-start.67 = (bf16[72,2176]{1,0:T(8,128)(2,1)}, bf16[72,2176]{1,0:T(8,128)(2,1)S(1)}, u32[]{:S(2)}, u32[]{:S(2)}) collective-permute-start(bf16[72,2176]{1,0:T(8,128)(2,1)} %get-tuple-element.868), channel_id=1, source_target_pairs={{0,2},{1,3},{2,0},{3,1},{4,6},{5,7},{6,4},{7,5},{8,10},{9,11},{10,... | collective-permute-start | bytes 940040 | tf_op jit(solution)/shard_map/ppermute | solution.py:585
  381.4 15.3 %collective-permute-start.68 = (bf16[72,2176]{1,0:T(8,128)(2,1)}, bf16[72,2176]{1,0:T(8,128)(2,1)S(1)}, u32[]{:S(2)}, u32[]{:S(2)}) collective-permute-start(bf16[72,2176]{1,0:T(8,128)(2,1)} %get-tuple-element.869), channel_id=1, source_target_pairs={{0,3},{1,2},{2,1},{3,0},{4,7},{5,6},{6,5},{7,4},{8,11},{9,10},{10,... | collective-permute-start | bytes 940040 | tf_op jit(solution)/shard_map/ppermute | solution.py:585
  397.1 19.2 %collective-permute-start.73 = (bf16[128,2176]{1,0:T(8,128)(2,1)S(1)}, bf16[128,2176]{1,0:T(8,128)(2,1)S(1)}, u32[]{:S(2)}, u32[]{:S(2)}) collective-permute-start(bf16[128,2176]{1,0:T(8,128)(2,1)S(1)} %shard_map.300), channel_id=1, source_target_pairs={{0,4},{1,5},{2,6},{3,7},{4,8},{5,9},{6,10},{7,11},{8,12},{9,13},{1... | collective-permute-start | bytes 1671176 | tf_op jit(solution)/shard_map/ppermute | solution.py:588
  416.8 16.2 %collective-permute-start.74 = (bf16[128,2176]{1,0:T(8,128)(2,1)S(1)}, bf16[128,2176]{1,0:T(8,128)(2,1)S(1)}, u32[]{:S(2)}, u32[]{:S(2)}) collective-permute-start(bf16[128,2176]{1,0:T(8,128)(2,1)S(1)} %shard_map.301), channel_id=1, source_target_pairs={{0,4},{1,5},{2,6},{3,7},{4,8},{5,9},{6,10},{7,11},{8,12},{9,13},{1... | collective-permute-start | bytes 1671176 | tf_op jit(solution)/shard_map/ppermute | solution.py:588
  461.5 16.4 %collective-permute-start.84 = (bf16[1024,768]{1,0:T(8,128)(2,1)S(1)}, bf16[1024,768]{1,0:T(8,128)(2,1)}, u32[]{:S(2)}, u32[]{:S(2)}) collective-permute-start(bf16[1024,768]{1,0:T(8,128)(2,1)S(1)} %convolution_convert_fusion.2), channel_id=1, source_target_pairs={{0,16},{16,0},{1,17},{17,1},{2,18},{18,2},{3,19},{19,3},{4,20},{20... | collective-permute-start | bytes 4718600 | tf_op jit(solution)/shard_map/ppermute | solution.py:596
  461.6 16.3 %collective-permute-start.83 = (bf16[128,2048]{1,0:T(8,128)(2,1)S(1)}, bf16[128,2048]{1,0:T(8,128)(2,1)S(1)}, u32[]{:S(2)}, u32[]{:S(2)}) collective-permute-start(bf16[128,2048]{1,0:T(8,128)(2,1)S(1)} %shard_map.302), channel_id=1, source_target_pairs={{0,4},{1,5},{2,6},{3,7},{4,8},{5,9},{6,10},{7,11},{8,12},{9,13},{1... | collective-permute-start | bytes 1572872 | tf_op jit(solution)/shard_map/ppermute | solution.py:588
  478.8 21.6 %collective-permute-start.88 = (bf16[512,2048]{1,0:T(8,128)(2,1)S(1)}, bf16[512,2048]{1,0:T(8,128)(2,1)S(1)}, u32[]{:S(2)}, u32[]{:S(2)}) collective-permute-start(bf16[512,2048]{1,0:T(8,128)(2,1)S(1)} %convolution_convert_fusion), channel_id=1, source_target_pairs={{0,16},{16,0},{1,17},{17,1},{2,18},{18,2},{3,19},{19,3},{4,20},{20... | collective-permute-start | bytes 6291464 | tf_op jit(solution)/shard_map/ppermute | solution.py:596
  484.9 15.5 %collective-permute-start.86 = (bf16[72,2048]{1,0:T(8,128)(2,1)S(1)}, bf16[72,2048]{1,0:T(8,128)(2,1)S(1)}, u32[]{:S(2)}, u32[]{:S(2)}) collective-permute-start(bf16[72,2048]{1,0:T(8,128)(2,1)S(1)} %copy-done.103), channel_id=1, source_target_pairs={{0,2},{1,3},{2,0},{3,1},{4,6},{5,7},{6,4},{7,5},{8,10},{9,11},{10,... | collective-permute-start | bytes 884744 | tf_op jit(solution)/shard_map/ppermute | solution.py:585
  485.2 15.2 %collective-permute-start.87 = (bf16[72,2048]{1,0:T(8,128)(2,1)S(1)}, bf16[72,2048]{1,0:T(8,128)(2,1)S(1)}, u32[]{:S(2)}, u32[]{:S(2)}) collective-permute-start(bf16[72,2048]{1,0:T(8,128)(2,1)S(1)} %copy-done.101), channel_id=1, source_target_pairs={{0,3},{1,2},{2,1},{3,0},{4,7},{5,6},{6,5},{7,4},{8,11},{9,10},{10,... | collective-permute-start | bytes 884744 | tf_op jit(solution)/shard_map/ppermute | solution.py:585
  503.6 26.1 %collective-permute-start.89 = (bf16[128,2048]{1,0:T(8,128)(2,1)S(1)}, bf16[128,2048]{1,0:T(8,128)(2,1)S(1)}, u32[]{:S(2)}, u32[]{:S(2)}) collective-permute-start(bf16[128,2048]{1,0:T(8,128)(2,1)S(1)} %shard_map.305), channel_id=1, source_target_pairs={{0,4},{1,5},{2,6},{3,7},{4,8},{5,9},{6,10},{7,11},{8,12},{9,13},{1... | collective-permute-start | bytes 1572872 | tf_op jit(solution)/shard_map/ppermute | solution.py:588
  503.8 25.9 %collective-permute-start.93 = (bf16[128,2048]{1,0:T(8,128)(2,1)S(1)}, bf16[128,2048]{1,0:T(8,128)(2,1)S(1)}, u32[]{:S(2)}, u32[]{:S(2)}) collective-permute-start(bf16[128,2048]{1,0:T(8,128)(2,1)S(1)} %get-tuple-element.994), channel_id=1, source_target_pairs={{0,1},{1,0},{2,3},{3,2},{4,5},{5,4},{6,7},{7,6},{8,9},{9,8},{10,11... | collective-permute-start | bytes 1572872 | tf_op jit(solution)/shard_map/ppermute | solution.py:585
  505.4 19.7 %collective-permute-start.90 = (bf16[72,2048]{1,0:T(8,128)(2,1)S(1)}, bf16[72,2048]{1,0:T(8,128)(2,1)S(1)}, u32[]{:S(2)}, u32[]{:S(2)}) collective-permute-start(bf16[72,2048]{1,0:T(8,128)(2,1)S(1)} %copy-done.97), channel_id=1, source_target_pairs={{0,1},{1,0},{2,3},{3,2},{4,5},{5,4},{6,7},{7,6},{8,9},{9,8},{10,11... | collective-permute-start | bytes 884744 | tf_op jit(solution)/shard_map/ppermute | solution.py:585
  507.0 18.1 %collective-permute-start.91 = (bf16[72,2048]{1,0:T(8,128)(2,1)S(1)}, bf16[72,2048]{1,0:T(8,128)(2,1)S(1)}, u32[]{:S(2)}, u32[]{:S(2)}) collective-permute-start(bf16[72,2048]{1,0:T(8,128)(2,1)S(1)} %copy-done.95), channel_id=1, source_target_pairs={{0,2},{1,3},{2,0},{3,1},{4,6},{5,7},{6,4},{7,5},{8,10},{9,11},{10,... | collective-permute-start | bytes 884744 | tf_op jit(solution)/shard_map/ppermute | solution.py:585
  507.3 22.4 %collective-permute-start.92 = (bf16[72,2048]{1,0:T(8,128)(2,1)S(1)}, bf16[72,2048]{1,0:T(8,128)(2,1)S(1)}, u32[]{:S(2)}, u32[]{:S(2)}) collective-permute-start(bf16[72,2048]{1,0:T(8,128)(2,1)S(1)} %copy-done.93), channel_id=1, source_target_pairs={{0,3},{1,2},{2,1},{3,0},{4,7},{5,6},{6,5},{7,4},{8,11},{9,10},{10,... | collective-permute-start | bytes 884744 | tf_op jit(solution)/shard_map/ppermute | solution.py:585
  531.9 25.9 %collective-permute-start.94 = (bf16[128,2048]{1,0:T(8,128)(2,1)}, bf16[128,2048]{1,0:T(8,128)(2,1)}, u32[]{:S(2)}, u32[]{:S(2)}) collective-permute-start(bf16[128,2048]{1,0:T(8,128)(2,1)} %shard_map.307), channel_id=1, source_target_pairs={{0,4},{1,5},{2,6},{3,7},{4,8},{5,9},{6,10},{7,11},{8,12},{9,13},{1... | collective-permute-start | bytes 1572872 | tf_op jit(solution)/shard_map/ppermute | solution.py:588
  532.9 24.9 %collective-permute-start.95 = (bf16[128,2048]{1,0:T(8,128)(2,1)}, bf16[128,2048]{1,0:T(8,128)(2,1)}, u32[]{:S(2)}, u32[]{:S(2)}) collective-permute-start(bf16[128,2048]{1,0:T(8,128)(2,1)} %get-tuple-element.1011), channel_id=1, source_target_pairs={{0,1},{1,0},{2,3},{3,2},{4,5},{5,4},{6,7},{7,6},{8,9},{9,8},{10,11... | collective-permute-start | bytes 1572872 | tf_op jit(solution)/shard_map/ppermute | solution.py:585
  533.6 24.2 %collective-permute-start.96 = (bf16[64,2048]{1,0:T(8,128)(2,1)}, bf16[64,2048]{1,0:T(8,128)(2,1)}, u32[]{:S(2)}, u32[]{:S(2)}) collective-permute-start(bf16[64,2048]{1,0:T(8,128)(2,1)} %get-tuple-element.1012), channel_id=1, source_target_pairs={{0,8},{1,9},{2,10},{3,11},{4,12},{5,13},{6,14},{7,15},{8,0},{9,1},... | collective-permute-start | bytes 786440 | tf_op jit(solution)/shard_map/ppermute | solution.py:585
  557.8 21.7 %collective-permute-start.101 = (bf16[1024,640]{0,1:T(8,128)(2,1)S(1)}, bf16[1024,640]{0,1:T(8,128)(2,1)S(1)}, u32[]{:S(2)}, u32[]{:S(2)}) collective-permute-start(bf16[1024,640]{0,1:T(8,128)(2,1)S(1)} %pad_maximum_fusion), channel_id=1, source_target_pairs={{0,16},{16,0},{1,17},{17,1},{2,18},{18,2},{3,19},{19,3},{4,20},{20... | collective-permute-start | bytes 3932168 | tf_op jit(solution)/shard_map/ppermute | solution.py:596
  562.5 15.1 %collective-permute-start.97 = (bf16[72,2048]{1,0:T(8,128)(2,1)S(1)}, bf16[72,2048]{1,0:T(8,128)(2,1)S(1)}, u32[]{:S(2)}, u32[]{:S(2)}) collective-permute-start(bf16[72,2048]{1,0:T(8,128)(2,1)S(1)} %copy-done.89), channel_id=1, source_target_pairs={{0,1},{1,0},{2,3},{3,2},{4,5},{5,4},{6,7},{7,6},{8,9},{9,8},{10,11... | collective-permute-start | bytes 884744 | tf_op jit(solution)/shard_map/ppermute | solution.py:585
  564.1 15.4 %collective-permute-start.98 = (bf16[72,2048]{1,0:T(8,128)(2,1)S(1)}, bf16[72,2048]{1,0:T(8,128)(2,1)S(1)}, u32[]{:S(2)}, u32[]{:S(2)}) collective-permute-start(bf16[72,2048]{1,0:T(8,128)(2,1)S(1)} %copy-done.87), channel_id=1, source_target_pairs={{0,2},{1,3},{2,0},{3,1},{4,6},{5,7},{6,4},{7,5},{8,10},{9,11},{10,... | collective-permute-start | bytes 884744 | tf_op jit(solution)/shard_map/ppermute | solution.py:585
  564.1 15.4 %collective-permute-start.99 = (bf16[72,2048]{1,0:T(8,128)(2,1)S(1)}, bf16[72,2048]{1,0:T(8,128)(2,1)S(1)}, u32[]{:S(2)}, u32[]{:S(2)}) collective-permute-start(bf16[72,2048]{1,0:T(8,128)(2,1)S(1)} %copy-done.85), channel_id=1, source_target_pairs={{0,3},{1,2},{2,1},{3,0},{4,7},{5,6},{6,5},{7,4},{8,11},{9,10},{10,... | collective-permute-start | bytes 884744 | tf_op jit(solution)/shard_map/ppermute | solution.py:585
  604.6 16.3 %collective-permute-start.104 = (bf16[768,1024]{1,0:T(8,128)(2,1)}, bf16[768,1024]{1,0:T(8,128)(2,1)}, u32[]{:S(2)}, u32[]{:S(2)}) collective-permute-start(bf16[768,1024]{1,0:T(8,128)(2,1)} %convolution_convert_fusion.1), channel_id=1, source_target_pairs={{0,16},{16,0},{1,17},{17,1},{2,18},{18,2},{3,19},{19,3},{4,20},{20... | collective-permute-start | bytes 4718600 | tf_op jit(solution)/shard_map/ppermute | solution.py:596
  604.6 16.3 %collective-permute-start.105 = (bf16[1024,512]{0,1:T(8,128)(2,1)}, bf16[1024,512]{0,1:T(8,128)(2,1)}, u32[]{:S(2)}, u32[]{:S(2)}) collective-permute-start(bf16[1024,512]{0,1:T(8,128)(2,1)} %convolution_convert_fusion.4), channel_id=1, source_target_pairs={{0,16},{16,0},{1,17},{17,1},{2,18},{18,2},{3,19},{19,3},{4,20},{20... | collective-permute-start | bytes 3145736 | tf_op jit(solution)/shard_map/ppermute | solution.py:596
  638.1 41.1 %collective-permute-start.108 = (bf16[128,2048]{1,0:T(8,128)(2,1)}, bf16[128,2048]{1,0:T(8,128)(2,1)}, u32[]{:S(2)}, u32[]{:S(2)}) collective-permute-start(bf16[128,2048]{1,0:T(8,128)(2,1)} %add_convert_fusion.2), channel_id=1, source_target_pairs={{0,0},{2,8},{4,16},{6,24},{1,1},{3,9},{5,17},{7,25},{8,2},{10,10},... | collective-permute-start | bytes 1572872 | tf_op jit(solution)/shard_map/ppermute | solution.py:862
  643.5 16.6 %collective-permute-start.109 = (bf16[256,640]{0,1:T(8,128)(2,1)}, bf16[256,640]{0,1:T(8,128)(2,1)}, u32[]{:S(2)}, u32[]{:S(2)}) collective-permute-start(bf16[256,640]{0,1:T(8,128)(2,1)} %pad_maximum_fusion.12), channel_id=1, source_target_pairs={{0,1},{1,0},{2,3},{3,2},{4,5},{5,4},{6,7},{7,6},{8,9},{9,8},{10,11... | collective-permute-start | bytes 983048 | tf_op jit(solution)/shard_map/ppermute | solution.py:585
  643.9 35.3 %collective-permute-start.110 = (bf16[256,640]{0,1:T(8,128)(2,1)}, bf16[256,640]{0,1:T(8,128)(2,1)}, u32[]{:S(2)}, u32[]{:S(2)}) collective-permute-start(bf16[256,640]{0,1:T(8,128)(2,1)} %add_convert_fusion.6), channel_id=1, source_target_pairs={{0,8},{1,9},{2,10},{3,11},{4,12},{5,13},{6,14},{7,15},{8,0},{9,1},... | collective-permute-start | bytes 983048 | tf_op jit(solution)/shard_map/ppermute | solution.py:585
  695.4 19.5 %collective-permute-start.118 = (bf16[128,2048]{1,0:T(8,128)(2,1)S(1)}, bf16[128,2048]{1,0:T(8,128)(2,1)S(1)}, u32[]{:S(2)}, u32[]{:S(2)}) collective-permute-start(bf16[128,2048]{1,0:T(8,128)(2,1)S(1)} %pad_maximum_fusion.7), channel_id=1, source_target_pairs={{0,2},{1,3},{2,0},{3,1},{4,6},{5,7},{6,4},{7,5},{8,10},{9,11},{10,... | collective-permute-start | bytes 1572872 | tf_op jit(solution)/shard_map/ppermute | solution.py:585
  696.6 19.1 %collective-permute-start.119 = (bf16[128,2048]{1,0:T(8,128)(2,1)S(1)}, bf16[128,2048]{1,0:T(8,128)(2,1)S(1)}, u32[]{:S(2)}, u32[]{:S(2)}) collective-permute-start(bf16[128,2048]{1,0:T(8,128)(2,1)S(1)} %pad_maximum_fusion.8), channel_id=1, source_target_pairs={{0,4},{1,5},{2,6},{3,7},{4,0},{5,1},{6,2},{7,3},{8,12},{9,13},{10,... | collective-permute-start | bytes 1572872 | tf_op jit(solution)/shard_map/ppermute | solution.py:585
  716.1 16.6 %collective-permute-start.122 = (bf16[64,1152]{0,1:T(8,128)(2,1)S(1)}, bf16[64,1152]{0,1:T(8,128)(2,1)S(1)}, u32[]{:S(2)}, u32[]{:S(2)}) collective-permute-start(bf16[64,1152]{0,1:T(8,128)(2,1)S(1)} %get-tuple-element.1168), channel_id=1, source_target_pairs={{0,6},{1,7},{2,4},{3,5},{4,2},{5,3},{6,0},{7,1},{8,14},{9,15},{10,... | collective-permute-start | bytes 442376 | tf_op jit(solution)/shard_map/ppermute | solution.py:585
  718.4 16.5 %collective-permute-start.124 = (bf16[64,1152]{0,1:T(8,128)(2,1)S(1)}, bf16[64,1152]{0,1:T(8,128)(2,1)S(1)}, u32[]{:S(2)}, u32[]{:S(2)}) collective-permute-start(bf16[64,1152]{0,1:T(8,128)(2,1)S(1)} %get-tuple-element.1170), channel_id=1, source_target_pairs={{0,4},{1,5},{2,6},{3,7},{4,0},{5,1},{6,2},{7,3},{8,12},{9,13},{10,... | collective-permute-start | bytes 442376 | tf_op jit(solution)/shard_map/ppermute | solution.py:585
  719.7 15.3 %collective-permute-start.120 = (bf16[256,384]{1,0:T(8,128)(2,1)S(1)}, bf16[256,384]{1,0:T(8,128)(2,1)S(1)}, u32[]{:S(2)}, u32[]{:S(2)}) collective-permute-start(bf16[256,384]{1,0:T(8,128)(2,1)S(1)} %pad_maximum_fusion.26), channel_id=1, source_target_pairs={{0,1},{1,0},{2,3},{3,2},{4,5},{5,4},{6,7},{7,6},{8,9},{9,8},{10,11... | collective-permute-start | bytes 589832 | tf_op jit(solution)/shard_map/ppermute | solution.py:585
  (303 other events, 2660.1 us)
Sparse Core Ops, SparseCore 0:
  21.9 12.4 all-gather.3
  190.4 10.1 all-gather.5
  260.6 11.4 all-gather.7

commit v4 on v3

--- a/solution.py
+++ b/solution.py
@@ -34,6 +34,21 @@
         jnp.concatenate([cosine, cosine], axis=-1),
         jnp.concatenate([-sine, sine], axis=-1),
     )
+
+
+def stack_kernel(rows, *refs):
+    *block_refs, out_ref = refs
+    blocks = [ref[...].astype(F32) for ref in block_refs]
+    stack = [block[:rows] for block in blocks] + [block[rows:] for block in blocks]
+    out_ref[...] = jnp.concatenate(stack, axis=0).astype(BF)
+
+
+def stack_rows(blocks, rows):
+    height, width = blocks[0].shape
+    return pl.pallas_call(
+        lambda *refs: stack_kernel(rows, *refs),
+        out_shape=jax.ShapeDtypeStruct((height * len(blocks), width), BF),
+    )(*blocks)
 
 
 def project_kernel(starts_ref, x_ref, cos_ref, sin_ref, gains_ref, *refs):
@@ -60,9 +75,9 @@
     turned_ref[:, HEAD_SIZE:] = jnp.where(last, second, turn(second, gain_q)).astype(BF)
 
 
-def project(starts, rows_in, cosine, sine, gains, *pieces):
+def project(rows, starts, rows_in, cosine, sine, gains, *pieces):
     count, width = rows_in.shape
-    height, columns = pieces[0].shape
+    height, columns = 4 * rows, pieces[0].shape[1]
     step = 2 * HEAD_SIZE
     whole = lambda array: pl.BlockSpec(array.shape, lambda i: (0, 0))
     strip = lambda height: pl.BlockSpec((height, step), lambda i: (0, i))
@@ -112,42 +127,80 @@
     )(grad, projected, cosine, sine, gain)
 
 
-def input_kernel(grad_ref, w_ref, hidden_ref, scale_ref, out_ref, gain_grad_ref):
+def input_kernel(grad_ref, w_ref, out_ref):
     dims = (((1,), (1,)), ((), ()))
-    out = lax.dot_general(grad_ref[...], w_ref[...], dims, preferred_element_type=F32)
-    out_ref[...] = out
-    gain_grad_ref[...] = jnp.sum(
-        out * hidden_ref[...].astype(F32) * scale_ref[...], axis=0, keepdims=True
-    )
-
-
-def input_gradient(proj_grad, weights, hidden, scale):
+    out_ref[...] = lax.dot_general(grad_ref[...], w_ref[...], dims, preferred_element_type=F32)
+
+
+def input_gradient(proj_grad, weights):
     count, columns = proj_grad.shape
     width = weights.shape[0]
     step = 256
-    whole = lambda array: pl.BlockSpec(array.shape, lambda i: (0, 0))
-    strip = lambda height: pl.BlockSpec((height, step), lambda i: (0, i))
     return pl.pallas_call(
         input_kernel,
         grid=(width // step,),
         in_specs=[
-            whole(proj_grad),
+            pl.BlockSpec((count, columns), lambda i: (0, 0)),
             pl.BlockSpec((step, columns), lambda i: (i, 0)),
-            strip(count),
-            whole(scale),
         ],
-        out_specs=[strip(count), strip(1)],
-        out_shape=[
-            jax.ShapeDtypeStruct((count, width), F32),
-            jax.ShapeDtypeStruct((1, width), F32),
-        ],
+        out_specs=pl.BlockSpec((count, step), lambda i: (0, i)),
+        out_shape=jax.ShapeDtypeStruct((count, width), F32),
         cost_estimate=pl.CostEstimate(
             flops=2 * count * width * columns,
             bytes_accessed=6 * (count + columns) * width,
             transcendentals=0,
         ),
         compiler_params=pltpu.CompilerParams(vmem_limit_bytes=24 * 2**20),
-    )(proj_grad, weights, hidden, scale)
+    )(proj_grad, weights)
+
+
+def output_kernel(order_ref, *refs):
+    *part_refs, own_ref, other_ref, out_ref, rows_ref, natural_ref = refs
+    half = own_ref.shape[0]
+
+    @pl.when(pl.program_id(0) == 0)
+    def _():
+        at = 0
+        for part_ref in part_refs:
+            width = part_ref.shape[1]
+            natural_ref[:, at : at + width] = part_ref[...]
+            at += width
+        for head in range(at // HEAD_SIZE):
+            start = pl.multiple_of(order_ref[head] * HEAD_SIZE, HEAD_SIZE)
+            here = slice(head * HEAD_SIZE, (head + 1) * HEAD_SIZE)
+            rows_ref[:, here] = natural_ref[:, pl.ds(start, HEAD_SIZE)]
+
+    out_ref[...] = jnp.dot(
+        rows_ref[:, :half], own_ref[...], preferred_element_type=F32
+    ) + jnp.dot(rows_ref[:, half:], other_ref[...], preferred_element_type=F32)
+
+
+def output_projection(order, parts, own, other):
+    count = parts[0].shape[0]
+    half, width = own.shape
+    columns = 2 * half
+    step = 256
+    strip = lambda height: pl.BlockSpec((height, step), lambda i: (0, i))
+    whole = lambda shape: pl.BlockSpec(shape, lambda i: (0, 0))
+    return pl.pallas_call(
+        output_kernel,
+        grid=(width // step,),
+        in_specs=[pl.BlockSpec(memory_space=pltpu.SMEM)]
+        + [whole(part.shape) for part in parts]
+        + [strip(half), strip(half)],
+        out_specs=[strip(count), whole((count, columns))],
+        out_shape=[
+            jax.ShapeDtypeStruct((count, width), F32),
+            jax.ShapeDtypeStruct((count, columns), BF),
+        ],
+        scratch_shapes=[pltpu.VMEM((count, columns), BF)],
+        cost_estimate=pl.CostEstimate(
+            flops=2 * count * width * columns,
+            bytes_accessed=4 * (count + columns) * width,
+            transcendentals=0,
+        ),
+        compiler_params=pltpu.CompilerParams(vmem_limit_bytes=24 * 2**20),
+    )(order, *parts, own, other)
 
 
 def forward_kernel(q_ref, kv_ref, vt_ref, place_ref, low_ref, high_ref, out_ref, p_ref):
@@ -327,21 +380,19 @@
 
 
 def expert_kernel(blocks, me_ref, *refs):
-    rows_refs, upstream_refs = refs[:blocks], refs[blocks : 2 * blocks]
-    refs = refs[2 * blocks :]
-    chooser_ref, router_ref, gate_ref, up_ref, down_ref = refs[:5]
-    back_refs, mixed_refs = refs[5 : 5 + blocks], refs[5 + blocks : 5 + 2 * blocks]
-    refs = refs[5 + 2 * blocks :]
+    rows_refs, refs = refs[:blocks], refs[blocks:]
+    upstream_ref, chooser_ref, router_ref, gate_ref, up_ref, down_ref = refs[:6]
+    back_refs, mixed_refs = refs[6 : 6 + blocks], refs[6 + blocks : 6 + 2 * blocks]
+    refs = refs[6 + 2 * blocks :]
     rows_ref, act_ref, out_grad_ref, gate_low_ref, up_low_ref = refs[:5]
-    upstream_ref, share_ref, returned_ref, pair_ref = refs[5:]
+    share_ref, returned_ref, pair_ref = refs[5:]
     step = pl.program_id(0)
     across = (((1,), (1,)), ((), ()))
 
     @pl.when(step == 0)
     def _():
-        whole = lambda parts: jnp.concatenate([ref[...].astype(F32) for ref in parts], axis=0)
-        rows_in = whole(rows_refs).astype(BF)
-        upstream = whole(upstream_refs)
+        rows_in = jnp.concatenate([ref[...].astype(F32) for ref in rows_refs], axis=0).astype(BF)
+        upstream = upstream_ref[...].astype(F32)
         logits = jnp.dot(rows_in, router_ref[...], preferred_element_type=F32)
         chosen = chooser_ref[...] > 0.0
         top = jnp.max(jnp.where(chosen, logits, MASKED), axis=1, keepdims=True)
@@ -351,7 +402,6 @@
         mine = jnp.sum(jnp.where(number == me_ref[0], exponent, 0.0), axis=1, keepdims=True)
         share = mine / jnp.where(total > 0.0, total, 1.0)
         rows_ref[...] = rows_in
-        upstream_ref[...] = upstream
         out_grad_ref[...] = (share * upstream).astype(BF)
         share_ref[...] = jnp.broadcast_to(share, share_ref.shape)
         returned_ref[...] = jnp.zeros_like(returned_ref)
@@ -376,7 +426,8 @@
     @pl.when(step == pl.num_programs(0) - 1)
     def _():
         returned = returned_ref[...].astype(BF).astype(F32)
-        gate_grad = jnp.sum(upstream_ref[...] * returned, axis=1, keepdims=True)
+        upstream = upstream_ref[...].astype(F32)
+        gate_grad = jnp.sum(upstream * returned, axis=1, keepdims=True)
         mixed = share_ref[:, :1] * returned
         pair = pair_ref[...]
         count = rows_refs[0].shape[0]
@@ -392,8 +443,8 @@
 
 def expert_rows(me, rows_in, upstream, chooser, router, gate, up, down):
     blocks = len(rows_in)
-    block = upstream[0].shape
-    slots, width = blocks * block[0], block[1]
+    slots, width = upstream.shape
+    block = (slots // blocks, width)
     ff = gate.shape[1]
     step = 256
     lanes = 128
@@ -410,13 +461,12 @@
         lambda *refs: expert_kernel(blocks, *refs),
         grid=(ff // step,),
         in_specs=[pl.BlockSpec(memory_space=pltpu.SMEM)]
-        + [whole(block)] * (2 * blocks)
-        + [whole(chooser.shape), whole(router.shape)]
+        + [whole(block)] * blocks
+        + [whole(upstream.shape), whole(chooser.shape), whole(router.shape)]
         + [columns(width), columns(width), pl.BlockSpec((step, width), lambda i: (i, 0))],
         out_specs=out_specs,
         out_shape=[shape(dims, kind) for dims, kind in out],
         scratch_shapes=[
-            pltpu.VMEM((slots, width), F32),
             pltpu.VMEM((slots, lanes), F32),
             pltpu.VMEM((slots, width), F32),
             pltpu.VMEM((slots, width), F32),
@@ -425,7 +475,7 @@
             flops=12 * slots * width * ff, bytes_accessed=6 * width * ff, transcendentals=0
         ),
         compiler_params=pltpu.CompilerParams(vmem_limit_bytes=44 * 2**20),
-    )(me, *rows_in, *upstream, chooser, router, gate, up, down)
+    )(me, *rows_in, upstream, chooser, router, gate, up, down)
 
 
 def table_kernel(capacity, ids_ref, pairs_ref, send_ref, back_ref, chosen_ref):
@@ -502,6 +552,8 @@
         self.asked = {}
         self.values = {}
         self.count = 0
+        self.strict = True
+        self.alone = False
 
     def start(self, task):
         self.count += 1
@@ -509,8 +561,12 @@
         return self.count
 
     def until(self, *wanted):
+        def waiting_now():
+            ready = [n for n in self.active if n in wanted] if self.alone else self.active
+            return [number for number in ready if number not in self.asked]
+
         while True:
-            while waiting := [number for number in self.active if number not in self.asked]:
+            while waiting := waiting_now():
                 for number in waiting:
                     task, came = self.active[number]
                     try:
@@ -520,22 +576,30 @@
                         del self.active[number]
             if all(number in self.values for number in wanted):
                 break
-            asked = self.asked
+            asked = {n: c for n, c in self.asked.items() if n in wanted or not self.alone}
             given = {number: [args for _, args in calls] for number, calls in asked.items()}
-            given = lax.optimization_barrier(given)
+            if self.strict:
+                given = lax.optimization_barrier(given)
             came = {
                 number: [call(*args) for (call, _), args in zip(calls, given[number])]
                 for number, calls in asked.items()
             }
-            came = lax.optimization_barrier(came)
+            if self.strict:
+                came = lax.optimization_barrier(came)
             for number, results in came.items():
                 self.active[number] = (self.active[number][0], results)
-            self.asked = {}
+            self.asked = {n: calls for n, calls in self.asked.items() if n not in asked}
         values = [self.values[number] for number in wanted]
         return values[0] if len(values) == 1 else values
 
     def run(self, task):
         return self.until(self.start(task))
+
+    def loosely(self, *wanted, alone=False):
+        self.strict, self.alone = False, alone
+        values = self.until(*wanted)
+        self.strict, self.alone = True, False
+        return values
 
 
 def hold(count, *values):
@@ -566,17 +630,22 @@
         self.square = n == 16
         if self.square:
             self.a = index % 2 + index // 8 * 2
-            self.b = index // 2 % 4
+            self.b = index // 2 % 2 * 2 + index // 4 % 2
         else:
             self.a, self.b = self.l, self.p
-        masks = (0, 2, 4, 6) if self.square else (0, 1, 2, 3)
+        masks = (0, 4, 2, 6) if self.square else (0, 1, 2, 3)
         self.places = [lambda v, k=k: self.flip(v, k) for k in range(4)]
         self.heads = [lambda v, m=m: self.flip(v, m) for m in masks]
         self.shifts = [lambda v, s=s: self.shift(v, s) for s in range(self.planes)]
         self.backs = [lambda v, s=s: self.shift(v, -s) for s in range(self.planes)]
 
     def device(self, a, b):
-        return a % 2 + b * 2 + a // 2 * 8 if self.square else a * 4 + b
+        if not self.square:
+            return a * 4 + b
+        return a % 2 + b // 2 * 2 + b % 2 * 4 + a // 2 * 8
+
+    def row_block(self, g, a):
+        return a % 2 + g * 2 + a // 2 * 4 if self.square else g * self.planes + a
 
     def block(self, r):
         return self.a ^ r if self.square else (self.a - r) % self.planes
@@ -630,21 +699,26 @@
         ]
         return cut(0, 0, count) + got_x.astype(F32) + got_y.astype(F32)
 
-    def block_gather(self, own, idle=(0, 0)):
+    def block_gather(self, own, idle=(0, 0), count=None, give=None):
         if not self.square:
             came = yield [(shift, (own,)) for shift in self.shifts[1:]]
             return [own] + came
         x, z = (lambda v: self.flip(v, 1)), (lambda v: self.flip(v, 8))
-        half = own.shape[0] // 2
+        count = count or own.shape[0]
+        half = count // 2 + own.shape[0] - count
         near, low = yield [(x, (own,)), (z, (own[:half],))]
         near, low = yield from hold(idle[0], near, low)
-        high, far_low = yield [(z, (own[half:],)), (x, (low,))]
+        rest = count - half
+        more = [own[half:]] if give is None else [own[half:], near[count:]]
+        high, far_low = yield [(z, (jnp.concatenate(more),)), (x, (low,))]
         high, far_low = yield from hold(idle[1], high, far_low)
-        (far_high,) = yield [(x, (high,))]
+        if give is not None:
+            give(jnp.concatenate([own[count:], near[count:], high[rest:]]))
+        (far_high,) = yield [(x, (high[:rest],))]
         return [
             own,
             near,
-            jnp.concatenate([low, high], axis=0),
+            jnp.concatenate([low, high[:rest]], axis=0),
             jnp.concatenate([far_low, far_high], axis=0),
         ]
 
@@ -667,19 +741,25 @@
         (came,) = yield [(x, (blocks[3].astype(BF),))]
         (came,) = yield from hold(idle, came)
         across = (blocks[2].astype(F32) + came.astype(F32)).astype(BF)
-        half = across.shape[0] // 2 if split else across.shape[0]
-        near, got = yield [(x, (blocks[1].astype(BF),)), (z, (across[:half],))]
         if split:
-            (more,) = yield [(z, (across[half:],))]
+            half = across.shape[0] // 2
+            (got,) = yield [(z, (across[:half],))]
+            near, more = yield [(x, (blocks[1].astype(BF),)), (z, (across[half:],))]
             got = jnp.concatenate([got, more], axis=0)
+        else:
+            near, got = yield [(x, (blocks[1].astype(BF),)), (z, (across,))]
         return blocks[0].astype(F32) + near.astype(F32) + got.astype(F32)
 
-    def twin_scatter(self, make, own, other, idle=None):
+    def twin_scatter(self, make, own, other, idle=None, now=False):
         low = lambda *args: make(*args).astype(BF)
-        (block,) = yield [(low, other)]
+        if now:
+            block = low(*other)
+        else:
+            (block,) = yield [(low, other)]
+        if idle is None:
+            came, total = yield [(self.twin, (block,)), (make, own)]
+            return total + came.astype(F32)
         (came,) = yield [(self.twin, (block,))]
-        if idle is None:
-            return make(*own) + came.astype(F32)
         (came,) = yield from hold(idle, came)
         (total,) = yield [(lambda came, *args: make(*args) + came.astype(F32), (came, *own))]
         return total
@@ -736,59 +816,9 @@
     ids = jnp.stack([links.l, links.p]).astype(jnp.int32)
     tables = {}
 
-    def gather_small():
-        piece = jnp.concatenate([small, pairs], axis=0)
-        blocks = yield from links.exchange(links.places, [piece] * 4)
-        line = jnp.stack(blocks)
-        if links.square:
-            low, high = (lambda v: links.flip(v, 4)), (lambda v: links.flip(v, 8))
-            (near,) = yield [(low, (line,))]
-            line = jnp.stack([line, near])
-            (across,) = yield [(high, (line,))]
-            line = jnp.stack([line[0], line[1], across[0], across[1]])
-        else:
-            came = yield [(shift, (line,)) for shift in links.shifts[1:]]
-            line = jnp.stack([line] + came)
-            yield from hold(1)
-        own_small = line[:, :, :small_rows]
-        (other_small,) = yield [(links.twin, (own_small,))]
-        return (yield from work(sort_small, line, other_small, rounds.values[hidden_task]))
-
-    def sort_small(line, other_small, block_hidden):
-        if links.square:
-            line = jnp.stack(links.natural([line[r] for r in range(4)], links.l))
-            other_small = jnp.stack(links.natural([other_small[r] for r in range(4)], links.l))
-        else:
-            line, other_small = links.turned_line(line), links.turned_line(other_small)
-        all_pairs = links.turned_line(line[:, :, small_rows:]).astype(F32)
-        all_pairs = all_pairs.reshape(planes, 4, 3, TOP, tokens)
-        found = slot_tables(ids, all_pairs, capacity, experts)
-        tables["send"], tables["back"], tables["chooser"] = found
-        line = jnp.stack([line[:, :, :small_rows], other_small], axis=2)
-        line = jnp.stack(links.natural([line[:, k] for k in range(4)], links.p), axis=1)
-        line = line.reshape(experts, 2, small_rows, lanes)
-        first, second = line[:, 0], line[:, 1]
-        swap = links.g == 1
-        small_all = jnp.concatenate(
-            [jnp.where(swap, second, first), jnp.where(swap, first, second)], axis=0
-        )
-        gains = small_all[:, router_rows:].reshape(devices, -1)
-        head_gains = gains[:, 2 * rows : gain_count].reshape(devices, 2, head_part)
-        values = block_hidden.astype(F32)
-        scale = lax.rsqrt(jnp.mean(values * values, axis=-1, keepdims=True) + EPS)
-        full_in = gains[:, :rows].reshape(MODEL_WIDTH).astype(F32)
-        return (
-            (values * scale * full_in).astype(BF),
-            scale,
-            small_all[:, :router_rows].reshape(MODEL_WIDTH, experts),
-            full_in,
-            gains[:, rows : 2 * rows].reshape(MODEL_WIDTH).astype(F32),
-            head_gains.swapaxes(0, 1).reshape(2, HEAD_SIZE).astype(F32),
-        )
-
-    small_task = spread(gather_small())
-
     qkv_width = QW + 2 * HEAD_SIZE
+    rider = jnp.concatenate([small, pairs], axis=0)
+    rider_rows = rider.shape[0]
 
     def own_columns(b):
         cut = lambda array, width: lax.dynamic_slice_in_dim(array, b * width, width, 1)
@@ -803,13 +833,79 @@
 
     def gather_qkv():
         blocks = [own_columns(links.b ^ k) for k in range(4)]
+        if not links.square:
+            blocks = yield from links.exchange(links.heads, blocks)
+            pieces = yield from links.block_gather(jnp.concatenate(blocks, axis=0))
+            others = yield [(links.twin, (piece,)) for piece in pieces]
+            return pieces + others
+        more = rider.reshape(-1, qkv_width)
+        held = more.shape[0]
+        more = jnp.pad(more, ((0, -held % 8), (0, 0)))
+        blocks = [jnp.concatenate([block, more], axis=0) for block in blocks]
         blocks = yield from links.exchange(links.heads, blocks)
-        pieces = yield from links.block_gather(jnp.concatenate(blocks, axis=0))
+        wide = stack_rows(blocks, rows)
+
+        def give(found):
+            found = found.reshape(4, 4, -1, qkv_width)[:, :, :held]
+            tables["riders"] = found.reshape(4, 4, rider_rows, lanes)
+
+        pieces = yield from links.block_gather(wide, count=4 * rows, give=give)
         others = yield [(links.twin, (piece,)) for piece in pieces]
         return pieces + others
 
+    def gather_small():
+        if links.square:
+            yield from hold(3)
+            parts = tables["riders"]
+            parts = jnp.stack(links.natural([parts[r] for r in range(4)], links.a))
+            parts = jnp.stack(links.natural([parts[:, k] for k in range(4)], links.b), axis=1)
+            parts = parts.reshape(2, 2, 2, 2, rider_rows, lanes).transpose(0, 3, 2, 1, 4, 5)
+            parts = parts.reshape(experts, rider_rows, lanes)
+        else:
+            blocks = yield from links.exchange(links.places, [rider] * 4)
+            line = jnp.stack(links.natural(blocks, links.p))
+            came = yield [(shift, (line,)) for shift in links.shifts[1:]]
+            parts = links.turned_line(jnp.stack([line] + came))
+            parts = parts.reshape(experts, rider_rows, lanes)
+            yield from hold(1)
+        own_small = parts[:, :small_rows]
+        (other_small,) = yield [(links.twin, (own_small,))]
+        tables["pairs"] = parts[:, small_rows:]
+        return (yield from work(sort_small, own_small, other_small, rounds.values[hidden_task]))
+
+    def sort_small(own_small, other_small, block_hidden):
+        swap = links.g == 1
+        small_all = jnp.concatenate(
+            [jnp.where(swap, other_small, own_small), jnp.where(swap, own_small, other_small)]
+        )
+        gains = small_all[:, router_rows:].reshape(devices, -1)
+        head_gains = gains[:, 2 * rows : gain_count].reshape(devices, 2, head_part)
+        values = block_hidden.astype(F32)
+        scale = lax.rsqrt(jnp.mean(values * values, axis=-1, keepdims=True) + EPS)
+        full_in = gains[:, :rows].reshape(MODEL_WIDTH).astype(F32)
+        return (
+            (values * scale * full_in).astype(BF),
+            small_all[:, :router_rows].reshape(MODEL_WIDTH, experts),
+            full_in,
+            gains[:, rows : 2 * rows].reshape(MODEL_WIDTH).astype(F32),
+            head_gains.swapaxes(0, 1).reshape(2, HEAD_SIZE).astype(F32),
+        )
+
+    def make_tables(pairs):
+        pairs = pairs.astype(F32).reshape(planes, 4, 3, TOP, tokens)
+        pairs = links.turned_line(pairs)
+        near = [lax.dynamic_index_in_dim(pairs, links.p ^ k, 1, keepdims=False) for k in range(4)]
+        return slot_tables(ids, jnp.stack(near, axis=1), capacity, experts)
+
+    exchange_task = spread(hold(1))
     qkv_task = spread(gather_qkv())
-    hidden_task = spread(later(1, links.head_gather(hidden)))
+
+    def gather_hidden():
+        (value,) = yield from hold(1, hidden)
+        return (yield from links.head_gather(value))
+
+    hidden_task = spread(gather_hidden())
+    small_task = spread(gather_small())
 
     aligned = capacity % 8 == 0
 
@@ -834,7 +930,10 @@
 
     def gather_upstream():
         pieces, out = [cotangent], []
-        plan = [(8, True, 0)] + [(0, s < planes - 1, s) for s in range(1, planes)]
+        yield from hold(2)
+        found = yield from work(make_tables, tables["pairs"])
+        tables["send"], tables["back"], tables["chooser"] = found
+        plan = [(1, True, 0)] + [(0, s < planes - 1, s) for s in range(1, planes)]
         for idle, hop, step in plan:
             yield from hold(idle)
             asks = [(links.onward, (pieces[-1],))] if hop else []
@@ -845,31 +944,44 @@
             if hop:
                 pieces.append(came[0])
             if step is not None:
-                out.append(in_places(blocks[0], came[-3:]))
+                out.append(jnp.concatenate([blocks[0]] + came[-3:], axis=0))
         return out
 
     upstream_task = spread(gather_upstream())
 
     head_rows = w_out.shape[0]
-    to_block = [
-        ((b * 2 + g) * planes + a, g * experts + links.device(a, b))
-        for g in range(2)
-        for a in range(planes)
-        for b in range(4)
-    ]
-    from_block = [(there, here) for here, there in to_block]
-    to_blocks = lambda value: lax.ppermute(value, ("dp", "expert"), to_block)
-    from_blocks = lambda value: lax.ppermute(value, ("dp", "expert"), from_block)
+    if links.square:
+        pairs_of = [(g, i) for g in range(2) for i in range(experts)]
+        line = lambda i: i & 3 | (i >> 3 & 1) << 2 | (i >> 2 & 1) << 3
+        swap_line = [(g * experts + i, g * experts + line(i)) for g, i in pairs_of]
+        swap_core = [
+            (g * experts + i, (i >> 1 & 1) * experts + (i & 13 | g << 1)) for g, i in pairs_of
+        ]
+        there = back = (swap_line, swap_core)
+    else:
+        to_block = [
+            (b * 2 * planes + links.row_block(g, a), g * experts + links.device(a, b))
+            for g in range(2)
+            for a in range(planes)
+            for b in range(4)
+        ]
+        there = (to_block, None)
+        back = ([(to, of) for of, to in to_block], None)
+
+    def moved(value, pairs_of):
+        return value if pairs_of is None else lax.ppermute(value, ("dp", "expert"), pairs_of)
 
     def gather_out():
-        (own,) = yield [(to_blocks, (w_out,))]
-        (own,) = yield from hold(1, own)
-        pieces = yield from links.block_gather(own, (1, 0))
+        pieces = yield from links.block_gather(rounds.values[move_task], (1, 0))
         pieces = jnp.concatenate(pieces, axis=0)
         (others,) = yield [(links.twin, (pieces,))]
-        return jnp.concatenate([pieces, others], axis=0)
-
-    out_task = spread(later(3, gather_out()))
+        return pieces, others
+
+    def move_out():
+        value = yield from work(lambda value: moved(value, there[0]), w_out)
+        return (yield from work(lambda value: moved(value, there[1]), value))
+
+    move_task = spread(move_out())
 
     device_of = jnp.stack(
         [links.device(links.block(r), links.b ^ k) for r in range(planes) for k in range(4)]
@@ -881,10 +993,22 @@
     high = all_slots[:block_tokens]
     low = high - position
 
-    found, block_hidden, qkv_pieces = rounds.until(small_task, hidden_task, qkv_task)
-    normalized, block_scale, full_router, full_in, full_mid, head_gains = found
+    rounds.until(exchange_task)
+    found, block_hidden, qkv_pieces, _ = rounds.loosely(
+        small_task, hidden_task, qkv_task, move_task, alone=True
+    )
+    out_task = spread(gather_out())
+    normalized, full_router, full_in, full_mid, head_gains = found
     w_qkv, projected, turned = rounds.run(
-        work(project, starts, normalized, cosine, sine, head_gains, *qkv_pieces)
+        work(
+            lambda *args: project(rows, *args),
+            starts,
+            normalized,
+            cosine,
+            sine,
+            head_gains,
+            *qkv_pieces,
+        )
     )
     keys_values = jnp.concatenate(
         rounds.run(links.block_gather_short(turned[:, QW:])), axis=0
@@ -901,25 +1025,32 @@
     def forward_part(query_rows):
         return attention_forward(query_rows, keys_values, values_turned, place_column, low, high)
 
+    bounds = [0, PER_KV // 2, PER_KV]
     attended = [
-        rounds.run(work(forward_part, part_of(turned[:, :QW], part, 4)))
-        for part in range(4)
+        rounds.run(work(forward_part, turned[:, low_head * HEAD_SIZE : high_head * HEAD_SIZE]))
+        for low_head, high_head in zip(bounds, bounds[1:])
     ]
-    attended = jnp.concatenate(attended, axis=1)
-    attended = jnp.concatenate(
-        [
+    block_out = rounds.until(out_task)
+    if head_rows == HEAD_SIZE:
+        order_of = [
+            links.row_block(links.g ^ t, links.block(r)) for t in range(2) for r in range(planes)
+        ]
+        order_of = jnp.stack(order_of).astype(jnp.int32)
+    else:
+        attended = jnp.concatenate(attended, axis=1)
+        attended = [
             lax.dynamic_slice_in_dim(
-                attended, ((links.g ^ t) * planes + links.block(r)) * head_rows, head_rows, 1
+                attended, links.row_block(links.g ^ t, links.block(r)) * head_rows, head_rows, 1
             )
             for t in range(2)
             for r in range(planes)
-        ],
-        axis=1,
-    )
-    block_out = rounds.until(out_task)
-
-    branch = jnp.dot(attended, block_out, preferred_element_type=F32)
-    branch = rounds.run(links.head_scatter(branch))
+        ]
+        attended = [jnp.concatenate(attended, axis=1)]
+        order_of = jnp.arange(PER_KV, dtype=jnp.int32)
+    branch, attended = rounds.run(
+        work(lambda *parts: output_projection(order_of, parts, *block_out), *attended)
+    )
+    branch = rounds.loosely(spread(links.head_scatter(branch)))
     x_float = hidden.astype(F32)
     x_one = x_float + branch
     norm_two, norm_two_back = jax.vjp(rms_scale, x_one, full_mid)
@@ -941,7 +1072,7 @@
         found = expert_rows(
             me,
             as_blocks(list(rows_in)),
-            as_blocks(upstream_slots[step]),
+            upstream_slots[step],
             tables["chooser"][step],
             full_router,
             gate_full,
@@ -953,22 +1084,20 @@
         return (by_place(found[0]), by_place(found[1]), found[2:])
 
     def return_mixture():
-        blocks = made[1][1]
-        back = yield to_places(blocks)
-        total = collect(in_places(blocks[0], back), 1, MODEL_WIDTH)
+        def add(step, came, back, kind=BF):
+            blocks = in_places(made[step][1][0], back)
+            return collect(blocks, step, MODEL_WIDTH, came, kind)
+
+        back = yield to_places(made[1][1])
+        total = add(1, None, back)
         yield from hold(2)
-        (came,) = yield [(links.onward, (total,))]
-        blocks = made[2][1]
-        back = yield to_places(blocks)
-        total = collect(in_places(blocks[0], back), 2, MODEL_WIDTH, came)
+        came, *back = yield [(links.onward, (total,))] + to_places(made[2][1])
+        total = add(2, came, back)
         for step in range(3, planes):
-            blocks = made[step][1]
-            came, *back = yield [(links.onward, (total,))] + to_places(blocks)
-            total = collect(in_places(blocks[0], back), step, MODEL_WIDTH, came)
-        (came,) = yield [(links.onward, (total,))]
-        blocks = made[0][1]
-        back = yield to_places(blocks)
-        return collect(in_places(blocks[0], back), 0, MODEL_WIDTH, came, F32)
+            came, *back = yield [(links.onward, (total,))] + to_places(made[step][1])
+            total = add(step, came, back)
+        came, *back = yield [(links.onward, (total,))] + to_places(made[0][1])
+        return add(0, came, back, F32)
 
     def experts_there_and_back():
         piece, ready, own_plane, total = xn_two, None, None, None
@@ -1025,7 +1154,7 @@
             by_rows,
             (half_of(rows_in, links.g), grads_in),
             (half_of(rows_in, 1 - links.g), grads_in),
-            idle=8,
+            idle=5,
         )
 
     def down_gradient():
@@ -1034,12 +1163,12 @@
             by_rows,
             (rows_in, half_of(grads_in, links.g)),
             (rows_in, half_of(grads_in, 1 - links.g)),
-            idle=3,
+            idle=2,
         )
 
     gate_task = spread(gate_up_gradient(3))
     up_task = spread(later(1, gate_up_gradient(4)))
-    down_task = spread(later(7, down_gradient()))
+    down_task = spread(later(5, down_gradient()))
     own_logits = jnp.dot(xn_two, full_router, preferred_element_type=F32)
     own_probs = masked_softmax(own_logits, own_chooser)
 
@@ -1053,21 +1182,23 @@
     x_one_grad = upstream + x_one_norm_grad
     branch_grad = x_one_grad.astype(BF)
 
-    block_grad = rounds.run(links.head_gather(branch_grad))
-
-    def head_gradients(block_grad, block_out):
-        grad = jnp.einsum("td,hd->th", block_grad, block_out, preferred_element_type=F32)
-        grad = grad.astype(BF)
+    block_grad = rounds.loosely(spread(links.head_gather(branch_grad)))
+
+    def head_gradients(block_grad):
+        grad = [
+            jnp.einsum("td,hd->th", block_grad, part, preferred_element_type=F32).astype(BF)
+            for part in block_out
+        ]
+        grad = jnp.concatenate(grad, axis=1)
         parts = []
+        where = {links.row_block(g, a): (g, a) for g in range(2) for a in range(planes)}
         for head in range(2 * planes):
-            twin, place = links.g ^ (head // planes), links.block(head % planes)
-            if links.square:
-                place = links.a ^ (head % planes)
-            at = (twin * planes + place) * head_rows
+            g, a = where[head]
+            at = ((links.g ^ g) * planes + links.block(a)) * head_rows
             parts.append(lax.dynamic_slice_in_dim(grad, at, head_rows, 1))
         return jnp.concatenate(parts, axis=1)
 
-    heads_task = spread(work(head_gradients, block_grad, block_out))
+    heads_task = spread(work(head_gradients, block_grad))
 
     def scatter_out():
         half = QW // 2
@@ -1077,12 +1208,15 @@
             ),
             (attended[:, :half], block_grad),
             (attended[:, half:], block_grad),
+            now=True,
         )
         grad = grad.astype(BF)
         blocks = [grad[r * head_rows : (r + 1) * head_rows] for r in range(planes)]
         grad = yield from links.block_scatter(blocks, split=True)
         (grad,) = yield from hold(2, grad.astype(BF))
-        grad = yield from work(from_blocks, grad)
+        grad = yield from work(lambda value: moved(value, back[1]), grad)
+        (grad,) = yield from hold(1, grad)
+        grad = yield from work(lambda value: moved(value, back[0]), grad)
         return grad.astype(F32)
 
     grad_out_task = spread(scatter_out())
@@ -1098,7 +1232,7 @@
     def half_rows(array, which):
         return lax.dynamic_slice_in_dim(array, which * (MODEL_WIDTH // 2), MODEL_WIDTH // 2, 0)
 
-    def query_gradient(grads_in, extra, idle):
+    def query_gradient(grads_in, extra):
         def make(which):
             grad = by_rows(half_of(normalized, which), grads_in)
             if extra is not None:
@@ -1106,8 +1240,7 @@
             return grad
 
         grad = yield from links.twin_scatter(make, (links.g,), (1 - links.g,))
-        blocks = yield from hold(idle[0], *owners_blocks(grad.astype(BF)))
-        grad = yield from links.block_scatter(blocks, idle=idle[1])
+        grad = yield from links.block_scatter(owners_blocks(grad.astype(BF)))
         return grad.astype(BF)
 
     def exchange_owners(grad):
@@ -1115,30 +1248,29 @@
         return links.exchange(links.heads, [grad[k] for k in range(4)])
 
     def key_value_gradient(key_value_grad, proj_grad):
-        half = lambda which: by_rows(half_of(normalized, which), key_value_grad)
-        found, other, own = yield [
-            (input_gradient, (proj_grad, w_qkv, block_hidden, block_scale)),
-            (half, (1 - links.g,)),
-            (half, (links.g,)),
+        sums = jnp.concatenate([grad_qgain, grad_kgain]).reshape(2, devices, head_part)
+        sums = jnp.pad(sums, ((0, 0), (0, 0), (0, rows - head_part))).reshape(2, MODEL_WIDTH).T
+        sums = jnp.pad(sums, ((0, 0), (0, lanes - sums.shape[1])))
+
+        def half(which):
+            grad = by_rows(half_of(normalized, which), key_value_grad)
+            return jnp.concatenate([grad, half_rows(sums, which)], axis=1)
+
+        came, xn_one_grad = yield [
+            (links.twin, (half(1 - links.g).astype(BF),)),
+            (input_gradient, (proj_grad, w_qkv)),
         ]
-        xn_one_grad, grad_in = found
         tables["scatter"] = spread(links.head_scatter(xn_one_grad))
-        sums = jnp.concatenate([grad_qgain, grad_kgain]).reshape(2, devices, head_part)
-        sums = jnp.pad(sums, ((0, 0), (0, 0), (0, rows - head_part)))
-        sums = jnp.concatenate([grad_in, sums.reshape(2, MODEL_WIDTH)], axis=0).T
-        sums = jnp.pad(sums, ((0, 0), (0, lanes - sums.shape[1])))
-        both = lambda grad, which: jnp.concatenate([grad, half_rows(sums, which)], axis=1)
-        (came,) = yield [(links.twin, (both(other, 1 - links.g).astype(BF),))]
-        grad = (both(own, links.g) + came.astype(F32)).astype(BF)
+        grad = (half(links.g) + came.astype(F32)).astype(BF)
         grad = yield from links.block_scatter(owners_blocks(grad))
-        return (yield from exchange_owners(grad.astype(BF)))
+        return grad.astype(BF)
 
     attended_grad = rounds.until(heads_task)
     grad_router = jnp.dot(xn_two.T, logit_grad, preferred_element_type=F32)
     first = jnp.concatenate([grad_router, grad_mid[:, None]], axis=1)
     first = jnp.pad(first, ((0, 0), (0, lanes - first.shape[1])))
     query_low_grads, query_tasks, key_terms, grad_qgain = [], [], None, None
-    parts = 4
+    parts = 2
     for part in range(parts):
         got = rounds.run(
             work(
@@ -1161,10 +1293,7 @@
         query_low_grads.append(got[0])
         key_terms = got[1] if part == 0 else key_terms + got[1]
         grad_qgain = got[2] if part == 0 else grad_qgain + got[2]
-        if part % 2:
-            low_grads = jnp.concatenate(query_low_grads[-2:], axis=1)
-            more, idle = (None, (1, 0)) if query_tasks else (first, (0, 1))
-            query_tasks.append(spread(query_gradient(low_grads, more, idle)))
+        query_tasks.append(spread(query_gradient(got[0], None if part else first)))
     key_terms = rounds.run(
         links.block_scatter(
             [key_terms[r * block_tokens : (r + 1) * block_tokens] for r in range(planes)]
@@ -1181,41 +1310,36 @@
     key_value_grad = jnp.concatenate([key_proj_grad, key_terms[:, HEAD_SIZE:].astype(BF)], axis=1)
     proj_grad = jnp.concatenate(query_low_grads + [key_value_grad], axis=1)
     key_value_task = spread(key_value_gradient(key_value_grad, proj_grad))
-    one, two = rounds.until(*query_tasks)
-    query_task = spread(exchange_owners(jnp.concatenate([one, two], axis=1)))
+    one, two, three = rounds.until(*query_tasks, key_value_task)
     xn_one_grad = rounds.until(tables["scatter"])
+    query_task = spread(exchange_owners(jnp.concatenate([one, two, three], axis=1)))
     _, norm_one_back = jax.vjp(lambda values: rms_scale(values, full_in), x_float)
     (x_norm_grad,) = norm_one_back(xn_one_grad)
     input_grad = (x_one_grad + x_norm_grad).astype(BF)
 
-    grad_gate, grad_up, grad_down, mixture, grad_out, grad_query, grad_kv = rounds.until(
-        gate_task,
-        up_task,
-        down_task,
-        tables["mixture"],
-        grad_out_task,
-        query_task,
-        key_value_task,
+    grad_gate, grad_up, grad_down, mixture, grad_out, owned = rounds.until(
+        gate_task, up_task, down_task, tables["mixture"], grad_out_task, query_task
     )
     result = (x_one + mixture).astype(BF)
     half = QW // 2
-    first = sum(block[:, half : half + lanes].astype(F32) for block in grad_query)
-    last = sum(block[:, 2 * HEAD_SIZE :].astype(F32) for block in grad_kv)
-
-    def whole(blocks):
-        return jnp.concatenate(links.natural(blocks, links.b), axis=1).astype(F32)
-
-    grad_query = whole(
-        [
-            jnp.concatenate([block[:, :half], block[:, half + lanes :]], axis=1)
-            for block in grad_query
-        ]
-    )
-    grad_key = whole([block[:, :HEAD_SIZE] for block in grad_kv])
-    grad_value = whole([block[:, HEAD_SIZE : 2 * HEAD_SIZE] for block in grad_kv])
+    at = QW + lanes
+    first = sum(block[:, half : half + lanes].astype(F32) for block in owned)
+    last = sum(block[:, at + 2 * HEAD_SIZE :].astype(F32) for block in owned)
+    owned = [block.astype(F32) for block in links.natural(owned, links.b)]
+    grad_query = jnp.concatenate(
+        [part for block in owned for part in (block[:, :half], block[:, half + lanes : at])], axis=1
+    )
+    grad_key = jnp.concatenate([block[:, at : at + HEAD_SIZE] for block in owned], axis=1)
+    grad_value = jnp.concatenate(
+        [block[:, at + HEAD_SIZE : at + 2 * HEAD_SIZE] for block in owned], axis=1
+    )
     grad_router, grad_mid = first[:, :experts], first[:, experts]
-    grad_in = last[:, 0]
-    grad_qgain, grad_kgain = last[:head_part, 1], last[:head_part, 2]
+    grad_qgain, grad_kgain = last[:head_part, 0], last[:head_part, 1]
+    grad_in = (
+        jnp.sum(w_query.astype(F32) * grad_query, axis=1)
+        + jnp.sum(key_projection_weight.astype(F32) * grad_key, axis=1)
+        + jnp.sum(value_projection_weight.astype(F32) * grad_value, axis=1)
+    ) / gain_in.astype(F32)
 
     return (
         result,

time: 763 us -> 697 us (0.913)
  starting transfers between devices: 159 us -> 130 us
  local copies, waits for them, and re-layouts: 131 us -> 111 us
  matrix products: 56.6 us -> 43.2 us
    ppermute x101 -> x93, starting transfers between devices: 128 us -> 109 us  [flip(): return lax.ppermute(value, 'expert', [(i, i ^ mask) for i in range(self.n)])]
    unnamed x527 -> x389, local copies, waits for them, and re-layouts: 72.4 us -> 59.2 us
    ppermute x13, starting transfers between devices: 12.4 us -> 1.59 us  [twin(): return lax.ppermute(value, 'dp', [(0, 1), (1, 0)])]
    ppermute x12, waiting for transfers between devices: 10.6 us -> 0.03 us  [shift(): lax.ppermute(value, 'expert', [(i, (i + step * 4) % self.n) for i in rang...]
    ppermute x101 -> x93, waiting for transfers between devices: 177 us -> 187 us  [flip(): return lax.ppermute(value, 'expert', [(i, i ^ mask) for i in range(self.n)])]
    pallas_call x4 -> x2, Pallas kernels: 40 us -> 39.1 us  [attention_backward(): pl.pallas_call(backward_kernel, grid=(columns // HEAD_SIZE, rows // step)...]
    pallas_call x4 -> x2, Pallas kernels: 19.1 us -> 19.1 us  [attention_forward(): pl.pallas_call(forward_kernel, grid=(columns // HEAD_SIZE, rows // step),...]
  transfers between devices with their start and end apart: 131 -> 125, of which waited for: 54 -> 45; matrix products, arithmetic and copies ran while one was open for 21% -> 19% of each run, Pallas kernels for 18% -> 21%
where the time goes in v4:
time: 697 us; the launch traced here: 687 us
  waiting for transfers between devices  187 us (27%)
  Pallas kernels  150 us (22%)
  starting transfers between devices  130 us (19%)
  local copies, waits for them, and re-layouts  111 us (16%)
  other arithmetic  47.5 us (7%)
  matrix products  43.2 us (6%)
  between operations  17.6 us (3%)
    ppermute x93, waiting for transfers between devices, flip(): return lax.ppermute(value, 'expert', [(i, i ^ mask) for i in range(self.n)])  187 us
    ppermute x93, starting transfers between devices, flip(): return lax.ppermute(value, 'expert', [(i, i ^ mask) for i in range(self.n)])  109 us
    unnamed x389, local copies, waits for them, and re-layouts  59.2 us
    pallas_call x4, Pallas kernels, expert_rows(): pl.pallas_call(lambda *refs: expert_kernel(blocks, *refs), grid=(ff // st...  44.2 us
    pallas_call x2, Pallas kernels, attention_backward(): pl.pallas_call(backward_kernel, grid=(columns // HEAD_SIZE, rows // step)...  39.1 us
    dot_general x12, matrix products, by_rows(): jnp.einsum('rd,rf->df', rows_in, grads_in, preferred_element_type=F32)  33.6 us
    pallas_call x2, Pallas kernels, attention_forward(): pl.pallas_call(forward_kernel, grid=(columns // HEAD_SIZE, rows // step),...  19.1 us
    ppermute x12, starting transfers between devices, shift(): lax.ppermute(value, 'expert', [(i, (i + step * 4) % self.n) for i in rang...  15.1 us
  transfers between devices with their start and end apart: 125, of which 45 were waited for; matrix products, arithmetic and copies ran while one was open for 19% of the time, Pallas kernels for 21%

profile of v4, /device:TPU:0, one launch (start us, length us, event | category | flops | bytes accessed | tf_op | source)
XLA Modules:
  0.0 686.8 jit_solution(15752935562150029736)
XLA Ops:
  13.7 6.1 collective-permute-start
  28.1 2.8 collective-permute-start.7
  44.2 10.7 %collective-permute-done.12 = bf16[160,1280]{1,0:T(8,128)(2,1)} collective-permute-done((bf16[160,1280]{1,0:T(8,128)(2,1)}, bf16[160,1280]{1,0:T(8,128)(2,1)}, u32[]{:S(2)}, u32[]{:S(2)}) %collective-permute-start.12) | collective-permute-done | bytes 409632 | tf_op jit(solution)/shard_map/ppermute | solution.py:654
  64.0 3.0 collective-permute-start.5
  67.1 4.7 collective-permute-done.10
  73.2 12.0 %collective-permute-done.5 = bf16[160,1280]{1,0:T(8,128)(2,1)S(1)} collective-permute-done((bf16[160,1280]{1,0:T(8,128)(2,1)S(1)}, bf16[160,1280]{1,0:T(8,128)(2,1)S(1)}, u32[]{:S(2)}, u32[]{:S(2)}) %collective-permute-start.5) | collective-permute-done | bytes 409632 | tf_op jit(solution)/shard_map/ppermute | solution.py:654
  90.7 5.0 collective-permute-done.14
  101.9 11.4 %shard_map.282 = (bf16[2048,1280]{1,0:T(8,128)(2,1)}, f32[512,1280]{1,0:T(8,128)}, bf16[512,1280]{1,0:T(8,128)(2,1)}) custom-call(s32[32]{0:T(128)} %add_multiply_fusion.1.starts_ref, bf16[512,2048]{1,0:T(8,128)(2,1)} %fusion.2.x_ref, f32[512,128]{1,0:T(8,128)} %get-tuple-element.493.cos_ref, f32[512,128]{1,0:T(8,128)} %get-tuple-element.494.sin_ref, ...), custom_call_target="tpu_custom_call" | custom-call | flops 2684354560 | bytes 7340032 | tf_op jit(solution)/shard_map/pallas_call | solution.py:84
  113.3 2.5 collective-permute-done.20
  116.8 2.6 copy.109
  122.9 3.7 shard_map.283
  128.7 7.4 %collective-permute-done.22 = bf16[512,256]{0,1:T(8,128)(2,1)} collective-permute-done((bf16[512,256]{0,1:T(8,128)(2,1)S(1)}, bf16[512,256]{0,1:T(8,128)(2,1)}, u32[]{:S(2)}, u32[]{:S(2)}) %collective-permute-start.22) | collective-permute-done | bytes 262176 | tf_op jit(solution)/shard_map/ppermute | solution.py:654
  141.7 8.3 %collective-permute-done.23 = bf16[64,2048]{1,0:T(8,128)(2,1)S(1)} collective-permute-done((bf16[64,2048]{1,0:T(8,128)(2,1)}, bf16[64,2048]{1,0:T(8,128)(2,1)S(1)}, u32[]{:S(2)}, u32[]{:S(2)}) %collective-permute-start.23) | collective-permute-done | bytes 262176 | tf_op jit(solution)/shard_map/ppermute | solution.py:654
  162.2 9.5 %shard_map.285.refs_0_ = bf16[512,512]{1,0:T(8,128)(2,1)S(1)} custom-call(bf16[512,512]{1,0:T(8,128)(2,1)S(1)} %copy-done.18, bf16[2048,256]{1,0:T(8,128)(2,1)S(1)} %copy.110.kv_ref, bf16[128,2048]{1,0:T(8,128)(2,1)S(1)} %get-tuple-element.1075.vt_ref, s32[2048,1]{1,0:T(8,128)S(1)} %copy.111.place_ref, s32[1,512]{1,0:T(1,128)S(1)} %bitcast.154, ...), custom_call_target="tpu_custom_call" | custom-call | flops 4294967296 | bytes 1048576 | tf_op jit(solution)/shard_map/pallas_call | solution.py:248
  173.2 3.0 collective-permute-done.30
  188.2 9.5 %shard_map.287.refs_1_ = bf16[512,512]{1,0:T(8,128)(2,1)S(1)} custom-call(bf16[512,512]{1,0:T(8,128)(2,1)S(1)} %copy-done.16, bf16[2048,256]{1,0:T(8,128)(2,1)S(1)} %copy.110.kv_ref, bf16[128,2048]{1,0:T(8,128)(2,1)S(1)} %copy-done.23, s32[2048,1]{1,0:T(8,128)S(1)} %copy.111.place_ref, s32[1,512]{1,0:T(1,128)S(1)} %bitcast.155, s32[1,512]{1,0:T(1,128)S(1)} %bitcast.159), custom_call_target="tpu_custom_call" | custom-call | flops 4294967296 | bytes 1048576 | tf_op jit(solution)/shard_map/pallas_call | solution.py:248
  207.3 3.1 fusion.96
  210.3 7.0 %shard_map.289 = (f32[512,2048]{1,0:T(8,128)S(1)}, bf16[512,1024]{1,0:T(8,128)(2,1)S(1)}) custom-call(s32[8]{0:T(128)S(1)} %stack.190.order_ref, bf16[512,512]{1,0:T(8,128)(2,1)S(1)} %copy-done.57, bf16[512,512]{1,0:T(8,128)(2,1)S(1)} %copy-done.59, bf16[512,2048]{1,0:T(8,128)(2,1)} %constant_dynamic-update-slice_fusion.11.refs_2_, ...), custom_call_target="tpu_custom_call" | custom-call | flops 2147483648 | bytes 12582912 | tf_op jit(solution)/shard_map/pallas_call | solution.py:185
  222.4 3.4 collective-permute-done.40
  237.6 10.1 %collective-permute-done.43 = bf16[128,2048]{1,0:T(8,128)(2,1)S(1)} collective-permute-done((bf16[128,2048]{1,0:T(8,128)(2,1)S(1)}, bf16[128,2048]{1,0:T(8,128)(2,1)S(1)}, u32[]{:S(2)}, u32[]{:S(2)}) %collective-permute-start.43) | collective-permute-done | bytes 524320 | tf_op jit(solution)/shard_map/ppermute | solution.py:654
  257.1 3.0 collective-permute-done.44.refs_2_
  260.0 4.7 collective-permute-done.45.refs_3_
  275.9 11.2 %shard_map.292 = (bf16[72,2176]{1,0:T(8,128)(2,1)S(1)}, bf16[72,2176]{1,0:T(8,128)(2,1)S(1)}, bf16[72,2176]{1,0:T(8,128)(2,1)S(1)}, bf16[72,2176]{1,0:T(8,128)(2...) custom-call(s32[1]{0:T(128)} %bitcast.68.refs_0_, ...), custom_call_target="tpu_custom_call" | custom-call | flops 5435817984 | bytes 9437184 | tf_op jit(solution)/shard_map/pallas_call | solution.py:460
  298.5 11.4 %shard_map.294 = (bf16[72,2176]{1,0:T(8,128)(2,1)S(1)}, bf16[72,2176]{1,0:T(8,128)(2,1)S(1)}, bf16[72,2176]{1,0:T(8,128)(2,1)S(1)}, bf16[72,2176]{1,0:T(8,128)(2...) custom-call(s32[1]{0:T(128)} %bitcast.68.refs_0_, ...), custom_call_target="tpu_custom_call" | custom-call | flops 5435817984 | bytes 9437184 | tf_op jit(solution)/shard_map/pallas_call | solution.py:460
  310.0 6.0 collective-permute-done.54.refs_4_
  317.7 2.8 collective-permute-start.58
  325.2 10.8 %shard_map.296 = (bf16[72,2176]{1,0:T(8,128)(2,1)S(1)}, bf16[72,2176]{1,0:T(8,128)(2,1)S(1)}, bf16[72,2176]{1,0:T(8,128)(2,1)S(1)}, bf16[72,2176]{1,0:T(8,128)(2...) custom-call(s32[1]{0:T(128)} %bitcast.68.refs_0_, ...), custom_call_target="tpu_custom_call" | custom-call | flops 5435817984 | bytes 9437184 | tf_op jit(solution)/shard_map/pallas_call | solution.py:460
  336.1 7.4 %collective-permute-done.58.refs_4_ = bf16[72,4224]{1,0:T(8,128)(2,1)S(1)} collective-permute-done((bf16[72,4224]{1,0:T(8,128)(2,1)S(1)}, bf16[72,4224]{1,0:T(8,128)(2,1)S(1)}, u32[]{:S(2)}, u32[]{:S(2)}) %collective-permute-start.58) | collective-permute-done | bytes 608288 | tf_op jit(solution)/shard_map/ppermute | solution.py:654
  344.3 3.4 collective-permute-start.61
  348.9 10.8 %shard_map.299 = (bf16[72,2176]{1,0:T(8,128)(2,1)S(1)}, bf16[72,2176]{1,0:T(8,128)(2,1)S(1)}, bf16[72,2176]{1,0:T(8,128)(2,1)S(1)}, bf16[72,2176]{1,0:T(8,128)(2...) custom-call(s32[1]{0:T(128)} %bitcast.68.refs_0_, ...), custom_call_target="tpu_custom_call" | custom-call | flops 5435817984 | bytes 9437184 | tf_op jit(solution)/shard_map/pallas_call | solution.py:460
  364.5 2.9 collective-permute-start.68
  370.1 4.2 collective-permute-done.66.refs_2_
  374.3 5.2 collective-permute-done.67.refs_3_
  380.0 4.5 collective-permute-start.70
  391.2 3.5 collective-permute-done.72.refs_3_
  397.9 2.7 constant_dynamic-slice_fusion.20
  402.2 5.8 collective-permute-done.75
  408.5 2.5 collective-permute-start.78
  411.1 3.4 collective-permute-done.77
  421.1 2.9 convolution_convert_fusion.6
  424.0 2.9 convolution_convert_fusion.5
  430.7 6.1 collective-permute-done.82.refs_4_
  447.3 19.4 %shard_map.305 = (bf16[512,512]{1,0:T(8,128)(2,1)S(1)}, f32[2048,256]{1,0:T(8,128)S(1)}, f32[1,128]{1,0:T(1,128)S(1)}) custom-call(bf16[512,512]{1,0:T(8,128)(2,1)S(1)} %copy-done.19, bf16[512,512]{1,0:T(8,128)(2,1)S(1)} %get-tuple-element.792.grad_ref, f32[512,512]{1,0:T(8,128)S(1)} %copy-done.15, bf16[2048,256]{1,0:T(8,128)(2,1)S(1)} %copy-done.10, ...), custom_call_target="tpu_custom_call" | custom-call | flops 5368709120 | bytes 2097152 | tf_op jit(solution)/shard_map/pallas_call | solution.py:320
  473.0 3.6 collective-permute-start.94
  482.2 19.6 %shard_map.307 = (bf16[512,512]{1,0:T(8,128)(2,1)S(1)}, f32[2048,256]{1,0:T(8,128)S(1)}, f32[1,128]{1,0:T(1,128)S(1)}) custom-call(bf16[512,512]{1,0:T(8,128)(2,1)S(1)} %copy-done.17, bf16[512,512]{1,0:T(8,128)(2,1)S(1)} %copy-done.24, f32[512,512]{1,0:T(8,128)S(1)} %copy-done.14, bf16[2048,256]{1,0:T(8,128)(2,1)S(1)} %copy-done.11, ...), custom_call_target="tpu_custom_call" | custom-call | flops 5368709120 | bytes 2097152 | tf_op jit(solution)/shard_map/pallas_call | solution.py:320
  512.0 5.0 convolution_convert_fusion.1
  520.4 3.1 collective-permute-done.96
  523.5 4.6 collective-permute-done.98
  543.0 3.3 constant_dynamic-slice_fusion.45
  551.3 3.3 fusion.22
  554.6 9.3 %collective-permute-done.102 = bf16[512,256]{1,0:T(8,128)(2,1)} collective-permute-done((bf16[512,256]{1,0:T(8,128)(2,1)}, bf16[512,256]{1,0:T(8,128)(2,1)}, u32[]{:S(2)}, u32[]{:S(2)}) %collective-permute-start.102) | collective-permute-done | bytes 262176 | tf_op jit(solution)/shard_map/ppermute | solution.py:654
  574.6 3.3 copy.125
  584.6 4.0 convert_add_fusion.2
  588.9 4.6 shard_map.310
  593.5 4.4 collective-permute-done.106
  604.3 2.9 collective-permute-start.112
  607.6 3.9 convert_add_fusion.1
  611.5 3.5 collective-permute-done.111
  616.2 2.9 collective-permute-done.110
  619.1 5.6 collective-permute-done.113
  628.7 5.3 convert_add_fusion
  634.3 6.8 collective-permute-done.115
  651.4 6.5 collective-permute-done.119
  657.9 7.0 %collective-permute-done.120 = bf16[64,1536]{0,1:T(8,128)(2,1)S(1)} collective-permute-done((bf16[64,1536]{0,1:T(8,128)(2,1)S(1)}, bf16[64,1536]{0,1:T(8,128)(2,1)S(1)}, u32[]{:S(2)}, u32[]{:S(2)}) %collective-permute-start.120) | collective-permute-done | bytes 196640 | tf_op jit(solution)/shard_map/ppermute | solution.py:654
  (824 shorter events, 293.5 us)
Async XLA Ops:
  7.2 265.5 %all-gather.4.cloned.1.call-start = ((), (), s32[]{:S(2)}) async-start(), calls=%async_computation | async-start | bytes 4718592 | tf_op jit(solution)/shard_map/all_gather | solution.py:802
  7.9 264.8 %all-gather.6.cloned.1.call-start = ((), (), s32[]{:S(2)}) async-start(), calls=%async_computation.1 | async-start | bytes 4718592 | tf_op jit(solution)/shard_map/all_gather | solution.py:803
  20.4 252.3 %all-gather.8.cloned.1.call-start = ((), (), s32[]{:S(2)}) async-start(), calls=%async_computation.2 | async-start | bytes 4718592 | tf_op jit(solution)/shard_map/all_gather | solution.py:804
  28.1 26.8 %collective-permute-start.7 = (bf16[128,2048]{1,0:T(8,128)(2,1)S(1)}, bf16[128,2048]{1,0:T(8,128)(2,1)}, u32[]{:S(2)}, u32[]{:S(2)}) collective-permute-start(bf16[128,2048]{1,0:T(8,128)(2,1)S(1)} %copy-done.69), channel_id=1, source_target_pairs={{0,4},{1,5},{2,6},{3,7},{4,0},{5,1},{6,2},{7,3},{8,12},{9,13},{10,... | collective-permute-start | bytes 1572872 | tf_op jit(solution)/shard_map/ppermute | solution.py:654
  34.9 20.0 %collective-permute-start.12 = (bf16[160,1280]{1,0:T(8,128)(2,1)}, bf16[160,1280]{1,0:T(8,128)(2,1)}, u32[]{:S(2)}, u32[]{:S(2)}) collective-permute-start(bf16[160,1280]{1,0:T(8,128)(2,1)} %slice.542), channel_id=1, source_target_pairs={{0,8},{1,9},{2,10},{3,11},{4,12},{5,13},{6,14},{7,15},{8,0},{9,1},... | collective-permute-start | bytes 1228808 | tf_op jit(solution)/shard_map/ppermute | solution.py:654
  36.9 21.6 %collective-permute-start.8 = (bf16[128,2048]{1,0:T(8,128)(2,1)S(1)}, bf16[128,2048]{1,0:T(8,128)(2,1)}, u32[]{:S(2)}, u32[]{:S(2)}) collective-permute-start(bf16[128,2048]{1,0:T(8,128)(2,1)S(1)} %copy-done.69), channel_id=1, source_target_pairs={{0,2},{1,3},{2,0},{3,1},{4,6},{5,7},{6,4},{7,5},{8,10},{9,11},{10,... | collective-permute-start | bytes 1572872 | tf_op jit(solution)/shard_map/ppermute | solution.py:654
  38.4 22.7 %collective-permute-start.6 = (bf16[128,2048]{1,0:T(8,128)(2,1)}, bf16[128,2048]{1,0:T(8,128)(2,1)S(1)}, u32[]{:S(2)}, u32[]{:S(2)}) collective-permute-start(bf16[128,2048]{1,0:T(8,128)(2,1)} %collective-permute-done.3), channel_id=1, source_target_pairs={{0,0},{1,1},{2,16},{3,17},{4,4},{5,5},{6,20},{7,21},{8,8},{9,9},{1... | collective-permute-start | bytes 1572872 | tf_op jit(solution)/shard_map/ppermute | solution.py:972
  40.7 22.4 %collective-permute-start.4 = (bf16[288,1280]{1,0:T(8,128)(2,1)}, bf16[288,1280]{1,0:T(8,128)(2,1)}, u32[]{:S(2)}, u32[]{:S(2)}) collective-permute-start(bf16[288,1280]{1,0:T(8,128)(2,1)} %shard_map.281.refs_0_), channel_id=1, source_target_pairs={{0,1},{1,0},{2,3},{3,2},{4,5},{5,4},{6,7},{7,6},{8,9},{9,8},{10,11... | collective-permute-start | bytes 2211848 | tf_op jit(solution)/shard_map/ppermute | solution.py:654
  54.9 44.3 %collective-permute-start.15 = (bf16[288,1280]{1,0:T(8,128)(2,1)}, bf16[288,1280]{1,0:T(8,128)(2,1)}, u32[]{:S(2)}, u32[]{:S(2)}) collective-permute-start(bf16[288,1280]{1,0:T(8,128)(2,1)} %shard_map.281.refs_0_), channel_id=1, source_target_pairs={{0,16},{16,0},{1,17},{17,1},{2,18},{18,2},{3,19},{19,3},{4,20},{20... | collective-permute-start | bytes 2211848 | tf_op jit(solution)/shard_map/ppermute | solution.py:665
  54.9 17.4 %collective-permute-start.13 = (bf16[160,1280]{1,0:T(8,128)(2,1)}, bf16[160,1280]{1,0:T(8,128)(2,1)S(1)}, u32[]{:S(2)}, u32[]{:S(2)}) collective-permute-start(bf16[160,1280]{1,0:T(8,128)(2,1)} %collective-permute-done.12), channel_id=1, source_target_pairs={{0,1},{1,0},{2,3},{3,2},{4,5},{5,4},{6,7},{7,6},{8,9},{9,8},{10,11... | collective-permute-start | bytes 1228808 | tf_op jit(solution)/shard_map/ppermute | solution.py:654
  64.0 21.1 %collective-permute-start.5 = (bf16[160,1280]{1,0:T(8,128)(2,1)S(1)}, bf16[160,1280]{1,0:T(8,128)(2,1)S(1)}, u32[]{:S(2)}, u32[]{:S(2)}) collective-permute-start(bf16[160,1280]{1,0:T(8,128)(2,1)S(1)} %pad_maximum_fusion.15), channel_id=1, source_target_pairs={{0,8},{1,9},{2,10},{3,11},{4,12},{5,13},{6,14},{7,15},{8,0},{9,1},... | collective-permute-start | bytes 1228808 | tf_op jit(solution)/shard_map/ppermute | solution.py:654
  67.1 32.1 %collective-permute-start.16 = (bf16[288,1280]{1,0:T(8,128)(2,1)}, bf16[288,1280]{1,0:T(8,128)(2,1)}, u32[]{:S(2)}, u32[]{:S(2)}) collective-permute-start(bf16[288,1280]{1,0:T(8,128)(2,1)} %collective-permute-done.4.refs_1_), channel_id=1, source_target_pairs={{0,16},{16,0},{1,17},{17,1},{2,18},{18,2},{3,19},{19,3},{4,20},{20... | collective-permute-start | bytes 2211848 | tf_op jit(solution)/shard_map/ppermute | solution.py:665
  154.5 21.7 %collective-permute-start.26 = (bf16[128,2048]{1,0:T(8,128)(2,1)S(1)}, bf16[128,2048]{1,0:T(8,128)(2,1)}, u32[]{:S(2)}, u32[]{:S(2)}) collective-permute-start(bf16[128,2048]{1,0:T(8,128)(2,1)S(1)} %copy-done.2), channel_id=1, source_target_pairs={{0,4},{1,5},{2,6},{3,7},{4,8},{5,9},{6,10},{7,11},{8,12},{9,13},{1... | collective-permute-start | bytes 1572872 | tf_op jit(solution)/shard_map/ppermute | solution.py:657
  156.0 20.1 %collective-permute-start.27 = (bf16[72,2048]{1,0:T(8,128)(2,1)}, bf16[72,2048]{1,0:T(8,128)(2,1)S(1)}, u32[]{:S(2)}, u32[]{:S(2)}) collective-permute-start(bf16[72,2048]{1,0:T(8,128)(2,1)} %copy-done.55), channel_id=1, source_target_pairs={{0,1},{1,0},{2,3},{3,2},{4,5},{5,4},{6,7},{7,6},{8,9},{9,8},{10,11... | collective-permute-start | bytes 884744 | tf_op jit(solution)/shard_map/ppermute | solution.py:654
  156.6 19.6 %collective-permute-start.28 = (bf16[72,2048]{1,0:T(8,128)(2,1)}, bf16[72,2048]{1,0:T(8,128)(2,1)S(1)}, u32[]{:S(2)}, u32[]{:S(2)}) collective-permute-start(bf16[72,2048]{1,0:T(8,128)(2,1)} %copy-done.54), channel_id=1, source_target_pairs={{0,2},{1,3},{2,0},{3,1},{4,6},{5,7},{6,4},{7,5},{8,10},{9,11},{10,... | collective-permute-start | bytes 884744 | tf_op jit(solution)/shard_map/ppermute | solution.py:654
  157.1 19.1 %collective-permute-start.29 = (bf16[72,2048]{1,0:T(8,128)(2,1)S(1)}, bf16[72,2048]{1,0:T(8,128)(2,1)S(1)}, u32[]{:S(2)}, u32[]{:S(2)}) collective-permute-start(bf16[72,2048]{1,0:T(8,128)(2,1)S(1)} %get-tuple-element.531), channel_id=1, source_target_pairs={{0,3},{1,2},{2,1},{3,0},{4,7},{5,6},{6,5},{7,4},{8,11},{9,10},{10,... | collective-permute-start | bytes 884744 | tf_op jit(solution)/shard_map/ppermute | solution.py:654
  159.5 16.7 %collective-permute-start.30 = (bf16[64,2048]{1,0:T(8,128)(2,1)}, bf16[64,2048]{1,0:T(8,128)(2,1)S(1)}, u32[]{:S(2)}, u32[]{:S(2)}) collective-permute-start(bf16[64,2048]{1,0:T(8,128)(2,1)} %copy-done.130), channel_id=1, source_target_pairs={{0,1},{1,0},{2,3},{3,2},{4,5},{5,4},{6,7},{7,6},{8,9},{9,8},{10,11... | collective-permute-start | bytes 786440 | tf_op jit(solution)/shard_map/ppermute | solution.py:654
  180.9 17.5 %collective-permute-start.35 = (bf16[512,2048]{1,0:T(8,128)(2,1)}, bf16[512,2048]{1,0:T(8,128)(2,1)}, u32[]{:S(2)}, u32[]{:S(2)}) collective-permute-start(bf16[512,2048]{1,0:T(8,128)(2,1)} %constant_dynamic-update-slice_fusion.11.refs_2_), channel_id=1, source_target_pairs={{0,16},{16,0},{1,17},{17,1},{2,18},{18,2},{3,19},{19,3},{4,20},{20... | collective-permute-start | bytes 6291464 | tf_op jit(solution)/shard_map/ppermute | solution.py:665
  181.0 17.4 %collective-permute-start.31 = (bf16[128,2048]{1,0:T(8,128)(2,1)}, bf16[128,2048]{1,0:T(8,128)(2,1)}, u32[]{:S(2)}, u32[]{:S(2)}) collective-permute-start(bf16[128,2048]{1,0:T(8,128)(2,1)} %collective-permute-done.26.refs_1_), channel_id=1, source_target_pairs={{0,4},{1,5},{2,6},{3,7},{4,8},{5,9},{6,10},{7,11},{8,12},{9,13},{1... | collective-permute-start | bytes 1572872 | tf_op jit(solution)/shard_map/ppermute | solution.py:657
  200.9 18.1 %collective-permute-start.36 = (bf16[128,2048]{1,0:T(8,128)(2,1)}, bf16[128,2048]{1,0:T(8,128)(2,1)S(1)}, u32[]{:S(2)}, u32[]{:S(2)}) collective-permute-start(bf16[128,2048]{1,0:T(8,128)(2,1)} %collective-permute-done.31.refs_1_), channel_id=1, source_target_pairs={{0,4},{1,5},{2,6},{3,7},{4,8},{5,9},{6,10},{7,11},{8,12},{9,13},{1... | collective-permute-start | bytes 1572872 | tf_op jit(solution)/shard_map/ppermute | solution.py:657
  229.1 18.6 %collective-permute-start.43 = (bf16[128,2048]{1,0:T(8,128)(2,1)S(1)}, bf16[128,2048]{1,0:T(8,128)(2,1)S(1)}, u32[]{:S(2)}, u32[]{:S(2)}) collective-permute-start(bf16[128,2048]{1,0:T(8,128)(2,1)S(1)} %pad_maximum_fusion.12), channel_id=1, source_target_pairs={{0,2},{1,3},{2,0},{3,1},{4,6},{5,7},{6,4},{7,5},{8,10},{9,11},{10,... | collective-permute-start | bytes 1572872 | tf_op jit(solution)/shard_map/ppermute | solution.py:654
  231.9 20.0 %collective-permute-start.63 = (bf16[72,2048]{1,0:T(8,128)(2,1)S(1)}, bf16[72,2048]{1,0:T(8,128)(2,1)S(1)}, u32[]{:S(2)}, u32[]{:S(2)}) collective-permute-start(bf16[72,2048]{1,0:T(8,128)(2,1)S(1)} %get-tuple-element.698), channel_id=1, source_target_pairs={{0,1},{1,0},{2,3},{3,2},{4,5},{5,4},{6,7},{7,6},{8,9},{9,8},{10,11... | collective-permute-start | bytes 884744 | tf_op jit(solution)/shard_map/ppermute | solution.py:654
  233.0 18.9 %collective-permute-start.64 = (bf16[72,2048]{1,0:T(8,128)(2,1)S(1)}, bf16[72,2048]{1,0:T(8,128)(2,1)S(1)}, u32[]{:S(2)}, u32[]{:S(2)}) collective-permute-start(bf16[72,2048]{1,0:T(8,128)(2,1)S(1)} %get-tuple-element.699), channel_id=1, source_target_pairs={{0,2},{1,3},{2,0},{3,1},{4,6},{5,7},{6,4},{7,5},{8,10},{9,11},{10,... | collective-permute-start | bytes 884744 | tf_op jit(solution)/shard_map/ppermute | solution.py:654
  234.0 17.8 %collective-permute-start.65 = (bf16[72,2048]{1,0:T(8,128)(2,1)S(1)}, bf16[72,2048]{1,0:T(8,128)(2,1)S(1)}, u32[]{:S(2)}, u32[]{:S(2)}) collective-permute-start(bf16[72,2048]{1,0:T(8,128)(2,1)S(1)} %get-tuple-element.700), channel_id=1, source_target_pairs={{0,3},{1,2},{2,1},{3,0},{4,7},{5,6},{6,5},{7,4},{8,11},{9,10},{10,... | collective-permute-start | bytes 884744 | tf_op jit(solution)/shard_map/ppermute | solution.py:654
  267.8 19.4 %collective-permute-start.51 = (bf16[128,2048]{1,0:T(8,128)(2,1)}, bf16[128,2048]{1,0:T(8,128)(2,1)}, u32[]{:S(2)}, u32[]{:S(2)}) collective-permute-start(bf16[128,2048]{1,0:T(8,128)(2,1)} %collective-permute-done.47.refs_1_), channel_id=1, source_target_pairs={{0,4},{1,5},{2,6},{3,7},{4,8},{5,9},{6,10},{7,11},{8,12},{9,13},{1... | collective-permute-start | bytes 1572872 | tf_op jit(solution)/shard_map/ppermute | solution.py:657
  269.2 17.9 %collective-permute-start.48 = (bf16[72,2048]{1,0:T(8,128)(2,1)}, bf16[72,2048]{1,0:T(8,128)(2,1)}, u32[]{:S(2)}, u32[]{:S(2)}) collective-permute-start(bf16[72,2048]{1,0:T(8,128)(2,1)} %get-tuple-element.581), channel_id=1, source_target_pairs={{0,1},{1,0},{2,3},{3,2},{4,5},{5,4},{6,7},{7,6},{8,9},{9,8},{10,11... | collective-permute-start | bytes 884744 | tf_op jit(solution)/shard_map/ppermute | solution.py:654
  269.8 17.4 %collective-permute-start.49 = (bf16[72,2048]{1,0:T(8,128)(2,1)}, bf16[72,2048]{1,0:T(8,128)(2,1)}, u32[]{:S(2)}, u32[]{:S(2)}) collective-permute-start(bf16[72,2048]{1,0:T(8,128)(2,1)} %get-tuple-element.582), channel_id=1, source_target_pairs={{0,2},{1,3},{2,0},{3,1},{4,6},{5,7},{6,4},{7,5},{8,10},{9,11},{10,... | collective-permute-start | bytes 884744 | tf_op jit(solution)/shard_map/ppermute | solution.py:654
  289.1 20.9 %collective-permute-start.52 = (bf16[72,4224]{1,0:T(8,128)(2,1)S(1)}, bf16[72,4224]{1,0:T(8,128)(2,1)S(1)}, u32[]{:S(2)}, u32[]{:S(2)}) collective-permute-start(bf16[72,4224]{1,0:T(8,128)(2,1)S(1)} %get-tuple-element.620), channel_id=1, source_target_pairs={{0,1},{1,0},{2,3},{3,2},{4,5},{5,4},{6,7},{7,6},{8,9},{9,8},{10,11... | collective-permute-start | bytes 1824776 | tf_op jit(solution)/shard_map/ppermute | solution.py:654
  289.7 20.3 %collective-permute-start.53 = (bf16[72,4224]{1,0:T(8,128)(2,1)S(1)}, bf16[72,4224]{1,0:T(8,128)(2,1)S(1)}, u32[]{:S(2)}, u32[]{:S(2)}) collective-permute-start(bf16[72,4224]{1,0:T(8,128)(2,1)S(1)} %get-tuple-element.621), channel_id=1, source_target_pairs={{0,2},{1,3},{2,0},{3,1},{4,6},{5,7},{6,4},{7,5},{8,10},{9,11},{10,... | collective-permute-start | bytes 1824776 | tf_op jit(solution)/shard_map/ppermute | solution.py:654
  291.4 24.6 %collective-permute-start.54 = (bf16[72,4224]{1,0:T(8,128)(2,1)S(1)}, bf16[72,4224]{1,0:T(8,128)(2,1)S(1)}, u32[]{:S(2)}, u32[]{:S(2)}) collective-permute-start(bf16[72,4224]{1,0:T(8,128)(2,1)S(1)} %get-tuple-element.622), channel_id=1, source_target_pairs={{0,3},{1,2},{2,1},{3,0},{4,7},{5,6},{6,5},{7,4},{8,11},{9,10},{10,... | collective-permute-start | bytes 1824776 | tf_op jit(solution)/shard_map/ppermute | solution.py:654
  292.7 17.3 %collective-permute-start.55 = (bf16[128,2048]{1,0:T(8,128)(2,1)}, bf16[128,2048]{1,0:T(8,128)(2,1)S(1)}, u32[]{:S(2)}, u32[]{:S(2)}) collective-permute-start(bf16[128,2048]{1,0:T(8,128)(2,1)} %collective-permute-done.51.refs_1_), channel_id=1, source_target_pairs={{0,4},{1,5},{2,6},{3,7},{4,8},{5,9},{6,10},{7,11},{8,12},{9,13},{1... | collective-permute-start | bytes 1572872 | tf_op jit(solution)/shard_map/ppermute | solution.py:657
  317.0 19.1 %collective-permute-start.56 = (bf16[72,4224]{1,0:T(8,128)(2,1)S(1)}, bf16[72,4224]{1,0:T(8,128)(2,1)S(1)}, u32[]{:S(2)}, u32[]{:S(2)}) collective-permute-start(bf16[72,4224]{1,0:T(8,128)(2,1)S(1)} %get-tuple-element.657), channel_id=1, source_target_pairs={{0,1},{1,0},{2,3},{3,2},{4,5},{5,4},{6,7},{7,6},{8,9},{9,8},{10,11... | collective-permute-start | bytes 1824776 | tf_op jit(solution)/shard_map/ppermute | solution.py:654
  317.1 19.0 %collective-permute-start.57 = (bf16[72,4224]{1,0:T(8,128)(2,1)S(1)}, bf16[72,4224]{1,0:T(8,128)(2,1)S(1)}, u32[]{:S(2)}, u32[]{:S(2)}) collective-permute-start(bf16[72,4224]{1,0:T(8,128)(2,1)S(1)} %get-tuple-element.658), channel_id=1, source_target_pairs={{0,2},{1,3},{2,0},{3,1},{4,6},{5,7},{6,4},{7,5},{8,10},{9,11},{10,... | collective-permute-start | bytes 1824776 | tf_op jit(solution)/shard_map/ppermute | solution.py:654
  317.7 25.7 %collective-permute-start.58 = (bf16[72,4224]{1,0:T(8,128)(2,1)S(1)}, bf16[72,4224]{1,0:T(8,128)(2,1)S(1)}, u32[]{:S(2)}, u32[]{:S(2)}) collective-permute-start(bf16[72,4224]{1,0:T(8,128)(2,1)S(1)} %get-tuple-element.659), channel_id=1, source_target_pairs={{0,3},{1,2},{2,1},{3,0},{4,7},{5,6},{6,5},{7,4},{8,11},{9,10},{10,... | collective-permute-start | bytes 1824776 | tf_op jit(solution)/shard_map/ppermute | solution.py:654
  343.9 19.5 %collective-permute-start.62 = (bf16[128,2176]{1,0:T(8,128)(2,1)S(1)}, bf16[128,2176]{1,0:T(8,128)(2,1)S(1)}, u32[]{:S(2)}, u32[]{:S(2)}) collective-permute-start(bf16[128,2176]{1,0:T(8,128)(2,1)S(1)} %shard_map.297), channel_id=1, source_target_pairs={{0,4},{1,5},{2,6},{3,7},{4,8},{5,9},{6,10},{7,11},{8,12},{9,13},{1... | collective-permute-start | bytes 1671176 | tf_op jit(solution)/shard_map/ppermute | solution.py:657
  344.2 19.2 %collective-permute-start.59 = (bf16[72,2176]{1,0:T(8,128)(2,1)S(1)}, bf16[72,2176]{1,0:T(8,128)(2,1)S(1)}, u32[]{:S(2)}, u32[]{:S(2)}) collective-permute-start(bf16[72,2176]{1,0:T(8,128)(2,1)S(1)} %get-tuple-element.688), channel_id=1, source_target_pairs={{0,1},{1,0},{2,3},{3,2},{4,5},{5,4},{6,7},{7,6},{8,9},{9,8},{10,11... | collective-permute-start | bytes 940040 | tf_op jit(solution)/shard_map/ppermute | solution.py:654
  344.3 19.1 %collective-permute-start.60 = (bf16[72,2176]{1,0:T(8,128)(2,1)S(1)}, bf16[72,2176]{1,0:T(8,128)(2,1)S(1)}, u32[]{:S(2)}, u32[]{:S(2)}) collective-permute-start(bf16[72,2176]{1,0:T(8,128)(2,1)S(1)} %get-tuple-element.689), channel_id=1, source_target_pairs={{0,2},{1,3},{2,0},{3,1},{4,6},{5,7},{6,4},{7,5},{8,10},{9,11},{10,... | collective-permute-start | bytes 940040 | tf_op jit(solution)/shard_map/ppermute | solution.py:654
  344.3 19.0 %collective-permute-start.61 = (bf16[72,2176]{1,0:T(8,128)(2,1)S(1)}, bf16[72,2176]{1,0:T(8,128)(2,1)S(1)}, u32[]{:S(2)}, u32[]{:S(2)}) collective-permute-start(bf16[72,2176]{1,0:T(8,128)(2,1)S(1)} %get-tuple-element.690), channel_id=1, source_target_pairs={{0,3},{1,2},{2,1},{3,0},{4,7},{5,6},{6,5},{7,4},{8,11},{9,10},{10,... | collective-permute-start | bytes 940040 | tf_op jit(solution)/shard_map/ppermute | solution.py:654
  390.4 26.3 %collective-permute-start.74 = (bf16[1024,768]{1,0:T(8,128)(2,1)S(1)}, bf16[1024,768]{1,0:T(8,128)(2,1)S(1)}, u32[]{:S(2)}, u32[]{:S(2)}) collective-permute-start(bf16[1024,768]{1,0:T(8,128)(2,1)S(1)} %fusion.7), channel_id=1, source_target_pairs={{0,16},{16,0},{1,17},{17,1},{2,18},{18,2},{3,19},{19,3},{4,20},{20... | collective-permute-start | bytes 4718600 | tf_op jit(solution)/shard_map/ppermute | solution.py:665
  416.7 20.2 %collective-permute-start.84 = (bf16[512,2048]{1,0:T(8,128)(2,1)S(1)}, bf16[512,2048]{1,0:T(8,128)(2,1)S(1)}, u32[]{:S(2)}, u32[]{:S(2)}) collective-permute-start(bf16[512,2048]{1,0:T(8,128)(2,1)S(1)} %convolution_convert_fusion), channel_id=1, source_target_pairs={{0,16},{16,0},{1,17},{17,1},{2,18},{18,2},{3,19},{19,3},{4,20},{20... | collective-permute-start | bytes 6291464 | tf_op jit(solution)/shard_map/ppermute | solution.py:665
  416.8 20.1 %collective-permute-start.83 = (bf16[1024,768]{1,0:T(8,128)(2,1)S(1)}, bf16[1024,768]{1,0:T(8,128)(2,1)S(1)}, u32[]{:S(2)}, u32[]{:S(2)}) collective-permute-start(bf16[1024,768]{1,0:T(8,128)(2,1)S(1)} %fusion.10), channel_id=1, source_target_pairs={{0,16},{16,0},{1,17},{17,1},{2,18},{18,2},{3,19},{19,3},{4,20},{20... | collective-permute-start | bytes 4718600 | tf_op jit(solution)/shard_map/ppermute | solution.py:665
  417.3 19.6 %collective-permute-start.79 = (bf16[128,2048]{1,0:T(8,128)(2,1)S(1)}, bf16[128,2048]{1,0:T(8,128)(2,1)S(1)}, u32[]{:S(2)}, u32[]{:S(2)}) collective-permute-start(bf16[128,2048]{1,0:T(8,128)(2,1)S(1)} %shard_map.302), channel_id=1, source_target_pairs={{0,4},{1,5},{2,6},{3,7},{4,8},{5,9},{6,10},{7,11},{8,12},{9,13},{1... | collective-permute-start | bytes 1572872 | tf_op jit(solution)/shard_map/ppermute | solution.py:657
  440.3 26.5 %collective-permute-start.85 = (bf16[128,2048]{1,0:T(8,128)(2,1)S(1)}, bf16[128,2048]{1,0:T(8,128)(2,1)S(1)}, u32[]{:S(2)}, u32[]{:S(2)}) collective-permute-start(bf16[128,2048]{1,0:T(8,128)(2,1)S(1)} %shard_map.304), channel_id=1, source_target_pairs={{0,4},{1,5},{2,6},{3,7},{4,8},{5,9},{6,10},{7,11},{8,12},{9,13},{1... | collective-permute-start | bytes 1572872 | tf_op jit(solution)/shard_map/ppermute | solution.py:657
  441.0 25.8 %collective-permute-start.89 = (bf16[128,2048]{1,0:T(8,128)(2,1)S(1)}, bf16[128,2048]{1,0:T(8,128)(2,1)S(1)}, u32[]{:S(2)}, u32[]{:S(2)}) collective-permute-start(bf16[128,2048]{1,0:T(8,128)(2,1)S(1)} %get-tuple-element.790), channel_id=1, source_target_pairs={{0,1},{1,0},{2,3},{3,2},{4,5},{5,4},{6,7},{7,6},{8,9},{9,8},{10,11... | collective-permute-start | bytes 1572872 | tf_op jit(solution)/shard_map/ppermute | solution.py:654
  443.7 23.0 %collective-permute-start.86 = (bf16[72,2048]{1,0:T(8,128)(2,1)S(1)}, bf16[72,2048]{1,0:T(8,128)(2,1)S(1)}, u32[]{:S(2)}, u32[]{:S(2)}) collective-permute-start(bf16[72,2048]{1,0:T(8,128)(2,1)S(1)} %get-tuple-element.785), channel_id=1, source_target_pairs={{0,1},{1,0},{2,3},{3,2},{4,5},{5,4},{6,7},{7,6},{8,9},{9,8},{10,11... | collective-permute-start | bytes 884744 | tf_op jit(solution)/shard_map/ppermute | solution.py:654
  444.2 22.6 %collective-permute-start.87 = (bf16[72,2048]{1,0:T(8,128)(2,1)S(1)}, bf16[72,2048]{1,0:T(8,128)(2,1)S(1)}, u32[]{:S(2)}, u32[]{:S(2)}) collective-permute-start(bf16[72,2048]{1,0:T(8,128)(2,1)S(1)} %get-tuple-element.786), channel_id=1, source_target_pairs={{0,2},{1,3},{2,0},{3,1},{4,6},{5,7},{6,4},{7,5},{8,10},{9,11},{10,... | collective-permute-start | bytes 884744 | tf_op jit(solution)/shard_map/ppermute | solution.py:654
  445.7 21.1 %collective-permute-start.88 = (bf16[72,2048]{1,0:T(8,128)(2,1)S(1)}, bf16[72,2048]{1,0:T(8,128)(2,1)S(1)}, u32[]{:S(2)}, u32[]{:S(2)}) collective-permute-start(bf16[72,2048]{1,0:T(8,128)(2,1)S(1)} %get-tuple-element.787), channel_id=1, source_target_pairs={{0,3},{1,2},{2,1},{3,0},{4,7},{5,6},{6,5},{7,4},{8,11},{9,10},{10,... | collective-permute-start | bytes 884744 | tf_op jit(solution)/shard_map/ppermute | solution.py:654
  469.3 35.2 %collective-permute-start.90 = (bf16[128,2048]{1,0:T(8,128)(2,1)}, bf16[128,2048]{1,0:T(8,128)(2,1)}, u32[]{:S(2)}, u32[]{:S(2)}) collective-permute-start(bf16[128,2048]{1,0:T(8,128)(2,1)} %shard_map.306), channel_id=1, source_target_pairs={{0,4},{1,5},{2,6},{3,7},{4,8},{5,9},{6,10},{7,11},{8,12},{9,13},{1... | collective-permute-start | bytes 1572872 | tf_op jit(solution)/shard_map/ppermute | solution.py:657
  469.5 34.9 %collective-permute-start.91 = (bf16[72,2048]{1,0:T(8,128)(2,1)}, bf16[72,2048]{1,0:T(8,128)(2,1)}, u32[]{:S(2)}, u32[]{:S(2)}) collective-permute-start(bf16[72,2048]{1,0:T(8,128)(2,1)} %copy-done.41), channel_id=1, source_target_pairs={{0,1},{1,0},{2,3},{3,2},{4,5},{5,4},{6,7},{7,6},{8,9},{9,8},{10,11... | collective-permute-start | bytes 884744 | tf_op jit(solution)/shard_map/ppermute | solution.py:654
  470.1 34.4 %collective-permute-start.92 = (bf16[72,2048]{1,0:T(8,128)(2,1)}, bf16[72,2048]{1,0:T(8,128)(2,1)}, u32[]{:S(2)}, u32[]{:S(2)}) collective-permute-start(bf16[72,2048]{1,0:T(8,128)(2,1)} %copy-done.40), channel_id=1, source_target_pairs={{0,2},{1,3},{2,0},{3,1},{4,6},{5,7},{6,4},{7,5},{8,10},{9,11},{10,... | collective-permute-start | bytes 884744 | tf_op jit(solution)/shard_map/ppermute | solution.py:654
  471.5 33.0 %collective-permute-start.93 = (bf16[72,2048]{1,0:T(8,128)(2,1)}, bf16[72,2048]{1,0:T(8,128)(2,1)}, u32[]{:S(2)}, u32[]{:S(2)}) collective-permute-start(bf16[72,2048]{1,0:T(8,128)(2,1)} %copy-done.39), channel_id=1, source_target_pairs={{0,3},{1,2},{2,1},{3,0},{4,7},{5,6},{6,5},{7,4},{8,11},{9,10},{10,... | collective-permute-start | bytes 884744 | tf_op jit(solution)/shard_map/ppermute | solution.py:654
  473.0 31.4 %collective-permute-start.94 = (bf16[64,2048]{1,0:T(8,128)(2,1)}, bf16[64,2048]{1,0:T(8,128)(2,1)}, u32[]{:S(2)}, u32[]{:S(2)}) collective-permute-start(bf16[64,2048]{1,0:T(8,128)(2,1)} %get-tuple-element.813), channel_id=1, source_target_pairs={{0,8},{1,9},{2,10},{3,11},{4,12},{5,13},{6,14},{7,15},{8,0},{9,1},... | collective-permute-start | bytes 786440 | tf_op jit(solution)/shard_map/ppermute | solution.py:654
  507.8 20.3 %collective-permute-start.97 = (bf16[1024,640]{0,1:T(8,128)(2,1)}, bf16[1024,640]{0,1:T(8,128)(2,1)}, u32[]{:S(2)}, u32[]{:S(2)}) collective-permute-start(bf16[1024,640]{0,1:T(8,128)(2,1)} %pad_maximum_fusion.1), channel_id=1, source_target_pairs={{0,16},{16,0},{1,17},{17,1},{2,18},{18,2},{3,19},{19,3},{4,20},{20... | collective-permute-start | bytes 3932168 | tf_op jit(solution)/shard_map/ppermute | solution.py:665
  507.8 20.3 %collective-permute-start.95 = (bf16[128,2048]{1,0:T(8,128)(2,1)}, bf16[128,2048]{1,0:T(8,128)(2,1)}, u32[]{:S(2)}, u32[]{:S(2)}) collective-permute-start(bf16[128,2048]{1,0:T(8,128)(2,1)} %get-tuple-element.843), channel_id=1, source_target_pairs={{0,1},{1,0},{2,3},{3,2},{4,5},{5,4},{6,7},{7,6},{8,9},{9,8},{10,11... | collective-permute-start | bytes 1572872 | tf_op jit(solution)/shard_map/ppermute | solution.py:654
  508.3 19.8 %collective-permute-start.98 = (bf16[512,256]{1,0:T(8,128)(2,1)}, bf16[512,256]{1,0:T(8,128)(2,1)}, u32[]{:S(2)}, u32[]{:S(2)}) collective-permute-start(bf16[512,256]{1,0:T(8,128)(2,1)} %get-tuple-element.849), channel_id=1, source_target_pairs={{0,1},{1,0},{2,3},{3,2},{4,5},{5,4},{6,7},{7,6},{8,9},{9,8},{10,11... | collective-permute-start | bytes 786440 | tf_op jit(solution)/shard_map/ppermute | solution.py:654
  537.3 27.5 %collective-permute-start.99 = (bf16[768,1024]{1,0:T(8,128)(2,1)}, bf16[768,1024]{1,0:T(8,128)(2,1)}, u32[]{:S(2)}, u32[]{:S(2)}) collective-permute-start(bf16[768,1024]{1,0:T(8,128)(2,1)} %convolution_convert_fusion.1), channel_id=1, source_target_pairs={{0,16},{16,0},{1,17},{17,1},{2,18},{18,2},{3,19},{19,3},{4,20},{20... | collective-permute-start | bytes 4718600 | tf_op jit(solution)/shard_map/ppermute | solution.py:665
  537.3 27.4 %collective-permute-start.101 = (bf16[1024,512]{0,1:T(8,128)(2,1)}, bf16[1024,512]{0,1:T(8,128)(2,1)}, u32[]{:S(2)}, u32[]{:S(2)}) collective-permute-start(bf16[1024,512]{0,1:T(8,128)(2,1)} %convolution_convert_fusion.2), channel_id=1, source_target_pairs={{0,16},{16,0},{1,17},{17,1},{2,18},{18,2},{3,19},{19,3},{4,20},{20... | collective-permute-start | bytes 3145736 | tf_op jit(solution)/shard_map/ppermute | solution.py:665
  581.8 17.3 %collective-permute-start.107 = (bf16[1024,384]{0,1:T(8,128)(2,1)S(1)}, bf16[1024,384]{0,1:T(8,128)(2,1)S(1)}, u32[]{:S(2)}, u32[]{:S(2)}) collective-permute-start(bf16[1024,384]{0,1:T(8,128)(2,1)S(1)} %pad_maximum_fusion.8), channel_id=1, source_target_pairs={{0,16},{16,0},{1,17},{17,1},{2,18},{18,2},{3,19},{19,3},{4,20},{20... | collective-permute-start | bytes 2359304 | tf_op jit(solution)/shard_map/ppermute | solution.py:665
  601.6 23.1 %collective-permute-start.108 = (bf16[128,2048]{1,0:T(8,128)(2,1)S(1)}, bf16[128,2048]{1,0:T(8,128)(2,1)S(1)}, u32[]{:S(2)}, u32[]{:S(2)}) collective-permute-start(bf16[128,2048]{1,0:T(8,128)(2,1)S(1)} %copy-done.109), channel_id=1, source_target_pairs={{0,0},{1,1},{2,16},{3,17},{4,4},{5,5},{6,20},{7,21},{8,8},{9,9},{1... | collective-permute-start | bytes 1572872 | tf_op jit(solution)/shard_map/ppermute | solution.py:972
  625.1 18.2 %collective-permute-start.116 = (bf16[128,2048]{1,0:T(8,128)(2,1)S(1)}, bf16[128,2048]{1,0:T(8,128)(2,1)S(1)}, u32[]{:S(2)}, u32[]{:S(2)}) collective-permute-start(bf16[128,2048]{1,0:T(8,128)(2,1)S(1)} %pad_maximum_fusion.13), channel_id=1, source_target_pairs={{0,4},{1,5},{2,6},{3,7},{4,0},{5,1},{6,2},{7,3},{8,12},{9,13},{10,... | collective-permute-start | bytes 1572872 | tf_op jit(solution)/shard_map/ppermute | solution.py:654
  625.2 18.1 %collective-permute-start.117 = (bf16[128,2048]{1,0:T(8,128)(2,1)S(1)}, bf16[128,2048]{1,0:T(8,128)(2,1)S(1)}, u32[]{:S(2)}, u32[]{:S(2)}) collective-permute-start(bf16[128,2048]{1,0:T(8,128)(2,1)S(1)} %pad_maximum_fusion.14), channel_id=1, source_target_pairs={{0,2},{1,3},{2,0},{3,1},{4,6},{5,7},{6,4},{7,5},{8,10},{9,11},{10,... | collective-permute-start | bytes 1572872 | tf_op jit(solution)/shard_map/ppermute | solution.py:654
  644.0 20.9 %collective-permute-start.118 = (bf16[128,2048]{1,0:T(8,128)(2,1)S(1)}, bf16[128,2048]{1,0:T(8,128)(2,1)S(1)}, u32[]{:S(2)}, u32[]{:S(2)}) collective-permute-start(bf16[128,2048]{1,0:T(8,128)(2,1)S(1)} %collective-permute-done.108), channel_id=1, source_target_pairs={{0,0},{1,1},{2,2},{3,3},{4,8},{5,9},{6,10},{7,11},{8,4},{9,5},{10,... | collective-permute-start | bytes 1572872 | tf_op jit(solution)/shard_map/ppermute | solution.py:972
  646.2 18.7 %collective-permute-start.120 = (bf16[64,1536]{0,1:T(8,128)(2,1)S(1)}, bf16[64,1536]{0,1:T(8,128)(2,1)S(1)}, u32[]{:S(2)}, u32[]{:S(2)}) collective-permute-start(bf16[64,1536]{0,1:T(8,128)(2,1)S(1)} %get-tuple-element.935), channel_id=1, source_target_pairs={{0,4},{1,5},{2,6},{3,7},{4,0},{5,1},{6,2},{7,3},{8,12},{9,13},{10,... | collective-permute-start | bytes 589832 | tf_op jit(solution)/shard_map/ppermute | solution.py:654
  647.9 17.0 %collective-permute-start.121 = (bf16[64,1536]{0,1:T(8,128)(2,1)S(1)}, bf16[64,1536]{0,1:T(8,128)(2,1)S(1)}, u32[]{:S(2)}, u32[]{:S(2)}) collective-permute-start(bf16[64,1536]{0,1:T(8,128)(2,1)S(1)} %get-tuple-element.936), channel_id=1, source_target_pairs={{0,2},{1,3},{2,0},{3,1},{4,6},{5,7},{6,4},{7,5},{8,10},{9,11},{10,... | collective-permute-start | bytes 589832 | tf_op jit(solution)/shard_map/ppermute | solution.py:654
  (232 other events, 1868.5 us)
Sparse Core Ops, SparseCore 0:
  9.6 14.8 all-gather.3
  26.0 13.2 all-gather.5
  182.0 11.0 all-gather.7

commit v5 on v4

--- a/solution.py
+++ b/solution.py
@@ -16,6 +16,7 @@
 EPS = 1e-06
 THETA = 1000000.0
 MASKED = -1e30
+KEY_STEP = 1024
 BF = jnp.bfloat16
 F32 = jnp.float32
 
@@ -203,32 +204,40 @@
     )(order, *parts, own, other)
 
 
-def forward_kernel(q_ref, kv_ref, vt_ref, place_ref, low_ref, high_ref, out_ref, p_ref):
+def forward_kernel(q_ref, kv_ref, vt_ref, place_ref, low_ref, high_ref, out_ref, p_ref, sum_ref):
     count, queries = p_ref.shape
-    step = min(512, count)
-    chunks = [slice(at, at + step) for at in range(0, count, step)]
+    step = min(KEY_STEP, count)
+    part = lambda i: pl.ds(pl.multiple_of(i * step, step), step)
     q, low, high = q_ref[...], low_ref[...], high_ref[...]
-    top = jnp.full((1, queries), MASKED, F32)
-    for chunk in chunks:
-        place = place_ref[chunk, :]
+
+    def score(i, top):
+        place = place_ref[part(i), :]
         seen = (place >= low) & (place <= high)
         scores = lax.dot_general(
-            kv_ref[chunk, :HEAD_SIZE], q, (((1,), (1,)), ((), ())), preferred_element_type=F32
+            kv_ref[part(i), :HEAD_SIZE], q, (((1,), (1,)), ((), ())), preferred_element_type=F32
         )
         scores = jnp.where(seen, scores * HEAD_SIZE**-0.5, MASKED)
-        p_ref[chunk, :] = scores
-        top = jnp.maximum(top, jnp.max(scores, axis=0, keepdims=True))
-    total = jnp.zeros((1, queries), F32)
-    for chunk in chunks:
-        exponent = jnp.exp(p_ref[chunk, :] - top)
-        p_ref[chunk, :] = exponent
-        total = total + jnp.sum(exponent, axis=0, keepdims=True)
+        p_ref[part(i), :] = scores
+        return jnp.maximum(top, jnp.max(scores, axis=0, keepdims=True))
+
+    top = lax.fori_loop(0, count // step, score, jnp.full((1, queries), MASKED, F32))
+
+    def lift(i, total):
+        exponent = jnp.exp(p_ref[part(i), :] - top)
+        p_ref[part(i), :] = exponent
+        return total + jnp.sum(exponent, axis=0, keepdims=True)
+
+    total = lax.fori_loop(0, count // step, lift, jnp.zeros((1, queries), F32))
     share = 1.0 / total
-    out = jnp.zeros((HEAD_SIZE, queries), F32)
-    for chunk in chunks:
-        probs = (p_ref[chunk, :] * share).astype(BF)
-        out = out + jnp.dot(vt_ref[:, chunk], probs, preferred_element_type=F32)
-    out_ref[...] = out.T.astype(BF)
+    sum_ref[...] = jnp.zeros_like(sum_ref)
+
+    def mix(i, carry):
+        probs = (p_ref[part(i), :] * share).astype(BF)
+        sum_ref[...] += jnp.dot(vt_ref[:, part(i)], probs, preferred_element_type=F32)
+        return carry
+
+    lax.fori_loop(0, count // step, mix, 0)
+    out_ref[...] = sum_ref[...].T.astype(BF)
 
 
 def attention_blocks(rows, count):
@@ -251,7 +260,7 @@
         in_specs=[head, whole(keys_values), whole(values_turned), whole(place), along, along],
         out_specs=head,
         out_shape=jax.ShapeDtypeStruct(q.shape, BF),
-        scratch_shapes=[pltpu.VMEM((count, step), F32)],
+        scratch_shapes=[pltpu.VMEM((count, step), F32), pltpu.VMEM((HEAD_SIZE, step), F32)],
         cost_estimate=pl.CostEstimate(
             flops=8 * rows * columns * count, bytes_accessed=4 * rows * columns, transcendentals=0
         ),
@@ -261,7 +270,7 @@
 
 def backward_kernel(
     q_ref, grad_ref, proj_ref, kv_ref, kt_ref, place_ref, low_ref, high_ref, cos_ref, sin_ref,
-    gain_ref, out_ref, dkv_ref, gain_grad_ref, p_ref, dp_ref,
+    gain_ref, out_ref, dkv_ref, gain_grad_ref, p_ref, dp_ref, dq_ref,
 ):
     @pl.when((pl.program_id(0) == 0) & (pl.program_id(1) == 0))
     def _():
@@ -269,8 +278,8 @@
         gain_grad_ref[...] = jnp.zeros_like(gain_grad_ref)
 
     count, queries = p_ref.shape
-    step = min(512, count)
-    chunks = [slice(at, at + step) for at in range(0, count, step)]
+    step = min(KEY_STEP, count)
+    part = lambda i: pl.ds(pl.multiple_of(i * step, step), step)
     scale = HEAD_SIZE**-0.5
     q, grad = q_ref[...], grad_ref[...]
     low, high = low_ref[...], high_ref[...]
@@ -279,34 +288,45 @@
         dims = (((1,), (1,)), ((), ()))
         return lax.dot_general(left, right, dims, preferred_element_type=F32)
 
-    top = jnp.full((1, queries), MASKED, F32)
-    for chunk in chunks:
-        place = place_ref[chunk, :]
+    def score(i, top):
+        place = place_ref[part(i), :]
         seen = (place >= low) & (place <= high)
-        scores = jnp.where(seen, across(kv_ref[chunk, :HEAD_SIZE], q) * scale, MASKED)
-        p_ref[chunk, :] = scores
-        top = jnp.maximum(top, jnp.max(scores, axis=0, keepdims=True))
-    total = inner = jnp.zeros((1, queries), F32)
-    for chunk in chunks:
-        exponent = jnp.exp(p_ref[chunk, :] - top)
-        p_ref[chunk, :] = exponent
+        scores = jnp.where(seen, across(kv_ref[part(i), :HEAD_SIZE], q) * scale, MASKED)
+        p_ref[part(i), :] = scores
+        return jnp.maximum(top, jnp.max(scores, axis=0, keepdims=True))
+
+    top = lax.fori_loop(0, count // step, score, jnp.full((1, queries), MASKED, F32))
+
+    def lift(i, sums):
+        total, inner = sums
+        exponent = jnp.exp(p_ref[part(i), :] - top)
+        p_ref[part(i), :] = exponent
         total = total + jnp.sum(exponent, axis=0, keepdims=True)
-        prob_grad = across(kv_ref[chunk, HEAD_SIZE:], grad)
-        dp_ref[chunk, :] = prob_grad
-        inner = inner + jnp.sum(exponent * prob_grad, axis=0, keepdims=True)
+        prob_grad = across(kv_ref[part(i), HEAD_SIZE:], grad)
+        dp_ref[part(i), :] = prob_grad
+        return total, inner + jnp.sum(exponent * prob_grad, axis=0, keepdims=True)
+
+    nothing = jnp.zeros((1, queries), F32)
+    total, inner = lax.fori_loop(0, count // step, lift, (nothing, nothing))
     share = 1.0 / total
     inner = inner * share
-    dq = jnp.zeros((HEAD_SIZE, queries), F32)
-    for chunk in chunks:
-        probs = p_ref[chunk, :] * share
-        score_grad = (probs * (dp_ref[chunk, :] - inner)).astype(BF)
-        dkv_ref[chunk, HEAD_SIZE:] += jnp.dot(probs.astype(BF), grad, preferred_element_type=F32)
-        dkv_ref[chunk, :HEAD_SIZE] += (
+    dq_ref[...] = jnp.zeros_like(dq_ref)
+
+    def back(i, carry):
+        probs = p_ref[part(i), :] * share
+        score_grad = (probs * (dp_ref[part(i), :] - inner)).astype(BF)
+        dkv_ref[part(i), HEAD_SIZE:] += jnp.dot(
+            probs.astype(BF), grad, preferred_element_type=F32
+        )
+        dkv_ref[part(i), :HEAD_SIZE] += (
             jnp.dot(score_grad, q, preferred_element_type=F32) * scale
         )
-        dq = dq + jnp.dot(kt_ref[:, chunk], score_grad, preferred_element_type=F32)
+        dq_ref[...] += jnp.dot(kt_ref[:, part(i)], score_grad, preferred_element_type=F32)
+        return carry
+
+    lax.fori_loop(0, count // step, back, 0)
     out_ref[...], gain_grad = unturned(
-        dq.T * scale, proj_ref[...], cos_ref[...], sin_ref[...], gain_ref[...]
+        dq_ref[...].T * scale, proj_ref[...], cos_ref[...], sin_ref[...], gain_ref[...]
     )
     gain_grad_ref[...] += gain_grad
 
@@ -328,12 +348,69 @@
             jax.ShapeDtypeStruct(keys_values.shape, F32),
             jax.ShapeDtypeStruct(gain.shape, F32),
         ],
-        scratch_shapes=[pltpu.VMEM((count, step), F32)] * 2,
+        scratch_shapes=[pltpu.VMEM((count, step), F32)] * 2
+        + [pltpu.VMEM((HEAD_SIZE, step), F32)],
         cost_estimate=pl.CostEstimate(
             flops=10 * rows * columns * count, bytes_accessed=8 * rows * columns, transcendentals=0
         ),
-        compiler_params=pltpu.CompilerParams(vmem_limit_bytes=limit),
+        compiler_params=pltpu.CompilerParams(vmem_limit_bytes=60 * 2**20),
     )(q, grad, projected, keys_values, keys_turned, place, low, high, cosine, sine, gain)
+
+
+def pack_kernel(*refs):
+    *array_refs, out_0, out_1, out_2, out_3 = refs
+    rows = out_0.shape[0]
+    for k, out_ref in enumerate((out_0, out_1, out_2, out_3)):
+        at = 0
+        for array_ref in array_refs:
+            width = array_ref.shape[1]
+            out_ref[:, at : at + width] = array_ref[k * rows : (k + 1) * rows, :]
+            at += width
+
+
+def pack_rows(*arrays):
+    rows = arrays[0].shape[0] // 4
+    width = sum(array.shape[1] for array in arrays)
+    return pl.pallas_call(
+        pack_kernel,
+        out_shape=[jax.ShapeDtypeStruct((rows, width), BF)] * 4,
+    )(*arrays)
+
+
+def finish_kernel(ids_ref, b0, b1, b2, b3, wq_ref, wk_ref, wv_ref, *refs):
+    gq_ref, gk_ref, gv_ref, first_ref, last_ref, inner_ref = refs
+    half = QW // 2
+    lanes = first_ref.shape[1]
+    at = QW + lanes
+    first = last = 0.0
+    for k, ref in enumerate((b0, b1, b2, b3)):
+        head = ids_ref[0] ^ k
+        block = ref[...].astype(F32)
+        wide = pl.multiple_of(head * QW, QW)
+        thin = pl.multiple_of(head * HEAD_SIZE, HEAD_SIZE)
+        gq_ref[:, pl.ds(wide, half)] = block[:, :half]
+        gq_ref[:, pl.ds(wide + half, half)] = block[:, half + lanes : at]
+        gk_ref[:, pl.ds(thin, HEAD_SIZE)] = block[:, at : at + HEAD_SIZE]
+        gv_ref[:, pl.ds(thin, HEAD_SIZE)] = block[:, at + HEAD_SIZE : at + 2 * HEAD_SIZE]
+        first = first + block[:, half : half + lanes]
+        last = last + block[:, at + 2 * HEAD_SIZE :]
+    first_ref[...] = first
+    last_ref[...] = last
+    inner = 0.0
+    for w_ref, g_ref in ((wq_ref, gq_ref), (wk_ref, gk_ref), (wv_ref, gv_ref)):
+        inner = inner + jnp.sum(w_ref[...].astype(F32) * g_ref[...], axis=1, keepdims=True)
+    inner_ref[...] = jnp.broadcast_to(inner, inner_ref.shape)
+
+
+def finish(b, blocks, *weights):
+    rows = blocks[0].shape[0]
+    sums = jax.ShapeDtypeStruct((rows, 128), F32)
+    return pl.pallas_call(
+        finish_kernel,
+        in_specs=[pl.BlockSpec(memory_space=pltpu.SMEM)]
+        + [pl.BlockSpec(memory_space=pltpu.VMEM)] * 7,
+        out_shape=[jax.ShapeDtypeStruct(weight.shape, F32) for weight in weights] + [sums] * 3,
+    )(b.astype(jnp.int32)[None], *blocks, *weights)
 
 
 def choose_kernel(blocks, table_ref, piece_ref, *refs):
@@ -553,7 +630,7 @@
         self.values = {}
         self.count = 0
         self.strict = True
-        self.alone = False
+        self.alone = None
 
     def start(self, task):
         self.count += 1
@@ -562,7 +639,7 @@
 
     def until(self, *wanted):
         def waiting_now():
-            ready = [n for n in self.active if n in wanted] if self.alone else self.active
+            ready = [n for n in self.active if n in self.alone] if self.alone else self.active
             return [number for number in ready if number not in self.asked]
 
         while True:
@@ -576,7 +653,7 @@
                         del self.active[number]
             if all(number in self.values for number in wanted):
                 break
-            asked = {n: c for n, c in self.asked.items() if n in wanted or not self.alone}
+            asked = {n: c for n, c in self.asked.items() if not self.alone or n in self.alone}
             given = {number: [args for _, args in calls] for number, calls in asked.items()}
             if self.strict:
                 given = lax.optimization_barrier(given)
@@ -595,10 +672,10 @@
     def run(self, task):
         return self.until(self.start(task))
 
-    def loosely(self, *wanted, alone=False):
-        self.strict, self.alone = False, alone
+    def loosely(self, *wanted, also=None):
+        self.strict, self.alone = False, None if also is None else wanted + also
         values = self.until(*wanted)
-        self.strict, self.alone = True, False
+        self.strict, self.alone = True, None
         return values
 
 
@@ -995,7 +1072,7 @@
 
     rounds.until(exchange_task)
     found, block_hidden, qkv_pieces, _ = rounds.loosely(
-        small_task, hidden_task, qkv_task, move_task, alone=True
+        small_task, hidden_task, qkv_task, move_task, also=()
     )
     out_task = spread(gather_out())
     normalized, full_router, full_in, full_mid, head_gains = found
@@ -1169,8 +1246,12 @@
     gate_task = spread(gate_up_gradient(3))
     up_task = spread(later(1, gate_up_gradient(4)))
     down_task = spread(later(5, down_gradient()))
-    own_logits = jnp.dot(xn_two, full_router, preferred_element_type=F32)
-    own_probs = masked_softmax(own_logits, own_chooser)
+
+    def route(rows_in):
+        logits = jnp.dot(rows_in, full_router, preferred_element_type=F32)
+        return masked_softmax(logits, own_chooser)
+
+    own_probs = route(lax.optimization_barrier((xn_two, moe_grad))[0])
 
     upstream = cotangent.astype(F32)
     chosen_grad = own_probs * (
@@ -1243,10 +1324,6 @@
         grad = yield from links.block_scatter(owners_blocks(grad.astype(BF)))
         return grad.astype(BF)
 
-    def exchange_owners(grad):
-        grad = grad.reshape(4, rows, grad.shape[1])
-        return links.exchange(links.heads, [grad[k] for k in range(4)])
-
     def key_value_gradient(key_value_grad, proj_grad):
         sums = jnp.concatenate([grad_qgain, grad_kgain]).reshape(2, devices, head_part)
         sums = jnp.pad(sums, ((0, 0), (0, 0), (0, rows - head_part))).reshape(2, MODEL_WIDTH).T
@@ -1258,7 +1335,7 @@
 
         came, xn_one_grad = yield [
             (links.twin, (half(1 - links.g).astype(BF),)),
-            (input_gradient, (proj_grad, w_qkv)),
+            (lambda proj_grad: input_gradient(proj_grad, w_qkv), (proj_grad,)),
         ]
         tables["scatter"] = spread(links.head_scatter(xn_one_grad))
         grad = (half(links.g) + came.astype(F32)).astype(BF)
@@ -1270,6 +1347,7 @@
     first = jnp.concatenate([grad_router, grad_mid[:, None]], axis=1)
     first = jnp.pad(first, ((0, 0), (0, lanes - first.shape[1])))
     query_low_grads, query_tasks, key_terms, grad_qgain = [], [], None, None
+
     parts = 2
     for part in range(parts):
         got = rounds.run(
@@ -1312,7 +1390,7 @@
     key_value_task = spread(key_value_gradient(key_value_grad, proj_grad))
     one, two, three = rounds.until(*query_tasks, key_value_task)
     xn_one_grad = rounds.until(tables["scatter"])
-    query_task = spread(exchange_owners(jnp.concatenate([one, two, three], axis=1)))
+    query_task = spread(links.exchange(links.heads, pack_rows(one, two, three)))
     _, norm_one_back = jax.vjp(lambda values: rms_scale(values, full_in), x_float)
     (x_norm_grad,) = norm_one_back(xn_one_grad)
     input_grad = (x_one_grad + x_norm_grad).astype(BF)
@@ -1321,25 +1399,11 @@
         gate_task, up_task, down_task, tables["mixture"], grad_out_task, query_task
     )
     result = (x_one + mixture).astype(BF)
-    half = QW // 2
-    at = QW + lanes
-    first = sum(block[:, half : half + lanes].astype(F32) for block in owned)
-    last = sum(block[:, at + 2 * HEAD_SIZE :].astype(F32) for block in owned)
-    owned = [block.astype(F32) for block in links.natural(owned, links.b)]
-    grad_query = jnp.concatenate(
-        [part for block in owned for part in (block[:, :half], block[:, half + lanes : at])], axis=1
-    )
-    grad_key = jnp.concatenate([block[:, at : at + HEAD_SIZE] for block in owned], axis=1)
-    grad_value = jnp.concatenate(
-        [block[:, at + HEAD_SIZE : at + 2 * HEAD_SIZE] for block in owned], axis=1
-    )
+    weights = (w_query, key_projection_weight, value_projection_weight)
+    grad_query, grad_key, grad_value, first, last, inner = finish(links.b, owned, *weights)
     grad_router, grad_mid = first[:, :experts], first[:, experts]
     grad_qgain, grad_kgain = last[:head_part, 0], last[:head_part, 1]
-    grad_in = (
-        jnp.sum(w_query.astype(F32) * grad_query, axis=1)
-        + jnp.sum(key_projection_weight.astype(F32) * grad_key, axis=1)
-        + jnp.sum(value_projection_weight.astype(F32) * grad_value, axis=1)
-    ) / gain_in.astype(F32)
+    grad_in = inner[:, 0] / gain_in.astype(F32)
 
     return (
         result,

time: 697 us -> 684 us (0.981)
  waiting for transfers between devices: 187 us -> 165 us
  local copies, waits for them, and re-layouts: 111 us -> 98.3 us
  Pallas kernels: 150 us -> 161 us
  starting transfers between devices: 130 us -> 139 us
    ppermute x93, waiting for transfers between devices: 187 us -> 164 us  [flip(): return lax.ppermute(value, 'expert', [(i, i ^ mask) for i in range(self.n)])]
    unnamed x389 -> x382, local copies, waits for them, and re-layouts: 59.2 us -> 48.1 us
    ppermute x4, starting transfers between devices: 4.98 us -> 13.1 us  [moved(): lax.ppermute(value, ('dp', 'expert'), pairs_of)]
  transfers between devices with their start and end apart: 125 -> 125, of which waited for: 45 -> 46; matrix products, arithmetic and copies ran while one was open for 19% -> 20% of each run, Pallas kernels for 21% -> 22%
where the time goes in v5:
time: 684 us; the launch traced here: 674 us
  waiting for transfers between devices  165 us (24%)
  Pallas kernels  161 us (24%)
  starting transfers between devices  139 us (20%)
  local copies, waits for them, and re-layouts  98.3 us (14%)
  other arithmetic  47.1 us (7%)
  matrix products  45.5 us (7%)
  between operations  17.6 us (3%)
    ppermute x93, waiting for transfers between devices, flip(): return lax.ppermute(value, 'expert', [(i, i ^ mask) for i in range(self.n)])  164 us
    ppermute x93, starting transfers between devices, flip(): return lax.ppermute(value, 'expert', [(i, i ^ mask) for i in range(self.n)])  110 us
    unnamed x382, local copies, waits for them, and re-layouts  48.1 us
    pallas_call x4, Pallas kernels, expert_rows(): pl.pallas_call(lambda *refs: expert_kernel(blocks, *refs), grid=(ff // st...  45.1 us
    pallas_call x2, Pallas kernels, attention_backward(): pl.pallas_call(backward_kernel, grid=(columns // HEAD_SIZE, rows // step)...  44.9 us
    dot_general x12, matrix products, by_rows(): jnp.einsum('rd,rf->df', rows_in, grads_in, preferred_element_type=F32)  36 us
    pallas_call x2, Pallas kernels, attention_forward(): pl.pallas_call(forward_kernel, grid=(columns // HEAD_SIZE, rows // step),...  20.7 us
    ppermute x12, starting transfers between devices, shift(): lax.ppermute(value, 'expert', [(i, (i + step * 4) % self.n) for i in rang...  14.8 us
  transfers between devices with their start and end apart: 125, of which 46 were waited for; matrix products, arithmetic and copies ran while one was open for 20% of the time, Pallas kernels for 22%

profile of v5, /device:TPU:0, one launch (start us, length us, event | category | flops | bytes accessed | tf_op | source)
XLA Modules:
  0.0 673.6 jit_solution(363479050110211043)
XLA Ops:
  13.7 6.1 collective-permute-start
  28.1 2.8 collective-permute-start.7
  38.4 5.3 collective-permute-start.6
  47.8 7.1 %collective-permute-done.12 = bf16[160,1280]{1,0:T(8,128)(2,1)} collective-permute-done((bf16[160,1280]{1,0:T(8,128)(2,1)}, bf16[160,1280]{1,0:T(8,128)(2,1)}, u32[]{:S(2)}, u32[]{:S(2)}) %collective-permute-start.12) | collective-permute-done | bytes 409632 | tf_op jit(solution)/shard_map/ppermute | solution.py:731
  65.1 3.0 collective-permute-start.5
  68.1 2.7 collective-permute-done.10
  72.1 14.1 %collective-permute-done.5 = bf16[160,1280]{1,0:T(8,128)(2,1)S(1)} collective-permute-done((bf16[160,1280]{1,0:T(8,128)(2,1)S(1)}, bf16[160,1280]{1,0:T(8,128)(2,1)S(1)}, u32[]{:S(2)}, u32[]{:S(2)}) %collective-permute-start.5) | collective-permute-done | bytes 409632 | tf_op jit(solution)/shard_map/ppermute | solution.py:731
  89.4 5.7 collective-permute-done.14
  102.6 11.4 %shard_map.282 = (bf16[2048,1280]{1,0:T(8,128)(2,1)}, f32[512,1280]{1,0:T(8,128)}, bf16[512,1280]{1,0:T(8,128)(2,1)}) custom-call(s32[32]{0:T(128)} %add_multiply_fusion.1.starts_ref, bf16[512,2048]{1,0:T(8,128)(2,1)} %fusion.2.x_ref, f32[512,128]{1,0:T(8,128)} %get-tuple-element.503.cos_ref, f32[512,128]{1,0:T(8,128)} %get-tuple-element.504.sin_ref, ...), custom_call_target="tpu_custom_call" | custom-call | flops 2684354560 | bytes 7340032 | tf_op jit(solution)/shard_map/pallas_call | solution.py:85
  116.0 2.6 copy.135
  123.2 3.7 shard_map.283
  128.0 7.7 %collective-permute-done.22 = bf16[512,256]{0,1:T(8,128)(2,1)} collective-permute-done((bf16[512,256]{0,1:T(8,128)(2,1)S(1)}, bf16[512,256]{0,1:T(8,128)(2,1)}, u32[]{:S(2)}, u32[]{:S(2)}) %collective-permute-start.22) | collective-permute-done | bytes 262176 | tf_op jit(solution)/shard_map/ppermute | solution.py:731
  141.4 7.2 %collective-permute-done.23 = bf16[64,2048]{1,0:T(8,128)(2,1)S(1)} collective-permute-done((bf16[64,2048]{1,0:T(8,128)(2,1)S(1)}, bf16[64,2048]{1,0:T(8,128)(2,1)S(1)}, u32[]{:S(2)}, u32[]{:S(2)}) %collective-permute-start.23) | collective-permute-done | bytes 262176 | tf_op jit(solution)/shard_map/ppermute | solution.py:731
  160.7 10.4 %shard_map.285.refs_0_ = bf16[512,512]{1,0:T(8,128)(2,1)S(1)} custom-call(bf16[512,512]{1,0:T(8,128)(2,1)S(1)} %copy-done.8, bf16[2048,256]{1,0:T(8,128)(2,1)S(1)} %copy.136.kv_ref, bf16[128,2048]{1,0:T(8,128)(2,1)S(1)} %get-tuple-element.1105.vt_ref, s32[2048,1]{1,0:T(8,128)S(1)} %copy.137.place_ref, s32[1,512]{1,0:T(1,128)S(1)} %bitcast.153, ...), custom_call_target="tpu_custom_call" | custom-call | flops 4294967296 | bytes 1048576 | tf_op jit(solution)/shard_map/pallas_call | solution.py:257
  186.0 10.4 %shard_map.287.refs_1_ = bf16[512,512]{1,0:T(8,128)(2,1)S(1)} custom-call(bf16[512,512]{1,0:T(8,128)(2,1)S(1)} %copy-done.7, bf16[2048,256]{1,0:T(8,128)(2,1)S(1)} %copy.136.kv_ref, bf16[128,2048]{1,0:T(8,128)(2,1)S(1)} %copy-done.10, s32[2048,1]{1,0:T(8,128)S(1)} %copy.137.place_ref, s32[1,512]{1,0:T(1,128)S(1)} %bitcast.154, s32[1,512]{1,0:T(1,128)S(1)} %bitcast.158), custom_call_target="tpu_custom_call" | custom-call | flops 4294967296 | bytes 1048576 | tf_op jit(solution)/shard_map/pallas_call | solution.py:257
  199.1 2.8 collective-permute-start.36
  207.1 3.1 fusion.97
  210.2 7.1 %shard_map.289 = (f32[512,2048]{1,0:T(8,128)S(1)}, bf16[512,1024]{1,0:T(8,128)(2,1)S(1)}) custom-call(s32[8]{0:T(128)S(1)} %stack.190.order_ref, bf16[512,512]{1,0:T(8,128)(2,1)S(1)} %copy-done.60, bf16[512,512]{1,0:T(8,128)(2,1)S(1)} %copy-done.62, bf16[512,2048]{1,0:T(8,128)(2,1)} %constant_dynamic-update-slice_fusion.11.refs_2_, ...), custom_call_target="tpu_custom_call" | custom-call | flops 2147483648 | bytes 12582912 | tf_op jit(solution)/shard_map/pallas_call | solution.py:186
  222.1 3.1 collective-permute-done.40
  231.2 2.6 collective-permute-start.63
  237.4 10.5 %collective-permute-done.43 = bf16[128,2048]{1,0:T(8,128)(2,1)S(1)} collective-permute-done((bf16[128,2048]{1,0:T(8,128)(2,1)S(1)}, bf16[128,2048]{1,0:T(8,128)(2,1)S(1)}, u32[]{:S(2)}, u32[]{:S(2)}) %collective-permute-start.43) | collective-permute-done | bytes 524320 | tf_op jit(solution)/shard_map/ppermute | solution.py:731
  254.1 2.6 collective-permute-start.46
  257.3 3.0 collective-permute-done.44.refs_2_
  260.7 3.1 collective-permute-done.46.refs_4_
  274.6 11.3 %shard_map.292 = (bf16[72,2176]{1,0:T(8,128)(2,1)S(1)}, bf16[72,2176]{1,0:T(8,128)(2,1)S(1)}, bf16[72,2176]{1,0:T(8,128)(2,1)S(1)}, bf16[72,2176]{1,0:T(8,128)(2...) custom-call(s32[1]{0:T(128)} %bitcast.68.refs_0_, ...), custom_call_target="tpu_custom_call" | custom-call | flops 5435817984 | bytes 9437184 | tf_op jit(solution)/shard_map/pallas_call | solution.py:537
  297.3 11.3 %shard_map.294 = (bf16[72,2176]{1,0:T(8,128)(2,1)S(1)}, bf16[72,2176]{1,0:T(8,128)(2,1)S(1)}, bf16[72,2176]{1,0:T(8,128)(2,1)S(1)}, bf16[72,2176]{1,0:T(8,128)(2...) custom-call(s32[1]{0:T(128)} %bitcast.68.refs_0_, ...), custom_call_target="tpu_custom_call" | custom-call | flops 5435817984 | bytes 9437184 | tf_op jit(solution)/shard_map/pallas_call | solution.py:537
  309.4 3.9 collective-permute-done.54.refs_4_
  315.1 3.2 collective-permute-start.57
  323.2 11.6 %shard_map.296 = (bf16[72,2176]{1,0:T(8,128)(2,1)S(1)}, bf16[72,2176]{1,0:T(8,128)(2,1)}, bf16[72,2176]{1,0:T(8,128)(2,1)}, bf16[72,2176]{1,0:T(8,128)(2,1)S(1)}...) custom-call(s32[1]{0:T(128)} %bitcast.68.refs_0_, ...), custom_call_target="tpu_custom_call" | custom-call | flops 5435817984 | bytes 9437184 | tf_op jit(solution)/shard_map/pallas_call | solution.py:537
  334.8 5.1 collective-permute-done.58.refs_4_
  346.9 10.9 %shard_map.299 = (bf16[72,2176]{1,0:T(8,128)(2,1)S(1)}, bf16[72,2176]{1,0:T(8,128)(2,1)S(1)}, bf16[72,2176]{1,0:T(8,128)(2,1)S(1)}, bf16[72,2176]{1,0:T(8,128)(2...) custom-call(s32[1]{0:T(128)} %bitcast.68.refs_0_, ...), custom_call_target="tpu_custom_call" | custom-call | flops 5435817984 | bytes 9437184 | tf_op jit(solution)/shard_map/pallas_call | solution.py:537
  368.4 3.2 collective-permute-done.66.refs_2_
  371.7 5.5 collective-permute-done.67.refs_3_
  378.6 3.9 collective-permute-start.70
  389.3 4.0 collective-permute-done.72.refs_3_
  396.9 2.8 constant_dynamic-slice_fusion.20
  401.3 4.3 collective-permute-done.75
  409.0 3.0 collective-permute-done.77
  419.6 2.9 convolution_convert_fusion.6
  422.5 2.9 convolution_convert_fusion.5
  429.2 6.6 collective-permute-done.82.refs_4_
  446.2 22.5 %shard_map.305 = (bf16[512,512]{1,0:T(8,128)(2,1)}, f32[2048,256]{1,0:T(8,128)}, f32[1,128]{1,0:T(1,128)}) custom-call(bf16[512,512]{1,0:T(8,128)(2,1)} %get-tuple-element.802.q_ref, bf16[512,512]{1,0:T(8,128)(2,1)} %get-tuple-element.803.grad_ref, f32[512,512]{1,0:T(8,128)} %get-tuple-element.804.proj_ref, bf16[2048,256]{1,0:T(8,128)(2,1)} %copy-done.6, ...), custom_call_target="tpu_custom_call" | custom-call | flops 5368709120 | bytes 2097152 | tf_op jit(solution)/shard_map/pallas_call | solution.py:340
  479.9 22.5 %shard_map.307 = (bf16[512,512]{1,0:T(8,128)(2,1)}, f32[2048,256]{1,0:T(8,128)}, f32[1,128]{1,0:T(1,128)}) custom-call(bf16[512,512]{1,0:T(8,128)(2,1)} %get-tuple-element.827.q_ref, bf16[512,512]{1,0:T(8,128)(2,1)} %get-tuple-element.828.grad_ref, f32[512,512]{1,0:T(8,128)} %get-tuple-element.829.proj_ref, bf16[2048,256]{1,0:T(8,128)(2,1)} %copy-done.6, ...), custom_call_target="tpu_custom_call" | custom-call | flops 5368709120 | bytes 2097152 | tf_op jit(solution)/shard_map/pallas_call | solution.py:340
  514.0 5.0 convolution_convert_fusion.1
  522.4 3.0 collective-permute-done.96
  525.5 4.0 collective-permute-done.98
  540.0 3.4 constant_dynamic-slice_fusion.45
  547.3 3.4 fusion.22
  550.7 8.6 %collective-permute-done.102 = bf16[512,256]{1,0:T(8,128)(2,1)S(1)} collective-permute-done((bf16[512,256]{1,0:T(8,128)(2,1)}, bf16[512,256]{1,0:T(8,128)(2,1)S(1)}, u32[]{:S(2)}, u32[]{:S(2)}) %collective-permute-start.102) | collective-permute-done | bytes 262176 | tf_op jit(solution)/shard_map/ppermute | solution.py:731
  564.5 2.8 fusion.19
  575.9 4.3 convert_add_fusion.2
  580.2 4.6 shard_map.310
  584.8 4.7 collective-permute-done.106
  595.4 2.9 collective-permute-start.112
  599.6 4.1 convert_add_fusion.1
  603.6 3.5 collective-permute-done.111
  610.2 6.1 collective-permute-done.113
  620.1 5.3 convert_add_fusion
  626.2 7.0 %collective-permute-done.115 = bf16[256,384]{1,0:T(8,128)(2,1)S(1)} collective-permute-done((bf16[256,384]{1,0:T(8,128)(2,1)S(1)}, bf16[256,384]{1,0:T(8,128)(2,1)S(1)}, u32[]{:S(2)}, u32[]{:S(2)}) %collective-permute-start.115) | collective-permute-done | bytes 196640 | tf_op jit(solution)/shard_map/ppermute | solution.py:731
  639.1 5.5 collective-permute-start.118
  644.7 3.5 collective-permute-start.121
  650.2 2.9 fusion.16
  653.7 2.5 collective-permute-done.121.b2
  656.2 2.6 shard_map.312
  (805 shorter events, 286.9 us)
Async XLA Ops:
  7.2 264.2 %all-gather.4.cloned.1.call-start = ((), (), s32[]{:S(2)}) async-start(), calls=%async_computation | async-start | bytes 4718592 | tf_op jit(solution)/shard_map/all_gather | solution.py:879
  7.9 263.5 %all-gather.6.cloned.1.call-start = ((), (), s32[]{:S(2)}) async-start(), calls=%async_computation.1 | async-start | bytes 4718592 | tf_op jit(solution)/shard_map/all_gather | solution.py:880
  20.4 251.0 %all-gather.8.cloned.1.call-start = ((), (), s32[]{:S(2)}) async-start(), calls=%async_computation.2 | async-start | bytes 4718592 | tf_op jit(solution)/shard_map/all_gather | solution.py:881
  28.1 26.8 %collective-permute-start.7 = (bf16[128,2048]{1,0:T(8,128)(2,1)S(1)}, bf16[128,2048]{1,0:T(8,128)(2,1)}, u32[]{:S(2)}, u32[]{:S(2)}) collective-permute-start(bf16[128,2048]{1,0:T(8,128)(2,1)S(1)} %copy-done.74), channel_id=1, source_target_pairs={{0,4},{1,5},{2,6},{3,7},{4,0},{5,1},{6,2},{7,3},{8,12},{9,13},{10,... | collective-permute-start | bytes 1572872 | tf_op jit(solution)/shard_map/ppermute | solution.py:731
  34.9 20.1 %collective-permute-start.12 = (bf16[160,1280]{1,0:T(8,128)(2,1)}, bf16[160,1280]{1,0:T(8,128)(2,1)}, u32[]{:S(2)}, u32[]{:S(2)}) collective-permute-start(bf16[160,1280]{1,0:T(8,128)(2,1)} %slice.426), channel_id=1, source_target_pairs={{0,8},{1,9},{2,10},{3,11},{4,12},{5,13},{6,14},{7,15},{8,0},{9,1},... | collective-permute-start | bytes 1228808 | tf_op jit(solution)/shard_map/ppermute | solution.py:731
  36.9 21.6 %collective-permute-start.8 = (bf16[128,2048]{1,0:T(8,128)(2,1)S(1)}, bf16[128,2048]{1,0:T(8,128)(2,1)}, u32[]{:S(2)}, u32[]{:S(2)}) collective-permute-start(bf16[128,2048]{1,0:T(8,128)(2,1)S(1)} %copy-done.74), channel_id=1, source_target_pairs={{0,2},{1,3},{2,0},{3,1},{4,6},{5,7},{6,4},{7,5},{8,10},{9,11},{10,... | collective-permute-start | bytes 1572872 | tf_op jit(solution)/shard_map/ppermute | solution.py:731
  38.4 22.7 %collective-permute-start.6 = (bf16[128,2048]{1,0:T(8,128)(2,1)}, bf16[128,2048]{1,0:T(8,128)(2,1)}, u32[]{:S(2)}, u32[]{:S(2)}) collective-permute-start(bf16[128,2048]{1,0:T(8,128)(2,1)} %collective-permute-done.3), channel_id=1, source_target_pairs={{0,0},{1,1},{2,16},{3,17},{4,4},{5,5},{6,20},{7,21},{8,8},{9,9},{1... | collective-permute-start | bytes 1572872 | tf_op jit(solution)/shard_map/ppermute | solution.py:1049
  44.4 19.8 %collective-permute-start.4 = (bf16[288,1280]{1,0:T(8,128)(2,1)}, bf16[288,1280]{1,0:T(8,128)(2,1)}, u32[]{:S(2)}, u32[]{:S(2)}) collective-permute-start(bf16[288,1280]{1,0:T(8,128)(2,1)} %shard_map.281.refs_0_), channel_id=1, source_target_pairs={{0,1},{1,0},{2,3},{3,2},{4,5},{5,4},{6,7},{7,6},{8,9},{9,8},{10,11... | collective-permute-start | bytes 2211848 | tf_op jit(solution)/shard_map/ppermute | solution.py:731
  54.9 43.7 %collective-permute-start.15 = (bf16[288,1280]{1,0:T(8,128)(2,1)}, bf16[288,1280]{1,0:T(8,128)(2,1)}, u32[]{:S(2)}, u32[]{:S(2)}) collective-permute-start(bf16[288,1280]{1,0:T(8,128)(2,1)} %shard_map.281.refs_0_), channel_id=1, source_target_pairs={{0,16},{16,0},{1,17},{17,1},{2,18},{18,2},{3,19},{19,3},{4,20},{20... | collective-permute-start | bytes 2211848 | tf_op jit(solution)/shard_map/ppermute | solution.py:742
  65.1 21.1 %collective-permute-start.5 = (bf16[160,1280]{1,0:T(8,128)(2,1)S(1)}, bf16[160,1280]{1,0:T(8,128)(2,1)S(1)}, u32[]{:S(2)}, u32[]{:S(2)}) collective-permute-start(bf16[160,1280]{1,0:T(8,128)(2,1)S(1)} %pad_maximum_fusion.14), channel_id=1, source_target_pairs={{0,8},{1,9},{2,10},{3,11},{4,12},{5,13},{6,14},{7,15},{8,0},{9,1},... | collective-permute-start | bytes 1228808 | tf_op jit(solution)/shard_map/ppermute | solution.py:731
  68.1 30.6 %collective-permute-start.16 = (bf16[288,1280]{1,0:T(8,128)(2,1)}, bf16[288,1280]{1,0:T(8,128)(2,1)}, u32[]{:S(2)}, u32[]{:S(2)}) collective-permute-start(bf16[288,1280]{1,0:T(8,128)(2,1)} %collective-permute-done.4.refs_1_), channel_id=1, source_target_pairs={{0,16},{16,0},{1,17},{17,1},{2,18},{18,2},{3,19},{19,3},{4,20},{20... | collective-permute-start | bytes 2211848 | tf_op jit(solution)/shard_map/ppermute | solution.py:742
  98.7 16.6 %collective-permute-start.19 = (bf16[128,2048]{1,0:T(8,128)(2,1)}, bf16[128,2048]{1,0:T(8,128)(2,1)S(1)}, u32[]{:S(2)}, u32[]{:S(2)}) collective-permute-start(bf16[128,2048]{1,0:T(8,128)(2,1)} %collective-permute-done.6), channel_id=1, source_target_pairs={{0,1},{1,0},{2,3},{3,2},{4,5},{5,4},{6,7},{7,6},{8,9},{9,8},{10,11... | collective-permute-start | bytes 1572872 | tf_op jit(solution)/shard_map/ppermute | solution.py:731
  153.1 21.5 %collective-permute-start.26 = (bf16[128,2048]{1,0:T(8,128)(2,1)S(1)}, bf16[128,2048]{1,0:T(8,128)(2,1)}, u32[]{:S(2)}, u32[]{:S(2)}) collective-permute-start(bf16[128,2048]{1,0:T(8,128)(2,1)S(1)} %copy-done.3), channel_id=1, source_target_pairs={{0,4},{1,5},{2,6},{3,7},{4,8},{5,9},{6,10},{7,11},{8,12},{9,13},{1... | collective-permute-start | bytes 1572872 | tf_op jit(solution)/shard_map/ppermute | solution.py:734
  154.6 19.9 %collective-permute-start.27 = (bf16[72,2048]{1,0:T(8,128)(2,1)}, bf16[72,2048]{1,0:T(8,128)(2,1)S(1)}, u32[]{:S(2)}, u32[]{:S(2)}) collective-permute-start(bf16[72,2048]{1,0:T(8,128)(2,1)} %copy-done.58), channel_id=1, source_target_pairs={{0,1},{1,0},{2,3},{3,2},{4,5},{5,4},{6,7},{7,6},{8,9},{9,8},{10,11... | collective-permute-start | bytes 884744 | tf_op jit(solution)/shard_map/ppermute | solution.py:731
  155.1 19.4 %collective-permute-start.28 = (bf16[72,2048]{1,0:T(8,128)(2,1)}, bf16[72,2048]{1,0:T(8,128)(2,1)S(1)}, u32[]{:S(2)}, u32[]{:S(2)}) collective-permute-start(bf16[72,2048]{1,0:T(8,128)(2,1)} %copy-done.57), channel_id=1, source_target_pairs={{0,2},{1,3},{2,0},{3,1},{4,6},{5,7},{6,4},{7,5},{8,10},{9,11},{10,... | collective-permute-start | bytes 884744 | tf_op jit(solution)/shard_map/ppermute | solution.py:731
  155.6 18.9 %collective-permute-start.29 = (bf16[72,2048]{1,0:T(8,128)(2,1)S(1)}, bf16[72,2048]{1,0:T(8,128)(2,1)S(1)}, u32[]{:S(2)}, u32[]{:S(2)}) collective-permute-start(bf16[72,2048]{1,0:T(8,128)(2,1)S(1)} %get-tuple-element.541), channel_id=1, source_target_pairs={{0,3},{1,2},{2,1},{3,0},{4,7},{5,6},{6,5},{7,4},{8,11},{9,10},{10,... | collective-permute-start | bytes 884744 | tf_op jit(solution)/shard_map/ppermute | solution.py:731
  158.0 16.4 %collective-permute-start.30 = (bf16[64,2048]{1,0:T(8,128)(2,1)}, bf16[64,2048]{1,0:T(8,128)(2,1)S(1)}, u32[]{:S(2)}, u32[]{:S(2)}) collective-permute-start(bf16[64,2048]{1,0:T(8,128)(2,1)} %copy-done.131), channel_id=1, source_target_pairs={{0,1},{1,0},{2,3},{3,2},{4,5},{5,4},{6,7},{7,6},{8,9},{9,8},{10,11... | collective-permute-start | bytes 786440 | tf_op jit(solution)/shard_map/ppermute | solution.py:731
  179.2 17.3 %collective-permute-start.35 = (bf16[512,2048]{1,0:T(8,128)(2,1)}, bf16[512,2048]{1,0:T(8,128)(2,1)}, u32[]{:S(2)}, u32[]{:S(2)}) collective-permute-start(bf16[512,2048]{1,0:T(8,128)(2,1)} %constant_dynamic-update-slice_fusion.11.refs_2_), channel_id=1, source_target_pairs={{0,16},{16,0},{1,17},{17,1},{2,18},{18,2},{3,19},{19,3},{4,20},{20... | collective-permute-start | bytes 6291464 | tf_op jit(solution)/shard_map/ppermute | solution.py:742
  179.3 17.2 %collective-permute-start.31 = (bf16[128,2048]{1,0:T(8,128)(2,1)}, bf16[128,2048]{1,0:T(8,128)(2,1)}, u32[]{:S(2)}, u32[]{:S(2)}) collective-permute-start(bf16[128,2048]{1,0:T(8,128)(2,1)} %collective-permute-done.26.refs_1_), channel_id=1, source_target_pairs={{0,4},{1,5},{2,6},{3,7},{4,8},{5,9},{6,10},{7,11},{8,12},{9,13},{1... | collective-permute-start | bytes 1572872 | tf_op jit(solution)/shard_map/ppermute | solution.py:734
  199.1 19.2 %collective-permute-start.36 = (bf16[128,2048]{1,0:T(8,128)(2,1)}, bf16[128,2048]{1,0:T(8,128)(2,1)S(1)}, u32[]{:S(2)}, u32[]{:S(2)}) collective-permute-start(bf16[128,2048]{1,0:T(8,128)(2,1)} %collective-permute-done.31.refs_1_), channel_id=1, source_target_pairs={{0,4},{1,5},{2,6},{3,7},{4,8},{5,9},{6,10},{7,11},{8,12},{9,13},{1... | collective-permute-start | bytes 1572872 | tf_op jit(solution)/shard_map/ppermute | solution.py:734
  228.1 19.8 %collective-permute-start.43 = (bf16[128,2048]{1,0:T(8,128)(2,1)S(1)}, bf16[128,2048]{1,0:T(8,128)(2,1)S(1)}, u32[]{:S(2)}, u32[]{:S(2)}) collective-permute-start(bf16[128,2048]{1,0:T(8,128)(2,1)S(1)} %pad_maximum_fusion.11), channel_id=1, source_target_pairs={{0,2},{1,3},{2,0},{3,1},{4,6},{5,7},{6,4},{7,5},{8,10},{9,11},{10,... | collective-permute-start | bytes 1572872 | tf_op jit(solution)/shard_map/ppermute | solution.py:731
  231.2 21.0 %collective-permute-start.63 = (bf16[72,2048]{1,0:T(8,128)(2,1)S(1)}, bf16[72,2048]{1,0:T(8,128)(2,1)S(1)}, u32[]{:S(2)}, u32[]{:S(2)}) collective-permute-start(bf16[72,2048]{1,0:T(8,128)(2,1)S(1)} %get-tuple-element.708), channel_id=1, source_target_pairs={{0,1},{1,0},{2,3},{3,2},{4,5},{5,4},{6,7},{7,6},{8,9},{9,8},{10,11... | collective-permute-start | bytes 884744 | tf_op jit(solution)/shard_map/ppermute | solution.py:731
  233.7 18.4 %collective-permute-start.64 = (bf16[72,2048]{1,0:T(8,128)(2,1)S(1)}, bf16[72,2048]{1,0:T(8,128)(2,1)S(1)}, u32[]{:S(2)}, u32[]{:S(2)}) collective-permute-start(bf16[72,2048]{1,0:T(8,128)(2,1)S(1)} %get-tuple-element.709), channel_id=1, source_target_pairs={{0,2},{1,3},{2,0},{3,1},{4,6},{5,7},{6,4},{7,5},{8,10},{9,11},{10,... | collective-permute-start | bytes 884744 | tf_op jit(solution)/shard_map/ppermute | solution.py:731
  233.8 18.3 %collective-permute-start.65 = (bf16[72,2048]{1,0:T(8,128)(2,1)S(1)}, bf16[72,2048]{1,0:T(8,128)(2,1)S(1)}, u32[]{:S(2)}, u32[]{:S(2)}) collective-permute-start(bf16[72,2048]{1,0:T(8,128)(2,1)S(1)} %get-tuple-element.710), channel_id=1, source_target_pairs={{0,3},{1,2},{2,1},{3,0},{4,7},{5,6},{6,5},{7,4},{8,11},{9,10},{10,... | collective-permute-start | bytes 884744 | tf_op jit(solution)/shard_map/ppermute | solution.py:731
  267.0 19.0 %collective-permute-start.51 = (bf16[128,2048]{1,0:T(8,128)(2,1)}, bf16[128,2048]{1,0:T(8,128)(2,1)}, u32[]{:S(2)}, u32[]{:S(2)}) collective-permute-start(bf16[128,2048]{1,0:T(8,128)(2,1)} %collective-permute-done.47.refs_1_), channel_id=1, source_target_pairs={{0,4},{1,5},{2,6},{3,7},{4,8},{5,9},{6,10},{7,11},{8,12},{9,13},{1... | collective-permute-start | bytes 1572872 | tf_op jit(solution)/shard_map/ppermute | solution.py:734
  267.9 18.0 %collective-permute-start.48 = (bf16[72,2048]{1,0:T(8,128)(2,1)}, bf16[72,2048]{1,0:T(8,128)(2,1)}, u32[]{:S(2)}, u32[]{:S(2)}) collective-permute-start(bf16[72,2048]{1,0:T(8,128)(2,1)} %get-tuple-element.591), channel_id=1, source_target_pairs={{0,1},{1,0},{2,3},{3,2},{4,5},{5,4},{6,7},{7,6},{8,9},{9,8},{10,11... | collective-permute-start | bytes 884744 | tf_op jit(solution)/shard_map/ppermute | solution.py:731
  269.2 16.7 %collective-permute-start.49 = (bf16[72,2048]{1,0:T(8,128)(2,1)}, bf16[72,2048]{1,0:T(8,128)(2,1)}, u32[]{:S(2)}, u32[]{:S(2)}) collective-permute-start(bf16[72,2048]{1,0:T(8,128)(2,1)} %get-tuple-element.592), channel_id=1, source_target_pairs={{0,2},{1,3},{2,0},{3,1},{4,6},{5,7},{6,4},{7,5},{8,10},{9,11},{10,... | collective-permute-start | bytes 884744 | tf_op jit(solution)/shard_map/ppermute | solution.py:731
  287.9 21.6 %collective-permute-start.52 = (bf16[72,4224]{1,0:T(8,128)(2,1)S(1)}, bf16[72,4224]{1,0:T(8,128)(2,1)S(1)}, u32[]{:S(2)}, u32[]{:S(2)}) collective-permute-start(bf16[72,4224]{1,0:T(8,128)(2,1)S(1)} %get-tuple-element.630), channel_id=1, source_target_pairs={{0,1},{1,0},{2,3},{3,2},{4,5},{5,4},{6,7},{7,6},{8,9},{9,8},{10,11... | collective-permute-start | bytes 1824776 | tf_op jit(solution)/shard_map/ppermute | solution.py:731
  289.2 20.2 %collective-permute-start.53 = (bf16[72,4224]{1,0:T(8,128)(2,1)S(1)}, bf16[72,4224]{1,0:T(8,128)(2,1)S(1)}, u32[]{:S(2)}, u32[]{:S(2)}) collective-permute-start(bf16[72,4224]{1,0:T(8,128)(2,1)S(1)} %get-tuple-element.631), channel_id=1, source_target_pairs={{0,2},{1,3},{2,0},{3,1},{4,6},{5,7},{6,4},{7,5},{8,10},{9,11},{10,... | collective-permute-start | bytes 1824776 | tf_op jit(solution)/shard_map/ppermute | solution.py:731
  290.3 23.0 %collective-permute-start.54 = (bf16[72,4224]{1,0:T(8,128)(2,1)S(1)}, bf16[72,4224]{1,0:T(8,128)(2,1)S(1)}, u32[]{:S(2)}, u32[]{:S(2)}) collective-permute-start(bf16[72,4224]{1,0:T(8,128)(2,1)S(1)} %get-tuple-element.632), channel_id=1, source_target_pairs={{0,3},{1,2},{2,1},{3,0},{4,7},{5,6},{6,5},{7,4},{8,11},{9,10},{10,... | collective-permute-start | bytes 1824776 | tf_op jit(solution)/shard_map/ppermute | solution.py:731
  291.4 18.0 %collective-permute-start.55 = (bf16[128,2048]{1,0:T(8,128)(2,1)}, bf16[128,2048]{1,0:T(8,128)(2,1)S(1)}, u32[]{:S(2)}, u32[]{:S(2)}) collective-permute-start(bf16[128,2048]{1,0:T(8,128)(2,1)} %collective-permute-done.51.refs_1_), channel_id=1, source_target_pairs={{0,4},{1,5},{2,6},{3,7},{4,8},{5,9},{6,10},{7,11},{8,12},{9,13},{1... | collective-permute-start | bytes 1572872 | tf_op jit(solution)/shard_map/ppermute | solution.py:734
  314.4 20.4 %collective-permute-start.56 = (bf16[72,4224]{1,0:T(8,128)(2,1)S(1)}, bf16[72,4224]{1,0:T(8,128)(2,1)S(1)}, u32[]{:S(2)}, u32[]{:S(2)}) collective-permute-start(bf16[72,4224]{1,0:T(8,128)(2,1)S(1)} %get-tuple-element.667), channel_id=1, source_target_pairs={{0,1},{1,0},{2,3},{3,2},{4,5},{5,4},{6,7},{7,6},{8,9},{9,8},{10,11... | collective-permute-start | bytes 1824776 | tf_op jit(solution)/shard_map/ppermute | solution.py:731
  315.1 19.7 %collective-permute-start.57 = (bf16[72,4224]{1,0:T(8,128)(2,1)S(1)}, bf16[72,4224]{1,0:T(8,128)(2,1)S(1)}, u32[]{:S(2)}, u32[]{:S(2)}) collective-permute-start(bf16[72,4224]{1,0:T(8,128)(2,1)S(1)} %get-tuple-element.668), channel_id=1, source_target_pairs={{0,2},{1,3},{2,0},{3,1},{4,6},{5,7},{6,4},{7,5},{8,10},{9,11},{10,... | collective-permute-start | bytes 1824776 | tf_op jit(solution)/shard_map/ppermute | solution.py:731
  318.4 21.6 %collective-permute-start.58 = (bf16[72,4224]{1,0:T(8,128)(2,1)S(1)}, bf16[72,4224]{1,0:T(8,128)(2,1)S(1)}, u32[]{:S(2)}, u32[]{:S(2)}) collective-permute-start(bf16[72,4224]{1,0:T(8,128)(2,1)S(1)} %get-tuple-element.669), channel_id=1, source_target_pairs={{0,3},{1,2},{2,1},{3,0},{4,7},{5,6},{6,5},{7,4},{8,11},{9,10},{10,... | collective-permute-start | bytes 1824776 | tf_op jit(solution)/shard_map/ppermute | solution.py:731
  340.4 20.4 %collective-permute-start.62 = (bf16[128,2176]{1,0:T(8,128)(2,1)S(1)}, bf16[128,2176]{1,0:T(8,128)(2,1)S(1)}, u32[]{:S(2)}, u32[]{:S(2)}) collective-permute-start(bf16[128,2176]{1,0:T(8,128)(2,1)S(1)} %shard_map.297), channel_id=1, source_target_pairs={{0,4},{1,5},{2,6},{3,7},{4,8},{5,9},{6,10},{7,11},{8,12},{9,13},{1... | collective-permute-start | bytes 1671176 | tf_op jit(solution)/shard_map/ppermute | solution.py:734
  340.7 20.2 %collective-permute-start.59 = (bf16[72,2176]{1,0:T(8,128)(2,1)}, bf16[72,2176]{1,0:T(8,128)(2,1)S(1)}, u32[]{:S(2)}, u32[]{:S(2)}) collective-permute-start(bf16[72,2176]{1,0:T(8,128)(2,1)} %get-tuple-element.698), channel_id=1, source_target_pairs={{0,1},{1,0},{2,3},{3,2},{4,5},{5,4},{6,7},{7,6},{8,9},{9,8},{10,11... | collective-permute-start | bytes 940040 | tf_op jit(solution)/shard_map/ppermute | solution.py:731
  342.2 18.6 %collective-permute-start.60 = (bf16[72,2176]{1,0:T(8,128)(2,1)}, bf16[72,2176]{1,0:T(8,128)(2,1)S(1)}, u32[]{:S(2)}, u32[]{:S(2)}) collective-permute-start(bf16[72,2176]{1,0:T(8,128)(2,1)} %get-tuple-element.699), channel_id=1, source_target_pairs={{0,2},{1,3},{2,0},{3,1},{4,6},{5,7},{6,4},{7,5},{8,10},{9,11},{10,... | collective-permute-start | bytes 940040 | tf_op jit(solution)/shard_map/ppermute | solution.py:731
  361.3 16.9 %collective-permute-start.69 = (bf16[128,2176]{1,0:T(8,128)(2,1)S(1)}, bf16[128,2176]{1,0:T(8,128)(2,1)S(1)}, u32[]{:S(2)}, u32[]{:S(2)}) collective-permute-start(bf16[128,2176]{1,0:T(8,128)(2,1)S(1)} %shard_map.300), channel_id=1, source_target_pairs={{0,4},{1,5},{2,6},{3,7},{4,8},{5,9},{6,10},{7,11},{8,12},{9,13},{1... | collective-permute-start | bytes 1671176 | tf_op jit(solution)/shard_map/ppermute | solution.py:734
  388.4 27.5 %collective-permute-start.74 = (bf16[1024,768]{1,0:T(8,128)(2,1)S(1)}, bf16[1024,768]{1,0:T(8,128)(2,1)S(1)}, u32[]{:S(2)}, u32[]{:S(2)}) collective-permute-start(bf16[1024,768]{1,0:T(8,128)(2,1)S(1)} %fusion.7), channel_id=1, source_target_pairs={{0,16},{16,0},{1,17},{17,1},{2,18},{18,2},{3,19},{19,3},{4,20},{20... | collective-permute-start | bytes 4718600 | tf_op jit(solution)/shard_map/ppermute | solution.py:742
  415.9 21.0 %collective-permute-start.84 = (bf16[512,2048]{1,0:T(8,128)(2,1)S(1)}, bf16[512,2048]{1,0:T(8,128)(2,1)S(1)}, u32[]{:S(2)}, u32[]{:S(2)}) collective-permute-start(bf16[512,2048]{1,0:T(8,128)(2,1)S(1)} %convolution_convert_fusion), channel_id=1, source_target_pairs={{0,16},{16,0},{1,17},{17,1},{2,18},{18,2},{3,19},{19,3},{4,20},{20... | collective-permute-start | bytes 6291464 | tf_op jit(solution)/shard_map/ppermute | solution.py:742
  416.0 19.8 %collective-permute-start.83 = (bf16[1024,768]{1,0:T(8,128)(2,1)S(1)}, bf16[1024,768]{1,0:T(8,128)(2,1)S(1)}, u32[]{:S(2)}, u32[]{:S(2)}) collective-permute-start(bf16[1024,768]{1,0:T(8,128)(2,1)S(1)} %fusion.10), channel_id=1, source_target_pairs={{0,16},{16,0},{1,17},{17,1},{2,18},{18,2},{3,19},{19,3},{4,20},{20... | collective-permute-start | bytes 4718600 | tf_op jit(solution)/shard_map/ppermute | solution.py:742
  416.5 19.3 %collective-permute-start.79 = (bf16[128,2048]{1,0:T(8,128)(2,1)S(1)}, bf16[128,2048]{1,0:T(8,128)(2,1)S(1)}, u32[]{:S(2)}, u32[]{:S(2)}) collective-permute-start(bf16[128,2048]{1,0:T(8,128)(2,1)S(1)} %shard_map.302), channel_id=1, source_target_pairs={{0,4},{1,5},{2,6},{3,7},{4,8},{5,9},{6,10},{7,11},{8,12},{9,13},{1... | collective-permute-start | bytes 1572872 | tf_op jit(solution)/shard_map/ppermute | solution.py:734
  440.3 28.4 %collective-permute-start.85 = (bf16[128,2048]{1,0:T(8,128)(2,1)S(1)}, bf16[128,2048]{1,0:T(8,128)(2,1)S(1)}, u32[]{:S(2)}, u32[]{:S(2)}) collective-permute-start(bf16[128,2048]{1,0:T(8,128)(2,1)S(1)} %shard_map.304), channel_id=1, source_target_pairs={{0,4},{1,5},{2,6},{3,7},{4,8},{5,9},{6,10},{7,11},{8,12},{9,13},{1... | collective-permute-start | bytes 1572872 | tf_op jit(solution)/shard_map/ppermute | solution.py:734
  440.8 27.9 %collective-permute-start.89 = (bf16[128,2048]{1,0:T(8,128)(2,1)}, bf16[128,2048]{1,0:T(8,128)(2,1)S(1)}, u32[]{:S(2)}, u32[]{:S(2)}) collective-permute-start(bf16[128,2048]{1,0:T(8,128)(2,1)} %get-tuple-element.801), channel_id=1, source_target_pairs={{0,1},{1,0},{2,3},{3,2},{4,5},{5,4},{6,7},{7,6},{8,9},{9,8},{10,11... | collective-permute-start | bytes 1572872 | tf_op jit(solution)/shard_map/ppermute | solution.py:731
  442.7 25.9 %collective-permute-start.86 = (bf16[72,2048]{1,0:T(8,128)(2,1)}, bf16[72,2048]{1,0:T(8,128)(2,1)S(1)}, u32[]{:S(2)}, u32[]{:S(2)}) collective-permute-start(bf16[72,2048]{1,0:T(8,128)(2,1)} %copy-done.38), channel_id=1, source_target_pairs={{0,1},{1,0},{2,3},{3,2},{4,5},{5,4},{6,7},{7,6},{8,9},{9,8},{10,11... | collective-permute-start | bytes 884744 | tf_op jit(solution)/shard_map/ppermute | solution.py:731
  444.3 24.4 %collective-permute-start.87 = (bf16[72,2048]{1,0:T(8,128)(2,1)}, bf16[72,2048]{1,0:T(8,128)(2,1)S(1)}, u32[]{:S(2)}, u32[]{:S(2)}) collective-permute-start(bf16[72,2048]{1,0:T(8,128)(2,1)} %copy-done.37), channel_id=1, source_target_pairs={{0,2},{1,3},{2,0},{3,1},{4,6},{5,7},{6,4},{7,5},{8,10},{9,11},{10,... | collective-permute-start | bytes 884744 | tf_op jit(solution)/shard_map/ppermute | solution.py:731
  444.9 23.8 %collective-permute-start.88 = (bf16[72,2048]{1,0:T(8,128)(2,1)}, bf16[72,2048]{1,0:T(8,128)(2,1)S(1)}, u32[]{:S(2)}, u32[]{:S(2)}) collective-permute-start(bf16[72,2048]{1,0:T(8,128)(2,1)} %copy-done.36), channel_id=1, source_target_pairs={{0,3},{1,2},{2,1},{3,0},{4,7},{5,6},{6,5},{7,4},{8,11},{9,10},{10,... | collective-permute-start | bytes 884744 | tf_op jit(solution)/shard_map/ppermute | solution.py:731
  472.2 33.7 %collective-permute-start.90 = (bf16[128,2048]{1,0:T(8,128)(2,1)S(1)}, bf16[128,2048]{1,0:T(8,128)(2,1)S(1)}, u32[]{:S(2)}, u32[]{:S(2)}) collective-permute-start(bf16[128,2048]{1,0:T(8,128)(2,1)S(1)} %shard_map.306), channel_id=1, source_target_pairs={{0,4},{1,5},{2,6},{3,7},{4,8},{5,9},{6,10},{7,11},{8,12},{9,13},{1... | collective-permute-start | bytes 1572872 | tf_op jit(solution)/shard_map/ppermute | solution.py:734
  474.1 31.7 %collective-permute-start.91 = (bf16[72,2048]{1,0:T(8,128)(2,1)}, bf16[72,2048]{1,0:T(8,128)(2,1)S(1)}, u32[]{:S(2)}, u32[]{:S(2)}) collective-permute-start(bf16[72,2048]{1,0:T(8,128)(2,1)} %copy-done.35), channel_id=1, source_target_pairs={{0,1},{1,0},{2,3},{3,2},{4,5},{5,4},{6,7},{7,6},{8,9},{9,8},{10,11... | collective-permute-start | bytes 884744 | tf_op jit(solution)/shard_map/ppermute | solution.py:731
  475.5 30.3 %collective-permute-start.92 = (bf16[72,2048]{1,0:T(8,128)(2,1)S(1)}, bf16[72,2048]{1,0:T(8,128)(2,1)S(1)}, u32[]{:S(2)}, u32[]{:S(2)}) collective-permute-start(bf16[72,2048]{1,0:T(8,128)(2,1)S(1)} %copy-done.34), channel_id=1, source_target_pairs={{0,2},{1,3},{2,0},{3,1},{4,6},{5,7},{6,4},{7,5},{8,10},{9,11},{10,... | collective-permute-start | bytes 884744 | tf_op jit(solution)/shard_map/ppermute | solution.py:731
  475.9 30.0 %collective-permute-start.93 = (bf16[72,2048]{1,0:T(8,128)(2,1)S(1)}, bf16[72,2048]{1,0:T(8,128)(2,1)S(1)}, u32[]{:S(2)}, u32[]{:S(2)}) collective-permute-start(bf16[72,2048]{1,0:T(8,128)(2,1)S(1)} %copy-done.32), channel_id=1, source_target_pairs={{0,3},{1,2},{2,1},{3,0},{4,7},{5,6},{6,5},{7,4},{8,11},{9,10},{10,... | collective-permute-start | bytes 884744 | tf_op jit(solution)/shard_map/ppermute | solution.py:731
  477.6 28.2 %collective-permute-start.94 = (bf16[64,2048]{1,0:T(8,128)(2,1)}, bf16[64,2048]{1,0:T(8,128)(2,1)}, u32[]{:S(2)}, u32[]{:S(2)}) collective-permute-start(bf16[64,2048]{1,0:T(8,128)(2,1)} %get-tuple-element.824), channel_id=1, source_target_pairs={{0,8},{1,9},{2,10},{3,11},{4,12},{5,13},{6,14},{7,15},{8,0},{9,1},... | collective-permute-start | bytes 786440 | tf_op jit(solution)/shard_map/ppermute | solution.py:731
  509.2 20.3 %collective-permute-start.97 = (bf16[1024,640]{1,0:T(8,128)(2,1)}, bf16[1024,640]{1,0:T(8,128)(2,1)}, u32[]{:S(2)}, u32[]{:S(2)}) collective-permute-start(bf16[1024,640]{1,0:T(8,128)(2,1)} %pad_maximum_fusion.1), channel_id=1, source_target_pairs={{0,16},{16,0},{1,17},{17,1},{2,18},{18,2},{3,19},{19,3},{4,20},{20... | collective-permute-start | bytes 3932168 | tf_op jit(solution)/shard_map/ppermute | solution.py:742
  509.2 20.3 %collective-permute-start.95 = (bf16[128,2048]{1,0:T(8,128)(2,1)}, bf16[128,2048]{1,0:T(8,128)(2,1)}, u32[]{:S(2)}, u32[]{:S(2)}) collective-permute-start(bf16[128,2048]{1,0:T(8,128)(2,1)} %get-tuple-element.854), channel_id=1, source_target_pairs={{0,1},{1,0},{2,3},{3,2},{4,5},{5,4},{6,7},{7,6},{8,9},{9,8},{10,11... | collective-permute-start | bytes 1572872 | tf_op jit(solution)/shard_map/ppermute | solution.py:731
  511.2 18.2 %collective-permute-start.98 = (bf16[512,256]{1,0:T(8,128)(2,1)}, bf16[512,256]{1,0:T(8,128)(2,1)}, u32[]{:S(2)}, u32[]{:S(2)}) collective-permute-start(bf16[512,256]{1,0:T(8,128)(2,1)} %get-tuple-element.860), channel_id=1, source_target_pairs={{0,1},{1,0},{2,3},{3,2},{4,5},{5,4},{6,7},{7,6},{8,9},{9,8},{10,11... | collective-permute-start | bytes 786440 | tf_op jit(solution)/shard_map/ppermute | solution.py:731
  537.0 23.3 %collective-permute-start.99 = (bf16[768,1024]{1,0:T(8,128)(2,1)}, bf16[768,1024]{1,0:T(8,128)(2,1)}, u32[]{:S(2)}, u32[]{:S(2)}) collective-permute-start(bf16[768,1024]{1,0:T(8,128)(2,1)} %convolution_convert_fusion.1), channel_id=1, source_target_pairs={{0,16},{16,0},{1,17},{17,1},{2,18},{18,2},{3,19},{19,3},{4,20},{20... | collective-permute-start | bytes 4718600 | tf_op jit(solution)/shard_map/ppermute | solution.py:742
  537.0 23.2 %collective-permute-start.101 = (bf16[1024,512]{1,0:T(8,128)(2,1)}, bf16[1024,512]{1,0:T(8,128)(2,1)}, u32[]{:S(2)}, u32[]{:S(2)}) collective-permute-start(bf16[1024,512]{1,0:T(8,128)(2,1)} %convolution_convert_fusion.2), channel_id=1, source_target_pairs={{0,16},{16,0},{1,17},{17,1},{2,18},{18,2},{3,19},{19,3},{4,20},{20... | collective-permute-start | bytes 3145736 | tf_op jit(solution)/shard_map/ppermute | solution.py:742
  543.8 16.5 %collective-permute-start.100 = (bf16[256,640]{1,0:T(8,128)(2,1)}, bf16[256,640]{1,0:T(8,128)(2,1)S(1)}, u32[]{:S(2)}, u32[]{:S(2)}) collective-permute-start(bf16[256,640]{1,0:T(8,128)(2,1)} %pad_maximum_fusion.16), channel_id=1, source_target_pairs={{0,1},{1,0},{2,3},{3,2},{4,5},{5,4},{6,7},{7,6},{8,9},{9,8},{10,11... | collective-permute-start | bytes 983048 | tf_op jit(solution)/shard_map/ppermute | solution.py:731
  573.7 18.2 %collective-permute-start.107 = (bf16[1024,384]{1,0:T(8,128)(2,1)S(1)}, bf16[1024,384]{1,0:T(8,128)(2,1)S(1)}, u32[]{:S(2)}, u32[]{:S(2)}) collective-permute-start(bf16[1024,384]{1,0:T(8,128)(2,1)S(1)} %pad_maximum_fusion.8), channel_id=1, source_target_pairs={{0,16},{16,0},{1,17},{17,1},{2,18},{18,2},{3,19},{19,3},{4,20},{20... | collective-permute-start | bytes 2359304 | tf_op jit(solution)/shard_map/ppermute | solution.py:742
  575.1 16.8 %collective-permute-start.105 = (bf16[256,640]{1,0:T(8,128)(2,1)S(1)}, bf16[256,640]{1,0:T(8,128)(2,1)S(1)}, u32[]{:S(2)}, u32[]{:S(2)}) collective-permute-start(bf16[256,640]{1,0:T(8,128)(2,1)S(1)} %add_convert_fusion.7), channel_id=1, source_target_pairs={{0,8},{1,9},{2,10},{3,11},{4,12},{5,13},{6,14},{7,15},{8,0},{9,1},... | collective-permute-start | bytes 983048 | tf_op jit(solution)/shard_map/ppermute | solution.py:731
  593.7 22.6 %collective-permute-start.108 = (bf16[128,2048]{1,0:T(8,128)(2,1)S(1)}, bf16[128,2048]{1,0:T(8,128)(2,1)S(1)}, u32[]{:S(2)}, u32[]{:S(2)}) collective-permute-start(bf16[128,2048]{1,0:T(8,128)(2,1)S(1)} %copy-done.103), channel_id=1, source_target_pairs={{0,0},{1,1},{2,16},{3,17},{4,4},{5,5},{6,20},{7,21},{8,8},{9,9},{1... | collective-permute-start | bytes 1572872 | tf_op jit(solution)/shard_map/ppermute | solution.py:1049
  617.2 18.2 %collective-permute-start.116 = (bf16[128,2048]{1,0:T(8,128)(2,1)S(1)}, bf16[128,2048]{1,0:T(8,128)(2,1)S(1)}, u32[]{:S(2)}, u32[]{:S(2)}) collective-permute-start(bf16[128,2048]{1,0:T(8,128)(2,1)S(1)} %pad_maximum_fusion.12), channel_id=1, source_target_pairs={{0,4},{1,5},{2,6},{3,7},{4,0},{5,1},{6,2},{7,3},{8,12},{9,13},{10,... | collective-permute-start | bytes 1572872 | tf_op jit(solution)/shard_map/ppermute | solution.py:731
  617.3 18.1 %collective-permute-start.117 = (bf16[128,2048]{1,0:T(8,128)(2,1)S(1)}, bf16[128,2048]{1,0:T(8,128)(2,1)S(1)}, u32[]{:S(2)}, u32[]{:S(2)}) collective-permute-start(bf16[128,2048]{1,0:T(8,128)(2,1)S(1)} %pad_maximum_fusion.13), channel_id=1, source_target_pairs={{0,2},{1,3},{2,0},{3,1},{4,6},{5,7},{6,4},{7,5},{8,10},{9,11},{10,... | collective-permute-start | bytes 1572872 | tf_op jit(solution)/shard_map/ppermute | solution.py:731
  639.1 17.0 %collective-permute-start.118 = (bf16[128,2048]{1,0:T(8,128)(2,1)}, bf16[128,2048]{1,0:T(8,128)(2,1)}, u32[]{:S(2)}, u32[]{:S(2)}) collective-permute-start(bf16[128,2048]{1,0:T(8,128)(2,1)} %copy-done.165), channel_id=1, source_target_pairs={{0,0},{1,1},{2,2},{3,3},{4,8},{5,9},{6,10},{7,11},{8,4},{9,5},{10,... | collective-permute-start | bytes 1572872 | tf_op jit(solution)/shard_map/ppermute | solution.py:1049
  (234 other events, 2400.3 us)
Sparse Core Ops, SparseCore 0:
  9.6 14.8 all-gather.3
  26.0 13.2 all-gather.5
  179.9 11.5 all-gather.7

commit v6 on v5

--- a/solution.py
+++ b/solution.py
@@ -1,3 +1,5 @@
+import math
+
 import jax
 import jax.numpy as jnp
 from jax import lax
@@ -17,6 +19,7 @@
 THETA = 1000000.0
 MASKED = -1e30
 KEY_STEP = 1024
+EXPONENT = HEAD_SIZE**-0.5 / math.log(2.0)
 BF = jnp.bfloat16
 F32 = jnp.float32
 
@@ -204,26 +207,43 @@
     )(order, *parts, own, other)
 
 
-def forward_kernel(q_ref, kv_ref, vt_ref, place_ref, low_ref, high_ref, out_ref, p_ref, sum_ref):
+def fill_bias(place_ref, low_ref, high_ref, bias_ref):
+    step = min(KEY_STEP, bias_ref.shape[0])
+
+    def fill(i, carry):
+        at = pl.ds(pl.multiple_of(i * step, step), step)
+        place = place_ref[at, :]
+        seen = (place >= low_ref[...]) & (place <= high_ref[...])
+        bias_ref[at, :] = jnp.where(seen, 0.0, MASKED)
+        return carry
+
+    lax.fori_loop(0, bias_ref.shape[0] // step, fill, 0)
+
+
+def forward_kernel(
+    q_ref, kv_ref, vt_ref, place_ref, low_ref, high_ref, out_ref, p_ref, bias_ref, sum_ref
+):
     count, queries = p_ref.shape
     step = min(KEY_STEP, count)
     part = lambda i: pl.ds(pl.multiple_of(i * step, step), step)
-    q, low, high = q_ref[...], low_ref[...], high_ref[...]
+    q = q_ref[...]
+
+    @pl.when((pl.program_id(0) == 0) | (pl.num_programs(1) > 1))
+    def _():
+        fill_bias(place_ref, low_ref, high_ref, bias_ref)
 
     def score(i, top):
-        place = place_ref[part(i), :]
-        seen = (place >= low) & (place <= high)
         scores = lax.dot_general(
             kv_ref[part(i), :HEAD_SIZE], q, (((1,), (1,)), ((), ())), preferred_element_type=F32
         )
-        scores = jnp.where(seen, scores * HEAD_SIZE**-0.5, MASKED)
+        scores = scores + bias_ref[part(i), :]
         p_ref[part(i), :] = scores
         return jnp.maximum(top, jnp.max(scores, axis=0, keepdims=True))
 
     top = lax.fori_loop(0, count // step, score, jnp.full((1, queries), MASKED, F32))
 
     def lift(i, total):
-        exponent = jnp.exp(p_ref[part(i), :] - top)
+        exponent = jnp.exp2((p_ref[part(i), :] - top) * EXPONENT)
         p_ref[part(i), :] = exponent
         return total + jnp.sum(exponent, axis=0, keepdims=True)
 
@@ -260,7 +280,8 @@
         in_specs=[head, whole(keys_values), whole(values_turned), whole(place), along, along],
         out_specs=head,
         out_shape=jax.ShapeDtypeStruct(q.shape, BF),
-        scratch_shapes=[pltpu.VMEM((count, step), F32), pltpu.VMEM((HEAD_SIZE, step), F32)],
+        scratch_shapes=[pltpu.VMEM((count, step), F32)] * 2
+        + [pltpu.VMEM((HEAD_SIZE, step), F32)],
         cost_estimate=pl.CostEstimate(
             flops=8 * rows * columns * count, bytes_accessed=4 * rows * columns, transcendentals=0
         ),
@@ -270,28 +291,29 @@
 
 def backward_kernel(
     q_ref, grad_ref, proj_ref, kv_ref, kt_ref, place_ref, low_ref, high_ref, cos_ref, sin_ref,
-    gain_ref, out_ref, dkv_ref, gain_grad_ref, p_ref, dp_ref, dq_ref,
+    gain_ref, out_ref, dkv_ref, gain_grad_ref, p_ref, dp_ref, bias_ref, dq_ref,
 ):
     @pl.when((pl.program_id(0) == 0) & (pl.program_id(1) == 0))
     def _():
         dkv_ref[...] = jnp.zeros_like(dkv_ref)
         gain_grad_ref[...] = jnp.zeros_like(gain_grad_ref)
 
+    @pl.when((pl.program_id(0) == 0) | (pl.num_programs(1) > 1))
+    def _():
+        fill_bias(place_ref, low_ref, high_ref, bias_ref)
+
     count, queries = p_ref.shape
     step = min(KEY_STEP, count)
     part = lambda i: pl.ds(pl.multiple_of(i * step, step), step)
     scale = HEAD_SIZE**-0.5
     q, grad = q_ref[...], grad_ref[...]
-    low, high = low_ref[...], high_ref[...]
 
     def across(left, right):
         dims = (((1,), (1,)), ((), ()))
         return lax.dot_general(left, right, dims, preferred_element_type=F32)
 
     def score(i, top):
-        place = place_ref[part(i), :]
-        seen = (place >= low) & (place <= high)
-        scores = jnp.where(seen, across(kv_ref[part(i), :HEAD_SIZE], q) * scale, MASKED)
+        scores = across(kv_ref[part(i), :HEAD_SIZE], q) + bias_ref[part(i), :]
         p_ref[part(i), :] = scores
         return jnp.maximum(top, jnp.max(scores, axis=0, keepdims=True))
 
@@ -299,7 +321,7 @@
 
     def lift(i, sums):
         total, inner = sums
-        exponent = jnp.exp(p_ref[part(i), :] - top)
+        exponent = jnp.exp2((p_ref[part(i), :] - top) * EXPONENT)
         p_ref[part(i), :] = exponent
         total = total + jnp.sum(exponent, axis=0, keepdims=True)
         prob_grad = across(kv_ref[part(i), HEAD_SIZE:], grad)
@@ -348,7 +370,7 @@
             jax.ShapeDtypeStruct(keys_values.shape, F32),
             jax.ShapeDtypeStruct(gain.shape, F32),
         ],
-        scratch_shapes=[pltpu.VMEM((count, step), F32)] * 2
+        scratch_shapes=[pltpu.VMEM((count, step), F32)] * 3
         + [pltpu.VMEM((HEAD_SIZE, step), F32)],
         cost_estimate=pl.CostEstimate(
             flops=10 * rows * columns * count, bytes_accessed=8 * rows * columns, transcendentals=0
@@ -377,10 +399,11 @@
     )(*arrays)
 
 
-def finish_kernel(ids_ref, b0, b1, b2, b3, wq_ref, wk_ref, wv_ref, *refs):
-    gq_ref, gk_ref, gv_ref, first_ref, last_ref, inner_ref = refs
+def finish_kernel(ids_ref, b0, b1, b2, b3, gain_ref, low_ref, wq_ref, wk_ref, wv_ref, *refs):
+    gq_ref, gk_ref, gv_ref, router_ref, out_ref, mid_ref, in_ref, q_ref, k_ref = refs
+    out_ref[...] = low_ref[...].astype(F32)
     half = QW // 2
-    lanes = first_ref.shape[1]
+    lanes = 128
     at = QW + lanes
     first = last = 0.0
     for k, ref in enumerate((b0, b1, b2, b3)):
@@ -394,23 +417,30 @@
         gv_ref[:, pl.ds(thin, HEAD_SIZE)] = block[:, at + HEAD_SIZE : at + 2 * HEAD_SIZE]
         first = first + block[:, half : half + lanes]
         last = last + block[:, at + 2 * HEAD_SIZE :]
-    first_ref[...] = first
-    last_ref[...] = last
     inner = 0.0
     for w_ref, g_ref in ((wq_ref, gq_ref), (wk_ref, gk_ref), (wv_ref, gv_ref)):
         inner = inner + jnp.sum(w_ref[...].astype(F32) * g_ref[...], axis=1, keepdims=True)
-    inner_ref[...] = jnp.broadcast_to(inner, inner_ref.shape)
-
-
-def finish(b, blocks, *weights):
+    experts = router_ref.shape[1]
+    router_ref[...] = first[:, :experts]
+    first, last = first.T, last.T
+    inner = jnp.broadcast_to(inner, (inner.shape[0], lanes)).T
+    mid_ref[...] = first[experts : experts + 1]
+    in_ref[...] = inner[0:1] / gain_ref[...]
+    part = q_ref.shape[1]
+    q_ref[...] = last[0:1, :part]
+    k_ref[...] = last[1:2, :part]
+
+
+def finish(b, blocks, gain, low, experts, head_part, *weights):
     rows = blocks[0].shape[0]
-    sums = jax.ShapeDtypeStruct((rows, 128), F32)
+    shapes = [weight.shape for weight in weights] + [(rows, experts), low.shape]
+    shapes += [(1, rows)] * 2 + [(1, head_part)] * 2
     return pl.pallas_call(
         finish_kernel,
         in_specs=[pl.BlockSpec(memory_space=pltpu.SMEM)]
-        + [pl.BlockSpec(memory_space=pltpu.VMEM)] * 7,
-        out_shape=[jax.ShapeDtypeStruct(weight.shape, F32) for weight in weights] + [sums] * 3,
-    )(b.astype(jnp.int32)[None], *blocks, *weights)
+        + [pl.BlockSpec(memory_space=pltpu.VMEM)] * 9,
+        out_shape=[jax.ShapeDtypeStruct(shape, F32) for shape in shapes],
+    )(b.astype(jnp.int32)[None], *blocks, gain, low, *weights)
 
 
 def choose_kernel(blocks, table_ref, piece_ref, *refs):
@@ -827,12 +857,13 @@
             near, got = yield [(x, (blocks[1].astype(BF),)), (z, (across,))]
         return blocks[0].astype(F32) + near.astype(F32) + got.astype(F32)
 
-    def twin_scatter(self, make, own, other, idle=None, now=False):
+    def twin_scatter(self, make, own, other, idle=None, now=False, rest=0):
         low = lambda *args: make(*args).astype(BF)
         if now:
             block = low(*other)
         else:
             (block,) = yield [(low, other)]
+            (block,) = yield from hold(rest, block)
         if idle is None:
             came, total = yield [(self.twin, (block,)), (make, own)]
             return total + came.astype(F32)
@@ -1034,7 +1065,11 @@
         swap_core = [
             (g * experts + i, (i >> 1 & 1) * experts + (i & 13 | g << 1)) for g, i in pairs_of
         ]
-        there = back = (swap_line, swap_core)
+        bit = lambda k: links.index // (1 << k) % 2
+        moves = bit(2) != bit(3), bit(1) != links.g
+        back = ((swap_line, moves[0]), (swap_core, moves[1]))
+        onto = dict(swap_core)
+        there = ([(i, onto[j]) for i, j in swap_line], moves[0] | moves[1])
     else:
         to_block = [
             (b * 2 * planes + links.row_block(g, a), g * experts + links.device(a, b))
@@ -1042,11 +1077,17 @@
             for a in range(planes)
             for b in range(4)
         ]
-        there = (to_block, None)
-        back = ([(to, of) for of, to in to_block], None)
-
-    def moved(value, pairs_of):
-        return value if pairs_of is None else lax.ppermute(value, ("dp", "expert"), pairs_of)
+        there = (to_block, True)
+        back = (([(to, of) for of, to in to_block], True), None)
+
+    def moved(value, swap):
+        if swap is None:
+            return value
+        pairs_of, moves = swap
+        if moves is True:
+            return lax.ppermute(value, ("dp", "expert"), pairs_of)
+        came = lax.ppermute(value, ("dp", "expert"), [(i, j) for i, j in pairs_of if i != j])
+        return jnp.where(moves, came, value)
 
     def gather_out():
         pieces = yield from links.block_gather(rounds.values[move_task], (1, 0))
@@ -1054,11 +1095,7 @@
         (others,) = yield [(links.twin, (pieces,))]
         return pieces, others
 
-    def move_out():
-        value = yield from work(lambda value: moved(value, there[0]), w_out)
-        return (yield from work(lambda value: moved(value, there[1]), value))
-
-    move_task = spread(move_out())
+    move_task = spread(work(lambda value: moved(value, there), w_out))
 
     device_of = jnp.stack(
         [links.device(links.block(r), links.b ^ k) for r in range(planes) for k in range(4)]
@@ -1225,26 +1262,18 @@
     def half_of(array, which):
         return lax.dynamic_slice_in_dim(array, which * half_width, half_width, 1)
 
-    def gate_up_gradient(place):
+    def gate_up_gradient(place, idle, rest):
         rows_in, grads_in = stacked(0), stacked(place)
-        return links.twin_scatter(
-            by_rows,
-            (half_of(rows_in, links.g), grads_in),
-            (half_of(rows_in, 1 - links.g), grads_in),
-            idle=5,
-        )
+        make = lambda which: by_rows(half_of(rows_in, which), grads_in)
+        return links.twin_scatter(make, (links.g,), (1 - links.g,), idle=idle, rest=rest)
 
     def down_gradient():
         rows_in, grads_in = stacked(1), stacked(2)
-        return links.twin_scatter(
-            by_rows,
-            (rows_in, half_of(grads_in, links.g)),
-            (rows_in, half_of(grads_in, 1 - links.g)),
-            idle=2,
-        )
-
-    gate_task = spread(gate_up_gradient(3))
-    up_task = spread(later(1, gate_up_gradient(4)))
+        make = lambda which: by_rows(rows_in, half_of(grads_in, which))
+        return links.twin_scatter(make, (links.g,), (1 - links.g,), idle=2)
+
+    gate_task = spread(gate_up_gradient(3, 5, 0))
+    up_task = spread(later(1, gate_up_gradient(4, 2, 3)))
     down_task = spread(later(5, down_gradient()))
 
     def route(rows_in):
@@ -1294,11 +1323,10 @@
         grad = grad.astype(BF)
         blocks = [grad[r * head_rows : (r + 1) * head_rows] for r in range(planes)]
         grad = yield from links.block_scatter(blocks, split=True)
-        (grad,) = yield from hold(2, grad.astype(BF))
-        grad = yield from work(lambda value: moved(value, back[1]), grad)
-        (grad,) = yield from hold(1, grad)
-        grad = yield from work(lambda value: moved(value, back[0]), grad)
-        return grad.astype(F32)
+        yield from hold(1)
+        grad = yield from work(lambda value: moved(value, back[1]), grad.astype(BF))
+        (grad,) = yield from hold(2, grad)
+        return (yield from work(lambda value: moved(value, back[0]), grad))
 
     grad_out_task = spread(scatter_out())
 
@@ -1400,10 +1428,11 @@
     )
     result = (x_one + mixture).astype(BF)
     weights = (w_query, key_projection_weight, value_projection_weight)
-    grad_query, grad_key, grad_value, first, last, inner = finish(links.b, owned, *weights)
-    grad_router, grad_mid = first[:, :experts], first[:, experts]
-    grad_qgain, grad_kgain = last[:head_part, 0], last[:head_part, 1]
-    grad_in = inner[:, 0] / gain_in.astype(F32)
+    found = finish(
+        links.b, owned, gain_in.astype(F32)[None], grad_out, experts, head_part, *weights
+    )
+    grad_query, grad_key, grad_value, grad_router, grad_out = found[:5]
+    grad_mid, grad_in, grad_qgain, grad_kgain = (row.reshape(-1) for row in found[5:])
 
     return (
         result,

time: 684 us -> 676 us (0.988)
  waiting for transfers between devices: 165 us -> 148 us
  other arithmetic: 47.1 us -> 60.4 us
  local copies, waits for them, and re-layouts: 98.3 us -> 89.9 us
    ppermute x93, waiting for transfers between devices: 164 us -> 146 us  [flip(): return lax.ppermute(value, 'expert', [(i, i ^ mask) for i in range(self.n)])]
    ppermute x4 -> x3, starting transfers between devices: 13.1 us -> 3.13 us  [moved(): lax.ppermute(value, ('dp', 'expert'), [(i, j) for i, j in pairs_of if i !...]
    unnamed x382 -> x406, local copies, waits for them, and re-layouts: 48.1 us -> 47.2 us
  transfers between devices with their start and end apart: 125 -> 124, of which waited for: 46 -> 40; matrix products, arithmetic and copies ran while one was open for 20% -> 22% of each run, Pallas kernels for 22% -> 22%
where the time goes in v6:
time: 676 us; the launch traced here: 664 us
  Pallas kernels  161 us (24%)
  waiting for transfers between devices  148 us (22%)
  starting transfers between devices  136 us (20%)
  local copies, waits for them, and re-layouts  89.9 us (13%)
  other arithmetic  60.4 us (9%)
  matrix products  51.7 us (8%)
  between operations  17.5 us (3%)
    ppermute x93, waiting for transfers between devices, flip(): return lax.ppermute(value, 'expert', [(i, i ^ mask) for i in range(self.n)])  146 us
    ppermute x93, starting transfers between devices, flip(): return lax.ppermute(value, 'expert', [(i, i ^ mask) for i in range(self.n)])  112 us
    unnamed x406, local copies, waits for them, and re-layouts  47.2 us
    pallas_call x4, Pallas kernels, expert_rows(): pl.pallas_call(lambda *refs: expert_kernel(blocks, *refs), grid=(ff // st...  46.1 us
    pallas_call x2, Pallas kernels, attention_backward(): pl.pallas_call(backward_kernel, grid=(columns // HEAD_SIZE, rows // step)...  44.1 us
    dot_general x12, matrix products, by_rows(): jnp.einsum('rd,rf->df', rows_in, grads_in, preferred_element_type=F32)  42.2 us
    pallas_call x2, Pallas kernels, attention_forward(): pl.pallas_call(forward_kernel, grid=(columns // HEAD_SIZE, rows // step),...  19.7 us
    ppermute x12, starting transfers between devices, shift(): lax.ppermute(value, 'expert', [(i, (i + step * 4) % self.n) for i in rang...  17.5 us
  transfers between devices with their start and end apart: 124, of which 40 were waited for; matrix products, arithmetic and copies ran while one was open for 22% of the time, Pallas kernels for 22%

profile of v6, /device:TPU:0, one launch (start us, length us, event | category | flops | bytes accessed | tf_op | source)
XLA Modules:
  0.0 664.0 jit_solution(9668124299044965850)
XLA Ops:
  12.9 6.2 collective-permute-start
  25.6 3.2 collective-permute-done.1.refs_1_
  28.8 3.3 collective-permute-done.2.refs_2_
  32.1 3.6 collective-permute-start.6
  36.4 2.4 shard_map.281.refs_0_
  45.0 18.0 %collective-permute-done.11 = bf16[160,1280]{1,0:T(8,128)(2,1)S(1)} collective-permute-done((bf16[160,1280]{1,0:T(8,128)(2,1)S(1)}, bf16[160,1280]{1,0:T(8,128)(2,1)S(1)}, u32[]{:S(2)}, u32[]{:S(2)}) %collective-permute-start.11) | collective-permute-done | bytes 409632 | tf_op jit(solution)/shard_map/ppermute | solution.py:761
  69.9 2.6 collective-permute-start.5
  72.5 3.4 collective-permute-done.9
  77.2 12.9 %collective-permute-done.5 = bf16[160,1280]{1,0:T(8,128)(2,1)S(1)} collective-permute-done((bf16[160,1280]{1,0:T(8,128)(2,1)S(1)}, bf16[160,1280]{1,0:T(8,128)(2,1)S(1)}, u32[]{:S(2)}, u32[]{:S(2)}) %collective-permute-start.5) | collective-permute-done | bytes 409632 | tf_op jit(solution)/shard_map/ppermute | solution.py:761
  96.0 4.6 collective-permute-done.13
  107.7 11.3 %shard_map.282 = (bf16[2048,1280]{1,0:T(8,128)(2,1)}, f32[512,1280]{1,0:T(8,128)}, bf16[512,1280]{1,0:T(8,128)(2,1)}) custom-call(s32[32]{0:T(128)} %add_multiply_fusion.1.starts_ref, bf16[512,2048]{1,0:T(8,128)(2,1)} %fusion.2.x_ref, f32[512,128]{1,0:T(8,128)} %get-tuple-element.500.cos_ref, f32[512,128]{1,0:T(8,128)} %get-tuple-element.501.sin_ref, ...), custom_call_target="tpu_custom_call" | custom-call | flops 2684354560 | bytes 7340032 | tf_op jit(solution)/shard_map/pallas_call | solution.py:88
  119.1 2.2 collective-permute-done.19
  121.3 2.7 copy.135
  126.9 3.7 shard_map.283
  130.7 2.3 fusion.122
  133.3 6.4 collective-permute-done.21
  147.0 7.0 %collective-permute-done.22 = bf16[64,2048]{1,0:T(8,128)(2,1)} collective-permute-done((bf16[64,2048]{1,0:T(8,128)(2,1)}, bf16[64,2048]{1,0:T(8,128)(2,1)}, u32[]{:S(2)}, u32[]{:S(2)}) %collective-permute-start.22) | collective-permute-done | bytes 262176 | tf_op jit(solution)/shard_map/ppermute | solution.py:761
  157.6 2.2 collective-permute-start.25
  166.9 9.9 %shard_map.285.refs_0_ = bf16[512,512]{1,0:T(8,128)(2,1)S(1)} custom-call(bf16[512,512]{1,0:T(8,128)(2,1)S(1)} %copy-done.12, bf16[2048,256]{1,0:T(8,128)(2,1)S(1)} %copy.136.kv_ref, bf16[128,2048]{1,0:T(8,128)(2,1)S(1)} %get-tuple-element.1095.vt_ref, s32[2048,1]{1,0:T(8,128)S(1)} %copy.137.place_ref, s32[1,512]{1,0:T(1,128)S(1)} %bitcast.155, ...), custom_call_target="tpu_custom_call" | custom-call | flops 4294967296 | bytes 1048576 | tf_op jit(solution)/shard_map/pallas_call | solution.py:277
  192.3 9.9 %shard_map.287.refs_1_ = bf16[512,512]{1,0:T(8,128)(2,1)S(1)} custom-call(bf16[512,512]{1,0:T(8,128)(2,1)S(1)} %copy-done.11, bf16[2048,256]{1,0:T(8,128)(2,1)S(1)} %copy.136.kv_ref, bf16[128,2048]{1,0:T(8,128)(2,1)S(1)} %copy-done.14, s32[2048,1]{1,0:T(8,128)S(1)} %copy.137.place_ref, s32[1,512]{1,0:T(1,128)S(1)} %bitcast.156, s32[1,512]{1,0:T(1,128)S(1)} %bitcast.160), custom_call_target="tpu_custom_call" | custom-call | flops 4294967296 | bytes 1048576 | tf_op jit(solution)/shard_map/pallas_call | solution.py:277
  211.4 3.1 fusion.118
  214.5 7.1 %shard_map.289 = (f32[512,2048]{1,0:T(8,128)S(1)}, bf16[512,1024]{1,0:T(8,128)(2,1)S(1)}) custom-call(s32[8]{0:T(128)S(1)} %stack.190.order_ref, bf16[512,512]{1,0:T(8,128)(2,1)S(1)} %copy-done.63, bf16[512,512]{1,0:T(8,128)(2,1)S(1)} %copy-done.65, bf16[512,2048]{1,0:T(8,128)(2,1)} %constant_dynamic-update-slice_fusion.11.refs_2_, ...), custom_call_target="tpu_custom_call" | custom-call | flops 2147483648 | bytes 12582912 | tf_op jit(solution)/shard_map/pallas_call | solution.py:189
  227.2 2.3 collective-permute-done.39
  229.5 3.4 collective-permute-done.41
  233.1 2.3 collective-permute-start.40
  242.8 8.0 %collective-permute-done.42 = bf16[128,2048]{1,0:T(8,128)(2,1)S(1)} collective-permute-done((bf16[128,2048]{1,0:T(8,128)(2,1)S(1)}, bf16[128,2048]{1,0:T(8,128)(2,1)S(1)}, u32[]{:S(2)}, u32[]{:S(2)}) %collective-permute-start.42) | collective-permute-done | bytes 524320 | tf_op jit(solution)/shard_map/ppermute | solution.py:761
  263.8 4.7 collective-permute-done.44.refs_3_
  268.6 2.4 shard_map.291
  279.3 12.1 %shard_map.292 = (bf16[72,2176]{1,0:T(8,128)(2,1)S(1)}, bf16[72,2176]{1,0:T(8,128)(2,1)S(1)}, bf16[72,2176]{1,0:T(8,128)(2,1)S(1)}, bf16[72,2176]{1,0:T(8,128)(2...) custom-call(s32[1]{0:T(128)} %bitcast.68.refs_0_, ...), custom_call_target="tpu_custom_call" | custom-call | flops 5435817984 | bytes 9437184 | tf_op jit(solution)/shard_map/pallas_call | solution.py:567
  301.8 11.5 %shard_map.294 = (bf16[72,2176]{1,0:T(8,128)(2,1)S(1)}, bf16[72,2176]{1,0:T(8,128)(2,1)S(1)}, bf16[72,2176]{1,0:T(8,128)(2,1)S(1)}, bf16[72,2176]{1,0:T(8,128)(2...) custom-call(s32[1]{0:T(128)} %bitcast.68.refs_0_, ...), custom_call_target="tpu_custom_call" | custom-call | flops 5435817984 | bytes 9437184 | tf_op jit(solution)/shard_map/pallas_call | solution.py:567
  313.3 5.7 collective-permute-done.53.refs_4_
  322.3 2.2 collective-permute-start.57
  329.6 11.7 %shard_map.296 = (bf16[72,2176]{1,0:T(8,128)(2,1)S(1)}, bf16[72,2176]{1,0:T(8,128)(2,1)}, bf16[72,2176]{1,0:T(8,128)(2,1)}, bf16[72,2176]{1,0:T(8,128)(2,1)}, bf...) custom-call(s32[1]{0:T(128)} %bitcast.68.refs_0_, ...), custom_call_target="tpu_custom_call" | custom-call | flops 5435817984 | bytes 9437184 | tf_op jit(solution)/shard_map/pallas_call | solution.py:567
  341.4 4.6 collective-permute-done.57.refs_4_
  351.6 10.8 %shard_map.299 = (bf16[72,2176]{1,0:T(8,128)(2,1)S(1)}, bf16[72,2176]{1,0:T(8,128)(2,1)S(1)}, bf16[72,2176]{1,0:T(8,128)(2,1)S(1)}, bf16[72,2176]{1,0:T(8,128)(2...) custom-call(s32[1]{0:T(128)} %bitcast.68.refs_0_, ...), custom_call_target="tpu_custom_call" | custom-call | flops 5435817984 | bytes 9437184 | tf_op jit(solution)/shard_map/pallas_call | solution.py:567
  371.7 6.6 collective-permute-done.65.refs_2_
  378.3 5.3 collective-permute-done.66.refs_3_
  384.6 2.7 collective-permute-start.69
  390.8 2.3 fusion.21
  394.0 3.5 collective-permute-done.71.refs_3_
  400.6 3.5 fusion.24
  404.9 5.9 collective-permute-done.74
  411.1 2.6 collective-permute-start.77
  413.7 3.5 collective-permute-done.76
  419.5 2.3 collective-permute-start.78
  425.3 2.9 convolution_convert_fusion.5
  428.2 2.9 convolution_convert_fusion.4
  433.8 4.8 collective-permute-done.80.refs_3_
  448.3 21.8 %shard_map.305 = (bf16[512,512]{1,0:T(8,128)(2,1)}, f32[2048,256]{1,0:T(8,128)}, f32[1,128]{1,0:T(1,128)}) custom-call(bf16[512,512]{1,0:T(8,128)(2,1)} %get-tuple-element.799.q_ref, bf16[512,512]{1,0:T(8,128)(2,1)} %get-tuple-element.800.grad_ref, f32[512,512]{1,0:T(8,128)} %get-tuple-element.801.proj_ref, bf16[2048,256]{1,0:T(8,128)(2,1)} %copy-done.10, ...), custom_call_target="tpu_custom_call" | custom-call | flops 5368709120 | bytes 2097152 | tf_op jit(solution)/shard_map/pallas_call | solution.py:362
  479.8 22.3 %shard_map.307 = (bf16[512,512]{1,0:T(8,128)(2,1)}, f32[2048,256]{1,0:T(8,128)}, f32[1,128]{1,0:T(1,128)}) custom-call(bf16[512,512]{1,0:T(8,128)(2,1)} %get-tuple-element.824.q_ref, bf16[512,512]{1,0:T(8,128)(2,1)} %get-tuple-element.825.grad_ref, f32[512,512]{1,0:T(8,128)} %get-tuple-element.826.proj_ref, bf16[2048,256]{1,0:T(8,128)(2,1)} %copy-done.10, ...), custom_call_target="tpu_custom_call" | custom-call | flops 5368709120 | bytes 2097152 | tf_op jit(solution)/shard_map/pallas_call | solution.py:362
  514.5 2.2 fusion.42
  516.8 5.1 fusion.27
  527.3 3.7 collective-permute-done.97
  544.6 2.4 add_convert_fusion.3
  549.8 7.1 %collective-permute-done.101 = bf16[512,256]{1,0:T(8,128)(2,1)} collective-permute-done((bf16[512,256]{1,0:T(8,128)(2,1)}, bf16[512,256]{1,0:T(8,128)(2,1)}, u32[]{:S(2)}, u32[]{:S(2)}) %collective-permute-start.101) | collective-permute-done | bytes 262176 | tf_op jit(solution)/shard_map/ppermute | solution.py:761
  563.1 2.5 convolution_convert_fusion.3
  579.3 6.7 %convert_add_fusion.2 = f32[1024,768]{1,0:T(8,128)} fusion(bf16[1024,768]{1,0:T(8,128)(2,1)} %copy-done.179, bf16[1152,768]{1,0:T(8,128)(2,1)} %copy-done.167, bf16[1152,2048]{1,0:T(8,128)(2,1)} %copy-done.129, s32[]{:T(128)S(6)} %select_n.1034), kind=kOutput, calls=%fused_computation.9 | convolution fusion | flops 1813512192 | bytes 8847364 | tf_op jit(solution)/shard_map/rd,rf->df/dot_general | solution.py:1258
  587.7 4.5 shard_map.310
  605.4 6.7 %convert_add_fusion.1 = f32[1024,768]{1,0:T(8,128)} fusion(bf16[1024,768]{1,0:T(8,128)(2,1)} %collective-permute-done.93, bf16[1152,768]{1,0:T(8,128)(2,1)} %copy-done.170, bf16[1152,2048]{1,0:T(8,128)(2,1)} %copy-done.129, s32[]{:T(128)S(6)} %select_n.1038), kind=kOutput, calls=%fused_computation.8 | convolution fusion | flops 1813512192 | bytes 8847364 | tf_op jit(solution)/shard_map/rd,rf->df/dot_general | solution.py:1258
  623.4 6.6 convert_add_fusion
  630.9 2.8 collective-permute-done.114
  641.6 3.5 collective-permute-start.118
  648.3 2.9 fusion.33
  652.8 3.1 shard_map.312
  (823 shorter events, 284.0 us)
Async XLA Ops:
  7.2 269.9 %all-gather.4.cloned.1.call-start = ((), (), s32[]{:S(2)}) async-start(), calls=%async_computation | async-start | bytes 4718592 | tf_op jit(solution)/shard_map/all_gather | solution.py:910
  7.9 269.1 %all-gather.6.cloned.1.call-start = ((), (), s32[]{:S(2)}) async-start(), calls=%async_computation.1 | async-start | bytes 4718592 | tf_op jit(solution)/shard_map/all_gather | solution.py:911
  20.3 256.8 %all-gather.8.cloned.1.call-start = ((), (), s32[]{:S(2)}) async-start(), calls=%async_computation.2 | async-start | bytes 4718592 | tf_op jit(solution)/shard_map/all_gather | solution.py:912
  32.1 31.4 %collective-permute-start.6 = (bf16[128,2048]{1,0:T(8,128)(2,1)S(1)}, bf16[128,2048]{1,0:T(8,128)(2,1)}, u32[]{:S(2)}, u32[]{:S(2)}) collective-permute-start(bf16[128,2048]{1,0:T(8,128)(2,1)S(1)} %copy-done.80), channel_id=1, source_target_pairs={{0,4},{1,5},{2,6},{3,7},{4,0},{5,1},{6,2},{7,3},{8,12},{9,13},{10,... | collective-permute-start | bytes 1572872 | tf_op jit(solution)/shard_map/ppermute | solution.py:761
  35.7 30.0 %collective-permute-start.7 = (bf16[128,2048]{1,0:T(8,128)(2,1)S(1)}, bf16[128,2048]{1,0:T(8,128)(2,1)}, u32[]{:S(2)}, u32[]{:S(2)}) collective-permute-start(bf16[128,2048]{1,0:T(8,128)(2,1)S(1)} %copy-done.80), channel_id=1, source_target_pairs={{0,2},{1,3},{2,0},{3,1},{4,6},{5,7},{6,4},{7,5},{8,10},{9,11},{10,... | collective-permute-start | bytes 1572872 | tf_op jit(solution)/shard_map/ppermute | solution.py:761
  38.8 30.2 %collective-permute-start.4 = (bf16[288,1280]{1,0:T(8,128)(2,1)}, bf16[288,1280]{1,0:T(8,128)(2,1)}, u32[]{:S(2)}, u32[]{:S(2)}) collective-permute-start(bf16[288,1280]{1,0:T(8,128)(2,1)} %shard_map.281.refs_0_), channel_id=1, source_target_pairs={{0,1},{1,0},{2,3},{3,2},{4,5},{5,4},{6,7},{7,6},{8,9},{9,8},{10,11... | collective-permute-start | bytes 2211848 | tf_op jit(solution)/shard_map/ppermute | solution.py:761
  41.3 62.8 %collective-permute-start.14 = (bf16[288,1280]{1,0:T(8,128)(2,1)}, bf16[288,1280]{1,0:T(8,128)(2,1)}, u32[]{:S(2)}, u32[]{:S(2)}) collective-permute-start(bf16[288,1280]{1,0:T(8,128)(2,1)} %shard_map.281.refs_0_), channel_id=1, source_target_pairs={{0,16},{16,0},{1,17},{17,1},{2,18},{18,2},{3,19},{19,3},{4,20},{20... | collective-permute-start | bytes 2211848 | tf_op jit(solution)/shard_map/ppermute | solution.py:772
  41.4 21.6 %collective-permute-start.11 = (bf16[160,1280]{1,0:T(8,128)(2,1)S(1)}, bf16[160,1280]{1,0:T(8,128)(2,1)S(1)}, u32[]{:S(2)}, u32[]{:S(2)}) collective-permute-start(bf16[160,1280]{1,0:T(8,128)(2,1)S(1)} %slice.405), channel_id=1, source_target_pairs={{0,8},{1,9},{2,10},{3,11},{4,12},{5,13},{6,14},{7,15},{8,0},{9,1},... | collective-permute-start | bytes 1228808 | tf_op jit(solution)/shard_map/ppermute | solution.py:761
  69.9 20.3 %collective-permute-start.5 = (bf16[160,1280]{1,0:T(8,128)(2,1)S(1)}, bf16[160,1280]{1,0:T(8,128)(2,1)S(1)}, u32[]{:S(2)}, u32[]{:S(2)}) collective-permute-start(bf16[160,1280]{1,0:T(8,128)(2,1)S(1)} %pad_maximum_fusion.14), channel_id=1, source_target_pairs={{0,8},{1,9},{2,10},{3,11},{4,12},{5,13},{6,14},{7,15},{8,0},{9,1},... | collective-permute-start | bytes 1228808 | tf_op jit(solution)/shard_map/ppermute | solution.py:761
  72.5 31.7 %collective-permute-start.15 = (bf16[288,1280]{1,0:T(8,128)(2,1)}, bf16[288,1280]{1,0:T(8,128)(2,1)}, u32[]{:S(2)}, u32[]{:S(2)}) collective-permute-start(bf16[288,1280]{1,0:T(8,128)(2,1)} %collective-permute-done.4.refs_1_), channel_id=1, source_target_pairs={{0,16},{16,0},{1,17},{17,1},{2,18},{18,2},{3,19},{19,3},{4,20},{20... | collective-permute-start | bytes 2211848 | tf_op jit(solution)/shard_map/ppermute | solution.py:772
  104.1 17.2 %collective-permute-start.18 = (bf16[128,2048]{1,0:T(8,128)(2,1)S(1)}, bf16[128,2048]{1,0:T(8,128)(2,1)S(1)}, u32[]{:S(2)}, u32[]{:S(2)}) collective-permute-start(bf16[128,2048]{1,0:T(8,128)(2,1)S(1)} %broadcast_select_fusion.2), channel_id=1, source_target_pairs={{0,1},{1,0},{2,3},{3,2},{4,5},{5,4},{6,7},{7,6},{8,9},{9,8},{10,11... | collective-permute-start | bytes 1572872 | tf_op jit(solution)/shard_map/ppermute | solution.py:761
  157.6 22.8 %collective-permute-start.25 = (bf16[128,2048]{1,0:T(8,128)(2,1)S(1)}, bf16[128,2048]{1,0:T(8,128)(2,1)}, u32[]{:S(2)}, u32[]{:S(2)}) collective-permute-start(bf16[128,2048]{1,0:T(8,128)(2,1)S(1)} %copy-done.3), channel_id=1, source_target_pairs={{0,4},{1,5},{2,6},{3,7},{4,8},{5,9},{6,10},{7,11},{8,12},{9,13},{1... | collective-permute-start | bytes 1572872 | tf_op jit(solution)/shard_map/ppermute | solution.py:764
  159.8 20.6 %collective-permute-start.26 = (bf16[72,2048]{1,0:T(8,128)(2,1)}, bf16[72,2048]{1,0:T(8,128)(2,1)S(1)}, u32[]{:S(2)}, u32[]{:S(2)}) collective-permute-start(bf16[72,2048]{1,0:T(8,128)(2,1)} %copy-done.61), channel_id=1, source_target_pairs={{0,1},{1,0},{2,3},{3,2},{4,5},{5,4},{6,7},{7,6},{8,9},{9,8},{10,11... | collective-permute-start | bytes 884744 | tf_op jit(solution)/shard_map/ppermute | solution.py:761
  161.3 19.1 %collective-permute-start.27 = (bf16[72,2048]{1,0:T(8,128)(2,1)}, bf16[72,2048]{1,0:T(8,128)(2,1)S(1)}, u32[]{:S(2)}, u32[]{:S(2)}) collective-permute-start(bf16[72,2048]{1,0:T(8,128)(2,1)} %copy-done.60), channel_id=1, source_target_pairs={{0,2},{1,3},{2,0},{3,1},{4,6},{5,7},{6,4},{7,5},{8,10},{9,11},{10,... | collective-permute-start | bytes 884744 | tf_op jit(solution)/shard_map/ppermute | solution.py:761
  162.1 18.3 %collective-permute-start.28 = (bf16[72,2048]{1,0:T(8,128)(2,1)}, bf16[72,2048]{1,0:T(8,128)(2,1)S(1)}, u32[]{:S(2)}, u32[]{:S(2)}) collective-permute-start(bf16[72,2048]{1,0:T(8,128)(2,1)} %copy-done.59), channel_id=1, source_target_pairs={{0,3},{1,2},{2,1},{3,0},{4,7},{5,6},{6,5},{7,4},{8,11},{9,10},{10,... | collective-permute-start | bytes 884744 | tf_op jit(solution)/shard_map/ppermute | solution.py:761
  163.3 17.1 %collective-permute-start.29 = (bf16[64,2048]{1,0:T(8,128)(2,1)}, bf16[64,2048]{1,0:T(8,128)(2,1)S(1)}, u32[]{:S(2)}, u32[]{:S(2)}) collective-permute-start(bf16[64,2048]{1,0:T(8,128)(2,1)} %collective-permute-done.22), channel_id=1, source_target_pairs={{0,1},{1,0},{2,3},{3,2},{4,5},{5,4},{6,7},{7,6},{8,9},{9,8},{10,11... | collective-permute-start | bytes 786440 | tf_op jit(solution)/shard_map/ppermute | solution.py:761
  184.8 17.8 %collective-permute-start.34 = (bf16[512,2048]{1,0:T(8,128)(2,1)}, bf16[512,2048]{1,0:T(8,128)(2,1)}, u32[]{:S(2)}, u32[]{:S(2)}) collective-permute-start(bf16[512,2048]{1,0:T(8,128)(2,1)} %constant_dynamic-update-slice_fusion.11.refs_2_), channel_id=1, source_target_pairs={{0,16},{16,0},{1,17},{17,1},{2,18},{18,2},{3,19},{19,3},{4,20},{20... | collective-permute-start | bytes 6291464 | tf_op jit(solution)/shard_map/ppermute | solution.py:772
  184.9 17.7 %collective-permute-start.30 = (bf16[128,2048]{1,0:T(8,128)(2,1)}, bf16[128,2048]{1,0:T(8,128)(2,1)}, u32[]{:S(2)}, u32[]{:S(2)}) collective-permute-start(bf16[128,2048]{1,0:T(8,128)(2,1)} %collective-permute-done.25.refs_1_), channel_id=1, source_target_pairs={{0,4},{1,5},{2,6},{3,7},{4,8},{5,9},{6,10},{7,11},{8,12},{9,13},{1... | collective-permute-start | bytes 1572872 | tf_op jit(solution)/shard_map/ppermute | solution.py:764
  186.6 15.6 %collective-permute-start.31 = (bf16[72,2048]{1,0:T(8,128)(2,1)}, bf16[72,2048]{1,0:T(8,128)(2,1)S(1)}, u32[]{:S(2)}, u32[]{:S(2)}) collective-permute-start(bf16[72,2048]{1,0:T(8,128)(2,1)} %copy-done.48), channel_id=1, source_target_pairs={{0,1},{1,0},{2,3},{3,2},{4,5},{5,4},{6,7},{7,6},{8,9},{9,8},{10,11... | collective-permute-start | bytes 884744 | tf_op jit(solution)/shard_map/ppermute | solution.py:761
  205.0 17.6 %collective-permute-start.35 = (bf16[128,2048]{1,0:T(8,128)(2,1)}, bf16[128,2048]{1,0:T(8,128)(2,1)S(1)}, u32[]{:S(2)}, u32[]{:S(2)}) collective-permute-start(bf16[128,2048]{1,0:T(8,128)(2,1)} %collective-permute-done.30.refs_1_), channel_id=1, source_target_pairs={{0,4},{1,5},{2,6},{3,7},{4,8},{5,9},{6,10},{7,11},{8,12},{9,13},{1... | collective-permute-start | bytes 1572872 | tf_op jit(solution)/shard_map/ppermute | solution.py:764
  237.3 18.2 %collective-permute-start.62 = (bf16[72,2048]{1,0:T(8,128)(2,1)S(1)}, bf16[72,2048]{1,0:T(8,128)(2,1)S(1)}, u32[]{:S(2)}, u32[]{:S(2)}) collective-permute-start(bf16[72,2048]{1,0:T(8,128)(2,1)S(1)} %get-tuple-element.705), channel_id=1, source_target_pairs={{0,1},{1,0},{2,3},{3,2},{4,5},{5,4},{6,7},{7,6},{8,9},{9,8},{10,11... | collective-permute-start | bytes 884744 | tf_op jit(solution)/shard_map/ppermute | solution.py:761
  237.4 18.1 %collective-permute-start.63 = (bf16[72,2048]{1,0:T(8,128)(2,1)S(1)}, bf16[72,2048]{1,0:T(8,128)(2,1)S(1)}, u32[]{:S(2)}, u32[]{:S(2)}) collective-permute-start(bf16[72,2048]{1,0:T(8,128)(2,1)S(1)} %get-tuple-element.706), channel_id=1, source_target_pairs={{0,2},{1,3},{2,0},{3,1},{4,6},{5,7},{6,4},{7,5},{8,10},{9,11},{10,... | collective-permute-start | bytes 884744 | tf_op jit(solution)/shard_map/ppermute | solution.py:761
  239.4 16.1 %collective-permute-start.64 = (bf16[72,2048]{1,0:T(8,128)(2,1)S(1)}, bf16[72,2048]{1,0:T(8,128)(2,1)S(1)}, u32[]{:S(2)}, u32[]{:S(2)}) collective-permute-start(bf16[72,2048]{1,0:T(8,128)(2,1)S(1)} %get-tuple-element.707), channel_id=1, source_target_pairs={{0,3},{1,2},{2,1},{3,0},{4,7},{5,6},{6,5},{7,4},{8,11},{9,10},{10,... | collective-permute-start | bytes 884744 | tf_op jit(solution)/shard_map/ppermute | solution.py:761
  271.7 19.8 %collective-permute-start.50 = (bf16[128,2048]{1,0:T(8,128)(2,1)}, bf16[128,2048]{1,0:T(8,128)(2,1)}, u32[]{:S(2)}, u32[]{:S(2)}) collective-permute-start(bf16[128,2048]{1,0:T(8,128)(2,1)} %collective-permute-done.46.refs_1_), channel_id=1, source_target_pairs={{0,4},{1,5},{2,6},{3,7},{4,8},{5,9},{6,10},{7,11},{8,12},{9,13},{1... | collective-permute-start | bytes 1572872 | tf_op jit(solution)/shard_map/ppermute | solution.py:764
  273.6 17.9 %collective-permute-start.47 = (bf16[72,2048]{1,0:T(8,128)(2,1)}, bf16[72,2048]{1,0:T(8,128)(2,1)}, u32[]{:S(2)}, u32[]{:S(2)}) collective-permute-start(bf16[72,2048]{1,0:T(8,128)(2,1)} %get-tuple-element.588), channel_id=1, source_target_pairs={{0,1},{1,0},{2,3},{3,2},{4,5},{5,4},{6,7},{7,6},{8,9},{9,8},{10,11... | collective-permute-start | bytes 884744 | tf_op jit(solution)/shard_map/ppermute | solution.py:761
  275.1 16.3 %collective-permute-start.48 = (bf16[72,2048]{1,0:T(8,128)(2,1)}, bf16[72,2048]{1,0:T(8,128)(2,1)}, u32[]{:S(2)}, u32[]{:S(2)}) collective-permute-start(bf16[72,2048]{1,0:T(8,128)(2,1)} %get-tuple-element.589), channel_id=1, source_target_pairs={{0,2},{1,3},{2,0},{3,1},{4,6},{5,7},{6,4},{7,5},{8,10},{9,11},{10,... | collective-permute-start | bytes 884744 | tf_op jit(solution)/shard_map/ppermute | solution.py:761
  293.2 20.1 %collective-permute-start.51 = (bf16[72,4224]{1,0:T(8,128)(2,1)S(1)}, bf16[72,4224]{1,0:T(8,128)(2,1)S(1)}, u32[]{:S(2)}, u32[]{:S(2)}) collective-permute-start(bf16[72,4224]{1,0:T(8,128)(2,1)S(1)} %get-tuple-element.627), channel_id=1, source_target_pairs={{0,1},{1,0},{2,3},{3,2},{4,5},{5,4},{6,7},{7,6},{8,9},{9,8},{10,11... | collective-permute-start | bytes 1824776 | tf_op jit(solution)/shard_map/ppermute | solution.py:761
  294.9 18.5 %collective-permute-start.52 = (bf16[72,4224]{1,0:T(8,128)(2,1)S(1)}, bf16[72,4224]{1,0:T(8,128)(2,1)S(1)}, u32[]{:S(2)}, u32[]{:S(2)}) collective-permute-start(bf16[72,4224]{1,0:T(8,128)(2,1)S(1)} %get-tuple-element.628), channel_id=1, source_target_pairs={{0,2},{1,3},{2,0},{3,1},{4,6},{5,7},{6,4},{7,5},{8,10},{9,11},{10,... | collective-permute-start | bytes 1824776 | tf_op jit(solution)/shard_map/ppermute | solution.py:761
  295.9 23.1 %collective-permute-start.53 = (bf16[72,4224]{1,0:T(8,128)(2,1)S(1)}, bf16[72,4224]{1,0:T(8,128)(2,1)S(1)}, u32[]{:S(2)}, u32[]{:S(2)}) collective-permute-start(bf16[72,4224]{1,0:T(8,128)(2,1)S(1)} %get-tuple-element.629), channel_id=1, source_target_pairs={{0,3},{1,2},{2,1},{3,0},{4,7},{5,6},{6,5},{7,4},{8,11},{9,10},{10,... | collective-permute-start | bytes 1824776 | tf_op jit(solution)/shard_map/ppermute | solution.py:761
  296.8 16.5 %collective-permute-start.54 = (bf16[128,2048]{1,0:T(8,128)(2,1)}, bf16[128,2048]{1,0:T(8,128)(2,1)S(1)}, u32[]{:S(2)}, u32[]{:S(2)}) collective-permute-start(bf16[128,2048]{1,0:T(8,128)(2,1)} %collective-permute-done.50.refs_1_), channel_id=1, source_target_pairs={{0,4},{1,5},{2,6},{3,7},{4,8},{5,9},{6,10},{7,11},{8,12},{9,13},{1... | collective-permute-start | bytes 1572872 | tf_op jit(solution)/shard_map/ppermute | solution.py:764
  320.9 20.5 %collective-permute-start.55 = (bf16[72,4224]{1,0:T(8,128)(2,1)}, bf16[72,4224]{1,0:T(8,128)(2,1)S(1)}, u32[]{:S(2)}, u32[]{:S(2)}) collective-permute-start(bf16[72,4224]{1,0:T(8,128)(2,1)} %get-tuple-element.664), channel_id=1, source_target_pairs={{0,1},{1,0},{2,3},{3,2},{4,5},{5,4},{6,7},{7,6},{8,9},{9,8},{10,11... | collective-permute-start | bytes 1824776 | tf_op jit(solution)/shard_map/ppermute | solution.py:761
  320.9 20.4 %collective-permute-start.56 = (bf16[72,4224]{1,0:T(8,128)(2,1)S(1)}, bf16[72,4224]{1,0:T(8,128)(2,1)S(1)}, u32[]{:S(2)}, u32[]{:S(2)}) collective-permute-start(bf16[72,4224]{1,0:T(8,128)(2,1)S(1)} %get-tuple-element.665), channel_id=1, source_target_pairs={{0,2},{1,3},{2,0},{3,1},{4,6},{5,7},{6,4},{7,5},{8,10},{9,11},{10,... | collective-permute-start | bytes 1824776 | tf_op jit(solution)/shard_map/ppermute | solution.py:761
  322.3 23.7 %collective-permute-start.57 = (bf16[72,4224]{1,0:T(8,128)(2,1)S(1)}, bf16[72,4224]{1,0:T(8,128)(2,1)S(1)}, u32[]{:S(2)}, u32[]{:S(2)}) collective-permute-start(bf16[72,4224]{1,0:T(8,128)(2,1)S(1)} %get-tuple-element.666), channel_id=1, source_target_pairs={{0,3},{1,2},{2,1},{3,0},{4,7},{5,6},{6,5},{7,4},{8,11},{9,10},{10,... | collective-permute-start | bytes 1824776 | tf_op jit(solution)/shard_map/ppermute | solution.py:761
  346.4 20.1 %collective-permute-start.61 = (bf16[128,2176]{1,0:T(8,128)(2,1)S(1)}, bf16[128,2176]{1,0:T(8,128)(2,1)S(1)}, u32[]{:S(2)}, u32[]{:S(2)}) collective-permute-start(bf16[128,2176]{1,0:T(8,128)(2,1)S(1)} %shard_map.297), channel_id=1, source_target_pairs={{0,4},{1,5},{2,6},{3,7},{4,8},{5,9},{6,10},{7,11},{8,12},{9,13},{1... | collective-permute-start | bytes 1671176 | tf_op jit(solution)/shard_map/ppermute | solution.py:764
  348.0 18.5 %collective-permute-start.58 = (bf16[72,2176]{1,0:T(8,128)(2,1)}, bf16[72,2176]{1,0:T(8,128)(2,1)S(1)}, u32[]{:S(2)}, u32[]{:S(2)}) collective-permute-start(bf16[72,2176]{1,0:T(8,128)(2,1)} %get-tuple-element.695), channel_id=1, source_target_pairs={{0,1},{1,0},{2,3},{3,2},{4,5},{5,4},{6,7},{7,6},{8,9},{9,8},{10,11... | collective-permute-start | bytes 940040 | tf_op jit(solution)/shard_map/ppermute | solution.py:761
  350.1 16.4 %collective-permute-start.59 = (bf16[72,2176]{1,0:T(8,128)(2,1)}, bf16[72,2176]{1,0:T(8,128)(2,1)S(1)}, u32[]{:S(2)}, u32[]{:S(2)}) collective-permute-start(bf16[72,2176]{1,0:T(8,128)(2,1)} %get-tuple-element.696), channel_id=1, source_target_pairs={{0,2},{1,3},{2,0},{3,1},{4,6},{5,7},{6,4},{7,5},{8,10},{9,11},{10,... | collective-permute-start | bytes 940040 | tf_op jit(solution)/shard_map/ppermute | solution.py:761
  350.1 16.4 %collective-permute-start.60 = (bf16[72,2176]{1,0:T(8,128)(2,1)}, bf16[72,2176]{1,0:T(8,128)(2,1)S(1)}, u32[]{:S(2)}, u32[]{:S(2)}) collective-permute-start(bf16[72,2176]{1,0:T(8,128)(2,1)} %get-tuple-element.697), channel_id=1, source_target_pairs={{0,3},{1,2},{2,1},{3,0},{4,7},{5,6},{6,5},{7,4},{8,11},{9,10},{10,... | collective-permute-start | bytes 940040 | tf_op jit(solution)/shard_map/ppermute | solution.py:761
  367.0 17.2 %collective-permute-start.68 = (bf16[128,2176]{1,0:T(8,128)(2,1)S(1)}, bf16[128,2176]{1,0:T(8,128)(2,1)S(1)}, u32[]{:S(2)}, u32[]{:S(2)}) collective-permute-start(bf16[128,2176]{1,0:T(8,128)(2,1)S(1)} %shard_map.300), channel_id=1, source_target_pairs={{0,4},{1,5},{2,6},{3,7},{4,8},{5,9},{6,10},{7,11},{8,12},{9,13},{1... | collective-permute-start | bytes 1671176 | tf_op jit(solution)/shard_map/ppermute | solution.py:764
  393.2 26.2 %collective-permute-start.73 = (bf16[1024,768]{1,0:T(8,128)(2,1)S(1)}, bf16[1024,768]{1,0:T(8,128)(2,1)S(1)}, u32[]{:S(2)}, u32[]{:S(2)}) collective-permute-start(bf16[1024,768]{1,0:T(8,128)(2,1)S(1)} %fusion.21), channel_id=1, source_target_pairs={{0,16},{16,0},{1,17},{17,1},{2,18},{18,2},{3,19},{19,3},{4,20},{20... | collective-permute-start | bytes 4718600 | tf_op jit(solution)/shard_map/ppermute | solution.py:772
  419.4 19.2 %collective-permute-start.82 = (bf16[512,2048]{1,0:T(8,128)(2,1)S(1)}, bf16[512,2048]{1,0:T(8,128)(2,1)S(1)}, u32[]{:S(2)}, u32[]{:S(2)}) collective-permute-start(bf16[512,2048]{1,0:T(8,128)(2,1)S(1)} %convolution_convert_fusion), channel_id=1, source_target_pairs={{0,16},{16,0},{1,17},{17,1},{2,18},{18,2},{3,19},{19,3},{4,20},{20... | collective-permute-start | bytes 6291464 | tf_op jit(solution)/shard_map/ppermute | solution.py:772
  419.5 19.1 %collective-permute-start.78 = (bf16[128,2048]{1,0:T(8,128)(2,1)S(1)}, bf16[128,2048]{1,0:T(8,128)(2,1)S(1)}, u32[]{:S(2)}, u32[]{:S(2)}) collective-permute-start(bf16[128,2048]{1,0:T(8,128)(2,1)S(1)} %shard_map.302), channel_id=1, source_target_pairs={{0,4},{1,5},{2,6},{3,7},{4,8},{5,9},{6,10},{7,11},{8,12},{9,13},{1... | collective-permute-start | bytes 1572872 | tf_op jit(solution)/shard_map/ppermute | solution.py:764
  442.0 28.1 %collective-permute-start.83 = (bf16[128,2048]{1,0:T(8,128)(2,1)S(1)}, bf16[128,2048]{1,0:T(8,128)(2,1)S(1)}, u32[]{:S(2)}, u32[]{:S(2)}) collective-permute-start(bf16[128,2048]{1,0:T(8,128)(2,1)S(1)} %shard_map.304), channel_id=1, source_target_pairs={{0,4},{1,5},{2,6},{3,7},{4,8},{5,9},{6,10},{7,11},{8,12},{9,13},{1... | collective-permute-start | bytes 1572872 | tf_op jit(solution)/shard_map/ppermute | solution.py:764
  442.5 27.7 %collective-permute-start.87 = (bf16[128,2048]{1,0:T(8,128)(2,1)}, bf16[128,2048]{1,0:T(8,128)(2,1)}, u32[]{:S(2)}, u32[]{:S(2)}) collective-permute-start(bf16[128,2048]{1,0:T(8,128)(2,1)} %get-tuple-element.798), channel_id=1, source_target_pairs={{0,1},{1,0},{2,3},{3,2},{4,5},{5,4},{6,7},{7,6},{8,9},{9,8},{10,11... | collective-permute-start | bytes 1572872 | tf_op jit(solution)/shard_map/ppermute | solution.py:761
  444.8 25.3 %collective-permute-start.84 = (bf16[72,2048]{1,0:T(8,128)(2,1)}, bf16[72,2048]{1,0:T(8,128)(2,1)S(1)}, u32[]{:S(2)}, u32[]{:S(2)}) collective-permute-start(bf16[72,2048]{1,0:T(8,128)(2,1)} %copy-done.40), channel_id=1, source_target_pairs={{0,1},{1,0},{2,3},{3,2},{4,5},{5,4},{6,7},{7,6},{8,9},{9,8},{10,11... | collective-permute-start | bytes 884744 | tf_op jit(solution)/shard_map/ppermute | solution.py:761
  445.9 24.2 %collective-permute-start.85 = (bf16[72,2048]{1,0:T(8,128)(2,1)}, bf16[72,2048]{1,0:T(8,128)(2,1)S(1)}, u32[]{:S(2)}, u32[]{:S(2)}) collective-permute-start(bf16[72,2048]{1,0:T(8,128)(2,1)} %copy-done.39), channel_id=1, source_target_pairs={{0,2},{1,3},{2,0},{3,1},{4,6},{5,7},{6,4},{7,5},{8,10},{9,11},{10,... | collective-permute-start | bytes 884744 | tf_op jit(solution)/shard_map/ppermute | solution.py:761
  446.5 23.6 %collective-permute-start.86 = (bf16[72,2048]{1,0:T(8,128)(2,1)S(1)}, bf16[72,2048]{1,0:T(8,128)(2,1)S(1)}, u32[]{:S(2)}, u32[]{:S(2)}) collective-permute-start(bf16[72,2048]{1,0:T(8,128)(2,1)S(1)} %copy-done.38), channel_id=1, source_target_pairs={{0,3},{1,2},{2,1},{3,0},{4,7},{5,6},{6,5},{7,4},{8,11},{9,10},{10,... | collective-permute-start | bytes 884744 | tf_op jit(solution)/shard_map/ppermute | solution.py:761
  472.8 32.8 %collective-permute-start.88 = (bf16[128,2048]{1,0:T(8,128)(2,1)S(1)}, bf16[128,2048]{1,0:T(8,128)(2,1)S(1)}, u32[]{:S(2)}, u32[]{:S(2)}) collective-permute-start(bf16[128,2048]{1,0:T(8,128)(2,1)S(1)} %shard_map.306), channel_id=1, source_target_pairs={{0,4},{1,5},{2,6},{3,7},{4,8},{5,9},{6,10},{7,11},{8,12},{9,13},{1... | collective-permute-start | bytes 1572872 | tf_op jit(solution)/shard_map/ppermute | solution.py:764
  474.6 31.0 %collective-permute-start.89 = (bf16[72,2048]{1,0:T(8,128)(2,1)}, bf16[72,2048]{1,0:T(8,128)(2,1)S(1)}, u32[]{:S(2)}, u32[]{:S(2)}) collective-permute-start(bf16[72,2048]{1,0:T(8,128)(2,1)} %get-tuple-element.816), channel_id=1, source_target_pairs={{0,1},{1,0},{2,3},{3,2},{4,5},{5,4},{6,7},{7,6},{8,9},{9,8},{10,11... | collective-permute-start | bytes 884744 | tf_op jit(solution)/shard_map/ppermute | solution.py:761
  475.2 30.3 %collective-permute-start.90 = (bf16[72,2048]{1,0:T(8,128)(2,1)}, bf16[72,2048]{1,0:T(8,128)(2,1)S(1)}, u32[]{:S(2)}, u32[]{:S(2)}) collective-permute-start(bf16[72,2048]{1,0:T(8,128)(2,1)} %get-tuple-element.817), channel_id=1, source_target_pairs={{0,2},{1,3},{2,0},{3,1},{4,6},{5,7},{6,4},{7,5},{8,10},{9,11},{10,... | collective-permute-start | bytes 884744 | tf_op jit(solution)/shard_map/ppermute | solution.py:761
  476.3 29.3 %collective-permute-start.91 = (bf16[72,2048]{1,0:T(8,128)(2,1)S(1)}, bf16[72,2048]{1,0:T(8,128)(2,1)S(1)}, u32[]{:S(2)}, u32[]{:S(2)}) collective-permute-start(bf16[72,2048]{1,0:T(8,128)(2,1)S(1)} %copy-done.36), channel_id=1, source_target_pairs={{0,3},{1,2},{2,1},{3,0},{4,7},{5,6},{6,5},{7,4},{8,11},{9,10},{10,... | collective-permute-start | bytes 884744 | tf_op jit(solution)/shard_map/ppermute | solution.py:761
  478.1 27.5 %collective-permute-start.92 = (bf16[64,2048]{1,0:T(8,128)(2,1)}, bf16[64,2048]{1,0:T(8,128)(2,1)S(1)}, u32[]{:S(2)}, u32[]{:S(2)}) collective-permute-start(bf16[64,2048]{1,0:T(8,128)(2,1)} %get-tuple-element.821), channel_id=1, source_target_pairs={{0,8},{1,9},{2,10},{3,11},{4,12},{5,13},{6,14},{7,15},{8,0},{9,1},... | collective-permute-start | bytes 786440 | tf_op jit(solution)/shard_map/ppermute | solution.py:761
  508.8 22.3 %collective-permute-start.93 = (bf16[1024,768]{1,0:T(8,128)(2,1)}, bf16[1024,768]{1,0:T(8,128)(2,1)}, u32[]{:S(2)}, u32[]{:S(2)}) collective-permute-start(bf16[1024,768]{1,0:T(8,128)(2,1)} %fusion.24), channel_id=1, source_target_pairs={{0,16},{16,0},{1,17},{17,1},{2,18},{18,2},{3,19},{19,3},{4,20},{20... | collective-permute-start | bytes 4718600 | tf_op jit(solution)/shard_map/ppermute | solution.py:772
  510.8 20.3 %collective-permute-start.96 = (bf16[1024,640]{1,0:T(8,128)(2,1)}, bf16[1024,640]{1,0:T(8,128)(2,1)}, u32[]{:S(2)}, u32[]{:S(2)}) collective-permute-start(bf16[1024,640]{1,0:T(8,128)(2,1)} %pad_maximum_fusion.1), channel_id=1, source_target_pairs={{0,16},{16,0},{1,17},{17,1},{2,18},{18,2},{3,19},{19,3},{4,20},{20... | collective-permute-start | bytes 3932168 | tf_op jit(solution)/shard_map/ppermute | solution.py:772
  511.3 19.8 %collective-permute-start.94 = (bf16[128,2048]{1,0:T(8,128)(2,1)}, bf16[128,2048]{1,0:T(8,128)(2,1)}, u32[]{:S(2)}, u32[]{:S(2)}) collective-permute-start(bf16[128,2048]{1,0:T(8,128)(2,1)} %get-tuple-element.850), channel_id=1, source_target_pairs={{0,1},{1,0},{2,3},{3,2},{4,5},{5,4},{6,7},{7,6},{8,9},{9,8},{10,11... | collective-permute-start | bytes 1572872 | tf_op jit(solution)/shard_map/ppermute | solution.py:761
  513.1 17.9 %collective-permute-start.97 = (bf16[512,256]{1,0:T(8,128)(2,1)S(1)}, bf16[512,256]{1,0:T(8,128)(2,1)}, u32[]{:S(2)}, u32[]{:S(2)}) collective-permute-start(bf16[512,256]{1,0:T(8,128)(2,1)S(1)} %get-tuple-element.856), channel_id=1, source_target_pairs={{0,1},{1,0},{2,3},{3,2},{4,5},{5,4},{6,7},{7,6},{8,9},{9,8},{10,11... | collective-permute-start | bytes 786440 | tf_op jit(solution)/shard_map/ppermute | solution.py:761
  536.3 21.5 %collective-permute-start.98 = (bf16[768,1024]{1,0:T(8,128)(2,1)}, bf16[768,1024]{1,0:T(8,128)(2,1)}, u32[]{:S(2)}, u32[]{:S(2)}) collective-permute-start(bf16[768,1024]{1,0:T(8,128)(2,1)} %fusion.27), channel_id=1, source_target_pairs={{0,16},{16,0},{1,17},{17,1},{2,18},{18,2},{3,19},{19,3},{4,20},{20... | collective-permute-start | bytes 4718600 | tf_op jit(solution)/shard_map/ppermute | solution.py:772
  536.3 21.4 %collective-permute-start.100 = (bf16[1024,512]{1,0:T(8,128)(2,1)}, bf16[1024,512]{1,0:T(8,128)(2,1)}, u32[]{:S(2)}, u32[]{:S(2)}) collective-permute-start(bf16[1024,512]{1,0:T(8,128)(2,1)} %convolution_convert_fusion.1), channel_id=1, source_target_pairs={{0,16},{16,0},{1,17},{17,1},{2,18},{18,2},{3,19},{19,3},{4,20},{20... | collective-permute-start | bytes 3145736 | tf_op jit(solution)/shard_map/ppermute | solution.py:772
  541.3 16.5 %collective-permute-start.99 = (bf16[256,640]{1,0:T(8,128)(2,1)}, bf16[256,640]{1,0:T(8,128)(2,1)}, u32[]{:S(2)}, u32[]{:S(2)}) collective-permute-start(bf16[256,640]{1,0:T(8,128)(2,1)} %pad_maximum_fusion.16), channel_id=1, source_target_pairs={{0,1},{1,0},{2,3},{3,2},{4,5},{5,4},{6,7},{7,6},{8,9},{9,8},{10,11... | collective-permute-start | bytes 983048 | tf_op jit(solution)/shard_map/ppermute | solution.py:761
  573.8 18.5 %collective-permute-start.103 = (bf16[128,2048]{1,0:T(8,128)(2,1)S(1)}, bf16[128,2048]{1,0:T(8,128)(2,1)}, u32[]{:S(2)}, u32[]{:S(2)}) collective-permute-start(bf16[128,2048]{1,0:T(8,128)(2,1)S(1)} %copy-done.91), channel_id=1, source_target_pairs={{2,16},{3,17},{6,20},{7,21},{10,24},{11,25},{14,28},{15,29},{16,2}... | collective-permute-start | bytes 1572872 | tf_op jit(solution)/shard_map/ppermute | solution.py:1089
  575.4 19.5 %collective-permute-start.107 = (bf16[1024,384]{1,0:T(8,128)(2,1)}, bf16[1024,384]{1,0:T(8,128)(2,1)}, u32[]{:S(2)}, u32[]{:S(2)}) collective-permute-start(bf16[1024,384]{1,0:T(8,128)(2,1)} %pad_maximum_fusion.8), channel_id=1, source_target_pairs={{0,16},{16,0},{1,17},{17,1},{2,18},{18,2},{3,19},{19,3},{4,20},{20... | collective-permute-start | bytes 2359304 | tf_op jit(solution)/shard_map/ppermute | solution.py:772
  577.2 16.1 %collective-permute-start.104 = (bf16[256,640]{1,0:T(8,128)(2,1)}, bf16[256,640]{1,0:T(8,128)(2,1)}, u32[]{:S(2)}, u32[]{:S(2)}) collective-permute-start(bf16[256,640]{1,0:T(8,128)(2,1)} %pad_maximum_fusion.17), channel_id=1, source_target_pairs={{0,1},{1,0},{2,3},{3,2},{4,5},{5,4},{6,7},{7,6},{8,9},{9,8},{10,11... | collective-permute-start | bytes 983048 | tf_op jit(solution)/shard_map/ppermute | solution.py:761
  578.0 16.9 %collective-permute-start.105 = (bf16[256,640]{1,0:T(8,128)(2,1)}, bf16[256,640]{1,0:T(8,128)(2,1)}, u32[]{:S(2)}, u32[]{:S(2)}) collective-permute-start(bf16[256,640]{1,0:T(8,128)(2,1)} %add_convert_fusion.7), channel_id=1, source_target_pairs={{0,8},{1,9},{2,10},{3,11},{4,12},{5,13},{6,14},{7,15},{8,0},{9,1},... | collective-permute-start | bytes 983048 | tf_op jit(solution)/shard_map/ppermute | solution.py:761
  618.6 17.2 %collective-permute-start.115 = (bf16[128,2048]{1,0:T(8,128)(2,1)S(1)}, bf16[128,2048]{1,0:T(8,128)(2,1)S(1)}, u32[]{:S(2)}, u32[]{:S(2)}) collective-permute-start(bf16[128,2048]{1,0:T(8,128)(2,1)S(1)} %pad_maximum_fusion.12), channel_id=1, source_target_pairs={{0,4},{1,5},{2,6},{3,7},{4,0},{5,1},{6,2},{7,3},{8,12},{9,13},{10,... | collective-permute-start | bytes 1572872 | tf_op jit(solution)/shard_map/ppermute | solution.py:761
  619.0 16.8 %collective-permute-start.116 = (bf16[128,2048]{1,0:T(8,128)(2,1)S(1)}, bf16[128,2048]{1,0:T(8,128)(2,1)S(1)}, u32[]{:S(2)}, u32[]{:S(2)}) collective-permute-start(bf16[128,2048]{1,0:T(8,128)(2,1)S(1)} %pad_maximum_fusion.13), channel_id=1, source_target_pairs={{0,2},{1,3},{2,0},{3,1},{4,6},{5,7},{6,4},{7,5},{8,10},{9,11},{10,... | collective-permute-start | bytes 1572872 | tf_op jit(solution)/shard_map/ppermute | solution.py:761
  (245 other events, 2420.5 us)
Sparse Core Ops, SparseCore 0:
  9.6 14.8 all-gather.3
  26.0 13.2 all-gather.5
  186.2 11.0 all-gather.7

commit v7 on v6

--- a/solution.py
+++ b/solution.py
@@ -1352,7 +1352,7 @@
         grad = yield from links.block_scatter(owners_blocks(grad.astype(BF)))
         return grad.astype(BF)
 
-    def key_value_gradient(key_value_grad, proj_grad):
+    def key_value_gradient(key_value_grad, query_grads):
         sums = jnp.concatenate([grad_qgain, grad_kgain]).reshape(2, devices, head_part)
         sums = jnp.pad(sums, ((0, 0), (0, 0), (0, rows - head_part))).reshape(2, MODEL_WIDTH).T
         sums = jnp.pad(sums, ((0, 0), (0, lanes - sums.shape[1])))
@@ -1363,7 +1363,10 @@
 
         came, xn_one_grad = yield [
             (links.twin, (half(1 - links.g).astype(BF),)),
-            (lambda proj_grad: input_gradient(proj_grad, w_qkv), (proj_grad,)),
+            (
+                lambda *parts: input_gradient(jnp.concatenate(parts, axis=1), w_qkv),
+                (*query_grads, key_value_grad),
+            ),
         ]
         tables["scatter"] = spread(links.head_scatter(xn_one_grad))
         grad = (half(links.g) + came.astype(F32)).astype(BF)
@@ -1414,8 +1417,7 @@
         head_gains[1:2],
     )
     key_value_grad = jnp.concatenate([key_proj_grad, key_terms[:, HEAD_SIZE:].astype(BF)], axis=1)
-    proj_grad = jnp.concatenate(query_low_grads + [key_value_grad], axis=1)
-    key_value_task = spread(key_value_gradient(key_value_grad, proj_grad))
+    key_value_task = spread(key_value_gradient(key_value_grad, query_low_grads))
     one, two, three = rounds.until(*query_tasks, key_value_task)
     xn_one_grad = rounds.until(tables["scatter"])
     query_task = spread(links.exchange(links.heads, pack_rows(one, two, three)))

time: 676 us -> 678 us (level)
    unnamed x406 -> x402, local copies, waits for them, and re-layouts: 47.2 us -> 46.4 us
where the time goes in v7:
time: 678 us; the launch traced here: 667 us
  Pallas kernels  160 us (24%)
  waiting for transfers between devices  150 us (22%)
  starting transfers between devices  134 us (20%)
  local copies, waits for them, and re-layouts  89.4 us (13%)
  other arithmetic  61.8 us (9%)
  matrix products  53.4 us (8%)
  between operations  17.6 us (3%)
    ppermute x93, waiting for transfers between devices, flip(): return lax.ppermute(value, 'expert', [(i, i ^ mask) for i in range(self.n)])  150 us
    ppermute x93, starting transfers between devices, flip(): return lax.ppermute(value, 'expert', [(i, i ^ mask) for i in range(self.n)])  113 us
    unnamed x402, local copies, waits for them, and re-layouts  46.4 us
    pallas_call x4, Pallas kernels, expert_rows(): pl.pallas_call(lambda *refs: expert_kernel(blocks, *refs), grid=(ff // st...  45.3 us
    pallas_call x2, Pallas kernels, attention_backward(): pl.pallas_call(backward_kernel, grid=(columns // HEAD_SIZE, rows // step)...  44.1 us
    dot_general x12, matrix products, by_rows(): jnp.einsum('rd,rf->df', rows_in, grads_in, preferred_element_type=F32)  43.8 us
    pallas_call x2, Pallas kernels, attention_forward(): pl.pallas_call(forward_kernel, grid=(columns // HEAD_SIZE, rows // step),...  19.8 us
    ppermute x12, starting transfers between devices, shift(): lax.ppermute(value, 'expert', [(i, (i + step * 4) % self.n) for i in rang...  15.4 us
  transfers between devices with their start and end apart: 124, of which 40 were waited for; matrix products, arithmetic and copies ran while one was open for 22% of the time, Pallas kernels for 22%

profile of v7, /device:TPU:0, one launch (start us, length us, event | category | flops | bytes accessed | tf_op | source)
XLA Modules:
  0.0 666.7 jit_solution(8827716089842255452)
XLA Ops:
  12.9 6.2 collective-permute-start
  25.6 3.2 collective-permute-done.1.refs_1_
  28.8 3.5 collective-permute-done.2.refs_2_
  32.3 3.6 collective-permute-start.6
  36.5 2.2 shard_map.281.refs_0_
  45.0 18.2 %collective-permute-done.11 = bf16[160,1280]{1,0:T(8,128)(2,1)S(1)} collective-permute-done((bf16[160,1280]{1,0:T(8,128)(2,1)S(1)}, bf16[160,1280]{1,0:T(8,128)(2,1)S(1)}, u32[]{:S(2)}, u32[]{:S(2)}) %collective-permute-start.11) | collective-permute-done | bytes 409632 | tf_op jit(solution)/shard_map/ppermute | solution.py:761
  70.1 2.5 collective-permute-start.5
  72.6 3.4 collective-permute-done.9
  77.3 13.0 %collective-permute-done.5 = bf16[160,1280]{1,0:T(8,128)(2,1)S(1)} collective-permute-done((bf16[160,1280]{1,0:T(8,128)(2,1)S(1)}, bf16[160,1280]{1,0:T(8,128)(2,1)S(1)}, u32[]{:S(2)}, u32[]{:S(2)}) %collective-permute-start.5) | collective-permute-done | bytes 409632 | tf_op jit(solution)/shard_map/ppermute | solution.py:761
  96.8 4.0 collective-permute-done.13
  107.9 11.4 %shard_map.282 = (bf16[2048,1280]{1,0:T(8,128)(2,1)}, f32[512,1280]{1,0:T(8,128)}, bf16[512,1280]{1,0:T(8,128)(2,1)}) custom-call(s32[32]{0:T(128)} %add_multiply_fusion.1.starts_ref, bf16[512,2048]{1,0:T(8,128)(2,1)} %fusion.2.x_ref, f32[512,128]{1,0:T(8,128)} %get-tuple-element.502.cos_ref, f32[512,128]{1,0:T(8,128)} %get-tuple-element.503.sin_ref, ...), custom_call_target="tpu_custom_call" | custom-call | flops 2684354560 | bytes 7340032 | tf_op jit(solution)/shard_map/pallas_call | solution.py:88
  121.2 2.7 copy.135
  127.1 3.7 shard_map.283
  133.3 6.5 collective-permute-done.21
  147.1 7.0 %collective-permute-done.22 = bf16[64,2048]{1,0:T(8,128)(2,1)S(1)} collective-permute-done((bf16[64,2048]{1,0:T(8,128)(2,1)}, bf16[64,2048]{1,0:T(8,128)(2,1)S(1)}, u32[]{:S(2)}, u32[]{:S(2)}) %collective-permute-start.22) | collective-permute-done | bytes 262176 | tf_op jit(solution)/shard_map/ppermute | solution.py:761
  154.9 2.1 pad_maximum_fusion.7
  167.1 9.9 %shard_map.285.refs_0_ = bf16[512,512]{1,0:T(8,128)(2,1)S(1)} custom-call(bf16[512,512]{1,0:T(8,128)(2,1)S(1)} %copy-done.8, bf16[2048,256]{1,0:T(8,128)(2,1)S(1)} %copy.136.kv_ref, bf16[128,2048]{1,0:T(8,128)(2,1)S(1)} %get-tuple-element.1099.vt_ref, s32[2048,1]{1,0:T(8,128)S(1)} %copy.137.place_ref, s32[1,512]{1,0:T(1,128)S(1)} %bitcast.155, ...), custom_call_target="tpu_custom_call" | custom-call | flops 4294967296 | bytes 1048576 | tf_op jit(solution)/shard_map/pallas_call | solution.py:277
  190.4 9.9 %shard_map.287.refs_1_ = bf16[512,512]{1,0:T(8,128)(2,1)S(1)} custom-call(bf16[512,512]{1,0:T(8,128)(2,1)S(1)} %copy-done.7, bf16[2048,256]{1,0:T(8,128)(2,1)S(1)} %copy.136.kv_ref, bf16[128,2048]{1,0:T(8,128)(2,1)S(1)} %copy-done.10, s32[2048,1]{1,0:T(8,128)S(1)} %copy.137.place_ref, s32[1,512]{1,0:T(1,128)S(1)} %bitcast.156, s32[1,512]{1,0:T(1,128)S(1)} %bitcast.160), custom_call_target="tpu_custom_call" | custom-call | flops 4294967296 | bytes 1048576 | tf_op jit(solution)/shard_map/pallas_call | solution.py:277
  211.9 3.1 fusion.116
  215.0 7.1 %shard_map.289 = (f32[512,2048]{1,0:T(8,128)S(1)}, bf16[512,1024]{1,0:T(8,128)(2,1)S(1)}) custom-call(s32[8]{0:T(128)S(1)} %stack.190.order_ref, bf16[512,512]{1,0:T(8,128)(2,1)S(1)} %copy-done.62, bf16[512,512]{1,0:T(8,128)(2,1)S(1)} %copy-done.64, bf16[512,2048]{1,0:T(8,128)(2,1)} %constant_dynamic-update-slice_fusion.11.refs_2_, ...), custom_call_target="tpu_custom_call" | custom-call | flops 2147483648 | bytes 12582912 | tf_op jit(solution)/shard_map/pallas_call | solution.py:189
  224.9 2.1 collective-permute-start.41
  229.9 3.6 collective-permute-done.41
  233.8 2.4 collective-permute-start.40
  243.6 7.9 %collective-permute-done.42 = bf16[128,2048]{1,0:T(8,128)(2,1)S(1)} collective-permute-done((bf16[128,2048]{1,0:T(8,128)(2,1)S(1)}, bf16[128,2048]{1,0:T(8,128)(2,1)S(1)}, u32[]{:S(2)}, u32[]{:S(2)}) %collective-permute-start.42) | collective-permute-done | bytes 524320 | tf_op jit(solution)/shard_map/ppermute | solution.py:761
  264.6 4.6 collective-permute-done.44.refs_3_
  269.2 2.4 shard_map.291
  279.3 11.3 %shard_map.292 = (bf16[72,2176]{1,0:T(8,128)(2,1)S(1)}, bf16[72,2176]{1,0:T(8,128)(2,1)S(1)}, bf16[72,2176]{1,0:T(8,128)(2,1)S(1)}, bf16[72,2176]{1,0:T(8,128)(2...) custom-call(s32[1]{0:T(128)} %bitcast.68.refs_0_, ...), custom_call_target="tpu_custom_call" | custom-call | flops 5435817984 | bytes 9437184 | tf_op jit(solution)/shard_map/pallas_call | solution.py:567
  302.3 11.4 %shard_map.294 = (bf16[72,2176]{1,0:T(8,128)(2,1)S(1)}, bf16[72,2176]{1,0:T(8,128)(2,1)S(1)}, bf16[72,2176]{1,0:T(8,128)(2,1)S(1)}, bf16[72,2176]{1,0:T(8,128)(2...) custom-call(s32[1]{0:T(128)} %bitcast.68.refs_0_, ...), custom_call_target="tpu_custom_call" | custom-call | flops 5435817984 | bytes 9437184 | tf_op jit(solution)/shard_map/pallas_call | solution.py:567
  313.7 5.7 collective-permute-done.53.refs_4_
  328.6 11.7 %shard_map.296 = (bf16[72,2176]{1,0:T(8,128)(2,1)S(1)}, bf16[72,2176]{1,0:T(8,128)(2,1)}, bf16[72,2176]{1,0:T(8,128)(2,1)}, bf16[72,2176]{1,0:T(8,128)(2,1)}, bf...) custom-call(s32[1]{0:T(128)} %bitcast.68.refs_0_, ...), custom_call_target="tpu_custom_call" | custom-call | flops 5435817984 | bytes 9437184 | tf_op jit(solution)/shard_map/pallas_call | solution.py:567
  340.4 6.4 collective-permute-done.57.refs_4_
  348.8 2.3 collective-permute-start.60
  351.1 10.8 %shard_map.299 = (bf16[72,2176]{1,0:T(8,128)(2,1)S(1)}, bf16[72,2176]{1,0:T(8,128)(2,1)S(1)}, bf16[72,2176]{1,0:T(8,128)(2,1)S(1)}, bf16[72,2176]{1,0:T(8,128)(2...) custom-call(s32[1]{0:T(128)} %bitcast.68.refs_0_, ...), custom_call_target="tpu_custom_call" | custom-call | flops 5435817984 | bytes 9437184 | tf_op jit(solution)/shard_map/pallas_call | solution.py:567
  368.3 2.3 collective-permute-start.67
  370.8 6.6 collective-permute-done.65.refs_2_
  377.4 5.3 collective-permute-done.66.refs_3_
  383.2 4.0 collective-permute-start.69
  390.8 2.4 fusion.21
  394.0 3.5 collective-permute-done.71.refs_3_
  401.6 3.5 fusion.24
  405.8 5.4 collective-permute-done.74
  414.3 3.4 collective-permute-done.76
  425.9 2.9 convolution_convert_fusion.5
  428.8 2.9 convolution_convert_fusion.4
  434.3 4.1 collective-permute-done.80.refs_3_
  448.2 21.8 %shard_map.305 = (bf16[512,512]{1,0:T(8,128)(2,1)}, f32[2048,256]{1,0:T(8,128)}, f32[1,128]{1,0:T(1,128)}) custom-call(bf16[512,512]{1,0:T(8,128)(2,1)} %get-tuple-element.801.q_ref, bf16[512,512]{1,0:T(8,128)(2,1)} %get-tuple-element.802.grad_ref, f32[512,512]{1,0:T(8,128)} %get-tuple-element.803.proj_ref, bf16[2048,256]{1,0:T(8,128)(2,1)} %copy-done.6, ...), custom_call_target="tpu_custom_call" | custom-call | flops 5368709120 | bytes 2097152 | tf_op jit(solution)/shard_map/pallas_call | solution.py:362
  478.0 3.3 collective-permute-start.92
  481.3 22.3 %shard_map.307 = (bf16[512,512]{1,0:T(8,128)(2,1)}, f32[2048,256]{1,0:T(8,128)}, f32[1,128]{1,0:T(1,128)}) custom-call(bf16[512,512]{1,0:T(8,128)(2,1)} %get-tuple-element.826.q_ref, bf16[512,512]{1,0:T(8,128)(2,1)} %get-tuple-element.827.grad_ref, f32[512,512]{1,0:T(8,128)} %get-tuple-element.828.proj_ref, bf16[2048,256]{1,0:T(8,128)(2,1)} %copy-done.6, ...), custom_call_target="tpu_custom_call" | custom-call | flops 5368709120 | bytes 2097152 | tf_op jit(solution)/shard_map/pallas_call | solution.py:362
  516.9 5.8 fusion.27
  528.1 4.4 collective-permute-done.97
  544.8 2.4 add_convert_fusion.3
  547.9 3.3 fusion.39
  551.2 7.0 %collective-permute-done.101 = bf16[512,256]{1,0:T(8,128)(2,1)S(1)} collective-permute-done((bf16[512,256]{1,0:T(8,128)(2,1)}, bf16[512,256]{1,0:T(8,128)(2,1)S(1)}, u32[]{:S(2)}, u32[]{:S(2)}) %collective-permute-start.101) | collective-permute-done | bytes 262176 | tf_op jit(solution)/shard_map/ppermute | solution.py:761
  561.0 2.2 shard_map.309
  564.2 2.5 convolution_convert_fusion.3
  578.8 6.7 %convert_add_fusion.2 = f32[1024,768]{1,0:T(8,128)} fusion(bf16[1024,768]{1,0:T(8,128)(2,1)} %copy-done.177, bf16[1152,768]{1,0:T(8,128)(2,1)} %copy-done.163, bf16[1152,2048]{1,0:T(8,128)(2,1)} %copy-done.130, s32[]{:T(128)S(6)} %select_n.1034), kind=kOutput, calls=%fused_computation.9 | convolution fusion | flops 1813512192 | bytes 8847364 | tf_op jit(solution)/shard_map/rd,rf->df/dot_general | solution.py:1258
  587.8 4.6 shard_map.310
  600.8 2.4 collective-permute-start.109
  605.8 6.6 convert_add_fusion.1
  625.8 6.6 convert_add_fusion
  634.2 2.2 collective-permute-done.114
  643.3 4.0 collective-permute-start.118
  650.9 3.0 fusion.33
  655.5 3.1 shard_map.312
  (820 shorter events, 283.1 us)
Async XLA Ops:
  7.2 269.9 %all-gather.4.cloned.1.call-start = ((), (), s32[]{:S(2)}) async-start(), calls=%async_computation | async-start | bytes 4718592 | tf_op jit(solution)/shard_map/all_gather | solution.py:910
  7.9 269.1 %all-gather.6.cloned.1.call-start = ((), (), s32[]{:S(2)}) async-start(), calls=%async_computation.1 | async-start | bytes 4718592 | tf_op jit(solution)/shard_map/all_gather | solution.py:911
  20.3 256.8 %all-gather.8.cloned.1.call-start = ((), (), s32[]{:S(2)}) async-start(), calls=%async_computation.2 | async-start | bytes 4718592 | tf_op jit(solution)/shard_map/all_gather | solution.py:912
  32.3 31.3 %collective-permute-start.6 = (bf16[128,2048]{1,0:T(8,128)(2,1)S(1)}, bf16[128,2048]{1,0:T(8,128)(2,1)}, u32[]{:S(2)}, u32[]{:S(2)}) collective-permute-start(bf16[128,2048]{1,0:T(8,128)(2,1)S(1)} %copy-done.78), channel_id=1, source_target_pairs={{0,4},{1,5},{2,6},{3,7},{4,0},{5,1},{6,2},{7,3},{8,12},{9,13},{10,... | collective-permute-start | bytes 1572872 | tf_op jit(solution)/shard_map/ppermute | solution.py:761
  35.8 30.1 %collective-permute-start.7 = (bf16[128,2048]{1,0:T(8,128)(2,1)S(1)}, bf16[128,2048]{1,0:T(8,128)(2,1)}, u32[]{:S(2)}, u32[]{:S(2)}) collective-permute-start(bf16[128,2048]{1,0:T(8,128)(2,1)S(1)} %copy-done.78), channel_id=1, source_target_pairs={{0,2},{1,3},{2,0},{3,1},{4,6},{5,7},{6,4},{7,5},{8,10},{9,11},{10,... | collective-permute-start | bytes 1572872 | tf_op jit(solution)/shard_map/ppermute | solution.py:761
  38.8 30.4 %collective-permute-start.4 = (bf16[288,1280]{1,0:T(8,128)(2,1)}, bf16[288,1280]{1,0:T(8,128)(2,1)}, u32[]{:S(2)}, u32[]{:S(2)}) collective-permute-start(bf16[288,1280]{1,0:T(8,128)(2,1)} %shard_map.281.refs_0_), channel_id=1, source_target_pairs={{0,1},{1,0},{2,3},{3,2},{4,5},{5,4},{6,7},{7,6},{8,9},{9,8},{10,11... | collective-permute-start | bytes 2211848 | tf_op jit(solution)/shard_map/ppermute | solution.py:761
  41.5 62.8 %collective-permute-start.14 = (bf16[288,1280]{1,0:T(8,128)(2,1)}, bf16[288,1280]{1,0:T(8,128)(2,1)}, u32[]{:S(2)}, u32[]{:S(2)}) collective-permute-start(bf16[288,1280]{1,0:T(8,128)(2,1)} %shard_map.281.refs_0_), channel_id=1, source_target_pairs={{0,16},{16,0},{1,17},{17,1},{2,18},{18,2},{3,19},{19,3},{4,20},{20... | collective-permute-start | bytes 2211848 | tf_op jit(solution)/shard_map/ppermute | solution.py:772
  41.6 21.6 %collective-permute-start.11 = (bf16[160,1280]{1,0:T(8,128)(2,1)S(1)}, bf16[160,1280]{1,0:T(8,128)(2,1)S(1)}, u32[]{:S(2)}, u32[]{:S(2)}) collective-permute-start(bf16[160,1280]{1,0:T(8,128)(2,1)S(1)} %slice.405), channel_id=1, source_target_pairs={{0,8},{1,9},{2,10},{3,11},{4,12},{5,13},{6,14},{7,15},{8,0},{9,1},... | collective-permute-start | bytes 1228808 | tf_op jit(solution)/shard_map/ppermute | solution.py:761
  70.1 20.3 %collective-permute-start.5 = (bf16[160,1280]{1,0:T(8,128)(2,1)S(1)}, bf16[160,1280]{1,0:T(8,128)(2,1)S(1)}, u32[]{:S(2)}, u32[]{:S(2)}) collective-permute-start(bf16[160,1280]{1,0:T(8,128)(2,1)S(1)} %pad_maximum_fusion.14), channel_id=1, source_target_pairs={{0,8},{1,9},{2,10},{3,11},{4,12},{5,13},{6,14},{7,15},{8,0},{9,1},... | collective-permute-start | bytes 1228808 | tf_op jit(solution)/shard_map/ppermute | solution.py:761
  72.6 31.8 %collective-permute-start.15 = (bf16[288,1280]{1,0:T(8,128)(2,1)}, bf16[288,1280]{1,0:T(8,128)(2,1)}, u32[]{:S(2)}, u32[]{:S(2)}) collective-permute-start(bf16[288,1280]{1,0:T(8,128)(2,1)} %collective-permute-done.4.refs_1_), channel_id=1, source_target_pairs={{0,16},{16,0},{1,17},{17,1},{2,18},{18,2},{3,19},{19,3},{4,20},{20... | collective-permute-start | bytes 2211848 | tf_op jit(solution)/shard_map/ppermute | solution.py:772
  104.3 16.9 %collective-permute-start.18 = (bf16[128,2048]{1,0:T(8,128)(2,1)S(1)}, bf16[128,2048]{1,0:T(8,128)(2,1)S(1)}, u32[]{:S(2)}, u32[]{:S(2)}) collective-permute-start(bf16[128,2048]{1,0:T(8,128)(2,1)S(1)} %broadcast_select_fusion.2), channel_id=1, source_target_pairs={{0,1},{1,0},{2,3},{3,2},{4,5},{5,4},{6,7},{7,6},{8,9},{9,8},{10,11... | collective-permute-start | bytes 1572872 | tf_op jit(solution)/shard_map/ppermute | solution.py:761
  158.5 21.5 %collective-permute-start.25 = (bf16[128,2048]{1,0:T(8,128)(2,1)S(1)}, bf16[128,2048]{1,0:T(8,128)(2,1)S(1)}, u32[]{:S(2)}, u32[]{:S(2)}) collective-permute-start(bf16[128,2048]{1,0:T(8,128)(2,1)S(1)} %copy-done.3), channel_id=1, source_target_pairs={{0,4},{1,5},{2,6},{3,7},{4,8},{5,9},{6,10},{7,11},{8,12},{9,13},{1... | collective-permute-start | bytes 1572872 | tf_op jit(solution)/shard_map/ppermute | solution.py:764
  160.0 20.0 %collective-permute-start.26 = (bf16[72,2048]{1,0:T(8,128)(2,1)}, bf16[72,2048]{1,0:T(8,128)(2,1)S(1)}, u32[]{:S(2)}, u32[]{:S(2)}) collective-permute-start(bf16[72,2048]{1,0:T(8,128)(2,1)} %copy-done.60), channel_id=1, source_target_pairs={{0,1},{1,0},{2,3},{3,2},{4,5},{5,4},{6,7},{7,6},{8,9},{9,8},{10,11... | collective-permute-start | bytes 884744 | tf_op jit(solution)/shard_map/ppermute | solution.py:761
  161.5 18.5 %collective-permute-start.27 = (bf16[72,2048]{1,0:T(8,128)(2,1)}, bf16[72,2048]{1,0:T(8,128)(2,1)S(1)}, u32[]{:S(2)}, u32[]{:S(2)}) collective-permute-start(bf16[72,2048]{1,0:T(8,128)(2,1)} %copy-done.59), channel_id=1, source_target_pairs={{0,2},{1,3},{2,0},{3,1},{4,6},{5,7},{6,4},{7,5},{8,10},{9,11},{10,... | collective-permute-start | bytes 884744 | tf_op jit(solution)/shard_map/ppermute | solution.py:761
  162.3 17.7 %collective-permute-start.28 = (bf16[72,2048]{1,0:T(8,128)(2,1)}, bf16[72,2048]{1,0:T(8,128)(2,1)S(1)}, u32[]{:S(2)}, u32[]{:S(2)}) collective-permute-start(bf16[72,2048]{1,0:T(8,128)(2,1)} %copy-done.58), channel_id=1, source_target_pairs={{0,3},{1,2},{2,1},{3,0},{4,7},{5,6},{6,5},{7,4},{8,11},{9,10},{10,... | collective-permute-start | bytes 884744 | tf_op jit(solution)/shard_map/ppermute | solution.py:761
  163.5 16.5 %collective-permute-start.29 = (bf16[64,2048]{1,0:T(8,128)(2,1)}, bf16[64,2048]{1,0:T(8,128)(2,1)S(1)}, u32[]{:S(2)}, u32[]{:S(2)}) collective-permute-start(bf16[64,2048]{1,0:T(8,128)(2,1)} %copy-done.140), channel_id=1, source_target_pairs={{0,1},{1,0},{2,3},{3,2},{4,5},{5,4},{6,7},{7,6},{8,9},{9,8},{10,11... | collective-permute-start | bytes 786440 | tf_op jit(solution)/shard_map/ppermute | solution.py:761
  183.4 18.2 %collective-permute-start.34 = (bf16[512,2048]{1,0:T(8,128)(2,1)}, bf16[512,2048]{1,0:T(8,128)(2,1)}, u32[]{:S(2)}, u32[]{:S(2)}) collective-permute-start(bf16[512,2048]{1,0:T(8,128)(2,1)} %constant_dynamic-update-slice_fusion.11.refs_2_), channel_id=1, source_target_pairs={{0,16},{16,0},{1,17},{17,1},{2,18},{18,2},{3,19},{19,3},{4,20},{20... | collective-permute-start | bytes 6291464 | tf_op jit(solution)/shard_map/ppermute | solution.py:772
  183.5 18.2 %collective-permute-start.30 = (bf16[128,2048]{1,0:T(8,128)(2,1)S(1)}, bf16[128,2048]{1,0:T(8,128)(2,1)}, u32[]{:S(2)}, u32[]{:S(2)}) collective-permute-start(bf16[128,2048]{1,0:T(8,128)(2,1)S(1)} %collective-permute-done.25.refs_1_), channel_id=1, source_target_pairs={{0,4},{1,5},{2,6},{3,7},{4,8},{5,9},{6,10},{7,11},{8,12},{9,13},{1... | collective-permute-start | bytes 1572872 | tf_op jit(solution)/shard_map/ppermute | solution.py:764
  204.1 19.0 %collective-permute-start.35 = (bf16[128,2048]{1,0:T(8,128)(2,1)}, bf16[128,2048]{1,0:T(8,128)(2,1)S(1)}, u32[]{:S(2)}, u32[]{:S(2)}) collective-permute-start(bf16[128,2048]{1,0:T(8,128)(2,1)} %collective-permute-done.30.refs_1_), channel_id=1, source_target_pairs={{0,4},{1,5},{2,6},{3,7},{4,8},{5,9},{6,10},{7,11},{8,12},{9,13},{1... | collective-permute-start | bytes 1572872 | tf_op jit(solution)/shard_map/ppermute | solution.py:764
  238.0 18.1 %collective-permute-start.62 = (bf16[72,2048]{1,0:T(8,128)(2,1)S(1)}, bf16[72,2048]{1,0:T(8,128)(2,1)S(1)}, u32[]{:S(2)}, u32[]{:S(2)}) collective-permute-start(bf16[72,2048]{1,0:T(8,128)(2,1)S(1)} %get-tuple-element.707), channel_id=1, source_target_pairs={{0,1},{1,0},{2,3},{3,2},{4,5},{5,4},{6,7},{7,6},{8,9},{9,8},{10,11... | collective-permute-start | bytes 884744 | tf_op jit(solution)/shard_map/ppermute | solution.py:761
  238.1 18.0 %collective-permute-start.63 = (bf16[72,2048]{1,0:T(8,128)(2,1)S(1)}, bf16[72,2048]{1,0:T(8,128)(2,1)S(1)}, u32[]{:S(2)}, u32[]{:S(2)}) collective-permute-start(bf16[72,2048]{1,0:T(8,128)(2,1)S(1)} %get-tuple-element.708), channel_id=1, source_target_pairs={{0,2},{1,3},{2,0},{3,1},{4,6},{5,7},{6,4},{7,5},{8,10},{9,11},{10,... | collective-permute-start | bytes 884744 | tf_op jit(solution)/shard_map/ppermute | solution.py:761
  240.2 16.0 %collective-permute-start.64 = (bf16[72,2048]{1,0:T(8,128)(2,1)S(1)}, bf16[72,2048]{1,0:T(8,128)(2,1)S(1)}, u32[]{:S(2)}, u32[]{:S(2)}) collective-permute-start(bf16[72,2048]{1,0:T(8,128)(2,1)S(1)} %get-tuple-element.709), channel_id=1, source_target_pairs={{0,3},{1,2},{2,1},{3,0},{4,7},{5,6},{6,5},{7,4},{8,11},{9,10},{10,... | collective-permute-start | bytes 884744 | tf_op jit(solution)/shard_map/ppermute | solution.py:761
  272.4 18.4 %collective-permute-start.50 = (bf16[128,2048]{1,0:T(8,128)(2,1)}, bf16[128,2048]{1,0:T(8,128)(2,1)}, u32[]{:S(2)}, u32[]{:S(2)}) collective-permute-start(bf16[128,2048]{1,0:T(8,128)(2,1)} %collective-permute-done.46.refs_1_), channel_id=1, source_target_pairs={{0,4},{1,5},{2,6},{3,7},{4,8},{5,9},{6,10},{7,11},{8,12},{9,13},{1... | collective-permute-start | bytes 1572872 | tf_op jit(solution)/shard_map/ppermute | solution.py:764
  273.6 17.1 %collective-permute-start.47 = (bf16[72,2048]{1,0:T(8,128)(2,1)}, bf16[72,2048]{1,0:T(8,128)(2,1)}, u32[]{:S(2)}, u32[]{:S(2)}) collective-permute-start(bf16[72,2048]{1,0:T(8,128)(2,1)} %get-tuple-element.590), channel_id=1, source_target_pairs={{0,1},{1,0},{2,3},{3,2},{4,5},{5,4},{6,7},{7,6},{8,9},{9,8},{10,11... | collective-permute-start | bytes 884744 | tf_op jit(solution)/shard_map/ppermute | solution.py:761
  274.4 16.3 %collective-permute-start.48 = (bf16[72,2048]{1,0:T(8,128)(2,1)}, bf16[72,2048]{1,0:T(8,128)(2,1)}, u32[]{:S(2)}, u32[]{:S(2)}) collective-permute-start(bf16[72,2048]{1,0:T(8,128)(2,1)} %get-tuple-element.591), channel_id=1, source_target_pairs={{0,2},{1,3},{2,0},{3,1},{4,6},{5,7},{6,4},{7,5},{8,10},{9,11},{10,... | collective-permute-start | bytes 884744 | tf_op jit(solution)/shard_map/ppermute | solution.py:761
  275.0 15.7 %collective-permute-start.49 = (bf16[72,2048]{1,0:T(8,128)(2,1)}, bf16[72,2048]{1,0:T(8,128)(2,1)}, u32[]{:S(2)}, u32[]{:S(2)}) collective-permute-start(bf16[72,2048]{1,0:T(8,128)(2,1)} %get-tuple-element.592), channel_id=1, source_target_pairs={{0,3},{1,2},{2,1},{3,0},{4,7},{5,6},{6,5},{7,4},{8,11},{9,10},{10,... | collective-permute-start | bytes 884744 | tf_op jit(solution)/shard_map/ppermute | solution.py:761
  292.7 21.0 %collective-permute-start.51 = (bf16[72,4224]{1,0:T(8,128)(2,1)S(1)}, bf16[72,4224]{1,0:T(8,128)(2,1)S(1)}, u32[]{:S(2)}, u32[]{:S(2)}) collective-permute-start(bf16[72,4224]{1,0:T(8,128)(2,1)S(1)} %get-tuple-element.629), channel_id=1, source_target_pairs={{0,1},{1,0},{2,3},{3,2},{4,5},{5,4},{6,7},{7,6},{8,9},{9,8},{10,11... | collective-permute-start | bytes 1824776 | tf_op jit(solution)/shard_map/ppermute | solution.py:761
  293.6 20.2 %collective-permute-start.52 = (bf16[72,4224]{1,0:T(8,128)(2,1)S(1)}, bf16[72,4224]{1,0:T(8,128)(2,1)S(1)}, u32[]{:S(2)}, u32[]{:S(2)}) collective-permute-start(bf16[72,4224]{1,0:T(8,128)(2,1)S(1)} %get-tuple-element.630), channel_id=1, source_target_pairs={{0,2},{1,3},{2,0},{3,1},{4,6},{5,7},{6,4},{7,5},{8,10},{9,11},{10,... | collective-permute-start | bytes 1824776 | tf_op jit(solution)/shard_map/ppermute | solution.py:761
  294.2 25.3 %collective-permute-start.53 = (bf16[72,4224]{1,0:T(8,128)(2,1)S(1)}, bf16[72,4224]{1,0:T(8,128)(2,1)S(1)}, u32[]{:S(2)}, u32[]{:S(2)}) collective-permute-start(bf16[72,4224]{1,0:T(8,128)(2,1)S(1)} %get-tuple-element.631), channel_id=1, source_target_pairs={{0,3},{1,2},{2,1},{3,0},{4,7},{5,6},{6,5},{7,4},{8,11},{9,10},{10,... | collective-permute-start | bytes 1824776 | tf_op jit(solution)/shard_map/ppermute | solution.py:761
  296.3 17.5 %collective-permute-start.54 = (bf16[128,2048]{1,0:T(8,128)(2,1)}, bf16[128,2048]{1,0:T(8,128)(2,1)S(1)}, u32[]{:S(2)}, u32[]{:S(2)}) collective-permute-start(bf16[128,2048]{1,0:T(8,128)(2,1)} %collective-permute-done.50.refs_1_), channel_id=1, source_target_pairs={{0,4},{1,5},{2,6},{3,7},{4,8},{5,9},{6,10},{7,11},{8,12},{9,13},{1... | collective-permute-start | bytes 1572872 | tf_op jit(solution)/shard_map/ppermute | solution.py:764
  320.5 19.9 %collective-permute-start.55 = (bf16[72,4224]{1,0:T(8,128)(2,1)S(1)}, bf16[72,4224]{1,0:T(8,128)(2,1)S(1)}, u32[]{:S(2)}, u32[]{:S(2)}) collective-permute-start(bf16[72,4224]{1,0:T(8,128)(2,1)S(1)} %get-tuple-element.666), channel_id=1, source_target_pairs={{0,1},{1,0},{2,3},{3,2},{4,5},{5,4},{6,7},{7,6},{8,9},{9,8},{10,11... | collective-permute-start | bytes 1824776 | tf_op jit(solution)/shard_map/ppermute | solution.py:761
  320.5 19.9 %collective-permute-start.56 = (bf16[72,4224]{1,0:T(8,128)(2,1)S(1)}, bf16[72,4224]{1,0:T(8,128)(2,1)S(1)}, u32[]{:S(2)}, u32[]{:S(2)}) collective-permute-start(bf16[72,4224]{1,0:T(8,128)(2,1)S(1)} %get-tuple-element.667), channel_id=1, source_target_pairs={{0,2},{1,3},{2,0},{3,1},{4,6},{5,7},{6,4},{7,5},{8,10},{9,11},{10,... | collective-permute-start | bytes 1824776 | tf_op jit(solution)/shard_map/ppermute | solution.py:761
  322.1 24.7 %collective-permute-start.57 = (bf16[72,4224]{1,0:T(8,128)(2,1)S(1)}, bf16[72,4224]{1,0:T(8,128)(2,1)S(1)}, u32[]{:S(2)}, u32[]{:S(2)}) collective-permute-start(bf16[72,4224]{1,0:T(8,128)(2,1)S(1)} %get-tuple-element.668), channel_id=1, source_target_pairs={{0,3},{1,2},{2,1},{3,0},{4,7},{5,6},{6,5},{7,4},{8,11},{9,10},{10,... | collective-permute-start | bytes 1824776 | tf_op jit(solution)/shard_map/ppermute | solution.py:761
  347.2 18.3 %collective-permute-start.61 = (bf16[128,2176]{1,0:T(8,128)(2,1)S(1)}, bf16[128,2176]{1,0:T(8,128)(2,1)S(1)}, u32[]{:S(2)}, u32[]{:S(2)}) collective-permute-start(bf16[128,2176]{1,0:T(8,128)(2,1)S(1)} %shard_map.297), channel_id=1, source_target_pairs={{0,4},{1,5},{2,6},{3,7},{4,8},{5,9},{6,10},{7,11},{8,12},{9,13},{1... | collective-permute-start | bytes 1671176 | tf_op jit(solution)/shard_map/ppermute | solution.py:764
  347.5 18.0 %collective-permute-start.58 = (bf16[72,2176]{1,0:T(8,128)(2,1)}, bf16[72,2176]{1,0:T(8,128)(2,1)S(1)}, u32[]{:S(2)}, u32[]{:S(2)}) collective-permute-start(bf16[72,2176]{1,0:T(8,128)(2,1)} %get-tuple-element.697), channel_id=1, source_target_pairs={{0,1},{1,0},{2,3},{3,2},{4,5},{5,4},{6,7},{7,6},{8,9},{9,8},{10,11... | collective-permute-start | bytes 940040 | tf_op jit(solution)/shard_map/ppermute | solution.py:761
  347.6 18.0 %collective-permute-start.59 = (bf16[72,2176]{1,0:T(8,128)(2,1)}, bf16[72,2176]{1,0:T(8,128)(2,1)S(1)}, u32[]{:S(2)}, u32[]{:S(2)}) collective-permute-start(bf16[72,2176]{1,0:T(8,128)(2,1)} %get-tuple-element.698), channel_id=1, source_target_pairs={{0,2},{1,3},{2,0},{3,1},{4,6},{5,7},{6,4},{7,5},{8,10},{9,11},{10,... | collective-permute-start | bytes 940040 | tf_op jit(solution)/shard_map/ppermute | solution.py:761
  348.8 16.8 %collective-permute-start.60 = (bf16[72,2176]{1,0:T(8,128)(2,1)}, bf16[72,2176]{1,0:T(8,128)(2,1)S(1)}, u32[]{:S(2)}, u32[]{:S(2)}) collective-permute-start(bf16[72,2176]{1,0:T(8,128)(2,1)} %get-tuple-element.699), channel_id=1, source_target_pairs={{0,3},{1,2},{2,1},{3,0},{4,7},{5,6},{6,5},{7,4},{8,11},{9,10},{10,... | collective-permute-start | bytes 940040 | tf_op jit(solution)/shard_map/ppermute | solution.py:761
  366.0 16.7 %collective-permute-start.68 = (bf16[128,2176]{1,0:T(8,128)(2,1)S(1)}, bf16[128,2176]{1,0:T(8,128)(2,1)S(1)}, u32[]{:S(2)}, u32[]{:S(2)}) collective-permute-start(bf16[128,2176]{1,0:T(8,128)(2,1)S(1)} %shard_map.300), channel_id=1, source_target_pairs={{0,4},{1,5},{2,6},{3,7},{4,8},{5,9},{6,10},{7,11},{8,12},{9,13},{1... | collective-permute-start | bytes 1671176 | tf_op jit(solution)/shard_map/ppermute | solution.py:764
  367.2 15.6 %collective-permute-start.66 = (bf16[72,2176]{1,0:T(8,128)(2,1)S(1)}, bf16[72,2176]{1,0:T(8,128)(2,1)S(1)}, u32[]{:S(2)}, u32[]{:S(2)}) collective-permute-start(bf16[72,2176]{1,0:T(8,128)(2,1)S(1)} %get-tuple-element.736), channel_id=1, source_target_pairs={{0,2},{1,3},{2,0},{3,1},{4,6},{5,7},{6,4},{7,5},{8,10},{9,11},{10,... | collective-permute-start | bytes 940040 | tf_op jit(solution)/shard_map/ppermute | solution.py:761
  393.2 27.0 %collective-permute-start.73 = (bf16[1024,768]{1,0:T(8,128)(2,1)S(1)}, bf16[1024,768]{1,0:T(8,128)(2,1)S(1)}, u32[]{:S(2)}, u32[]{:S(2)}) collective-permute-start(bf16[1024,768]{1,0:T(8,128)(2,1)S(1)} %fusion.21), channel_id=1, source_target_pairs={{0,16},{16,0},{1,17},{17,1},{2,18},{18,2},{3,19},{19,3},{4,20},{20... | collective-permute-start | bytes 4718600 | tf_op jit(solution)/shard_map/ppermute | solution.py:772
  420.2 18.3 %collective-permute-start.82 = (bf16[512,2048]{1,0:T(8,128)(2,1)S(1)}, bf16[512,2048]{1,0:T(8,128)(2,1)S(1)}, u32[]{:S(2)}, u32[]{:S(2)}) collective-permute-start(bf16[512,2048]{1,0:T(8,128)(2,1)S(1)} %convolution_convert_fusion), channel_id=1, source_target_pairs={{0,16},{16,0},{1,17},{17,1},{2,18},{18,2},{3,19},{19,3},{4,20},{20... | collective-permute-start | bytes 6291464 | tf_op jit(solution)/shard_map/ppermute | solution.py:772
  420.3 18.2 %collective-permute-start.78 = (bf16[128,2048]{1,0:T(8,128)(2,1)S(1)}, bf16[128,2048]{1,0:T(8,128)(2,1)S(1)}, u32[]{:S(2)}, u32[]{:S(2)}) collective-permute-start(bf16[128,2048]{1,0:T(8,128)(2,1)S(1)} %shard_map.302), channel_id=1, source_target_pairs={{0,4},{1,5},{2,6},{3,7},{4,8},{5,9},{6,10},{7,11},{8,12},{9,13},{1... | collective-permute-start | bytes 1572872 | tf_op jit(solution)/shard_map/ppermute | solution.py:764
  441.8 28.2 %collective-permute-start.83 = (bf16[128,2048]{1,0:T(8,128)(2,1)S(1)}, bf16[128,2048]{1,0:T(8,128)(2,1)S(1)}, u32[]{:S(2)}, u32[]{:S(2)}) collective-permute-start(bf16[128,2048]{1,0:T(8,128)(2,1)S(1)} %shard_map.304), channel_id=1, source_target_pairs={{0,4},{1,5},{2,6},{3,7},{4,8},{5,9},{6,10},{7,11},{8,12},{9,13},{1... | collective-permute-start | bytes 1572872 | tf_op jit(solution)/shard_map/ppermute | solution.py:764
  442.2 27.8 %collective-permute-start.87 = (bf16[128,2048]{1,0:T(8,128)(2,1)}, bf16[128,2048]{1,0:T(8,128)(2,1)}, u32[]{:S(2)}, u32[]{:S(2)}) collective-permute-start(bf16[128,2048]{1,0:T(8,128)(2,1)} %get-tuple-element.800), channel_id=1, source_target_pairs={{0,1},{1,0},{2,3},{3,2},{4,5},{5,4},{6,7},{7,6},{8,9},{9,8},{10,11... | collective-permute-start | bytes 1572872 | tf_op jit(solution)/shard_map/ppermute | solution.py:761
  444.7 25.3 %collective-permute-start.84 = (bf16[72,2048]{1,0:T(8,128)(2,1)}, bf16[72,2048]{1,0:T(8,128)(2,1)S(1)}, u32[]{:S(2)}, u32[]{:S(2)}) collective-permute-start(bf16[72,2048]{1,0:T(8,128)(2,1)} %copy-done.38), channel_id=1, source_target_pairs={{0,1},{1,0},{2,3},{3,2},{4,5},{5,4},{6,7},{7,6},{8,9},{9,8},{10,11... | collective-permute-start | bytes 884744 | tf_op jit(solution)/shard_map/ppermute | solution.py:761
  445.6 24.3 %collective-permute-start.85 = (bf16[72,2048]{1,0:T(8,128)(2,1)}, bf16[72,2048]{1,0:T(8,128)(2,1)}, u32[]{:S(2)}, u32[]{:S(2)}) collective-permute-start(bf16[72,2048]{1,0:T(8,128)(2,1)} %copy-done.37), channel_id=1, source_target_pairs={{0,2},{1,3},{2,0},{3,1},{4,6},{5,7},{6,4},{7,5},{8,10},{9,11},{10,... | collective-permute-start | bytes 884744 | tf_op jit(solution)/shard_map/ppermute | solution.py:761
  446.4 23.6 %collective-permute-start.86 = (bf16[72,2048]{1,0:T(8,128)(2,1)}, bf16[72,2048]{1,0:T(8,128)(2,1)}, u32[]{:S(2)}, u32[]{:S(2)}) collective-permute-start(bf16[72,2048]{1,0:T(8,128)(2,1)} %copy-done.36), channel_id=1, source_target_pairs={{0,3},{1,2},{2,1},{3,0},{4,7},{5,6},{6,5},{7,4},{8,11},{9,10},{10,... | collective-permute-start | bytes 884744 | tf_op jit(solution)/shard_map/ppermute | solution.py:761
  473.7 33.3 %collective-permute-start.88 = (bf16[128,2048]{1,0:T(8,128)(2,1)S(1)}, bf16[128,2048]{1,0:T(8,128)(2,1)S(1)}, u32[]{:S(2)}, u32[]{:S(2)}) collective-permute-start(bf16[128,2048]{1,0:T(8,128)(2,1)S(1)} %shard_map.306), channel_id=1, source_target_pairs={{0,4},{1,5},{2,6},{3,7},{4,8},{5,9},{6,10},{7,11},{8,12},{9,13},{1... | collective-permute-start | bytes 1572872 | tf_op jit(solution)/shard_map/ppermute | solution.py:764
  474.5 32.5 %collective-permute-start.89 = (bf16[72,2048]{1,0:T(8,128)(2,1)}, bf16[72,2048]{1,0:T(8,128)(2,1)S(1)}, u32[]{:S(2)}, u32[]{:S(2)}) collective-permute-start(bf16[72,2048]{1,0:T(8,128)(2,1)} %copy-done.35), channel_id=1, source_target_pairs={{0,1},{1,0},{2,3},{3,2},{4,5},{5,4},{6,7},{7,6},{8,9},{9,8},{10,11... | collective-permute-start | bytes 884744 | tf_op jit(solution)/shard_map/ppermute | solution.py:761
  475.9 31.1 %collective-permute-start.90 = (bf16[72,2048]{1,0:T(8,128)(2,1)}, bf16[72,2048]{1,0:T(8,128)(2,1)S(1)}, u32[]{:S(2)}, u32[]{:S(2)}) collective-permute-start(bf16[72,2048]{1,0:T(8,128)(2,1)} %copy-done.34), channel_id=1, source_target_pairs={{0,2},{1,3},{2,0},{3,1},{4,6},{5,7},{6,4},{7,5},{8,10},{9,11},{10,... | collective-permute-start | bytes 884744 | tf_op jit(solution)/shard_map/ppermute | solution.py:761
  476.2 30.8 %collective-permute-start.91 = (bf16[72,2048]{1,0:T(8,128)(2,1)}, bf16[72,2048]{1,0:T(8,128)(2,1)}, u32[]{:S(2)}, u32[]{:S(2)}) collective-permute-start(bf16[72,2048]{1,0:T(8,128)(2,1)} %copy-done.33), channel_id=1, source_target_pairs={{0,3},{1,2},{2,1},{3,0},{4,7},{5,6},{6,5},{7,4},{8,11},{9,10},{10,... | collective-permute-start | bytes 884744 | tf_op jit(solution)/shard_map/ppermute | solution.py:761
  478.0 29.0 %collective-permute-start.92 = (bf16[64,2048]{1,0:T(8,128)(2,1)}, bf16[64,2048]{1,0:T(8,128)(2,1)}, u32[]{:S(2)}, u32[]{:S(2)}) collective-permute-start(bf16[64,2048]{1,0:T(8,128)(2,1)} %get-tuple-element.823), channel_id=1, source_target_pairs={{0,8},{1,9},{2,10},{3,11},{4,12},{5,13},{6,14},{7,15},{8,0},{9,1},... | collective-permute-start | bytes 786440 | tf_op jit(solution)/shard_map/ppermute | solution.py:761
  510.3 22.2 %collective-permute-start.93 = (bf16[1024,768]{1,0:T(8,128)(2,1)}, bf16[1024,768]{1,0:T(8,128)(2,1)}, u32[]{:S(2)}, u32[]{:S(2)}) collective-permute-start(bf16[1024,768]{1,0:T(8,128)(2,1)} %fusion.24), channel_id=1, source_target_pairs={{0,16},{16,0},{1,17},{17,1},{2,18},{18,2},{3,19},{19,3},{4,20},{20... | collective-permute-start | bytes 4718600 | tf_op jit(solution)/shard_map/ppermute | solution.py:772
  512.2 20.3 %collective-permute-start.96 = (bf16[1024,640]{1,0:T(8,128)(2,1)}, bf16[1024,640]{1,0:T(8,128)(2,1)}, u32[]{:S(2)}, u32[]{:S(2)}) collective-permute-start(bf16[1024,640]{1,0:T(8,128)(2,1)} %pad_maximum_fusion.1), channel_id=1, source_target_pairs={{0,16},{16,0},{1,17},{17,1},{2,18},{18,2},{3,19},{19,3},{4,20},{20... | collective-permute-start | bytes 3932168 | tf_op jit(solution)/shard_map/ppermute | solution.py:772
  512.7 19.8 %collective-permute-start.94 = (bf16[128,2048]{1,0:T(8,128)(2,1)}, bf16[128,2048]{1,0:T(8,128)(2,1)}, u32[]{:S(2)}, u32[]{:S(2)}) collective-permute-start(bf16[128,2048]{1,0:T(8,128)(2,1)} %get-tuple-element.852), channel_id=1, source_target_pairs={{0,1},{1,0},{2,3},{3,2},{4,5},{5,4},{6,7},{7,6},{8,9},{9,8},{10,11... | collective-permute-start | bytes 1572872 | tf_op jit(solution)/shard_map/ppermute | solution.py:761
  513.8 18.7 %collective-permute-start.97 = (bf16[512,256]{1,0:T(8,128)(2,1)}, bf16[512,256]{1,0:T(8,128)(2,1)}, u32[]{:S(2)}, u32[]{:S(2)}) collective-permute-start(bf16[512,256]{1,0:T(8,128)(2,1)} %get-tuple-element.858), channel_id=1, source_target_pairs={{0,1},{1,0},{2,3},{3,2},{4,5},{5,4},{6,7},{7,6},{8,9},{9,8},{10,11... | collective-permute-start | bytes 786440 | tf_op jit(solution)/shard_map/ppermute | solution.py:761
  537.8 21.2 %collective-permute-start.98 = (bf16[768,1024]{1,0:T(8,128)(2,1)}, bf16[768,1024]{1,0:T(8,128)(2,1)}, u32[]{:S(2)}, u32[]{:S(2)}) collective-permute-start(bf16[768,1024]{1,0:T(8,128)(2,1)} %fusion.27), channel_id=1, source_target_pairs={{0,16},{16,0},{1,17},{17,1},{2,18},{18,2},{3,19},{19,3},{4,20},{20... | collective-permute-start | bytes 4718600 | tf_op jit(solution)/shard_map/ppermute | solution.py:772
  537.8 21.2 %collective-permute-start.100 = (bf16[1024,512]{1,0:T(8,128)(2,1)}, bf16[1024,512]{1,0:T(8,128)(2,1)}, u32[]{:S(2)}, u32[]{:S(2)}) collective-permute-start(bf16[1024,512]{1,0:T(8,128)(2,1)} %convolution_convert_fusion.1), channel_id=1, source_target_pairs={{0,16},{16,0},{1,17},{17,1},{2,18},{18,2},{3,19},{19,3},{4,20},{20... | collective-permute-start | bytes 3145736 | tf_op jit(solution)/shard_map/ppermute | solution.py:772
  542.7 16.3 %collective-permute-start.99 = (bf16[256,640]{1,0:T(8,128)(2,1)}, bf16[256,640]{1,0:T(8,128)(2,1)S(1)}, u32[]{:S(2)}, u32[]{:S(2)}) collective-permute-start(bf16[256,640]{1,0:T(8,128)(2,1)} %pad_maximum_fusion.16), channel_id=1, source_target_pairs={{0,1},{1,0},{2,3},{3,2},{4,5},{5,4},{6,7},{7,6},{8,9},{9,8},{10,11... | collective-permute-start | bytes 983048 | tf_op jit(solution)/shard_map/ppermute | solution.py:761
  573.9 18.5 %collective-permute-start.103 = (bf16[128,2048]{1,0:T(8,128)(2,1)}, bf16[128,2048]{1,0:T(8,128)(2,1)}, u32[]{:S(2)}, u32[]{:S(2)}) collective-permute-start(bf16[128,2048]{1,0:T(8,128)(2,1)} %add_convert_fusion.3), channel_id=1, source_target_pairs={{2,16},{3,17},{6,20},{7,21},{10,24},{11,25},{14,28},{15,29},{16,2}... | collective-permute-start | bytes 1572872 | tf_op jit(solution)/shard_map/ppermute | solution.py:1089
  575.5 19.1 %collective-permute-start.107 = (bf16[1024,384]{1,0:T(8,128)(2,1)}, bf16[1024,384]{1,0:T(8,128)(2,1)}, u32[]{:S(2)}, u32[]{:S(2)}) collective-permute-start(bf16[1024,384]{1,0:T(8,128)(2,1)} %pad_maximum_fusion.8), channel_id=1, source_target_pairs={{0,16},{16,0},{1,17},{17,1},{2,18},{18,2},{3,19},{19,3},{4,20},{20... | collective-permute-start | bytes 2359304 | tf_op jit(solution)/shard_map/ppermute | solution.py:772
  576.8 16.6 %collective-permute-start.104 = (bf16[256,640]{1,0:T(8,128)(2,1)}, bf16[256,640]{1,0:T(8,128)(2,1)}, u32[]{:S(2)}, u32[]{:S(2)}) collective-permute-start(bf16[256,640]{1,0:T(8,128)(2,1)} %pad_maximum_fusion.17), channel_id=1, source_target_pairs={{0,1},{1,0},{2,3},{3,2},{4,5},{5,4},{6,7},{7,6},{8,9},{9,8},{10,11... | collective-permute-start | bytes 983048 | tf_op jit(solution)/shard_map/ppermute | solution.py:761
  577.9 16.7 %collective-permute-start.105 = (bf16[256,640]{1,0:T(8,128)(2,1)}, bf16[256,640]{1,0:T(8,128)(2,1)}, u32[]{:S(2)}, u32[]{:S(2)}) collective-permute-start(bf16[256,640]{1,0:T(8,128)(2,1)} %add_convert_fusion.7), channel_id=1, source_target_pairs={{0,8},{1,9},{2,10},{3,11},{4,12},{5,13},{6,14},{7,15},{8,0},{9,1},... | collective-permute-start | bytes 983048 | tf_op jit(solution)/shard_map/ppermute | solution.py:761
  620.9 16.6 %collective-permute-start.115 = (bf16[128,2048]{1,0:T(8,128)(2,1)}, bf16[128,2048]{1,0:T(8,128)(2,1)S(1)}, u32[]{:S(2)}, u32[]{:S(2)}) collective-permute-start(bf16[128,2048]{1,0:T(8,128)(2,1)} %pad_maximum_fusion.12), channel_id=1, source_target_pairs={{0,4},{1,5},{2,6},{3,7},{4,0},{5,1},{6,2},{7,3},{8,12},{9,13},{10,... | collective-permute-start | bytes 1572872 | tf_op jit(solution)/shard_map/ppermute | solution.py:761
  (243 other events, 2213.7 us)
Sparse Core Ops, SparseCore 0:
  9.6 14.8 all-gather.3
  26.0 13.2 all-gather.5
  184.3 12.4 all-gather.7
